TPU v7x, 512 devices: a whole 4x8x8 slice. The times are simulated.
512 devices in a mesh: ctx: 16 (over x, y_hi, core), exp: 8 (over z), hid: 4 (over y_lo).
Axes of the slice: x: 4, y: 8 (y_hi: 2, y_lo: 4; y = y_hi * 4 + y_lo), z: 8, core: 2. Of those that a mesh axis runs over, the one named last changes fastest.
Arguments:
- queries: bfloat16 [2048, 4096], P('ctx', ('exp', 'hid')), may hold values from -16 to 16
- key_heads: bfloat16 [2048, 1024], P('ctx', 'exp'), may hold values from -16 to 16
- value_heads: bfloat16 [2048, 1024], P('ctx', 'exp'), may hold values from -8 to 8
- residual: bfloat16 [2048, 4096], P(('ctx', 'exp'), 'hid'), may hold values from -3 to 3
- out_weight: bfloat16 [4096, 4096], P(('exp', 'hid')), may hold values from -0.09375 to 0.09375
- norm_gain: float32 [4096], P('hid'), may hold values from 0.1 to 1.9
- gate_weight: bfloat16 [8, 4096, 8192], P('exp', 'hid', 'ctx'), may hold values from -0.09375 to 0.09375
- up_weight: bfloat16 [8, 4096, 8192], P('exp', 'hid', 'ctx'), may hold values from -0.09375 to 0.09375
- down_weight: bfloat16 [8, 8192, 4096], P('exp', 'ctx', 'hid'), may hold values from -0.0625 to 0.0625
- expert_ids: int32 [2048, 2], P(('ctx', 'exp')), may hold values from 0 to 7, all different within a row; in each aligned block of 16 rows (0 to 15, 16 to 31, ...) at most 6 rows name the same one
- expert_weights: float32 [2048, 2], P(('ctx', 'exp')), may hold values from 0.5 to 2
Outputs:
- layer_out: bfloat16 [2048, 4096], P(('ctx', 'exp'), 'hid')
Inputs may be any that keep to these rules, and one draw needn't show every extreme that they name: `expert_ids`: each row names 2 different experts. Within each aligned block of 16 rows no expert is named by more than 6 rows, a bound that some block reaches.
All inputs are finite; a program needn't handle non-finite values.
Results may differ from a plain program's by a relative error of at most 0.015.
Values may be sent and summed in bfloat16 or wider, within the bound.
No kernel may reach another device: no remote copies, remote signals or barrier semaphores. Data moves between devices by JAX's collectives and lax.ppermute only.
A program may use at most 64 MiB of HBM per device.

v0:
```python
import math

import jax
import jax.numpy as jnp
from jax import lax
from jax.sharding import PartitionSpec as P

HEADS = 32
KV_HEADS = 8
HEAD = 128
D = 4096
TOP = 2


def shards(
    queries,
    key_heads,
    value_heads,
    residual,
    out_weight,
    norm_gain,
    gate_weight,
    up_weight,
    down_weight,
    expert_ids,
    expert_weights,
):
    ctx_count = lax.axis_size("ctx")
    exp_count = lax.axis_size("exp")
    hid_count = lax.axis_size("hid")
    tok_rows = queries.shape[0]
    query_count = queries.shape[1] // HEAD
    kv_count = key_heads.shape[1] // HEAD
    group_size = HEADS // KV_HEADS
    query_spot = lax.axis_index("ctx") * tok_rows + jnp.arange(tok_rows, dtype=jnp.int32)
    kv_pick = (
        lax.axis_index("hid") * query_count + jnp.arange(query_count, dtype=jnp.int32)
    ) // group_size
    query_block = queries.reshape(tok_rows, query_count, HEAD)
    score_scale = 1.0 / math.sqrt(HEAD)

    def attend(status, pieces):
        running, denom, accum = status
        key_piece, value_piece = pieces
        length = key_piece.shape[0]
        chosen_keys = jnp.take(key_piece.reshape(length, kv_count, HEAD), kv_pick, axis=1)
        chosen_values = jnp.take(value_piece.reshape(length, kv_count, HEAD), kv_pick, axis=1)
        scores = (
            jnp.einsum("rjd,njd->jrn", query_block, chosen_keys, preferred_element_type=jnp.float32)
            * score_scale
        )
        allowed = query_spot[:, None] >= jnp.arange(length, dtype=jnp.int32)[None, :]
        scores = jnp.where(allowed[None], scores, -1e30)
        new_max = jnp.maximum(running, jnp.max(scores, axis=2))
        weights = jnp.where(allowed[None], jnp.exp(scores - new_max[:, :, None]), 0.0)
        denom = jnp.sum(weights, axis=2)
        accum = jnp.einsum(
            "jrn,njd->jrd",
            weights.astype(jnp.bfloat16),
            chosen_values,
            preferred_element_type=jnp.float32,
        )
        return (new_max, denom, accum)

    initial = (
        jnp.full((query_count, tok_rows), -1e30, jnp.float32),
        jnp.zeros((query_count, tok_rows), jnp.float32),
        jnp.zeros((query_count, tok_rows, HEAD), jnp.float32),
    )
    pieces = (
        lax.all_gather(key_heads, "ctx", axis=0, tiled=True),
        lax.all_gather(value_heads, "ctx", axis=0, tiled=True),
    )
    running, denom, accum = lax.cond(
        jnp.int32(0) <= query_spot[tok_rows - 1],
        lambda inner: attend(inner, pieces),
        lambda inner: inner,
        initial,
    )
    attended = (accum / denom[:, :, None]).astype(jnp.bfloat16)
    attended = attended.transpose(1, 0, 2).reshape(tok_rows, query_count * HEAD)
    projected = jnp.dot(attended, out_weight, preferred_element_type=jnp.float32)
    row_count = tok_rows // exp_count
    width_part = D // hid_count
    partials = (
        projected.reshape(exp_count, row_count, hid_count, width_part)
        .transpose(0, 2, 1, 3)
        .reshape(exp_count * hid_count * row_count, width_part)
    )
    mixed_rows = lax.psum_scatter(partials, ("exp", "hid"), scatter_dimension=0, tiled=True)
    stream = residual.astype(jnp.float32) + mixed_rows
    stream_bf = stream.astype(jnp.bfloat16)
    expert_count = exp_count * gate_weight.shape[0]
    assigned = row_count * TOP
    capacity = min(row_count, 3 * row_count * TOP // (2 * expert_count))
    flat_ids = expert_ids.reshape(assigned)
    onehot = (flat_ids[:, None] == jnp.arange(expert_count, dtype=jnp.int32)[None, :]).astype(
        jnp.int32
    )
    slot_index = jnp.sum((jnp.cumsum(onehot, axis=0) - onehot) * onehot, axis=1)
    target = flat_ids * capacity + slot_index
    selector = (
        jnp.arange(expert_count * capacity, dtype=jnp.int32)[:, None] == target[None, :]
    ).astype(jnp.bfloat16)
    repeated = jnp.repeat(stream_bf, TOP, axis=0)
    outgoing = jnp.dot(selector, repeated, preferred_element_type=jnp.float32).astype(jnp.bfloat16)
    copies = jnp.broadcast_to(outgoing[None], (ctx_count,) + outgoing.shape).reshape(
        ctx_count * expert_count * capacity, width_part
    )
    incoming = lax.all_to_all(copies, ("ctx", "exp"), split_axis=0, concat_axis=0, tiled=True)
    widened = incoming.astype(jnp.float32)
    scaled = (widened * norm_gain).astype(jnp.bfloat16)
    gate_part = jnp.dot(scaled, gate_weight[0], preferred_element_type=jnp.float32)
    up_part = jnp.dot(scaled, up_weight[0], preferred_element_type=jnp.float32)
    square = jnp.sum(widened * widened, axis=1)
    gate_sum, up_sum, square_sum = lax.psum((gate_part, up_part, square), "hid")
    inverse = lax.rsqrt(square_sum / D + 1e-05)[:, None]
    active = (jax.nn.silu(gate_sum * inverse) * (up_sum * inverse)).astype(jnp.bfloat16)
    partial_out = jnp.dot(active, down_weight[0], preferred_element_type=jnp.float32).astype(
        jnp.bfloat16
    )
    returned = lax.all_to_all(partial_out, ("ctx", "exp"), split_axis=0, concat_axis=0, tiled=True)
    summed = jnp.sum(
        returned.reshape(ctx_count, expert_count * capacity, width_part).astype(jnp.float32), axis=0
    )
    picked = jnp.dot(selector.astype(jnp.float32).T, summed, precision=lax.Precision.HIGHEST)
    combined = jnp.sum(
        picked.reshape(row_count, TOP, width_part) * expert_weights[:, :, None], axis=1
    )
    return (stream + combined).astype(jnp.bfloat16)


def solution(mesh):
    return jax.shard_map(
        shards,
        mesh=mesh,
        in_specs=(
            P("ctx", ("exp", "hid")),
            P("ctx", "exp"),
            P("ctx", "exp"),
            P(("ctx", "exp"), "hid"),
            P(("exp", "hid"), None),
            P("hid"),
            P("exp", "hid", "ctx"),
            P("exp", "hid", "ctx"),
            P("exp", "ctx", "hid"),
            P(("ctx", "exp"), None),
            P(("ctx", "exp"), None),
        ),
        out_specs=P(("ctx", "exp"), "hid"),
        check_vma=False,
    )
```

profile of v0, /device:TPU:16, one launch (start us, length us, event | category | flops | bytes accessed | tf_op | source)
XLA Modules:
  0.0 548.4 jit_solution(16361591857896097729)
XLA Ops:
  6.5 0.0 copy-start
  6.5 0.0 copy-start.2
  6.5 0.0 reduce-scatter.2.cloned.1.call-start
  6.5 0.6 slice.3
  7.8 0.0 copy-start.10
  7.8 34.0 %all_gather.6 = bf16[2048,128]{1,0:T(8,128)(2,1)} all-gather(bf16[128,128]{1,0:T(8,128)(2,1)} %param.14), channel_id=1, replica_groups=mesh['ctx'=16,'exp'=8,'hid'=4] {'ctx'}, dimensions={0}, use_global_device_ids=true | all-gather | bytes 557056 | tf_op jit(solution)/shard_map/all_gather | solution.py:71
  41.9 28.0 %all_gather.7 = bf16[2048,128]{1,0:T(8,128)(2,1)} all-gather(bf16[128,128]{1,0:T(8,128)(2,1)} %param.15), channel_id=1, replica_groups=mesh['ctx'=16,'exp'=8,'hid'=4] {'ctx'}, dimensions={0}, use_global_device_ids=true | all-gather | bytes 557056 | tf_op jit(solution)/shard_map/all_gather | solution.py:72
  69.9 0.0 copy-done.2
  69.9 0.7 copy.27
  70.5 0.0 copy-done.10
  70.5 2.4 conditional.1
  70.6 0.0 copy-start.3
  70.6 1.5 fusion.33
  72.1 0.0 copy-done.3
  72.1 0.4 convolution_bitcast_fusion
  72.6 0.3 fusion.3
  72.9 0.1 divide_convert_fusion
  73.0 1.8 fusion.34
  74.8 0.0 copy-start.7
  74.8 0.0 copy-start.5
  74.8 0.0 reduce-scatter.2.cloned.1.call-update
  74.8 0.0 all-reduce.3.cloned.1.call-start
  74.8 0.6 copy-done.7
  75.5 0.1 copy.24
  75.5 0.1 reshape.161
  75.6 0.1 fusion.29
  75.7 0.1 reduce_window_sum.11
  75.8 0.2 select_reduce_fusion
  76.0 169.3 %reduce-scatter.2.cloned.1.call-done = f32[16,1024]{1,0:T(8,128)} async-done(((f32[512,1024]{1,0:T(8,128)}), f32[16,1024]{1,0:T(8,128)}) %reduce-scatter.2.cloned.1.call-update) | async-done | bytes 65552 | tf_op jit(solution)/shard_map/reduce_scatter | solution.py:90
  245.2 0.0 copy-done.5
  245.2 0.8 fusion.28
  246.1 0.1 convolution_convert_fusion.1
  246.3 1.4 broadcast_in_dim.57
  247.6 2.5 all_to_all.12
  250.1 0.0 copy-start.6
  250.1 60.6 %all_to_all.18 = bf16[128,6,1024]{2,1,0:T(8,128)(2,1)S(1)} all-to-all(bf16[128,6,1024]{2,1,0:T(8,128)(2,1)S(1)} %all_to_all.12), channel_id=1, replica_groups=mesh['ctx'=16,'exp'=8,'hid'=4] {'ctx','exp'}, dimensions={0} | all-to-all | bytes 3145728 | tf_op jit(solution)/shard_map/all_to_all | solution.py:110
  310.8 0.0 copy-done.6
  310.8 0.8 fusion.18
  311.6 1.4 convert_element_type.68
  313.0 0.0 copy-start.1
  313.0 0.0 copy-start.9
  313.0 4.0 fusion.21
  317.0 0.0 copy-done.1
  317.0 0.0 copy-done.9
  317.0 2.1 fusion.23
  319.1 0.0 all-reduce.3.cloned.1.call-update
  319.2 0.1 reduce_sum.54
  319.3 20.3 %psum.22 = f32[768]{0:T(1024)S(1)} all-reduce(f32[768]{0:T(1024)S(1)} %reduce_sum.54), channel_id=1, replica_groups=mesh['ctx'=16,'exp'=8,'hid'=4] {'hid'}, use_global_device_ids=true, to_apply=%region_9.10 | all-reduce | flops 768 | bytes 6144 | tf_op jit(solution)/shard_map/psum | solution.py:116
  339.6 120.6 %all-reduce.3.cloned.1.call-done = (f32[768,512]{1,0:T(8,128)}, f32[768,512]{1,0:T(8,128)}) async-done(((f32[768,512]{1,0:T(8,128)}, f32[768,512]{1,0:T(8,128)}), (f32[768,512]{1,0:T(8,128)}, f32[768,512]{1,0:T(8,128)})) %all-reduce.3.cloned.1.call-update) | async-done | bytes 3145744 | tf_op jit(solution)/shard_map/psum | solution.py:116
  460.1 0.0 copy-done
  460.1 3.0 convolution_convert_fusion
  463.1 1.6 all_to_all.14
  464.8 14.2 %all-to-all-start.1 = ((bf16[128,6,1024]{2,1,0:T(8,128)(2,1)}), bf16[128,6,1024]{2,1,0:T(8,128)(2,1)S(1)}, u32[]{:S(2)}, u32[]{:S(2)}) async-start(bf16[128,6,1024]{2,1,0:T(8,128)(2,1)} %all_to_all.14), calls=%async_computation.2 | async-start | bytes 4194304 | tf_op jit(solution)/shard_map/all_to_all | solution.py:122
  479.0 0.1 reduce_sum.52
  479.1 0.1 copy.25
  479.2 57.4 %all-to-all-done.1 = bf16[128,6,1024]{2,1,0:T(8,128)(2,1)S(1)} async-done(((bf16[128,6,1024]{2,1,0:T(8,128)(2,1)}), bf16[128,6,1024]{2,1,0:T(8,128)(2,1)S(1)}, u32[]{:S(2)}, u32[]{:S(2)}) %all-to-all-start.1) | async-done | bytes 1572896 | tf_op jit(solution)/shard_map/all_to_all | solution.py:122
  536.6 1.9 reshape.180
  538.5 0.0 copy-start.8
  538.5 0.0 copy-start.4
  538.5 2.1 reduce_sum.55
  540.6 0.0 copy-done.8
  540.6 0.3 fusion.19
  540.9 0.0 copy-done.4
  540.9 0.6 add_convert_fusion
  (7 shorter events, 0.1 us)
Async XLA Ops:
  6.5 453.6 %copy-start = (bf16[1,512,1024]{2,1,0:T(8,128)(2,1)S(1)}, bf16[1,512,1024]{2,1,0:T(8,128)(2,1)}, u32[]{:S(2)}) copy-start(bf16[1,512,1024]{2,1,0:T(8,128)(2,1)} %param.21) | copy-start | bytes 3145732
  6.5 63.3 %copy-start.2 = (bf16[128,4096]{1,0:T(8,128)(2,1)S(1)}, bf16[128,4096]{1,0:T(8,128)(2,1)}, u32[]{:S(2)}) copy-start(bf16[128,4096]{1,0:T(8,128)(2,1)} %param.17) | copy-start | bytes 3145732
  6.5 238.7 %reduce-scatter.2.cloned.1.call-start = ((), (), s32[]{:S(2)}) async-start(), calls=%async_computation.3 | async-start | bytes 2162688 | tf_op jit(solution)/shard_map/reduce_scatter | solution.py:90
  7.8 62.7 %copy-start.10 = (bf16[128,128]{1,0:T(8,128)(2,1)S(1)}, bf16[128,128]{1,0:T(8,128)(2,1)}, u32[]{:S(2)}) copy-start(bf16[128,128]{1,0:T(8,128)(2,1)} %param.13) | copy-start | bytes 98308
  70.6 1.6 copy-start.3
  74.8 0.7 copy-start.7
  74.8 170.4 %copy-start.5 = (bf16[16,1024]{1,0:T(8,128)(2,1)S(1)}, bf16[16,1024]{1,0:T(8,128)(2,1)}, u32[]{:S(2)}) copy-start(bf16[16,1024]{1,0:T(8,128)(2,1)} %param.16) | copy-start | bytes 98308
  74.8 385.3 %all-reduce.3.cloned.1.call-start = ((), (), s32[]{:S(2)}) async-start(), calls=%async_computation.4 | async-start | bytes 6291456 | tf_op jit(solution)/shard_map/psum | solution.py:116
  250.1 60.6 %copy-start.6 = (f32[1024]{0:T(1024)S(1)}, f32[1024]{0:T(1024)}, u32[]{:S(2)}) copy-start(f32[1024]{0:T(1024)} %param.18) | copy-start | bytes 12292
  313.0 4.0 copy-start.1
  313.0 4.0 copy-start.9
  464.8 71.8 %all-to-all-start.1 = ((bf16[128,6,1024]{2,1,0:T(8,128)(2,1)}), bf16[128,6,1024]{2,1,0:T(8,128)(2,1)S(1)}, u32[]{:S(2)}, u32[]{:S(2)}) async-start(bf16[128,6,1024]{2,1,0:T(8,128)(2,1)} %all_to_all.14), calls=%async_computation.2 | async-start | bytes 4194304 | tf_op jit(solution)/shard_map/all_to_all | solution.py:122
  538.5 2.1 copy-start.8
  538.5 2.4 copy-start.4
Sparse Core Ops, SparseCore 0:
  74.9 170.2 reduce-scatter.1
  319.3 140.7 all-reduce.2
where the time goes:
time: 549 us; the launch traced here: 548 us
  waiting for transfers between devices  347 us (63%)
  blocking collectives  143 us (26%)
  starting transfers between devices  14.3 us (3%)
  between operations  14.2 us (3%)
  matrix products  13.3 us (2%)
  local copies, waits for them, and re-layouts  11.2 us (2%)
    reduce_scatter x1, waiting for transfers between devices, shards(): lax.psum_scatter(partials, ('exp', 'hid'), scatter_dimension=0, tiled=True)  169 us
    psum x1, waiting for transfers between devices, shards(): gate_sum, up_sum, square_sum = lax.psum((gate_part, up_part, square), 'hid')  121 us
    all_to_all x1, blocking collectives, shards(): lax.all_to_all(copies, ('ctx', 'exp'), split_axis=0, concat_axis=0, tiled...  60.6 us
    all_to_all x1, waiting for transfers between devices, shards(): lax.all_to_all(partial_out, ('ctx', 'exp'), split_axis=0, concat_axis=0,...  57.4 us
    all_gather x1, blocking collectives, shards(): lax.all_gather(key_heads, 'ctx', axis=0, tiled=True)  34 us
    all_gather x1, blocking collectives, shards(): lax.all_gather(value_heads, 'ctx', axis=0, tiled=True)  28 us
    psum x1, blocking collectives, shards(): gate_sum, up_sum, square_sum = lax.psum((gate_part, up_part, square), 'hid')  20.3 us
    all_to_all x1, starting transfers between devices, shards(): lax.all_to_all(partial_out, ('ctx', 'exp'), split_axis=0, concat_axis=0,...  14.2 us
  transfers between devices with their start and end apart: 3, of which 3 were waited for; matrix products, arithmetic and copies ran while one was open for 0% of the time, Pallas kernels for 0%

commit v1 on v0

v1 whole, which is shorter than its diff:
```python
import math

import jax
import jax.numpy as jnp
from jax import lax
from jax.sharding import Mesh
from jax.sharding import PartitionSpec as P

HEADS = 32
KV_HEADS = 8
HEAD = 128
D = 4096
TOP = 2
EXPERTS = 8
CAP = 6
CTX = ("x", "yh", "core")
PLANE = ("x", "yh")


def swap(value, axes):
    return lax.all_to_all(value, axes, split_axis=0, concat_axis=0, tiled=True)


def gather_ctx(value):
    plane = lax.axis_size(PLANE)
    spread = swap(jnp.broadcast_to(value[None], (plane,) + value.shape), PLANE)
    return lax.all_gather(spread, "core", axis=0, tiled=False)


def shards(
    queries,
    key_heads,
    value_heads,
    residual,
    out_weight,
    norm_gain,
    gate_weight,
    up_weight,
    down_weight,
    expert_ids,
    expert_weights,
):
    f32, bf16 = jnp.float32, jnp.bfloat16
    plane = lax.axis_size(PLANE)
    cores = lax.axis_size("core")
    exp_count = lax.axis_size("exp")
    hid_count = lax.axis_size("hid")
    ctx_count = plane * cores
    tok_rows = queries.shape[0]
    row_count = tok_rows // exp_count
    width_part = D // hid_count

    with jax.named_scope("kv_gather"):
        pieces = gather_ctx(jnp.concatenate([key_heads, value_heads], axis=1))
        pieces = pieces.reshape(ctx_count * tok_rows, 2 * HEAD)
        keys, values = pieces[:, :HEAD], pieces[:, HEAD:]
    with jax.named_scope("attention"):
        spot = lax.axis_index(CTX) * tok_rows + jnp.arange(tok_rows, dtype=jnp.int32)
        column = jnp.arange(ctx_count * tok_rows, dtype=jnp.int32)
        block, inside = column // tok_rows, column % tok_rows
        key_spot = ((block % plane) * cores + block // plane) * tok_rows + inside
        allowed = spot[:, None] >= key_spot[None, :]
        scores = lax.dot_general(queries, keys, (((1,), (1,)), ((), ())), preferred_element_type=f32)
        scores = jnp.where(allowed, scores * (1.0 / math.sqrt(HEAD)), -1e30)
        top = jnp.max(scores, axis=1, keepdims=True)
        weights = jnp.where(allowed, jnp.exp(scores - top), 0.0)
        denom = jnp.sum(weights, axis=1, keepdims=True)
        attended = jnp.dot(weights.astype(bf16), values, preferred_element_type=f32)
        attended = (attended / denom).astype(bf16)
    with jax.named_scope("projection"):
        projected = jnp.dot(attended, out_weight, preferred_element_type=f32).astype(bf16)
        partials = (
            projected.reshape(exp_count, row_count, hid_count, width_part)
            .transpose(0, 2, 1, 3)
            .reshape(exp_count * hid_count, row_count, width_part)
        )
        mixed = jnp.sum(swap(partials, ("exp", "hid")).astype(f32), axis=0)
        stream = residual.astype(f32) + mixed
        stream_bf = stream.astype(bf16)

    with jax.named_scope("routing"):
        assigned = row_count * TOP
        flat_ids = expert_ids.reshape(assigned)
        onehot = (flat_ids[:, None] == jnp.arange(EXPERTS, dtype=jnp.int32)[None, :]).astype(jnp.int32)
        slot_index = jnp.sum((jnp.cumsum(onehot, axis=0) - onehot) * onehot, axis=1)
        target = (flat_ids * CAP + slot_index).reshape(row_count, TOP)
        slots = jnp.arange(EXPERTS * CAP, dtype=jnp.int32)
        hits = target[:, :, None] == slots[None, None, :]
        selector = jnp.any(hits, axis=1).astype(bf16)
        mixer = jnp.sum(jnp.where(hits, expert_weights[:, :, None], 0.0), axis=1)
    with jax.named_scope("dispatch"):
        outgoing = lax.dot_general(
            selector, stream_bf, (((0,), (0,)), ((), ())), preferred_element_type=f32
        ).astype(bf16)
        arrived = swap(outgoing.reshape(exp_count, CAP, width_part), "exp")
        rows = gather_ctx(arrived.reshape(exp_count * CAP, width_part))
        total = ctx_count * exp_count * CAP
        rows = rows.reshape(total, width_part)

    with jax.named_scope("gate_up"):
        widened = rows.astype(f32)
        scaled = (widened * norm_gain).astype(bf16)
        square = jnp.sum(widened * widened, axis=1)
        high = square.astype(bf16)
        low = (square - high.astype(f32)).astype(bf16)
        ff_part = gate_weight.shape[2]
        piece = ff_part // hid_count
        norm_rows = total * 2 // (2 * piece)
        pad_rows = -(-norm_rows // 16) * 16
        tail = jnp.concatenate([high, low]).reshape(norm_rows, 2 * piece)
        tail = jnp.pad(tail, ((0, pad_rows - norm_rows), (0, 0)))
        gate = jnp.dot(scaled, gate_weight[0], preferred_element_type=f32).astype(bf16)
        up = jnp.dot(scaled, up_weight[0], preferred_element_type=f32).astype(bf16)
        outbound = jnp.stack(
            [
                jnp.concatenate(
                    [
                        jnp.concatenate(
                            [gate[:, h * piece : (h + 1) * piece], up[:, h * piece : (h + 1) * piece]], axis=1
                        ),
                        tail,
                    ],
                    axis=0,
                )
                for h in range(hid_count)
            ]
        )
        summed = jnp.sum(swap(outbound, "hid").astype(f32), axis=0)
        norms = summed[total : total + norm_rows].reshape(2, total)
        inverse = lax.rsqrt((norms[0] + norms[1]) / D + 1e-05)[:, None]
        gate_sum, up_sum = summed[:total, :piece], summed[:total, piece:]
        active = (jax.nn.silu(gate_sum * inverse) * (up_sum * inverse)).astype(bf16)
    with jax.named_scope("down"):
        active = lax.all_gather(active, "hid", axis=1, tiled=True)
        partial_out = jnp.dot(active, down_weight[0], preferred_element_type=f32).astype(bf16)
        back = swap(partial_out.reshape(cores, total // cores, width_part), "core")
        back = jnp.sum(back.astype(f32), axis=0).astype(bf16)
        back = swap(back.reshape(plane, exp_count * CAP, width_part), PLANE)
        back = jnp.sum(back.astype(f32), axis=0).astype(bf16)
        back = swap(back.reshape(exp_count, CAP, width_part), "exp")
        back = back.reshape(EXPERTS * CAP, width_part).astype(f32)
    with jax.named_scope("combine"):
        combined = jnp.dot(mixer, back, precision=lax.Precision.HIGHEST)
        return (stream + combined).astype(bf16)


def solution(mesh):
    ctx, exp, hid = mesh.devices.shape
    split = Mesh(mesh.devices.reshape(ctx // 4, 2, 2, exp, hid), CTX + ("exp", "hid"))
    return jax.shard_map(
        shards,
        mesh=split,
        in_specs=(
            P(CTX, ("exp", "hid")),
            P(CTX, "exp"),
            P(CTX, "exp"),
            P(CTX + ("exp",), "hid"),
            P(("exp", "hid"), None),
            P("hid"),
            P("exp", "hid", CTX),
            P("exp", "hid", CTX),
            P("exp", CTX, "hid"),
            P(CTX + ("exp",), None),
            P(CTX + ("exp",), None),
        ),
        out_specs=P(CTX + ("exp",), "hid"),
        check_vma=False,
    )
```

time: 549 us -> 283 us (0.52)
  waiting for transfers between devices: 347 us -> 62 us
  blocking collectives: 143 us -> 167 us
    reduce_scatter x1 -> x0, waiting for transfers between devices: 169 us -> none  [shards(): lax.psum_scatter(partials, ('exp', 'hid'), scatter_dimension=0, tiled=True)]
    psum x1 -> x0, waiting for transfers between devices: 121 us -> none  [shards(): gate_sum, up_sum, square_sum = lax.psum((gate_part, up_part, square), 'hid')]
    all_to_all x1 -> x6, blocking collectives: 60.6 us -> 148 us  [swap(): return lax.all_to_all(value, axes, split_axis=0, concat_axis=0, tiled=True)]
    all_gather x2 -> x1, blocking collectives: 62.1 us -> 18.4 us  [shards(): active = lax.all_gather(active, 'hid', axis=1, tiled=True)]
    all_gather x0 -> x2, waiting for transfers between devices: none -> 25.3 us  [gather_ctx(): return lax.all_gather(spread, 'core', axis=0, tiled=False)]
    all_to_all x1 -> x2, waiting for transfers between devices: 57.4 us -> 36.6 us  [swap(): return lax.all_to_all(value, axes, split_axis=0, concat_axis=0, tiled=True)]
    psum x1 -> x0, blocking collectives: 20.3 us -> none  [shards(): gate_sum, up_sum, square_sum = lax.psum((gate_part, up_part, square), 'hid')]
    dot_general x8 -> x7, matrix products: 13.3 us -> 8.16 us  [the longest x1 2.42 us: shards(): jnp.dot(attended, out_weight, preferred_element_type=f32).astype(bf16)]
  transfers between devices with their start and end apart: 3 -> 4, of which waited for: 3 -> 4; matrix products, arithmetic and copies ran while one was open for 0% -> 0% of each run, Pallas kernels for 0% -> 0%
where the time goes in v1:
time: 283 us; the launch traced here: 282 us
  blocking collectives  167 us (59%)
  waiting for transfers between devices  62 us (22%)
  starting transfers between devices  18.4 us (7%)
  between operations  13.7 us (5%)
  matrix products  8.16 us (3%)
  local copies, waits for them, and re-layouts  7.47 us (3%)
  other arithmetic  5.69 us (2%)
    all_to_all x6, blocking collectives, swap(): return lax.all_to_all(value, axes, split_axis=0, concat_axis=0, tiled=True)  148 us
    all_to_all x2, waiting for transfers between devices, swap(): return lax.all_to_all(value, axes, split_axis=0, concat_axis=0, tiled=True)  36.6 us
    all_gather x2, waiting for transfers between devices, gather_ctx(): return lax.all_gather(spread, 'core', axis=0, tiled=False)  25.3 us
    all_gather x1, blocking collectives, shards(): active = lax.all_gather(active, 'hid', axis=1, tiled=True)  18.4 us
    all_to_all x2, starting transfers between devices, swap(): return lax.all_to_all(value, axes, split_axis=0, concat_axis=0, tiled=True)  18.4 us
  transfers between devices with their start and end apart: 4, of which 4 were waited for; matrix products, arithmetic and copies ran while one was open for 0% of the time, Pallas kernels for 0%

profile of v1, /device:TPU:16, one launch (start us, length us, event | category | flops | bytes accessed | tf_op | source)
XLA Modules:
  0.0 282.2 jit_solution(11088064930792449066)
XLA Ops:
  6.5 0.0 copy-start
  6.5 0.0 all-gather.5.cloned.1.call-start
  6.5 0.9 pad_maximum_fusion.1
  7.5 27.3 %all_to_all.40 = bf16[8,128,256]{2,1,0:T(8,128)(2,1)} all-to-all(bf16[8,128,256]{2,1,0:T(8,128)(2,1)S(1)} %broadcast_in_dim.25), channel_id=1, replica_groups=mesh['x'=4,'yh'=2,'core'=2,'exp'=8,'hid'=4] {'x','yh'}, dimensions={0} | all-to-all | bytes 1048576 | tf_op jit(solution)/shard_map/kv_gather/all_to_all | solution.py:21
  34.7 0.0 all-gather.5.cloned.1.call-update
  34.8 16.6 %all-gather.5.cloned.1.call-done = bf16[16,128,256]{2,1,0:T(8,128)(2,1)} async-done(((bf16[8,128,256]{2,1,0:T(8,128)(2,1)}), bf16[16,128,256]{2,1,0:T(8,128)(2,1)}) %all-gather.5.cloned.1.call-update) | async-done | bytes 1048592 | tf_op jit(solution)/shard_map/kv_gather/all_gather | solution.py:27
  51.4 0.0 copy-done.8
  51.4 1.6 fusion.64
  53.0 0.4 fusion.10
  53.5 2.4 convolution_convert_fusion
  55.9 0.8 reshape.139
  56.7 0.0 copy-start.4
  56.7 1.3 copy.49
  58.0 11.0 %all-to-all-start.1 = ((bf16[32,16,1024]{2,1,0:T(8,128)(2,1)}), bf16[32,16,1024]{2,1,0:T(8,128)(2,1)S(1)}, u32[]{:S(2)}, u32[]{:S(2)}) async-start(bf16[32,16,1024]{2,1,0:T(8,128)(2,1)} %bitcast.3), calls=%async_computation.1 | async-start | bytes 2097152 | tf_op jit(solution)/shard_map/projection/all_to_all | solution.py:21
  69.0 0.0 all-gather.7.cloned.1.call-start
  69.1 0.1 copy.50
  69.2 0.1 eq.31
  69.2 0.1 fusion.37
  69.3 0.1 reduce_window_sum.11
  69.4 0.2 select_reduce_fusion.1
  69.6 0.1 reduce_sum.85
  69.6 0.1 copy.51
  69.7 0.1 fusion.36
  69.8 27.6 %all-to-all-done.1 = bf16[32,16,1024]{2,1,0:T(8,128)(2,1)S(1)} async-done(((bf16[32,16,1024]{2,1,0:T(8,128)(2,1)}), bf16[32,16,1024]{2,1,0:T(8,128)(2,1)S(1)}, u32[]{:S(2)}, u32[]{:S(2)}) %all-to-all-start.1) | async-done | bytes 1048608 | tf_op jit(solution)/shard_map/projection/all_to_all | solution.py:21
  97.5 0.2 convert_reduce_fusion.1
  97.6 0.2 convolution_convert_fusion.4
  97.9 11.8 %all_to_all.41 = bf16[8,6,1024]{2,1,0:T(8,128)(2,1)S(1)} all-to-all(bf16[8,6,1024]{2,1,0:T(8,128)(2,1)S(1)} %reshape.141), channel_id=1, replica_groups=mesh['x'=4,'yh'=2,'core'=2,'exp'=8,'hid'=4] {'exp'}, dimensions={0} | all-to-all | bytes 196608 | tf_op jit(solution)/shard_map/dispatch/all_to_all | solution.py:21
  109.7 0.1 broadcast_in_dim.47
  109.8 29.7 %all_to_all.42 = bf16[8,48,1024]{2,1,0:T(8,128)(2,1)} all-to-all(bf16[8,48,1024]{2,1,0:T(8,128)(2,1)S(1)} %broadcast_in_dim.47), channel_id=1, replica_groups=mesh['x'=4,'yh'=2,'core'=2,'exp'=8,'hid'=4] {'x','yh'}, dimensions={0} | all-to-all | bytes 1572864 | tf_op jit(solution)/shard_map/dispatch/all_to_all | solution.py:21
  139.6 0.0 all-gather.7.cloned.1.call-update
  139.6 8.7 %all-gather.7.cloned.1.call-done = bf16[16,48,1024]{2,1,0:T(8,128)(2,1)} async-done(((bf16[8,48,1024]{2,1,0:T(8,128)(2,1)}), bf16[16,48,1024]{2,1,0:T(8,128)(2,1)}) %all-gather.7.cloned.1.call-update) | async-done | bytes 1572880 | tf_op jit(solution)/shard_map/dispatch/all_gather | solution.py:27
  148.3 1.9 fusion.1
  150.2 0.1 reduce_sum.88
  150.3 0.1 copy.52
  150.4 0.0 copy-start.6
  150.4 0.4 fusion
  150.9 0.8 copy-done.6
  151.7 1.1 convolution_convert_fusion.2
  152.7 0.2 copy-done.7
  152.9 1.1 convolution_convert_fusion.3
  154.0 0.1 fusion.62
  154.1 0.2 fusion.30
  154.2 0.3 pad_maximum_fusion
  154.6 2.4 copy.53
  156.9 41.0 %all_to_all.43 = bf16[4,784,256]{2,1,0:T(8,128)(2,1)S(1)} all-to-all(bf16[4,784,256]{2,1,0:T(8,128)(2,1)} %copy.53), channel_id=1, replica_groups=mesh['x'=4,'yh'=2,'core'=2,'exp'=8,'hid'=4] {'hid'}, dimensions={0} | all-to-all | bytes 3211264 | tf_op jit(solution)/shard_map/gate_up/all_to_all | solution.py:21
  197.9 0.2 convert_reduce_fusion
  198.2 0.1 fusion.61
  198.3 0.2 copy.60
  198.5 0.2 copy.63
  198.6 0.1 multiply_convert_fusion
  198.8 18.4 %all_gather.19 = bf16[768,512]{0,1:T(8,128)(2,1)S(1)} all-gather(bf16[768,128]{0,1:T(8,128)(2,1)S(1)} %multiply_convert_fusion), channel_id=1, replica_groups=mesh['x'=4,'yh'=2,'core'=2,'exp'=8,'hid'=4] {'hid'}, dimensions={1}, use_global_device_ids=true | all-gather | bytes 983040 | tf_op jit(solution)/shard_map/down/all_gather | solution.py:134
  217.1 0.0 copy-done
  217.1 1.0 convolution_convert_fusion.1
  218.2 5.0 %all_to_all.44 = bf16[2,384,1024]{2,1,0:T(8,128)(2,1)S(1)} all-to-all(bf16[2,384,1024]{2,1,0:T(8,128)(2,1)S(1)} %bitcast.43), channel_id=1, replica_groups=mesh['x'=4,'yh'=2,'core'=2,'exp'=8,'hid'=4] {'core'}, dimensions={0} | all-to-all | bytes 3145728 | tf_op jit(solution)/shard_map/down/all_to_all | solution.py:21
  223.2 0.4 reduce_sum.90
  223.6 0.0 copy-start.5
  223.6 33.6 %all_to_all.45 = bf16[8,48,1024]{2,1,0:T(8,128)(2,1)S(1)} all-to-all(bf16[8,48,1024]{2,1,0:T(8,128)(2,1)S(1)} %bitcast.40), channel_id=1, replica_groups=mesh['x'=4,'yh'=2,'core'=2,'exp'=8,'hid'=4] {'x','yh'}, dimensions={0} | all-to-all | bytes 1572864 | tf_op jit(solution)/shard_map/down/all_to_all | solution.py:21
  257.2 0.1 reduce_sum.91
  257.4 0.7 reshape.144
  258.0 7.4 %all-to-all-start.7 = ((bf16[8,6,1024]{2,1,0:T(8,128)(2,1)}), bf16[8,6,1024]{2,1,0:T(8,128)(2,1)S(1)}, u32[]{:S(2)}, u32[]{:S(2)}) async-start(bf16[8,6,1024]{2,1,0:T(8,128)(2,1)} %reshape.144), calls=%async_computation.7 | async-start | bytes 262144 | tf_op jit(solution)/shard_map/down/all_to_all | solution.py:21
  265.4 0.0 copy-done.5
  265.4 0.1 select_reduce_fusion
  265.5 9.0 %all-to-all-done.7 = bf16[8,6,1024]{2,1,0:T(8,128)(2,1)S(1)} async-done(((bf16[8,6,1024]{2,1,0:T(8,128)(2,1)}), bf16[8,6,1024]{2,1,0:T(8,128)(2,1)S(1)}, u32[]{:S(2)}, u32[]{:S(2)}) %all-to-all-start.7) | async-done | bytes 98336 | tf_op jit(solution)/shard_map/down/all_to_all | solution.py:21
  274.5 0.8 fusion.5
  (20 shorter events, 0.2 us)
Async XLA Ops:
  6.5 210.6 %copy-start = (bf16[1,512,1024]{2,1,0:T(8,128)(2,1)S(1)}, bf16[1,512,1024]{2,1,0:T(8,128)(2,1)}, u32[]{:S(2)}) copy-start(bf16[1,512,1024]{2,1,0:T(8,128)(2,1)} %param.19) | copy-start | bytes 3145732
  6.5 44.9 %copy-start.8 = (bf16[128,128]{1,0:T(8,128)(2,1)S(1)}, bf16[128,128]{1,0:T(8,128)(2,1)}, u32[]{:S(2)}) copy-start(bf16[128,128]{1,0:T(8,128)(2,1)} %param.11) | copy-start | bytes 98308
  6.5 44.9 %all-gather.5.cloned.1.call-start = ((), (), s32[]{:S(2)}) async-start(), calls=%async_computation.8 | async-start | bytes 1572864 | tf_op jit(solution)/shard_map/kv_gather/all_gather | solution.py:27
  56.7 12.4 %copy-start.4 = (s32[16,2]{0,1:T(2,128)S(1)}, s32[16,2]{0,1:T(2,128)}, u32[]{:S(2)}) copy-start(s32[16,2]{0,1:T(2,128)} %param.20) | copy-start | bytes 388
  58.0 39.6 %copy-start.2 = (bf16[16,1024]{1,0:T(8,128)(2,1)S(1)}, bf16[16,1024]{1,0:T(8,128)(2,1)}, u32[]{:S(2)}) copy-start(bf16[16,1024]{1,0:T(8,128)(2,1)} %param.14) | copy-start | bytes 98308
  58.0 39.4 %all-to-all-start.1 = ((bf16[32,16,1024]{2,1,0:T(8,128)(2,1)}), bf16[32,16,1024]{2,1,0:T(8,128)(2,1)S(1)}, u32[]{:S(2)}, u32[]{:S(2)}) async-start(bf16[32,16,1024]{2,1,0:T(8,128)(2,1)} %bitcast.3), calls=%async_computation.1 | async-start | bytes 2097152 | tf_op jit(solution)/shard_map/projection/all_to_all | solution.py:21
  69.0 79.3 %all-gather.7.cloned.1.call-start = ((), (), s32[]{:S(2)}) async-start(), calls=%async_computation.9 | async-start | bytes 2359296 | tf_op jit(solution)/shard_map/dispatch/all_gather | solution.py:27
  139.6 10.9 %copy-start.3 = (f32[1024]{0:T(1024)S(1)}, f32[1024]{0:T(1024)}, u32[]{:S(2)}) copy-start(f32[1024]{0:T(1024)} %param.16) | copy-start | bytes 12292
  148.3 2.2 copy-start.1
  150.4 1.2 copy-start.6
  151.7 1.2 copy-start.7
  223.6 41.8 %copy-start.5 = (f32[16,2]{0,1:T(2,128)S(1)}, f32[16,2]{0,1:T(2,128)}, u32[]{:S(2)}) copy-start(f32[16,2]{0,1:T(2,128)} %param.21) | copy-start | bytes 388
  258.0 16.5 %all-to-all-start.7 = ((bf16[8,6,1024]{2,1,0:T(8,128)(2,1)}), bf16[8,6,1024]{2,1,0:T(8,128)(2,1)S(1)}, u32[]{:S(2)}, u32[]{:S(2)}) async-start(bf16[8,6,1024]{2,1,0:T(8,128)(2,1)} %reshape.144), calls=%async_computation.7 | async-start | bytes 262144 | tf_op jit(solution)/shard_map/down/all_to_all | solution.py:21
Sparse Core Ops, SparseCore 0:
  34.9 16.4 all-gather.4
  139.7 8.5 all-gather.6

commit v2 on v1

--- a/solution.py
+++ b/solution.py
@@ -21,10 +21,12 @@
     return lax.all_to_all(value, axes, split_axis=0, concat_axis=0, tiled=True)
 
 
-def gather_ctx(value):
-    plane = lax.axis_size(PLANE)
-    spread = swap(jnp.broadcast_to(value[None], (plane,) + value.shape), PLANE)
-    return lax.all_gather(spread, "core", axis=0, tiled=False)
+def spread(value, axes):
+    return swap(jnp.broadcast_to(value[None], (lax.axis_size(axes),) + value.shape), axes)
+
+
+def both_cores(value):
+    return value, lax.ppermute(value, "core", [(0, 1), (1, 0)])
 
 
 def shards(
@@ -51,14 +53,16 @@
     width_part = D // hid_count
 
     with jax.named_scope("kv_gather"):
-        pieces = gather_ctx(jnp.concatenate([key_heads, value_heads], axis=1))
+        pieces = spread(jnp.concatenate([key_heads, value_heads], axis=1), PLANE)
+        pieces = jnp.concatenate(both_cores(pieces), axis=0)
         pieces = pieces.reshape(ctx_count * tok_rows, 2 * HEAD)
         keys, values = pieces[:, :HEAD], pieces[:, HEAD:]
     with jax.named_scope("attention"):
         spot = lax.axis_index(CTX) * tok_rows + jnp.arange(tok_rows, dtype=jnp.int32)
         column = jnp.arange(ctx_count * tok_rows, dtype=jnp.int32)
         block, inside = column // tok_rows, column % tok_rows
-        key_spot = ((block % plane) * cores + block // plane) * tok_rows + inside
+        core = lax.axis_index("core") ^ (block // plane)
+        key_spot = ((block % plane) * cores + core) * tok_rows + inside
         allowed = spot[:, None] >= key_spot[None, :]
         scores = lax.dot_general(queries, keys, (((1,), (1,)), ((), ())), preferred_element_type=f32)
         scores = jnp.where(allowed, scores * (1.0 / math.sqrt(HEAD)), -1e30)
@@ -71,10 +75,10 @@
         projected = jnp.dot(attended, out_weight, preferred_element_type=f32).astype(bf16)
         partials = (
             projected.reshape(exp_count, row_count, hid_count, width_part)
-            .transpose(0, 2, 1, 3)
-            .reshape(exp_count * hid_count, row_count, width_part)
+            .transpose(2, 0, 1, 3)
+            .reshape(hid_count * exp_count, row_count, width_part)
         )
-        mixed = jnp.sum(swap(partials, ("exp", "hid")).astype(f32), axis=0)
+        mixed = jnp.sum(swap(partials, ("hid", "exp")).astype(f32), axis=0)
         stream = residual.astype(f32) + mixed
         stream_bf = stream.astype(bf16)
 
@@ -92,10 +96,13 @@
         outgoing = lax.dot_general(
             selector, stream_bf, (((0,), (0,)), ((), ())), preferred_element_type=f32
         ).astype(bf16)
-        arrived = swap(outgoing.reshape(exp_count, CAP, width_part), "exp")
-        rows = gather_ctx(arrived.reshape(exp_count * CAP, width_part))
+        outgoing = outgoing.reshape(1, exp_count, CAP, width_part)
+        halves = lax.axis_size("yh")
+        outgoing = jnp.broadcast_to(outgoing, (halves, exp_count, CAP, width_part))
+        arrived = swap(outgoing.reshape(halves * exp_count, CAP, width_part), ("yh", "exp"))
+        arrived = spread(arrived.reshape(halves * exp_count * CAP, width_part), "x")
         total = ctx_count * exp_count * CAP
-        rows = rows.reshape(total, width_part)
+        rows = jnp.concatenate(both_cores(arrived), axis=0).reshape(total, width_part)
 
     with jax.named_scope("gate_up"):
         widened = rows.astype(f32)
@@ -133,12 +140,15 @@
     with jax.named_scope("down"):
         active = lax.all_gather(active, "hid", axis=1, tiled=True)
         partial_out = jnp.dot(active, down_weight[0], preferred_element_type=f32).astype(bf16)
-        back = swap(partial_out.reshape(cores, total // cores, width_part), "core")
+        own, other = jnp.split(partial_out, 2, axis=0)
+        other = lax.ppermute(other, "core", [(0, 1), (1, 0)])
+        back = (own.astype(f32) + other.astype(f32)).astype(bf16)
+        lines = lax.axis_size("x")
+        back = swap(back.reshape(lines, total // cores // lines, width_part), "x")
         back = jnp.sum(back.astype(f32), axis=0).astype(bf16)
-        back = swap(back.reshape(plane, exp_count * CAP, width_part), PLANE)
-        back = jnp.sum(back.astype(f32), axis=0).astype(bf16)
-        back = swap(back.reshape(exp_count, CAP, width_part), "exp")
-        back = back.reshape(EXPERTS * CAP, width_part).astype(f32)
+        back = swap(back.reshape(halves * exp_count, CAP, width_part), ("yh", "exp"))
+        back = back.reshape(halves, EXPERTS * CAP, width_part).astype(f32)
+        back = jnp.sum(back, axis=0)
     with jax.named_scope("combine"):
         combined = jnp.dot(mixer, back, precision=lax.Precision.HIGHEST)
         return (stream + combined).astype(bf16)

time: 283 us -> 224 us (0.79)
  blocking collectives: 167 us -> 131 us
  waiting for transfers between devices: 62 us -> 48 us
  between operations: 13.7 us -> 0.34 us
  starting transfers between devices: 18.4 us -> 26.1 us
    all_to_all x6 -> x5, blocking collectives: 148 us -> 112 us  [swap(): return lax.all_to_all(value, axes, split_axis=0, concat_axis=0, tiled=True)]
    all_gather x2 -> x0, waiting for transfers between devices: 25.3 us -> none  [gather_ctx(): return lax.all_gather(spread, 'core', axis=0, tiled=False)]
    ppermute x0 -> x3, waiting for transfers between devices: none -> 6.34 us  [the longest x2 4.09 us: both_cores(): return (value, lax.ppermute(value, 'core', [(0, 1), (1, 0)]))]
    ppermute x0 -> x3, starting transfers between devices: none -> 5.87 us  [the longest x2 3.95 us: both_cores(): return (value, lax.ppermute(value, 'core', [(0, 1), (1, 0)]))]
    all_to_all x2, waiting for transfers between devices: 36.6 us -> 41.7 us  [swap(): return lax.all_to_all(value, axes, split_axis=0, concat_axis=0, tiled=True)]
  transfers between devices with their start and end apart: 4 -> 5, of which waited for: 4 -> 5; matrix products, arithmetic and copies ran while one was open for 0% -> 0% of each run, Pallas kernels for 0% -> 0%
where the time goes in v2:
time: 224 us
  blocking collectives  131 us (58%)
  waiting for transfers between devices  48 us (21%)
  starting transfers between devices  26.1 us (12%)
  local copies, waits for them, and re-layouts  7.35 us (3%)
  matrix products  7.09 us (3%)
  other arithmetic  3.94 us (2%)
    all_to_all x5, blocking collectives, swap(): return lax.all_to_all(value, axes, split_axis=0, concat_axis=0, tiled=True)  112 us
    all_to_all x2, waiting for transfers between devices, swap(): return lax.all_to_all(value, axes, split_axis=0, concat_axis=0, tiled=True)  41.7 us
    all_to_all x2, starting transfers between devices, swap(): return lax.all_to_all(value, axes, split_axis=0, concat_axis=0, tiled=True)  20.2 us
    all_gather x1, blocking collectives, shards(): active = lax.all_gather(active, 'hid', axis=1, tiled=True)  18.4 us
  transfers between devices with their start and end apart: 5, of which 5 were waited for; matrix products, arithmetic and copies ran while one was open for 0% of the time, Pallas kernels for 0%

profile of v2, /device:TPU:16, one launch (start us, length us, event | category | flops | bytes accessed | tf_op | source)
XLA Modules:
  0.0 223.5 jit_solution(6692575779043160480)
XLA Ops:
  0.0 0.0 copy-start
  0.0 0.9 pad_maximum_fusion.3
  0.9 0.0 copy-start.8
  0.9 27.2 %all_to_all.35 = bf16[8,128,256]{2,1,0:T(8,128)(2,1)S(1)} all-to-all(bf16[8,128,256]{2,1,0:T(8,128)(2,1)S(1)} %broadcast_in_dim.48), channel_id=1, replica_groups=mesh['x'=4,'yh'=2,'core'=2,'exp'=8,'hid'=4] {'x','yh'}, dimensions={0} | all-to-all | bytes 1048576 | tf_op jit(solution)/shard_map/kv_gather/all_to_all | solution.py:21
  28.1 1.9 collective-permute-start
  30.1 1.8 collective-permute-done
  31.9 0.1 pad_maximum_fusion.2
  32.0 0.4 fusion.65
  32.5 0.5 copy-done.1
  33.0 0.4 fusion.10
  33.4 2.4 %convolution_convert_fusion = bf16[128,4096]{1,0:T(8,128)(2,1)S(1)} fusion(bf16[128,4096]{1,0:T(8,128)(2,1)} %param.15, f32[128,2048]{0,1:T(8,128)S(1)} %get-tuple-element.24, bf16[2048,256]{1,0:T(8,128)(2,1)} %bitcast.38, f32[128]{0:T(128)S(1)} %get-tuple-element.23, s32[128]{0:T(128)S(1)} %iota_add_fusion, s32[2048]{0:T(1024)S(1)} %fusion.47, f32[128]{0:T(128)S(1)} %fusion.10), kind=kOutput, calls=%fused_computation | convolution fusion | flops 202932224 | bytes 3679744 | tf_op jit(solution)/shard_map/projection/dot_general | solution.py:75
  35.8 0.8 reshape.172
  36.7 0.0 copy-start.4
  36.7 1.3 copy.49
  38.0 13.0 %all-to-all-start.1 = ((bf16[32,16,1024]{2,1,0:T(8,128)(2,1)}), bf16[32,16,1024]{2,1,0:T(8,128)(2,1)S(1)}, u32[]{:S(2)}, u32[]{:S(2)}) async-start(bf16[32,16,1024]{2,1,0:T(8,128)(2,1)} %bitcast.3), calls=%async_computation.1 | async-start | bytes 2097152 | tf_op jit(solution)/shard_map/projection/all_to_all | solution.py:21
  51.0 0.1 copy.50
  51.0 0.1 eq.31
  51.1 0.1 fusion.37
  51.2 0.1 reduce_window_sum.11
  51.3 0.2 select_reduce_fusion.1
  51.5 0.1 reduce_sum.82
  51.5 0.1 copy.51
  51.6 0.1 fusion.36
  51.7 27.0 %all-to-all-done.1 = bf16[32,16,1024]{2,1,0:T(8,128)(2,1)S(1)} async-done(((bf16[32,16,1024]{2,1,0:T(8,128)(2,1)}), bf16[32,16,1024]{2,1,0:T(8,128)(2,1)S(1)}, u32[]{:S(2)}, u32[]{:S(2)}) %all-to-all-start.1) | async-done | bytes 1048608 | tf_op jit(solution)/shard_map/projection/all_to_all | solution.py:21
  78.7 0.2 convert_reduce_fusion.1
  78.9 0.2 convolution_convert_fusion.4
  79.2 17.6 %all_to_all.36 = bf16[16,6,1024]{2,1,0:T(8,128)(2,1)S(1)} all-to-all(bf16[16,6,1024]{2,1,0:T(8,128)(2,1)S(1)} %bitcast.41), channel_id=1, replica_groups=mesh['x'=4,'yh'=2,'core'=2,'exp'=8,'hid'=4] {'yh','exp'}, dimensions={0} | all-to-all | bytes 393216 | tf_op jit(solution)/shard_map/dispatch/all_to_all | solution.py:21
  96.7 0.1 broadcast_in_dim.55
  96.8 0.1 broadcast_in_dim.56
  96.9 11.9 %all_to_all.37 = bf16[4,96,1024]{2,1,0:T(8,128)(2,1)S(1)} all-to-all(bf16[4,96,1024]{2,1,0:T(8,128)(2,1)S(1)} %broadcast_in_dim.56), channel_id=1, replica_groups=mesh['x'=4,'yh'=2,'core'=2,'exp'=8,'hid'=4] {'x'}, dimensions={0} | all-to-all | bytes 1572864 | tf_op jit(solution)/shard_map/dispatch/all_to_all | solution.py:21
  108.8 2.0 collective-permute-start.1
  110.8 2.3 %collective-permute-done.1 = bf16[4,96,1024]{2,1,0:T(8,128)(2,1)S(1)} collective-permute-done((bf16[4,96,1024]{2,1,0:T(8,128)(2,1)S(1)}, bf16[4,96,1024]{2,1,0:T(8,128)(2,1)S(1)}, u32[]{:S(2)}, u32[]{:S(2)}) %collective-permute-start.1) | collective-permute-done | bytes 786464 | tf_op jit(solution)/shard_map/dispatch/ppermute | solution.py:29
  113.1 0.5 fusion
  113.7 0.0 copy-start.7
  113.7 1.1 convolution_convert_fusion.2
  114.7 0.1 copy-done.7
  114.9 1.1 convolution_convert_fusion.3
  116.0 0.1 reduce_sum.85
  116.1 0.1 copy.52
  116.2 0.1 fusion.63
  116.3 0.2 fusion.30
  116.5 0.3 pad_maximum_fusion
  116.8 2.4 %copy.53 = bf16[4,784,256]{2,1,0:T(8,128)(2,1)} copy(bf16[4,784,256]{1,2,0:T(8,128)(2,1)S(1)} %pad_maximum_fusion) | data formatting | bytes 3211264 | tf_op jit(solution)/shard_map/gate_up/stack | solution.py:121
  119.2 40.4 %all_to_all.38 = bf16[4,784,256]{2,1,0:T(8,128)(2,1)S(1)} all-to-all(bf16[4,784,256]{2,1,0:T(8,128)(2,1)} %copy.53), channel_id=1, replica_groups=mesh['x'=4,'yh'=2,'core'=2,'exp'=8,'hid'=4] {'hid'}, dimensions={0} | all-to-all | bytes 3211264 | tf_op jit(solution)/shard_map/gate_up/all_to_all | solution.py:21
  159.6 0.2 convert_reduce_fusion
  159.9 0.1 fusion.62
  159.9 0.2 copy.60
  160.1 0.2 copy.63
  160.3 0.1 multiply_convert_fusion
  160.4 18.4 %all_gather.3 = bf16[768,512]{0,1:T(8,128)(2,1)S(1)} all-gather(bf16[768,128]{0,1:T(8,128)(2,1)S(1)} %multiply_convert_fusion), channel_id=1, replica_groups=mesh['x'=4,'yh'=2,'core'=2,'exp'=8,'hid'=4] {'hid'}, dimensions={1}, use_global_device_ids=true | all-gather | bytes 983040 | tf_op jit(solution)/shard_map/down/all_gather | solution.py:141
  178.8 1.0 convolution_convert_fusion.1
  179.9 0.1 split.9
  179.9 1.9 collective-permute-start.2
  181.8 2.3 %collective-permute-done.2 = bf16[384,1024]{1,0:T(8,128)(2,1)S(1)} collective-permute-done((bf16[384,1024]{1,0:T(8,128)(2,1)S(1)}, bf16[384,1024]{1,0:T(8,128)(2,1)S(1)}, u32[]{:S(2)}, u32[]{:S(2)}) %collective-permute-start.2) | collective-permute-done | bytes 786464 | tf_op jit(solution)/shard_map/down/ppermute | solution.py:144
  184.1 0.3 add_convert_fusion
  184.4 0.0 copy-start.5
  184.4 15.3 %all_to_all.39 = bf16[4,96,1024]{2,1,0:T(8,128)(2,1)S(1)} all-to-all(bf16[4,96,1024]{2,1,0:T(8,128)(2,1)S(1)} %bitcast.36), channel_id=1, replica_groups=mesh['x'=4,'yh'=2,'core'=2,'exp'=8,'hid'=4] {'x'}, dimensions={0} | all-to-all | bytes 1572864 | tf_op jit(solution)/shard_map/down/all_to_all | solution.py:21
  199.7 0.1 reduce_sum.87
  199.8 0.8 reshape.176
  200.6 7.2 %all-to-all-start.6 = ((bf16[16,6,1024]{2,1,0:T(8,128)(2,1)}), bf16[16,6,1024]{2,1,0:T(8,128)(2,1)S(1)}, u32[]{:S(2)}, u32[]{:S(2)}) async-start(bf16[16,6,1024]{2,1,0:T(8,128)(2,1)} %reshape.176), calls=%async_computation.6 | async-start | bytes 524288 | tf_op jit(solution)/shard_map/down/all_to_all | solution.py:21
  207.8 0.1 select_reduce_fusion
  207.9 14.7 %all-to-all-done.6 = bf16[16,6,1024]{2,1,0:T(8,128)(2,1)S(1)} async-done(((bf16[16,6,1024]{2,1,0:T(8,128)(2,1)}), bf16[16,6,1024]{2,1,0:T(8,128)(2,1)S(1)}, u32[]{:S(2)}, u32[]{:S(2)}) %all-to-all-start.6) | async-done | bytes 196640 | tf_op jit(solution)/shard_map/down/all_to_all | solution.py:21
  222.6 0.1 reshape.177
  222.7 0.8 fusion.5
  (22 shorter events, 0.2 us)
Async XLA Ops:
  0.0 178.8 %copy-start = (bf16[1,512,1024]{2,1,0:T(8,128)(2,1)S(1)}, bf16[1,512,1024]{2,1,0:T(8,128)(2,1)}, u32[]{:S(2)}) copy-start(bf16[1,512,1024]{2,1,0:T(8,128)(2,1)} %param.19) | copy-start | bytes 3145732
  0.9 31.1 %copy-start.8 = (bf16[128,128]{1,0:T(8,128)(2,1)S(1)}, bf16[128,128]{1,0:T(8,128)(2,1)}, u32[]{:S(2)}) copy-start(bf16[128,128]{1,0:T(8,128)(2,1)} %param.11) | copy-start | bytes 98308
  28.1 3.8 %collective-permute-start = (bf16[8,128,256]{2,1,0:T(8,128)(2,1)S(1)}, bf16[8,128,256]{2,1,0:T(8,128)(2,1)S(1)}, u32[]{:S(2)}, u32[]{:S(2)}) collective-permute-start(bf16[8,128,256]{2,1,0:T(8,128)(2,1)S(1)} %all_to_all.35), channel_id=1, source_target_pairs={{0,32},{32,0},{1,33},{33,1},{2,34},{34,2},{3,35},{35,3},{4,36},{36... | collective-permute-start | bytes 1572872 | tf_op jit(solution)/shard_map/kv_gather/ppermute | solution.py:29
  32.0 1.0 copy-start.1
  36.7 14.3 %copy-start.4 = (s32[16,2]{0,1:T(2,128)S(1)}, s32[16,2]{0,1:T(2,128)}, u32[]{:S(2)}) copy-start(s32[16,2]{0,1:T(2,128)} %param.20) | copy-start | bytes 388
  38.0 40.9 %copy-start.2 = (bf16[16,1024]{1,0:T(8,128)(2,1)S(1)}, bf16[16,1024]{1,0:T(8,128)(2,1)}, u32[]{:S(2)}) copy-start(bf16[16,1024]{1,0:T(8,128)(2,1)} %param.14) | copy-start | bytes 98308
  38.0 40.7 %all-to-all-start.1 = ((bf16[32,16,1024]{2,1,0:T(8,128)(2,1)}), bf16[32,16,1024]{2,1,0:T(8,128)(2,1)S(1)}, u32[]{:S(2)}, u32[]{:S(2)}) async-start(bf16[32,16,1024]{2,1,0:T(8,128)(2,1)} %bitcast.3), calls=%async_computation.1 | async-start | bytes 2097152 | tf_op jit(solution)/shard_map/projection/all_to_all | solution.py:21
  96.7 16.4 %copy-start.3 = (f32[1024]{0:T(1024)S(1)}, f32[1024]{0:T(1024)}, u32[]{:S(2)}) copy-start(f32[1024]{0:T(1024)} %param.16) | copy-start | bytes 12292
  108.8 4.8 %copy-start.6 = (bf16[1,1024,512]{2,1,0:T(8,128)(2,1)S(1)}, bf16[1,1024,512]{2,1,0:T(8,128)(2,1)}, u32[]{:S(2)}) copy-start(bf16[1,1024,512]{2,1,0:T(8,128)(2,1)} %param.18) | copy-start | bytes 3145732
  108.8 4.3 %collective-permute-start.1 = (bf16[4,96,1024]{2,1,0:T(8,128)(2,1)S(1)}, bf16[4,96,1024]{2,1,0:T(8,128)(2,1)S(1)}, u32[]{:S(2)}, u32[]{:S(2)}) collective-permute-start(bf16[4,96,1024]{2,1,0:T(8,128)(2,1)S(1)} %all_to_all.37), channel_id=1, source_target_pairs={{0,32},{32,0},{1,33},{33,1},{2,34},{34,2},{3,35},{35,3},{4,36},{36... | collective-permute-start | bytes 2359304 | tf_op jit(solution)/shard_map/dispatch/ppermute | solution.py:29
  113.7 1.2 copy-start.7
  179.9 4.2 %collective-permute-start.2 = (bf16[384,1024]{1,0:T(8,128)(2,1)S(1)}, bf16[384,1024]{1,0:T(8,128)(2,1)S(1)}, u32[]{:S(2)}, u32[]{:S(2)}) collective-permute-start(bf16[384,1024]{1,0:T(8,128)(2,1)S(1)} %split.9), channel_id=1, source_target_pairs={{0,32},{32,0},{1,33},{33,1},{2,34},{34,2},{3,35},{35,3},{4,36},{36... | collective-permute-start | bytes 2359304 | tf_op jit(solution)/shard_map/down/ppermute | solution.py:144
  184.4 23.4 %copy-start.5 = (f32[16,2]{0,1:T(2,128)S(1)}, f32[16,2]{0,1:T(2,128)}, u32[]{:S(2)}) copy-start(f32[16,2]{0,1:T(2,128)} %param.21) | copy-start | bytes 388
  200.6 22.0 %all-to-all-start.6 = ((bf16[16,6,1024]{2,1,0:T(8,128)(2,1)}), bf16[16,6,1024]{2,1,0:T(8,128)(2,1)S(1)}, u32[]{:S(2)}, u32[]{:S(2)}) async-start(bf16[16,6,1024]{2,1,0:T(8,128)(2,1)} %reshape.176), calls=%async_computation.6 | async-start | bytes 524288 | tf_op jit(solution)/shard_map/down/all_to_all | solution.py:21

commit v3 on v2

v3 whole, which is shorter than its diff:
```python
import math

import jax
import jax.numpy as jnp
from jax import lax
from jax.experimental import pallas as pl
from jax.experimental.pallas import tpu as pltpu
from jax.sharding import Mesh
from jax.sharding import PartitionSpec as P

HEADS = 32
KV_HEADS = 8
HEAD = 128
D = 4096
TOP = 2
EXPERTS = 8
CAP = 6
CTX = ("x", "yh", "core")
PLANE = ("x", "yh")
F32, BF16 = jnp.float32, jnp.bfloat16
TAIL = 16


def swap(value, axes):
    return lax.all_to_all(value, axes, split_axis=0, concat_axis=0, tiled=True)


def spread(value, axes):
    return swap(jnp.broadcast_to(value[None], (lax.axis_size(axes),) + value.shape), axes)


def other_core(value):
    return lax.ppermute(value, "core", [(0, 1), (1, 0)])


def whole(kernel, out_shapes, flops, smem=0):
    def call(*operands):
        spaces = [pltpu.SMEM] * smem + [pltpu.VMEM] * (len(operands) - smem)
        moved = sum(math.prod(a.shape) * a.dtype.itemsize for a in operands)
        moved += sum(math.prod(a.shape) * a.dtype.itemsize for a in out_shapes)
        return pl.pallas_call(
            kernel,
            out_shape=out_shapes,
            in_specs=[pl.BlockSpec(memory_space=space) for space in spaces],
            out_specs=[pl.BlockSpec(memory_space=pltpu.VMEM)] * len(out_shapes),
            compiler_params=pltpu.CompilerParams(vmem_limit_bytes=24 * 1024 * 1024),
            cost_estimate=pl.CostEstimate(flops=flops, bytes_accessed=moved, transcendentals=0),
        )(*operands)

    return call


def dot_nt(left, right):
    return lax.dot_general(left, right, (((1,), (1,)), ((), ())), preferred_element_type=F32)


def attention_kernel(place, query, near, far, weight, ids, shares, out, selector, mixer):
    ctx, core = place[0], place[1]
    rows, keys = query.shape[0], near.shape[0]
    spot = ctx * rows + lax.broadcasted_iota(jnp.int32, (rows, keys), 0)
    column = lax.broadcasted_iota(jnp.int32, (rows, keys), 1)
    base = (column // rows) * (2 * rows) + column % rows
    scores = []
    for half, source in enumerate((near, far)):
        key_spot = base + (core ^ half) * rows
        product = dot_nt(query[...], source[:, :HEAD]) * (1.0 / math.sqrt(HEAD))
        scores.append(jnp.where(spot >= key_spot, product, -1e30))
    top = jnp.maximum(*(jnp.max(score, axis=1, keepdims=True) for score in scores))
    denom, total = 0.0, 0.0
    for score, source in zip(scores, (near, far)):
        weights = jnp.exp(score - top)
        denom = denom + jnp.sum(weights, axis=1, keepdims=True)
        total = total + jnp.dot(weights.astype(BF16), source[:, HEAD:], preferred_element_type=F32)
    attended = (total / denom).astype(BF16)
    parts, _, width = out.shape
    for part in range(parts):
        columns = weight[:, part * width : (part + 1) * width]
        out[part] = jnp.dot(attended, columns, preferred_element_type=F32).astype(BF16)

    tokens, slots = mixer.shape
    lane = lax.broadcasted_iota(jnp.int32, (tokens, 128), 1)
    chosen = [ids[:, k : k + 1] for k in range(TOP)]
    named = [(lane == chosen[k]).astype(F32) for k in range(TOP)]
    earlier = lax.broadcasted_iota(jnp.int32, (tokens, tokens), 0) > lax.broadcasted_iota(
        jnp.int32, (tokens, tokens), 1
    )
    before = jnp.dot(earlier.astype(BF16), (named[0] + named[1]).astype(BF16), preferred_element_type=F32)
    slot_lane = lax.broadcasted_iota(jnp.int32, (tokens, slots), 1)
    mixed, picked = 0.0, 0.0
    for k in range(TOP):
        slot = jnp.sum(before * named[k], axis=1, keepdims=True).astype(jnp.int32)
        hit = (slot_lane == chosen[k] * CAP + slot).astype(F32)
        picked = picked + hit
        mixed = mixed + hit * shares[:, k : k + 1]
    selector[...] = picked.astype(BF16)
    mixer[...] = mixed


def gate_up_kernel(place, near, far, gain, gate, up, *outs):
    hid = place[0]
    piece = gate.shape[1] // len(outs)
    half = near.shape[0]
    ones = jnp.ones((8, near.shape[1]), BF16)
    sums = []
    for index, source in enumerate((near, far)):
        rows = source[...].astype(F32)
        scaled = (rows * gain[...]).astype(BF16)
        for k, out in enumerate(outs):
            start = pl.multiple_of((hid ^ k) * piece, piece)
            weight = jnp.concatenate([gate[:, pl.ds(start, piece)], up[:, pl.ds(start, piece)]], axis=1)
            product = jnp.dot(scaled, weight, preferred_element_type=F32)
            out[index * half : (index + 1) * half, :] = product.astype(BF16)
        square = rows * rows
        high = square.astype(BF16)
        low = (square - high.astype(F32)).astype(BF16)
        sums.append(dot_nt(ones, high) + dot_nt(ones, low))
    norm = jnp.concatenate(sums, axis=1)
    high = norm.astype(BF16).astype(F32)
    low = norm - high
    width = 2 * piece
    groups = norm.shape[1] // width
    line = lax.broadcasted_iota(jnp.int32, (8, width), 0)
    tail = jnp.zeros((8, width), F32)
    for group in range(groups):
        lanes = slice(group * width, (group + 1) * width)
        tail = jnp.where(line == group, high[:, lanes], tail)
        tail = jnp.where(line == group + groups, low[:, lanes], tail)
    tail = jnp.concatenate([tail, jnp.zeros((TAIL - 8, width), F32)], axis=0).astype(BF16)
    for out in outs:
        out[2 * half :, :] = tail


def active_kernel(*refs):
    parts, out = refs[:-1], refs[-1]
    total, piece = out.shape
    width = 2 * piece
    groups = total // width
    tail = sum(part[total:, :].astype(F32) for part in parts)
    for group in range(groups):
        norm = tail[group : group + 1, :] + tail[group + groups : group + groups + 1, :]
        inverse = lax.rsqrt(norm / D + 1e-05)
        inverse = jnp.broadcast_to(inverse, (piece, width)).T
        rows = slice(group * width, (group + 1) * width)
        summed = sum(part[rows, :].astype(F32) for part in parts)
        gate = summed[:, :piece] * inverse
        up = summed[:, piece:] * inverse
        out[rows, :] = (gate / (1.0 + jnp.exp(-gate)) * up).astype(BF16)


def down_kernel(active, weight, near, far):
    half = near.shape[0]
    for index, out in enumerate((near, far)):
        rows = slice(index * half, (index + 1) * half)
        left = jnp.concatenate([active[h, rows, :] for h in range(active.shape[0])], axis=1)
        out[...] = jnp.dot(left, weight[...], preferred_element_type=F32).astype(BF16)


def shards(
    queries,
    key_heads,
    value_heads,
    residual,
    out_weight,
    norm_gain,
    gate_weight,
    up_weight,
    down_weight,
    expert_ids,
    expert_weights,
):
    plane = lax.axis_size(PLANE)
    lines, halves = lax.axis_size("x"), lax.axis_size("yh")
    exp_count = lax.axis_size("exp")
    hid_count = lax.axis_size("hid")
    tok_rows = queries.shape[0]
    row_count = tok_rows // exp_count
    width_part = D // hid_count
    shape = jax.ShapeDtypeStruct

    with jax.named_scope("kv_gather"):
        near = spread(jnp.concatenate([key_heads, value_heads], axis=1), PLANE)
        near = near.reshape(plane * tok_rows, 2 * HEAD)
        far = other_core(near)
    with jax.named_scope("attention"):
        place = jnp.stack([lax.axis_index(CTX), lax.axis_index("core")]).astype(jnp.int32)
        partials, selector, mixer = whole(
            attention_kernel,
            [
                shape((hid_count, tok_rows, width_part), BF16),
                shape((row_count, EXPERTS * CAP), BF16),
                shape((row_count, EXPERTS * CAP), F32),
            ],
            flops=2 * tok_rows * HEAD * (4 * plane * tok_rows + D),
            smem=1,
        )(place, queries, near, far, out_weight, expert_ids, expert_weights)
    with jax.named_scope("projection"):
        partials = partials.reshape(hid_count * exp_count, row_count, width_part)
        mixed = jnp.sum(swap(partials, ("hid", "exp")).astype(F32), axis=0)
        stream = residual.astype(F32) + mixed
        stream_bf = stream.astype(BF16)

    with jax.named_scope("dispatch"):
        outgoing = lax.dot_general(
            selector, stream_bf, (((0,), (0,)), ((), ())), preferred_element_type=F32
        ).astype(BF16)
        outgoing = outgoing.reshape(1, exp_count, CAP, width_part)
        outgoing = jnp.broadcast_to(outgoing, (halves, exp_count, CAP, width_part))
        arrived = swap(outgoing.reshape(halves * exp_count, CAP, width_part), ("yh", "exp"))
        arrived = spread(arrived.reshape(halves * exp_count * CAP, width_part), "x")
        half = plane * exp_count * CAP
        total = 2 * half
        near = arrived.reshape(half, width_part)
        far = other_core(near)

    with jax.named_scope("gate_up"):
        ff_part = gate_weight.shape[2]
        piece = ff_part // hid_count
        parts = whole(
            gate_up_kernel,
            [shape((total + TAIL, 2 * piece), BF16)] * hid_count,
            flops=4 * total * width_part * ff_part,
            smem=1,
        )(
            lax.axis_index("hid").astype(jnp.int32).reshape(1),
            near,
            far,
            norm_gain.reshape(1, width_part),
            gate_weight[0],
            up_weight[0],
        )
        arrivals = [parts[0]]
        for k in reversed(range(1, hid_count)):
            arrivals.append(lax.ppermute(parts[k], "hid", [(h, h ^ k) for h in range(hid_count)]))
    with jax.named_scope("active"):
        (active,) = whole(active_kernel, [shape((total, piece), BF16)], flops=total * piece * 20)(*arrivals)
        active = lax.all_gather(active, "hid", axis=0, tiled=False)
    with jax.named_scope("down"):
        near, far = whole(
            down_kernel, [shape((half, width_part), BF16)] * 2, flops=2 * total * ff_part * width_part
        )(active, down_weight[0])
        far = other_core(far)
        back = (near.astype(F32) + far.astype(F32)).astype(BF16)
        back = swap(back.reshape(lines, half // lines, width_part), "x")
        back = jnp.sum(back.astype(F32), axis=0).astype(BF16)
        back = swap(back.reshape(halves * exp_count, CAP, width_part), ("yh", "exp"))
        back = back.reshape(halves, EXPERTS * CAP, width_part).astype(F32)
        back = jnp.sum(back, axis=0)
    with jax.named_scope("combine"):
        combined = jnp.dot(mixer, back, precision=lax.Precision.HIGHEST)
        return (stream + combined).astype(BF16)


def solution(mesh):
    ctx, exp, hid = mesh.devices.shape
    split = Mesh(mesh.devices.reshape(ctx // 4, 2, 2, exp, hid), CTX + ("exp", "hid"))
    return jax.shard_map(
        shards,
        mesh=split,
        in_specs=(
            P(CTX, ("exp", "hid")),
            P(CTX, "exp"),
            P(CTX, "exp"),
            P(CTX + ("exp",), "hid"),
            P(("exp", "hid"), None),
            P("hid"),
            P("exp", "hid", CTX),
            P("exp", "hid", CTX),
            P("exp", CTX, "hid"),
            P(CTX + ("exp",), None),
            P(CTX + ("exp",), None),
        ),
        out_specs=P(CTX + ("exp",), "hid"),
        check_vma=False,
    )
```

time: 224 us -> 213 us (0.951)
  blocking collectives: 131 us -> 152 us
  waiting for transfers between devices: 48 us -> 34.8 us
  starting transfers between devices: 26.1 us -> 15 us
  Pallas kernels: 0 us -> 6.81 us
  local copies, waits for them, and re-layouts: 7.35 us -> 1.18 us
  matrix products: 7.09 us -> 1.03 us
  other arithmetic: 3.94 us -> 1.57 us
    all_to_all x2 -> x0, waiting for transfers between devices: 41.7 us -> none  [swap(): return lax.all_to_all(value, axes, split_axis=0, concat_axis=0, tiled=True)]
    ppermute x3 -> x6, waiting for transfers between devices: 6.34 us -> 34.8 us  [the longest x3 28.5 us: shards(): lax.ppermute(parts[k], 'hid', [(h, h ^ k) for h in range(hid_count)])]
    all_to_all x5 -> x6, blocking collectives: 112 us -> 133 us  [swap(): return lax.all_to_all(value, axes, split_axis=0, concat_axis=0, tiled=True)]
    all_to_all x2 -> x0, starting transfers between devices: 20.2 us -> none  [swap(): return lax.all_to_all(value, axes, split_axis=0, concat_axis=0, tiled=True)]
    ppermute x3 -> x6, starting transfers between devices: 5.87 us -> 15 us  [the longest x3 9.22 us: shards(): lax.ppermute(parts[k], 'hid', [(h, h ^ k) for h in range(hid_count)])]
    pallas_call x0 -> x4, Pallas kernels: none -> 6.81 us  [call(): pl.pallas_call(kernel, out_shape=out_shapes, in_specs=[pl.BlockSpec(memor...]
    dot_general x5 -> x0, matrix products: 6.03 us -> none  [the longest x1 2.44 us: shards(): jnp.dot(attended, out_weight, preferred_element_type=f32).astype(bf16)]
    another operation x1 -> x0, local copies, waits for them, and re-layouts: 2.38 us -> none  [shards(): jnp.stack([jnp.concatenate([jnp.concatenate([gate[:, h * piece:(h + 1) *...]
  transfers between devices with their start and end apart: 5 -> 6, of which waited for: 5 -> 5; matrix products, arithmetic and copies ran while one was open for 0% -> 0% of each run, Pallas kernels for 0% -> 0%
where the time goes in v3:
time: 213 us
  blocking collectives  152 us (71%)
  waiting for transfers between devices  34.8 us (16%)
  starting transfers between devices  15 us (7%)
  Pallas kernels  6.81 us (3%)
    all_to_all x6, blocking collectives, swap(): return lax.all_to_all(value, axes, split_axis=0, concat_axis=0, tiled=True)  133 us
    ppermute x3, waiting for transfers between devices, shards(): lax.ppermute(parts[k], 'hid', [(h, h ^ k) for h in range(hid_count)])  28.5 us
    all_gather x1, blocking collectives, shards(): active = lax.all_gather(active, 'hid', axis=0, tiled=False)  19.2 us
    ppermute x3, starting transfers between devices, shards(): lax.ppermute(parts[k], 'hid', [(h, h ^ k) for h in range(hid_count)])  9.22 us
    pallas_call x4, Pallas kernels, call(): pl.pallas_call(kernel, out_shape=out_shapes, in_specs=[pl.BlockSpec(memor...  6.81 us
    ppermute x3, waiting for transfers between devices, other_core(): return lax.ppermute(value, 'core', [(0, 1), (1, 0)])  6.24 us
    ppermute x3, starting transfers between devices, other_core(): return lax.ppermute(value, 'core', [(0, 1), (1, 0)])  5.74 us
  transfers between devices with their start and end apart: 6, of which 5 were waited for; matrix products, arithmetic and copies ran while one was open for 0% of the time, Pallas kernels for 0%

profile of v3, /device:TPU:16, one launch (start us, length us, event | category | flops | bytes accessed | tf_op | source)
XLA Modules:
  0.0 212.7 jit_solution(6442488417116161847)
XLA Ops:
  0.0 0.0 copy-start.7
  0.0 0.0 copy-start.8
  0.0 0.0 copy-start
  0.0 0.0 copy-start.1
  0.0 0.9 pad_maximum_fusion
  0.9 27.2 %all_to_all.30 = bf16[8,128,256]{2,1,0:T(8,128)(2,1)S(1)} all-to-all(bf16[8,128,256]{2,1,0:T(8,128)(2,1)S(1)} %broadcast_in_dim.20), channel_id=1, replica_groups=mesh['x'=4,'yh'=2,'core'=2,'exp'=8,'hid'=4] {'x','yh'}, dimensions={0} | all-to-all | bytes 1048576 | tf_op jit(solution)/shard_map/kv_gather/all_to_all | solution.py:25
  28.1 1.9 collective-permute-start
  30.0 0.0 copy-done.7
  30.0 0.1 copy.14.ids
  30.1 0.0 copy-done.8
  30.1 0.1 copy.15.shares
  30.2 0.1 pad_add_fusion.place
  30.3 1.6 collective-permute-done.far
  31.9 0.0 copy-done
  31.9 0.0 copy-done.1
  31.9 1.8 attention.1
  33.7 40.4 %all_to_all.31 = bf16[32,16,1024]{2,1,0:T(8,128)(2,1)S(1)} all-to-all(bf16[32,16,1024]{2,1,0:T(8,128)(2,1)S(1)} %bitcast.18), channel_id=1, replica_groups=mesh['x'=4,'yh'=2,'core'=2,'exp'=8,'hid'=4] {'hid','exp'}, dimensions={0} | all-to-all | bytes 2097152 | tf_op jit(solution)/shard_map/projection/all_to_all | solution.py:25
  74.1 0.0 copy-start.6
  74.1 0.2 convert_reduce_fusion
  74.3 0.6 copy-done.6
  74.9 0.2 convolution_convert_fusion
  75.1 17.6 %all_to_all.32 = bf16[16,6,1024]{2,1,0:T(8,128)(2,1)S(1)} all-to-all(bf16[16,6,1024]{2,1,0:T(8,128)(2,1)S(1)} %bitcast.27), channel_id=1, replica_groups=mesh['x'=4,'yh'=2,'core'=2,'exp'=8,'hid'=4] {'yh','exp'}, dimensions={0} | all-to-all | bytes 393216 | tf_op jit(solution)/shard_map/dispatch/all_to_all | solution.py:25
  92.7 0.1 broadcast_in_dim.23
  92.8 0.0 copy-start.2
  92.8 0.0 copy-start.3
  92.8 0.0 copy-start.5
  92.8 0.1 broadcast_in_dim.24
  92.9 12.0 %all_to_all.33 = bf16[4,96,1024]{2,1,0:T(8,128)(2,1)S(1)} all-to-all(bf16[4,96,1024]{2,1,0:T(8,128)(2,1)S(1)} %broadcast_in_dim.24), channel_id=1, replica_groups=mesh['x'=4,'yh'=2,'core'=2,'exp'=8,'hid'=4] {'x'}, dimensions={0} | all-to-all | bytes 1572864 | tf_op jit(solution)/shard_map/dispatch/all_to_all | solution.py:25
  104.9 1.9 collective-permute-start.1
  106.9 2.4 %collective-permute-done.1.far = bf16[384,1024]{1,0:T(8,128)(2,1)} collective-permute-done((bf16[384,1024]{1,0:T(8,128)(2,1)S(1)}, bf16[384,1024]{1,0:T(8,128)(2,1)}, u32[]{:S(2)}, u32[]{:S(2)}) %collective-permute-start.1) | collective-permute-done | bytes 786464 | tf_op jit(solution)/shard_map/dispatch/ppermute | solution.py:33
  109.2 0.0 copy-done.2
  109.2 0.0 copy-done.3
  109.2 0.0 copy-done.5
  109.2 3.7 %gate_up.1 = (bf16[784,256]{1,0:T(8,128)(2,1)S(1)}, bf16[784,256]{1,0:T(8,128)(2,1)S(1)}, bf16[784,256]{1,0:T(8,128)(2,1)S(1)}, bf16[784,256]{1,0:T(8,128)(2,1)S(1)}) custom-call(s32[1]{0:T(128)} %bitcast.4.place, bf16[384,1024]{1,0:T(8,128)(2,1)S(1)} %bitcast.20, bf16[384,1024]{1,0:T(8,128)(2,1)} %collective-permute-done.1.far, f32[1,1024]{1,0:T(1,128)S(1)} %bitcast.25, ...), custom_call_target="tpu_custom_call" | custom-call | flops 1610612736 | bytes 5279748 | tf_op jit(solution)/shard_map/gate_up/pallas_call | solution.py:41
  113.0 3.1 %collective-permute-start.2 = (bf16[784,256]{1,0:T(8,128)(2,1)S(1)}, bf16[784,256]{1,0:T(8,128)(2,1)S(1)}, u32[]{:S(2)}, u32[]{:S(2)}) collective-permute-start(bf16[784,256]{1,0:T(8,128)(2,1)S(1)} %get-tuple-element.18), channel_id=1, source_target_pairs={{0,3},{1,2},{2,1},{3,0},{4,7},{5,6},{6,5},{7,4},{8,11},{9,10},{10,... | collective-permute-start | bytes 1204232 | tf_op jit(solution)/shard_map/gate_up/ppermute | solution.py:233
  116.1 4.0 %collective-permute-start.3 = (bf16[784,256]{1,0:T(8,128)(2,1)S(1)}, bf16[784,256]{1,0:T(8,128)(2,1)S(1)}, u32[]{:S(2)}, u32[]{:S(2)}) collective-permute-start(bf16[784,256]{1,0:T(8,128)(2,1)S(1)} %get-tuple-element.19), channel_id=1, source_target_pairs={{0,2},{1,3},{2,0},{3,1},{4,6},{5,7},{6,4},{7,5},{8,10},{9,11},{10,... | collective-permute-start | bytes 1204232 | tf_op jit(solution)/shard_map/gate_up/ppermute | solution.py:233
  120.1 2.1 collective-permute-start.4
  122.2 22.0 %collective-permute-done.2.refs_1_ = bf16[784,256]{1,0:T(8,128)(2,1)S(1)} collective-permute-done((bf16[784,256]{1,0:T(8,128)(2,1)S(1)}, bf16[784,256]{1,0:T(8,128)(2,1)S(1)}, u32[]{:S(2)}, u32[]{:S(2)}) %collective-permute-start.2) | collective-permute-done | bytes 401440 | tf_op jit(solution)/shard_map/gate_up/ppermute | solution.py:233
  144.2 6.5 %collective-permute-done.3.refs_2_ = bf16[784,256]{1,0:T(8,128)(2,1)S(1)} collective-permute-done((bf16[784,256]{1,0:T(8,128)(2,1)S(1)}, bf16[784,256]{1,0:T(8,128)(2,1)S(1)}, u32[]{:S(2)}, u32[]{:S(2)}) %collective-permute-start.3) | collective-permute-done | bytes 401440 | tf_op jit(solution)/shard_map/gate_up/ppermute | solution.py:233
  150.7 0.0 collective-permute-done.4.refs_3_
  150.7 0.0 copy-start.4
  150.7 0.3 active.1
  151.1 19.2 %all-gather = bf16[3072,128]{1,0:T(8,128)(2,1)S(1)} all-gather(bf16[768,128]{1,0:T(8,128)(2,1)S(1)} %active.1), channel_id=2, replica_groups=mesh['x'=4,'yh'=2,'core'=2,'exp'=8,'hid'=4] {'hid'}, dimensions={0}, use_global_device_ids=true | all-gather | bytes 983040 | tf_op jit(solution)/shard_map/active/all_gather | solution.py:236
  170.3 0.0 copy-done.4
  170.3 1.0 down.1
  171.3 1.9 collective-permute-start.5
  173.2 2.3 %collective-permute-done.5 = bf16[384,1024]{1,0:T(8,128)(2,1)S(1)} collective-permute-done((bf16[384,1024]{1,0:T(8,128)(2,1)S(1)}, bf16[384,1024]{1,0:T(8,128)(2,1)S(1)}, u32[]{:S(2)}, u32[]{:S(2)}) %collective-permute-start.5) | collective-permute-done | bytes 786464 | tf_op jit(solution)/shard_map/down/ppermute | solution.py:33
  175.5 0.3 add_convert_fusion
  175.8 15.3 %all_to_all.34 = bf16[4,96,1024]{2,1,0:T(8,128)(2,1)S(1)} all-to-all(bf16[4,96,1024]{2,1,0:T(8,128)(2,1)S(1)} %bitcast.26), channel_id=1, replica_groups=mesh['x'=4,'yh'=2,'core'=2,'exp'=8,'hid'=4] {'x'}, dimensions={0} | all-to-all | bytes 1572864 | tf_op jit(solution)/shard_map/down/all_to_all | solution.py:25
  191.1 0.1 reduce_sum.31
  191.2 0.1 reshape.39
  191.3 20.5 %all_to_all.35 = bf16[16,6,1024]{2,1,0:T(8,128)(2,1)S(1)} all-to-all(bf16[16,6,1024]{2,1,0:T(8,128)(2,1)S(1)} %reshape.39), channel_id=1, replica_groups=mesh['x'=4,'yh'=2,'core'=2,'exp'=8,'hid'=4] {'yh','exp'}, dimensions={0} | all-to-all | bytes 393216 | tf_op jit(solution)/shard_map/down/all_to_all | solution.py:25
  211.8 0.1 reshape.40
  211.9 0.8 fusion
  (4 shorter events, 0.1 us)
Async XLA Ops:
  0.0 30.0 %copy-start.7 = (s32[16,2]{0,1:T(2,128)S(1)}, s32[16,2]{0,1:T(2,128)}, u32[]{:S(2)}) copy-start(s32[16,2]{0,1:T(2,128)} %param.20) | copy-start | bytes 388
  0.0 30.1 %copy-start.8 = (f32[16,2]{0,1:T(2,128)S(1)}, f32[16,2]{0,1:T(2,128)}, u32[]{:S(2)}) copy-start(f32[16,2]{0,1:T(2,128)} %param.21) | copy-start | bytes 388
  0.0 31.9 %copy-start = (bf16[128,4096]{1,0:T(8,128)(2,1)S(1)}, bf16[128,4096]{1,0:T(8,128)(2,1)}, u32[]{:S(2)}) copy-start(bf16[128,4096]{1,0:T(8,128)(2,1)} %weight.1) | copy-start | bytes 3145732
  0.0 31.9 %copy-start.1 = (bf16[128,128]{1,0:T(8,128)(2,1)S(1)}, bf16[128,128]{1,0:T(8,128)(2,1)}, u32[]{:S(2)}) copy-start(bf16[128,128]{1,0:T(8,128)(2,1)} %query.1) | copy-start | bytes 98308
  28.1 3.8 %collective-permute-start = (bf16[1024,256]{1,0:T(8,128)(2,1)S(1)}, bf16[1024,256]{1,0:T(8,128)(2,1)S(1)}, u32[]{:S(2)}, u32[]{:S(2)}) collective-permute-start(bf16[1024,256]{1,0:T(8,128)(2,1)S(1)} %bitcast.16), channel_id=1, source_target_pairs={{0,32},{32,0},{1,33},{33,1},{2,34},{34,2},{3,35},{35,3},{4,36},{36... | collective-permute-start | bytes 1572872 | tf_op jit(solution)/shard_map/kv_gather/ppermute | solution.py:33
  74.1 0.8 copy-start.6
  92.8 16.5 %copy-start.2 = (bf16[1,1024,512]{2,1,0:T(8,128)(2,1)S(1)}, bf16[1,1024,512]{2,1,0:T(8,128)(2,1)}, u32[]{:S(2)}) copy-start(bf16[1,1024,512]{2,1,0:T(8,128)(2,1)} %param.17) | copy-start | bytes 3145732
  92.8 16.5 %copy-start.3 = (bf16[1,1024,512]{2,1,0:T(8,128)(2,1)S(1)}, bf16[1,1024,512]{2,1,0:T(8,128)(2,1)}, u32[]{:S(2)}) copy-start(bf16[1,1024,512]{2,1,0:T(8,128)(2,1)} %param.18) | copy-start | bytes 3145732
  92.8 16.4 %copy-start.5 = (f32[1024]{0:T(1024)S(1)}, f32[1024]{0:T(1024)}, u32[]{:S(2)}) copy-start(f32[1024]{0:T(1024)} %param.16) | copy-start | bytes 12292
  104.9 4.3 %collective-permute-start.1 = (bf16[384,1024]{1,0:T(8,128)(2,1)S(1)}, bf16[384,1024]{1,0:T(8,128)(2,1)}, u32[]{:S(2)}, u32[]{:S(2)}) collective-permute-start(bf16[384,1024]{1,0:T(8,128)(2,1)S(1)} %bitcast.19), channel_id=1, source_target_pairs={{0,32},{32,0},{1,33},{33,1},{2,34},{34,2},{3,35},{35,3},{4,36},{36... | collective-permute-start | bytes 2359304 | tf_op jit(solution)/shard_map/dispatch/ppermute | solution.py:33
  113.0 31.2 %collective-permute-start.2 = (bf16[784,256]{1,0:T(8,128)(2,1)S(1)}, bf16[784,256]{1,0:T(8,128)(2,1)S(1)}, u32[]{:S(2)}, u32[]{:S(2)}) collective-permute-start(bf16[784,256]{1,0:T(8,128)(2,1)S(1)} %get-tuple-element.18), channel_id=1, source_target_pairs={{0,3},{1,2},{2,1},{3,0},{4,7},{5,6},{6,5},{7,4},{8,11},{9,10},{10,... | collective-permute-start | bytes 1204232 | tf_op jit(solution)/shard_map/gate_up/ppermute | solution.py:233
  116.1 34.6 %collective-permute-start.3 = (bf16[784,256]{1,0:T(8,128)(2,1)S(1)}, bf16[784,256]{1,0:T(8,128)(2,1)S(1)}, u32[]{:S(2)}, u32[]{:S(2)}) collective-permute-start(bf16[784,256]{1,0:T(8,128)(2,1)S(1)} %get-tuple-element.19), channel_id=1, source_target_pairs={{0,2},{1,3},{2,0},{3,1},{4,6},{5,7},{6,4},{7,5},{8,10},{9,11},{10,... | collective-permute-start | bytes 1204232 | tf_op jit(solution)/shard_map/gate_up/ppermute | solution.py:233
  120.1 30.6 %collective-permute-start.4 = (bf16[784,256]{1,0:T(8,128)(2,1)S(1)}, bf16[784,256]{1,0:T(8,128)(2,1)S(1)}, u32[]{:S(2)}, u32[]{:S(2)}) collective-permute-start(bf16[784,256]{1,0:T(8,128)(2,1)S(1)} %get-tuple-element.20), channel_id=1, source_target_pairs={{0,1},{1,0},{2,3},{3,2},{4,5},{5,4},{6,7},{7,6},{8,9},{9,8},{10,11... | collective-permute-start | bytes 1204232 | tf_op jit(solution)/shard_map/gate_up/ppermute | solution.py:233
  150.7 19.6 %copy-start.4 = (bf16[1,512,1024]{2,1,0:T(8,128)(2,1)S(1)}, bf16[1,512,1024]{2,1,0:T(8,128)(2,1)}, u32[]{:S(2)}) copy-start(bf16[1,512,1024]{2,1,0:T(8,128)(2,1)} %param.19) | copy-start | bytes 3145732
  171.3 4.2 %collective-permute-start.5 = (bf16[384,1024]{1,0:T(8,128)(2,1)S(1)}, bf16[384,1024]{1,0:T(8,128)(2,1)S(1)}, u32[]{:S(2)}, u32[]{:S(2)}) collective-permute-start(bf16[384,1024]{1,0:T(8,128)(2,1)S(1)} %get-tuple-element.22), channel_id=1, source_target_pairs={{0,32},{32,0},{1,33},{33,1},{2,34},{34,2},{3,35},{35,3},{4,36},{36... | collective-permute-start | bytes 2359304 | tf_op jit(solution)/shard_map/down/ppermute | solution.py:33

commit v4 on v3

--- a/solution.py
+++ b/solution.py
@@ -31,6 +31,10 @@
 
 def other_core(value):
     return lax.ppermute(value, "core", [(0, 1), (1, 0)])
+
+
+def to_peer(value, offset):
+    return lax.ppermute(value, "hid", [(h, h ^ offset) for h in range(lax.axis_size("hid"))])
 
 
 def whole(kernel, out_shapes, flops, smem=0):
@@ -96,63 +100,120 @@
     mixer[...] = mixed
 
 
-def gate_up_kernel(place, near, far, gain, gate, up, *outs):
-    hid = place[0]
-    piece = gate.shape[1] // len(outs)
-    half = near.shape[0]
-    ones = jnp.ones((8, near.shape[1]), BF16)
-    sums = []
-    for index, source in enumerate((near, far)):
-        rows = source[...].astype(F32)
-        scaled = (rows * gain[...]).astype(BF16)
-        for k, out in enumerate(outs):
-            start = pl.multiple_of((hid ^ k) * piece, piece)
-            weight = jnp.concatenate([gate[:, pl.ds(start, piece)], up[:, pl.ds(start, piece)]], axis=1)
-            product = jnp.dot(scaled, weight, preferred_element_type=F32)
-            out[index * half : (index + 1) * half, :] = product.astype(BF16)
-        square = rows * rows
+def gate_up_kernel(place, rows, gain, weight, *refs):
+    outs, scaled, product = refs[:-2], refs[-2], refs[-1]
+    step, hid = pl.program_id(0), place[0]
+    count, depth = rows.shape
+    piece = outs[0].shape[1] // 2
+
+    @pl.when(step == 0)
+    def _():
+        widened = rows[...].astype(F32)
+        scaled[...] = (widened * gain[...]).astype(BF16)
+        square = jnp.concatenate([widened * widened, jnp.zeros((128 - count, depth), F32)], axis=0)
         high = square.astype(BF16)
         low = (square - high.astype(F32)).astype(BF16)
-        sums.append(dot_nt(ones, high) + dot_nt(ones, low))
-    norm = jnp.concatenate(sums, axis=1)
-    high = norm.astype(BF16).astype(F32)
-    low = norm - high
-    width = 2 * piece
-    groups = norm.shape[1] // width
-    line = lax.broadcasted_iota(jnp.int32, (8, width), 0)
-    tail = jnp.zeros((8, width), F32)
-    for group in range(groups):
-        lanes = slice(group * width, (group + 1) * width)
-        tail = jnp.where(line == group, high[:, lanes], tail)
-        tail = jnp.where(line == group + groups, low[:, lanes], tail)
-    tail = jnp.concatenate([tail, jnp.zeros((TAIL - 8, width), F32)], axis=0).astype(BF16)
-    for out in outs:
-        out[2 * half :, :] = tail
+        ones = jnp.ones((TAIL, depth), BF16)
+        norm = dot_nt(ones, high) + dot_nt(ones, low)
+        high = norm.astype(BF16).astype(F32)
+        line = lax.broadcasted_iota(jnp.int32, (TAIL, 128), 0)
+        tail = jnp.where(line == 0, high, jnp.where(line == 1, norm - high, 0.0)).astype(BF16)
+        for out in outs:
+            out[count:, :] = jnp.concatenate([tail, jnp.zeros((TAIL, 2 * piece - 128), BF16)], axis=1)
+
+    @pl.when(step > 0)
+    def _():
+        for out in outs:
+            out[count:, :] = jnp.zeros((TAIL, 2 * piece), BF16)
+
+    product[...] = jnp.dot(scaled[...], weight[0], preferred_element_type=F32)
+    for k, out in enumerate(outs):
+        start = pl.multiple_of((hid ^ k) * piece, piece)
+        other = pl.multiple_of((hid ^ k) * piece + len(outs) * piece, piece)
+        out[:count, :piece] = product[:, pl.ds(start, piece)].astype(BF16)
+        out[:count, piece:] = product[:, pl.ds(other, piece)].astype(BF16)
+
+
+def gate_up(place, rows, gain, weight, peers):
+    count, depth = rows.shape
+    slices, _, columns = weight.shape
+    share = columns // peers
+    return pl.pallas_call(
+        gate_up_kernel,
+        out_shape=[jax.ShapeDtypeStruct((count + TAIL, slices * share), BF16)] * peers,
+        grid=(slices,),
+        in_specs=[
+            pl.BlockSpec(memory_space=pltpu.SMEM),
+            pl.BlockSpec((count, depth), lambda s: (0, 0)),
+            pl.BlockSpec((1, depth), lambda s: (0, 0)),
+            pl.BlockSpec((1, depth, columns), lambda s: (s, 0, 0)),
+        ],
+        out_specs=[pl.BlockSpec((count + TAIL, share), lambda s: (0, s))] * peers,
+        scratch_shapes=[pltpu.VMEM((count, depth), BF16), pltpu.VMEM((count, columns), F32)],
+        compiler_params=pltpu.CompilerParams(vmem_limit_bytes=52 * 1024 * 1024),
+        cost_estimate=pl.CostEstimate(
+            flops=2 * count * depth * columns * slices,
+            bytes_accessed=2 * depth * columns * slices,
+            transcendentals=0,
+        ),
+    )(place, rows, gain, weight)
 
 
 def active_kernel(*refs):
     parts, out = refs[:-1], refs[-1]
-    total, piece = out.shape
-    width = 2 * piece
-    groups = total // width
-    tail = sum(part[total:, :].astype(F32) for part in parts)
-    for group in range(groups):
-        norm = tail[group : group + 1, :] + tail[group + groups : group + groups + 1, :]
-        inverse = lax.rsqrt(norm / D + 1e-05)
-        inverse = jnp.broadcast_to(inverse, (piece, width)).T
-        rows = slice(group * width, (group + 1) * width)
-        summed = sum(part[rows, :].astype(F32) for part in parts)
-        gate = summed[:, :piece] * inverse
-        up = summed[:, piece:] * inverse
-        out[rows, :] = (gate / (1.0 + jnp.exp(-gate)) * up).astype(BF16)
-
-
-def down_kernel(active, weight, near, far):
-    half = near.shape[0]
-    for index, out in enumerate((near, far)):
-        rows = slice(index * half, (index + 1) * half)
-        left = jnp.concatenate([active[h, rows, :] for h in range(active.shape[0])], axis=1)
-        out[...] = jnp.dot(left, weight[...], preferred_element_type=F32).astype(BF16)
+    piece = out.shape[1]
+    count = parts[0].shape[0] - TAIL
+    tail = sum(part[count:, :piece].astype(F32) for part in parts)
+    inverse = lax.rsqrt((tail[0:1, :] + tail[1:2, :]) / D + 1e-05)
+    inverse = jnp.broadcast_to(inverse, (piece, piece)).T[:count, :]
+    for index in range(out.shape[0] // count):
+        start = 2 * index * piece
+        gate = sum(part[:count, start : start + piece].astype(F32) for part in parts) * inverse
+        up = sum(part[:count, start + piece : start + 2 * piece].astype(F32) for part in parts) * inverse
+        out[index * count : (index + 1) * count, :] = (gate / (1.0 + jnp.exp(-gate)) * up).astype(BF16)
+
+
+def down_kernel(place, *refs):
+    parts, (weight, out, left, total) = refs[:-4], refs[-4:]
+    step, hid = pl.program_id(0), place[0]
+    piece = parts[0].shape[1]
+    for k, part in enumerate(parts):
+        left[:, pl.ds(pl.multiple_of((hid ^ k) * piece, piece), piece)] = part[...]
+    product = jnp.dot(left[...], weight[0], preferred_element_type=F32)
+
+    @pl.when(step == 0)
+    def _():
+        total[...] = product
+
+    @pl.when(step > 0)
+    def _():
+        total[...] += product
+
+    @pl.when(step == pl.num_programs(0) - 1)
+    def _():
+        out[...] = total[...].astype(BF16)
+
+
+def down(place, parts, weight):
+    rows, piece = parts[0].shape
+    slices, depth, columns = weight.shape
+    count = rows // slices
+    return pl.pallas_call(
+        down_kernel,
+        out_shape=jax.ShapeDtypeStruct((count, columns), BF16),
+        grid=(slices,),
+        in_specs=[pl.BlockSpec(memory_space=pltpu.SMEM)]
+        + [pl.BlockSpec((count, piece), lambda s: (s, 0))] * len(parts)
+        + [pl.BlockSpec((1, depth, columns), lambda s: (s, 0, 0))],
+        out_specs=pl.BlockSpec((count, columns), lambda s: (0, 0)),
+        scratch_shapes=[pltpu.VMEM((count, depth), BF16), pltpu.VMEM((count, columns), F32)],
+        compiler_params=pltpu.CompilerParams(vmem_limit_bytes=52 * 1024 * 1024),
+        cost_estimate=pl.CostEstimate(
+            flops=2 * count * depth * columns * slices,
+            bytes_accessed=2 * depth * columns * slices,
+            transcendentals=0,
+        ),
+    )(place, *parts, weight)
 
 
 def shards(
@@ -169,7 +230,7 @@
     expert_weights,
 ):
     plane = lax.axis_size(PLANE)
-    lines, halves = lax.axis_size("x"), lax.axis_size("yh")
+    halves = lax.axis_size("yh")
     exp_count = lax.axis_size("exp")
     hid_count = lax.axis_size("hid")
     tok_rows = queries.shape[0]
@@ -177,6 +238,10 @@
     width_part = D // hid_count
     shape = jax.ShapeDtypeStruct
 
+    with jax.named_scope("weight_gather"):
+        gate_up_weight = jnp.concatenate([gate_weight[0], up_weight[0]], axis=1)
+        gate_up_weight = lax.all_gather(gate_up_weight, ("x", "core"), axis=0, tiled=False)
+        down_all = lax.all_gather(down_weight[0], ("x", "core"), axis=0, tiled=False)
     with jax.named_scope("kv_gather"):
         near = spread(jnp.concatenate([key_heads, value_heads], axis=1), PLANE)
         near = near.reshape(plane * tok_rows, 2 * HEAD)
@@ -206,42 +271,19 @@
         outgoing = outgoing.reshape(1, exp_count, CAP, width_part)
         outgoing = jnp.broadcast_to(outgoing, (halves, exp_count, CAP, width_part))
         arrived = swap(outgoing.reshape(halves * exp_count, CAP, width_part), ("yh", "exp"))
-        arrived = spread(arrived.reshape(halves * exp_count * CAP, width_part), "x")
-        half = plane * exp_count * CAP
-        total = 2 * half
-        near = arrived.reshape(half, width_part)
-        far = other_core(near)
+        rows = arrived.reshape(halves * exp_count * CAP, width_part)
 
     with jax.named_scope("gate_up"):
-        ff_part = gate_weight.shape[2]
-        piece = ff_part // hid_count
-        parts = whole(
-            gate_up_kernel,
-            [shape((total + TAIL, 2 * piece), BF16)] * hid_count,
-            flops=4 * total * width_part * ff_part,
-            smem=1,
-        )(
-            lax.axis_index("hid").astype(jnp.int32).reshape(1),
-            near,
-            far,
-            norm_gain.reshape(1, width_part),
-            gate_weight[0],
-            up_weight[0],
-        )
-        arrivals = [parts[0]]
-        for k in reversed(range(1, hid_count)):
-            arrivals.append(lax.ppermute(parts[k], "hid", [(h, h ^ k) for h in range(hid_count)]))
+        spot = lax.axis_index("hid").astype(jnp.int32).reshape(1)
+        parts = gate_up(spot, rows, norm_gain.reshape(1, width_part), gate_up_weight, hid_count)
+        arrivals = [parts[0]] + [to_peer(parts[k], k) for k in reversed(range(1, hid_count))]
     with jax.named_scope("active"):
-        (active,) = whole(active_kernel, [shape((total, piece), BF16)], flops=total * piece * 20)(*arrivals)
-        active = lax.all_gather(active, "hid", axis=0, tiled=False)
+        piece = down_weight.shape[1] // hid_count
+        count = rows.shape[0] * gate_up_weight.shape[0]
+        (active,) = whole(active_kernel, [shape((count, piece), BF16)], flops=count * piece * 20)(*arrivals)
+        actives = {0: active} | {k: to_peer(active, k) for k in reversed(range(1, hid_count))}
     with jax.named_scope("down"):
-        near, far = whole(
-            down_kernel, [shape((half, width_part), BF16)] * 2, flops=2 * total * ff_part * width_part
-        )(active, down_weight[0])
-        far = other_core(far)
-        back = (near.astype(F32) + far.astype(F32)).astype(BF16)
-        back = swap(back.reshape(lines, half // lines, width_part), "x")
-        back = jnp.sum(back.astype(F32), axis=0).astype(BF16)
+        back = down(spot, [actives[k] for k in range(hid_count)], down_all)
         back = swap(back.reshape(halves * exp_count, CAP, width_part), ("yh", "exp"))
         back = back.reshape(halves, EXPERTS * CAP, width_part).astype(F32)
         back = jnp.sum(back, axis=0)

time: 213 us -> 226 us (1.061)
  the two profiles are of different devices: /device:TPU:16 before, /device:TPU:8 now
where the time goes in v4:
time: 226 us; the launch traced here: 225 us
  blocking collectives  91.5 us (40%)
  waiting for transfers between devices  68.4 us (30%)
  starting transfers between devices  25.7 us (11%)
  Pallas kernels  19.7 us (9%)
  between operations  13.6 us (6%)
  other arithmetic  3.55 us (2%)
    all_to_all x3, blocking collectives, swap(): return lax.all_to_all(value, axes, split_axis=0, concat_axis=0, tiled=True)  91.5 us
    ppermute x6, waiting for transfers between devices, to_peer(): lax.ppermute(value, 'hid', [(h, h ^ offset) for h in range(lax.axis_size(...  49 us
    ppermute x6, starting transfers between devices, to_peer(): lax.ppermute(value, 'hid', [(h, h ^ offset) for h in range(lax.axis_size(...  19 us
    all_to_all x1, waiting for transfers between devices, swap(): return lax.all_to_all(value, axes, split_axis=0, concat_axis=0, tiled=True)  14.6 us
    pallas_call x1, Pallas kernels, gate_up(): pl.pallas_call(gate_up_kernel, out_shape=[jax.ShapeDtypeStruct((count + T...  10.6 us
    pallas_call x1, Pallas kernels, down(): pl.pallas_call(down_kernel, out_shape=jax.ShapeDtypeStruct((count, column...  6.93 us
    all_to_all x1, starting transfers between devices, swap(): return lax.all_to_all(value, axes, split_axis=0, concat_axis=0, tiled=True)  4.83 us
  transfers between devices with their start and end apart: 10, of which 8 were waited for; matrix products, arithmetic and copies ran while one was open for 1% of the time, Pallas kernels for 6%

profile of v4, /device:TPU:8, one launch (start us, length us, event | category | flops | bytes accessed | tf_op | source)
XLA Modules:
  0.0 224.8 jit_solution(6696562144946159687)
XLA Ops:
  6.5 0.0 copy-start.4
  6.5 0.0 copy-start.5
  6.5 0.0 all-gather.6.cloned.1.call-start
  6.5 0.0 copy-start.6
  6.5 0.0 copy-start.7
  6.5 0.0 copy-start
  6.6 0.0 copy-start.1
  6.6 3.3 %pad_maximum_fusion = bf16[1024,1024]{1,0:T(8,128)(2,1)} fusion(bf16[1024,512]{1,0:T(8,128)(2,1)} %bitcast.18, bf16[1024,512]{1,0:T(8,128)(2,1)} %bitcast.19), kind=kLoop, calls=%fused_computation | loop fusion | flops 4194304 | bytes 4194304 | tf_op jit(solution)/shard_map/weight_gather/concatenate | solution.py:242
  9.9 0.0 all-gather.6.cloned.1.call-update
  9.9 0.0 copy-start.3
  9.9 0.0 all-gather.4.cloned.1.call-start
  9.9 0.7 all-gather.4.cloned.1.call-update
  10.6 0.0 copy-done.4
  10.7 0.0 copy-done.5
  10.7 0.0 copy-start.2
  10.7 28.1 %all_to_all.20 = bf16[8,128,256]{2,1,0:T(8,128)(2,1)S(1)} all-to-all(bf16[8,128,256]{2,1,0:T(8,128)(2,1)S(1)} %broadcast_in_dim.6), channel_id=1, replica_groups=mesh['x'=4,'yh'=2,'core'=2,'exp'=8,'hid'=4] {'x','yh'}, dimensions={0} | all-to-all | bytes 1048576 | tf_op jit(solution)/shard_map/kv_gather/all_to_all | solution.py:25
  38.8 1.9 collective-permute-start
  40.8 0.0 copy-done.6
  40.8 0.1 copy.16.ids
  40.9 0.0 copy-done.7
  40.9 0.1 copy.17.shares
  40.9 0.1 pad_add_fusion.place
  41.0 1.6 collective-permute-done.far
  42.6 0.0 copy-done
  42.6 0.0 copy-done.1
  42.6 1.8 attention.1
  44.4 39.3 %all_to_all.21 = bf16[32,16,1024]{2,1,0:T(8,128)(2,1)S(1)} all-to-all(bf16[32,16,1024]{2,1,0:T(8,128)(2,1)S(1)} %bitcast.15), channel_id=1, replica_groups=mesh['x'=4,'yh'=2,'core'=2,'exp'=8,'hid'=4] {'hid','exp'}, dimensions={0} | all-to-all | bytes 2097152 | tf_op jit(solution)/shard_map/projection/all_to_all | solution.py:25
  83.7 0.2 convert_reduce_fusion
  83.9 0.0 copy-done.3
  83.9 0.2 convolution_convert_fusion
  84.2 0.7 broadcast_in_dim.15
  84.9 4.8 %all-to-all-start.2 = ((bf16[16,6,1024]{2,1,0:T(8,128)(2,1)}), bf16[16,6,1024]{2,1,0:T(8,128)(2,1)S(1)}, u32[]{:S(2)}, u32[]{:S(2)}) async-start(bf16[16,6,1024]{2,1,0:T(8,128)(2,1)} %bitcast.5), calls=%async_computation.2 | async-start | bytes 524288 | tf_op jit(solution)/shard_map/dispatch/all_to_all | solution.py:25
  89.7 14.6 %all-to-all-done.2 = bf16[16,6,1024]{2,1,0:T(8,128)(2,1)S(1)} async-done(((bf16[16,6,1024]{2,1,0:T(8,128)(2,1)}), bf16[16,6,1024]{2,1,0:T(8,128)(2,1)S(1)}, u32[]{:S(2)}, u32[]{:S(2)}) %all-to-all-start.2) | async-done | bytes 196640 | tf_op jit(solution)/shard_map/dispatch/all_to_all | solution.py:25
  104.4 0.1 reshape.31.rows
  104.4 2.4 %all-gather.6.cloned.1.call-done = bf16[8192,1024]{1,0:T(8,128)(2,1)} async-done(((bf16[1024,1024]{1,0:T(8,128)(2,1)}), bf16[8192,1024]{1,0:T(8,128)(2,1)}) %all-gather.6.cloned.1.call-update) | async-done | bytes 16777232 | tf_op jit(solution)/shard_map/weight_gather/all_gather | solution.py:243
  106.8 0.0 copy-done.2
  106.8 10.6 %gate_up.1 = (bf16[112,2048]{1,0:T(8,128)(2,1)S(1)}, bf16[112,2048]{1,0:T(8,128)(2,1)S(1)}, bf16[112,2048]{1,0:T(8,128)(2,1)S(1)}, bf16[112,2048]{1,0:T(8,128)(2,1)}) custom-call(s32[1]{0:T(128)} %bitcast.4.place, bf16[96,1024]{1,0:T(8,128)(2,1)S(1)} %reshape.31.rows, f32[1,1024]{1,0:T(1,128)S(1)} %bitcast.16, bf16[8,1024,1024]{2,1,0:T(8,128)(2,1)} %bitcast.17), custom_call_target="tpu_custom_call" | custom-call | flops 1610612736 | bytes 16777216 | tf_op jit(solution)/shard_map/gate_up/pallas_call | solution.py:141
  117.5 2.8 %collective-permute-start.1 = (bf16[112,2048]{1,0:T(8,128)(2,1)}, bf16[112,2048]{1,0:T(8,128)(2,1)S(1)}, u32[]{:S(2)}, u32[]{:S(2)}) collective-permute-start(bf16[112,2048]{1,0:T(8,128)(2,1)} %get-tuple-element.16), channel_id=1, source_target_pairs={{0,3},{1,2},{2,1},{3,0},{4,7},{5,6},{6,5},{7,4},{8,11},{9,10},{10,... | collective-permute-start | bytes 1376264 | tf_op jit(solution)/shard_map/gate_up/ppermute | solution.py:37
  120.3 2.6 %collective-permute-start.2 = (bf16[112,2048]{1,0:T(8,128)(2,1)S(1)}, bf16[112,2048]{1,0:T(8,128)(2,1)S(1)}, u32[]{:S(2)}, u32[]{:S(2)}) collective-permute-start(bf16[112,2048]{1,0:T(8,128)(2,1)S(1)} %get-tuple-element.17), channel_id=1, source_target_pairs={{0,2},{1,3},{2,0},{3,1},{4,6},{5,7},{6,4},{7,5},{8,10},{9,11},{10,... | collective-permute-start | bytes 1376264 | tf_op jit(solution)/shard_map/gate_up/ppermute | solution.py:37
  122.8 3.9 %collective-permute-start.3 = (bf16[112,2048]{1,0:T(8,128)(2,1)S(1)}, bf16[112,2048]{1,0:T(8,128)(2,1)S(1)}, u32[]{:S(2)}, u32[]{:S(2)}) collective-permute-start(bf16[112,2048]{1,0:T(8,128)(2,1)S(1)} %get-tuple-element.18), channel_id=1, source_target_pairs={{0,1},{1,0},{2,3},{3,2},{4,5},{5,4},{6,7},{7,6},{8,9},{9,8},{10,11... | collective-permute-start | bytes 1376264 | tf_op jit(solution)/shard_map/gate_up/ppermute | solution.py:37
  126.7 24.8 %collective-permute-done.1.refs_1_ = bf16[112,2048]{1,0:T(8,128)(2,1)S(1)} collective-permute-done((bf16[112,2048]{1,0:T(8,128)(2,1)}, bf16[112,2048]{1,0:T(8,128)(2,1)S(1)}, u32[]{:S(2)}, u32[]{:S(2)}) %collective-permute-start.1) | collective-permute-done | bytes 458784 | tf_op jit(solution)/shard_map/gate_up/ppermute | solution.py:37
  151.5 8.7 %collective-permute-done.2.refs_2_ = bf16[112,2048]{1,0:T(8,128)(2,1)S(1)} collective-permute-done((bf16[112,2048]{1,0:T(8,128)(2,1)S(1)}, bf16[112,2048]{1,0:T(8,128)(2,1)S(1)}, u32[]{:S(2)}, u32[]{:S(2)}) %collective-permute-start.2) | collective-permute-done | bytes 458784 | tf_op jit(solution)/shard_map/gate_up/ppermute | solution.py:37
  160.2 0.0 collective-permute-done.3.refs_3_
  160.2 0.4 active.1.refs_0_
  160.5 4.5 %collective-permute-start.4 = (bf16[768,128]{1,0:T(8,128)(2,1)S(1)}, bf16[768,128]{1,0:T(8,128)(2,1)S(1)}, u32[]{:S(2)}, u32[]{:S(2)}) collective-permute-start(bf16[768,128]{1,0:T(8,128)(2,1)S(1)} %active.1.refs_0_), channel_id=1, source_target_pairs={{0,1},{1,0},{2,3},{3,2},{4,5},{5,4},{6,7},{7,6},{8,9},{9,8},{10,11... | collective-permute-start | bytes 589832 | tf_op jit(solution)/shard_map/active/ppermute | solution.py:37
  165.0 2.7 %collective-permute-start.5 = (bf16[768,128]{1,0:T(8,128)(2,1)S(1)}, bf16[768,128]{1,0:T(8,128)(2,1)S(1)}, u32[]{:S(2)}, u32[]{:S(2)}) collective-permute-start(bf16[768,128]{1,0:T(8,128)(2,1)S(1)} %active.1.refs_0_), channel_id=1, source_target_pairs={{0,2},{1,3},{2,0},{3,1},{4,6},{5,7},{6,4},{7,5},{8,10},{9,11},{10,... | collective-permute-start | bytes 589832 | tf_op jit(solution)/shard_map/active/ppermute | solution.py:37
  167.8 2.6 %collective-permute-start.6 = (bf16[768,128]{1,0:T(8,128)(2,1)S(1)}, bf16[768,128]{1,0:T(8,128)(2,1)S(1)}, u32[]{:S(2)}, u32[]{:S(2)}) collective-permute-start(bf16[768,128]{1,0:T(8,128)(2,1)S(1)} %active.1.refs_0_), channel_id=1, source_target_pairs={{0,3},{1,2},{2,1},{3,0},{4,7},{5,6},{6,5},{7,4},{8,11},{9,10},{10,... | collective-permute-start | bytes 589832 | tf_op jit(solution)/shard_map/active/ppermute | solution.py:37
  170.3 0.0 all-gather.4.cloned.1.call-done.refs_4_
  170.3 0.7 collective-permute-done.4.refs_1_
  171.0 10.5 %collective-permute-done.5.refs_2_ = bf16[768,128]{1,0:T(8,128)(2,1)S(1)} collective-permute-done((bf16[768,128]{1,0:T(8,128)(2,1)S(1)}, bf16[768,128]{1,0:T(8,128)(2,1)S(1)}, u32[]{:S(2)}, u32[]{:S(2)}) %collective-permute-start.5) | collective-permute-done | bytes 196640 | tf_op jit(solution)/shard_map/active/ppermute | solution.py:37
  181.5 4.4 %collective-permute-done.6.refs_3_ = bf16[768,128]{1,0:T(8,128)(2,1)S(1)} collective-permute-done((bf16[768,128]{1,0:T(8,128)(2,1)S(1)}, bf16[768,128]{1,0:T(8,128)(2,1)S(1)}, u32[]{:S(2)}, u32[]{:S(2)}) %collective-permute-start.6) | collective-permute-done | bytes 196640 | tf_op jit(solution)/shard_map/active/ppermute | solution.py:37
  185.9 6.9 %down.1 = bf16[96,1024]{1,0:T(8,128)(2,1)S(1)} custom-call(s32[1]{0:T(128)} %bitcast.4.place, bf16[768,128]{1,0:T(8,128)(2,1)S(1)} %active.1.refs_0_, bf16[768,128]{1,0:T(8,128)(2,1)S(1)} %collective-permute-done.4.refs_1_, bf16[768,128]{1,0:T(8,128)(2,1)S(1)} %collective-permute-done.5.refs_2_, bf16[768,128]{1,0:T(8,128)(2,1)S(1)} %collective-permute-done.6.refs_3_, ...), custom_call_target="tpu_custom_call" | custom-call | flops 805306368 | bytes 8388608 | tf_op jit(solution)/shard_map/down/pallas_call | solution.py:201
  192.8 0.1 reshape.33
  192.9 24.1 %all_to_all.22 = bf16[16,6,1024]{2,1,0:T(8,128)(2,1)S(1)} all-to-all(bf16[16,6,1024]{2,1,0:T(8,128)(2,1)S(1)} %reshape.33), channel_id=1, replica_groups=mesh['x'=4,'yh'=2,'core'=2,'exp'=8,'hid'=4] {'yh','exp'}, dimensions={0} | all-to-all | bytes 393216 | tf_op jit(solution)/shard_map/down/all_to_all | solution.py:25
  217.0 0.1 reshape.34
  217.1 0.8 fusion
  (4 shorter events, 0.1 us)
Async XLA Ops:
  6.5 4.1 %copy-start.4 = (bf16[128,128]{1,0:T(8,128)(2,1)S(1)}, bf16[128,128]{1,0:T(8,128)(2,1)}, u32[]{:S(2)}) copy-start(bf16[128,128]{1,0:T(8,128)(2,1)} %param.13) | copy-start | bytes 98308
  6.5 4.1 %copy-start.5 = (bf16[128,128]{1,0:T(8,128)(2,1)S(1)}, bf16[128,128]{1,0:T(8,128)(2,1)}, u32[]{:S(2)}) copy-start(bf16[128,128]{1,0:T(8,128)(2,1)} %param.12) | copy-start | bytes 98308
  6.5 100.3 %all-gather.6.cloned.1.call-start = ((), (), s32[]{:S(2)}) async-start(), calls=%async_computation.5 | async-start | bytes 18874368 | tf_op jit(solution)/shard_map/weight_gather/all_gather | solution.py:243
  6.5 34.2 %copy-start.6 = (s32[16,2]{0,1:T(2,128)S(1)}, s32[16,2]{0,1:T(2,128)}, u32[]{:S(2)}) copy-start(s32[16,2]{0,1:T(2,128)} %param.20) | copy-start | bytes 388
  6.5 34.3 %copy-start.7 = (f32[16,2]{0,1:T(2,128)S(1)}, f32[16,2]{0,1:T(2,128)}, u32[]{:S(2)}) copy-start(f32[16,2]{0,1:T(2,128)} %param.21) | copy-start | bytes 388
  6.5 36.1 %copy-start = (bf16[128,4096]{1,0:T(8,128)(2,1)S(1)}, bf16[128,4096]{1,0:T(8,128)(2,1)}, u32[]{:S(2)}) copy-start(bf16[128,4096]{1,0:T(8,128)(2,1)} %weight.1) | copy-start | bytes 3145732
  6.6 36.1 %copy-start.1 = (bf16[128,128]{1,0:T(8,128)(2,1)S(1)}, bf16[128,128]{1,0:T(8,128)(2,1)}, u32[]{:S(2)}) copy-start(bf16[128,128]{1,0:T(8,128)(2,1)} %query.1) | copy-start | bytes 98308
  9.9 74.0 %copy-start.3 = (bf16[16,1024]{1,0:T(8,128)(2,1)S(1)}, bf16[16,1024]{1,0:T(8,128)(2,1)}, u32[]{:S(2)}) copy-start(bf16[16,1024]{1,0:T(8,128)(2,1)} %param.14) | copy-start | bytes 98308
  9.9 160.4 %all-gather.4.cloned.1.call-start = ((), (), s32[]{:S(2)}) async-start(), calls=%async_computation.4 | async-start | bytes 9437184 | tf_op jit(solution)/shard_map/weight_gather/all_gather | solution.py:244
  10.7 96.1 %copy-start.2 = (f32[1024]{0:T(1024)S(1)}, f32[1024]{0:T(1024)}, u32[]{:S(2)}) copy-start(f32[1024]{0:T(1024)} %param.16) | copy-start | bytes 12292
  38.8 3.8 %collective-permute-start = (bf16[1024,256]{1,0:T(8,128)(2,1)S(1)}, bf16[1024,256]{1,0:T(8,128)(2,1)S(1)}, u32[]{:S(2)}, u32[]{:S(2)}) collective-permute-start(bf16[1024,256]{1,0:T(8,128)(2,1)S(1)} %bitcast.13), channel_id=1, source_target_pairs={{0,32},{32,0},{1,33},{33,1},{2,34},{34,2},{3,35},{35,3},{4,36},{36... | collective-permute-start | bytes 1572872 | tf_op jit(solution)/shard_map/kv_gather/ppermute | solution.py:33
  84.9 19.5 %all-to-all-start.2 = ((bf16[16,6,1024]{2,1,0:T(8,128)(2,1)}), bf16[16,6,1024]{2,1,0:T(8,128)(2,1)S(1)}, u32[]{:S(2)}, u32[]{:S(2)}) async-start(bf16[16,6,1024]{2,1,0:T(8,128)(2,1)} %bitcast.5), calls=%async_computation.2 | async-start | bytes 524288 | tf_op jit(solution)/shard_map/dispatch/all_to_all | solution.py:25
  117.5 34.0 %collective-permute-start.1 = (bf16[112,2048]{1,0:T(8,128)(2,1)}, bf16[112,2048]{1,0:T(8,128)(2,1)S(1)}, u32[]{:S(2)}, u32[]{:S(2)}) collective-permute-start(bf16[112,2048]{1,0:T(8,128)(2,1)} %get-tuple-element.16), channel_id=1, source_target_pairs={{0,3},{1,2},{2,1},{3,0},{4,7},{5,6},{6,5},{7,4},{8,11},{9,10},{10,... | collective-permute-start | bytes 1376264 | tf_op jit(solution)/shard_map/gate_up/ppermute | solution.py:37
  120.3 39.9 %collective-permute-start.2 = (bf16[112,2048]{1,0:T(8,128)(2,1)S(1)}, bf16[112,2048]{1,0:T(8,128)(2,1)S(1)}, u32[]{:S(2)}, u32[]{:S(2)}) collective-permute-start(bf16[112,2048]{1,0:T(8,128)(2,1)S(1)} %get-tuple-element.17), channel_id=1, source_target_pairs={{0,2},{1,3},{2,0},{3,1},{4,6},{5,7},{6,4},{7,5},{8,10},{9,11},{10,... | collective-permute-start | bytes 1376264 | tf_op jit(solution)/shard_map/gate_up/ppermute | solution.py:37
  122.8 37.3 %collective-permute-start.3 = (bf16[112,2048]{1,0:T(8,128)(2,1)S(1)}, bf16[112,2048]{1,0:T(8,128)(2,1)S(1)}, u32[]{:S(2)}, u32[]{:S(2)}) collective-permute-start(bf16[112,2048]{1,0:T(8,128)(2,1)S(1)} %get-tuple-element.18), channel_id=1, source_target_pairs={{0,1},{1,0},{2,3},{3,2},{4,5},{5,4},{6,7},{7,6},{8,9},{9,8},{10,11... | collective-permute-start | bytes 1376264 | tf_op jit(solution)/shard_map/gate_up/ppermute | solution.py:37
  160.5 10.5 %collective-permute-start.4 = (bf16[768,128]{1,0:T(8,128)(2,1)S(1)}, bf16[768,128]{1,0:T(8,128)(2,1)S(1)}, u32[]{:S(2)}, u32[]{:S(2)}) collective-permute-start(bf16[768,128]{1,0:T(8,128)(2,1)S(1)} %active.1.refs_0_), channel_id=1, source_target_pairs={{0,1},{1,0},{2,3},{3,2},{4,5},{5,4},{6,7},{7,6},{8,9},{9,8},{10,11... | collective-permute-start | bytes 589832 | tf_op jit(solution)/shard_map/active/ppermute | solution.py:37
  165.0 16.5 %collective-permute-start.5 = (bf16[768,128]{1,0:T(8,128)(2,1)S(1)}, bf16[768,128]{1,0:T(8,128)(2,1)S(1)}, u32[]{:S(2)}, u32[]{:S(2)}) collective-permute-start(bf16[768,128]{1,0:T(8,128)(2,1)S(1)} %active.1.refs_0_), channel_id=1, source_target_pairs={{0,2},{1,3},{2,0},{3,1},{4,6},{5,7},{6,4},{7,5},{8,10},{9,11},{10,... | collective-permute-start | bytes 589832 | tf_op jit(solution)/shard_map/active/ppermute | solution.py:37
  167.8 18.1 %collective-permute-start.6 = (bf16[768,128]{1,0:T(8,128)(2,1)S(1)}, bf16[768,128]{1,0:T(8,128)(2,1)S(1)}, u32[]{:S(2)}, u32[]{:S(2)}) collective-permute-start(bf16[768,128]{1,0:T(8,128)(2,1)S(1)} %active.1.refs_0_), channel_id=1, source_target_pairs={{0,3},{1,2},{2,1},{3,0},{4,7},{5,6},{6,5},{7,4},{8,11},{9,10},{10,... | collective-permute-start | bytes 589832 | tf_op jit(solution)/shard_map/active/ppermute | solution.py:37
Sparse Core Ops, SparseCore 0:
  10.0 96.7 all-gather.5
  109.0 53.7 all-gather.3

commit v5 on v3

--- a/solution.py
+++ b/solution.py
@@ -33,16 +33,18 @@
     return lax.ppermute(value, "core", [(0, 1), (1, 0)])
 
 
-def whole(kernel, out_shapes, flops, smem=0):
+def whole(kernel, out_shapes, flops, smem=0, held=(0, 0), scratch=()):
     def call(*operands):
-        spaces = [pltpu.SMEM] * smem + [pltpu.VMEM] * (len(operands) - smem)
+        spaces = [pltpu.SMEM] * smem + [pltpu.VMEM] * (len(operands) - smem - held[0]) + [pl.ANY] * held[0]
+        out_spaces = [pltpu.VMEM] * (len(out_shapes) - held[1]) + [pl.ANY] * held[1]
         moved = sum(math.prod(a.shape) * a.dtype.itemsize for a in operands)
         moved += sum(math.prod(a.shape) * a.dtype.itemsize for a in out_shapes)
         return pl.pallas_call(
             kernel,
             out_shape=out_shapes,
             in_specs=[pl.BlockSpec(memory_space=space) for space in spaces],
-            out_specs=[pl.BlockSpec(memory_space=pltpu.VMEM)] * len(out_shapes),
+            out_specs=[pl.BlockSpec(memory_space=space) for space in out_spaces],
+            scratch_shapes=scratch,
             compiler_params=pltpu.CompilerParams(vmem_limit_bytes=24 * 1024 * 1024),
             cost_estimate=pl.CostEstimate(flops=flops, bytes_accessed=moved, transcendentals=0),
         )(*operands)
@@ -54,7 +56,17 @@
     return lax.dot_general(left, right, (((1,), (1,)), ((), ())), preferred_element_type=F32)
 
 
-def attention_kernel(place, query, near, far, weight, ids, shares, out, selector, mixer):
+def attention_kernel(
+    place, query, near, far, weight, ids, shares, gate, up, down, out, selector, mixer, gate_up, down_out, sems
+):
+    columns = gate.shape[1]
+    copies = [
+        pltpu.make_async_copy(gate, gate_up.at[:, pl.ds(0, columns)], sems.at[0]),
+        pltpu.make_async_copy(up, gate_up.at[:, pl.ds(columns, columns)], sems.at[1]),
+        pltpu.make_async_copy(down, down_out, sems.at[2]),
+    ]
+    for copy in copies:
+        copy.start()
     ctx, core = place[0], place[1]
     rows, keys = query.shape[0], near.shape[0]
     spot = ctx * rows + lax.broadcasted_iota(jnp.int32, (rows, keys), 0)
@@ -94,65 +106,61 @@
         mixed = mixed + hit * shares[:, k : k + 1]
     selector[...] = picked.astype(BF16)
     mixer[...] = mixed
-
-
-def gate_up_kernel(place, near, far, gain, gate, up, *outs):
+    for copy in copies:
+        copy.wait()
+
+
+def gate_up_kernel(place, rows, gain, near, far, *outs):
     hid = place[0]
-    piece = gate.shape[1] // len(outs)
-    half = near.shape[0]
-    ones = jnp.ones((8, near.shape[1]), BF16)
-    sums = []
-    for index, source in enumerate((near, far)):
-        rows = source[...].astype(F32)
-        scaled = (rows * gain[...]).astype(BF16)
-        for k, out in enumerate(outs):
-            start = pl.multiple_of((hid ^ k) * piece, piece)
-            weight = jnp.concatenate([gate[:, pl.ds(start, piece)], up[:, pl.ds(start, piece)]], axis=1)
-            product = jnp.dot(scaled, weight, preferred_element_type=F32)
-            out[index * half : (index + 1) * half, :] = product.astype(BF16)
-        square = rows * rows
-        high = square.astype(BF16)
-        low = (square - high.astype(F32)).astype(BF16)
-        sums.append(dot_nt(ones, high) + dot_nt(ones, low))
-    norm = jnp.concatenate(sums, axis=1)
+    count, depth = rows.shape
+    piece = outs[0].shape[1] // 4
+    widened = rows[...].astype(F32)
+    scaled = (widened * gain[...]).astype(BF16)
+    for k, out in enumerate(outs):
+        start = pl.multiple_of((hid ^ k) * piece, piece)
+        other = pl.multiple_of((hid ^ k) * piece + len(outs) * piece, piece)
+        for index, weight in enumerate((near, far)):
+            columns = jnp.concatenate([weight[:, pl.ds(start, piece)], weight[:, pl.ds(other, piece)]], axis=1)
+            product = jnp.dot(scaled, columns, preferred_element_type=F32)
+            out[:count, 2 * index * piece : 2 * (index + 1) * piece] = product.astype(BF16)
+    square = widened * widened
+    high = square.astype(BF16)
+    low = (square - high.astype(F32)).astype(BF16)
+    ones = jnp.ones((TAIL, depth), BF16)
+    norm = dot_nt(ones, high) + dot_nt(ones, low)
     high = norm.astype(BF16).astype(F32)
-    low = norm - high
-    width = 2 * piece
-    groups = norm.shape[1] // width
-    line = lax.broadcasted_iota(jnp.int32, (8, width), 0)
-    tail = jnp.zeros((8, width), F32)
-    for group in range(groups):
-        lanes = slice(group * width, (group + 1) * width)
-        tail = jnp.where(line == group, high[:, lanes], tail)
-        tail = jnp.where(line == group + groups, low[:, lanes], tail)
-    tail = jnp.concatenate([tail, jnp.zeros((TAIL - 8, width), F32)], axis=0).astype(BF16)
+    line = lax.broadcasted_iota(jnp.int32, norm.shape, 0)
+    tail = jnp.where(line == 0, high, jnp.where(line == 1, norm - high, 0.0)).astype(BF16)
+    tail = jnp.concatenate([tail, jnp.zeros((TAIL, 4 * piece - count), BF16)], axis=1)
     for out in outs:
-        out[2 * half :, :] = tail
+        out[count:, :] = tail
 
 
 def active_kernel(*refs):
     parts, out = refs[:-1], refs[-1]
-    total, piece = out.shape
-    width = 2 * piece
-    groups = total // width
-    tail = sum(part[total:, :].astype(F32) for part in parts)
-    for group in range(groups):
-        norm = tail[group : group + 1, :] + tail[group + groups : group + groups + 1, :]
-        inverse = lax.rsqrt(norm / D + 1e-05)
-        inverse = jnp.broadcast_to(inverse, (piece, width)).T
-        rows = slice(group * width, (group + 1) * width)
-        summed = sum(part[rows, :].astype(F32) for part in parts)
-        gate = summed[:, :piece] * inverse
-        up = summed[:, piece:] * inverse
-        out[rows, :] = (gate / (1.0 + jnp.exp(-gate)) * up).astype(BF16)
-
-
-def down_kernel(active, weight, near, far):
-    half = near.shape[0]
-    for index, out in enumerate((near, far)):
-        rows = slice(index * half, (index + 1) * half)
+    piece = out.shape[1]
+    count = parts[0].shape[0] - TAIL
+    tail = sum(part[count:, :].astype(F32) for part in parts)
+    inverse = lax.rsqrt((tail[0:1, :] + tail[1:2, :]) / D + 1e-05)
+    for group in range(count // piece):
+        first = group * piece
+        factor = jnp.broadcast_to(inverse[:, first : first + piece], (piece, piece)).T
+        summed = sum(part[first : first + piece, :].astype(F32) for part in parts)
+        for index in range(out.shape[0] // count):
+            gate = summed[:, 2 * index * piece : (2 * index + 1) * piece] * factor
+            up = summed[:, (2 * index + 1) * piece : 2 * (index + 1) * piece] * factor
+            active = (gate / (1.0 + jnp.exp(-gate)) * up).astype(BF16)
+            out[index * count + first : index * count + first + piece, :] = active
+
+
+def down_kernel(active, near, far, out):
+    count = out.shape[0]
+    total = 0.0
+    for index, weight in enumerate((near, far)):
+        rows = slice(index * count, (index + 1) * count)
         left = jnp.concatenate([active[h, rows, :] for h in range(active.shape[0])], axis=1)
-        out[...] = jnp.dot(left, weight[...], preferred_element_type=F32).astype(BF16)
+        total = total + jnp.dot(left, weight[...], preferred_element_type=F32)
+    out[...] = total.astype(BF16)
 
 
 def shards(
@@ -175,6 +183,8 @@
     tok_rows = queries.shape[0]
     row_count = tok_rows // exp_count
     width_part = D // hid_count
+    ff_part = gate_weight.shape[2]
+    piece = ff_part // hid_count
     shape = jax.ShapeDtypeStruct
 
     with jax.named_scope("kv_gather"):
@@ -183,16 +193,32 @@
         far = other_core(near)
     with jax.named_scope("attention"):
         place = jnp.stack([lax.axis_index(CTX), lax.axis_index("core")]).astype(jnp.int32)
-        partials, selector, mixer = whole(
+        partials, selector, mixer, gate_up_near, down_near = whole(
             attention_kernel,
             [
                 shape((hid_count, tok_rows, width_part), BF16),
                 shape((row_count, EXPERTS * CAP), BF16),
                 shape((row_count, EXPERTS * CAP), F32),
+                shape((width_part, 2 * ff_part), BF16),
+                shape((ff_part, width_part), BF16),
             ],
             flops=2 * tok_rows * HEAD * (4 * plane * tok_rows + D),
             smem=1,
-        )(place, queries, near, far, out_weight, expert_ids, expert_weights)
+            held=(3, 2),
+            scratch=[pltpu.SemaphoreType.DMA((3,))],
+        )(
+            place,
+            queries,
+            near,
+            far,
+            out_weight,
+            expert_ids,
+            expert_weights,
+            gate_weight[0],
+            up_weight[0],
+            down_weight[0],
+        )
+        gate_up_far, down_far = other_core(gate_up_near), other_core(down_near)
     with jax.named_scope("projection"):
         partials = partials.reshape(hid_count * exp_count, row_count, width_part)
         mixed = jnp.sum(swap(partials, ("hid", "exp")).astype(F32), axis=0)
@@ -207,40 +233,33 @@
         outgoing = jnp.broadcast_to(outgoing, (halves, exp_count, CAP, width_part))
         arrived = swap(outgoing.reshape(halves * exp_count, CAP, width_part), ("yh", "exp"))
         arrived = spread(arrived.reshape(halves * exp_count * CAP, width_part), "x")
-        half = plane * exp_count * CAP
-        total = 2 * half
-        near = arrived.reshape(half, width_part)
-        far = other_core(near)
+        count = lines * halves * exp_count * CAP
+        rows = arrived.reshape(count, width_part)
 
     with jax.named_scope("gate_up"):
-        ff_part = gate_weight.shape[2]
-        piece = ff_part // hid_count
         parts = whole(
             gate_up_kernel,
-            [shape((total + TAIL, 2 * piece), BF16)] * hid_count,
-            flops=4 * total * width_part * ff_part,
+            [shape((count + TAIL, 4 * piece), BF16)] * hid_count,
+            flops=8 * count * width_part * ff_part,
             smem=1,
         )(
             lax.axis_index("hid").astype(jnp.int32).reshape(1),
-            near,
-            far,
+            rows,
             norm_gain.reshape(1, width_part),
-            gate_weight[0],
-            up_weight[0],
+            gate_up_near,
+            gate_up_far,
         )
         arrivals = [parts[0]]
         for k in reversed(range(1, hid_count)):
             arrivals.append(lax.ppermute(parts[k], "hid", [(h, h ^ k) for h in range(hid_count)]))
     with jax.named_scope("active"):
-        (active,) = whole(active_kernel, [shape((total, piece), BF16)], flops=total * piece * 20)(*arrivals)
+        (active,) = whole(active_kernel, [shape((2 * count, piece), BF16)], flops=count * piece * 40)(*arrivals)
         active = lax.all_gather(active, "hid", axis=0, tiled=False)
     with jax.named_scope("down"):
-        near, far = whole(
-            down_kernel, [shape((half, width_part), BF16)] * 2, flops=2 * total * ff_part * width_part
-        )(active, down_weight[0])
-        far = other_core(far)
-        back = (near.astype(F32) + far.astype(F32)).astype(BF16)
-        back = swap(back.reshape(lines, half // lines, width_part), "x")
+        (back,) = whole(
+            down_kernel, [shape((count, width_part), BF16)], flops=4 * count * ff_part * width_part
+        )(active, down_near, down_far)
+        back = swap(back.reshape(lines, count // lines, width_part), "x")
         back = jnp.sum(back.astype(F32), axis=0).astype(BF16)
         back = swap(back.reshape(halves * exp_count, CAP, width_part), ("yh", "exp"))
         back = back.reshape(halves, EXPERTS * CAP, width_part).astype(F32)

time: 213 us -> 206 us (0.967)
  the two profiles are of different devices: /device:TPU:16 before, /device:TPU:2 now
where the time goes in v5:
time: 206 us; the launch traced here: 205 us
  blocking collectives  93.7 us (45%)
  waiting for transfers between devices  58.6 us (28%)
  starting transfers between devices  34.3 us (17%)
  Pallas kernels  8.97 us (4%)
  local copies, waits for them, and re-layouts  7.22 us (4%)
    all_to_all x4, blocking collectives, swap(): return lax.all_to_all(value, axes, split_axis=0, concat_axis=0, tiled=True)  76 us
    all_to_all x2, waiting for transfers between devices, swap(): return lax.all_to_all(value, axes, split_axis=0, concat_axis=0, tiled=True)  32.9 us
    ppermute x3, waiting for transfers between devices, shards(): lax.ppermute(parts[k], 'hid', [(h, h ^ k) for h in range(hid_count)])  25.4 us
    all_to_all x2, starting transfers between devices, swap(): return lax.all_to_all(value, axes, split_axis=0, concat_axis=0, tiled=True)  18.4 us
    all_gather x1, blocking collectives, shards(): active = lax.all_gather(active, 'hid', axis=0, tiled=False)  17.7 us
    ppermute x3, starting transfers between devices, shards(): lax.ppermute(parts[k], 'hid', [(h, h ^ k) for h in range(hid_count)])  10.1 us
    pallas_call x4, Pallas kernels, call(): pl.pallas_call(kernel, out_shape=out_shapes, in_specs=[pl.BlockSpec(memor...  8.97 us
    unnamed x16, local copies, waits for them, and re-layouts  5.96 us
  transfers between devices with their start and end apart: 8, of which 5 were waited for; matrix products, arithmetic and copies ran while one was open for 1% of the time, Pallas kernels for 2%

profile of v5, /device:TPU:2, one launch (start us, length us, event | category | flops | bytes accessed | tf_op | source)
XLA Modules:
  0.0 205.3 jit_solution(4835740718779090496)
XLA Ops:
  0.0 0.0 copy-start
  0.0 0.9 pad_maximum_fusion
  0.9 25.2 %all_to_all.30 = bf16[8,128,256]{2,1,0:T(8,128)(2,1)S(1)} all-to-all(bf16[8,128,256]{2,1,0:T(8,128)(2,1)S(1)} %broadcast_in_dim.20), channel_id=1, replica_groups=mesh['x'=4,'yh'=2,'core'=2,'exp'=8,'hid'=4] {'x','yh'}, dimensions={0} | all-to-all | bytes 1048576 | tf_op jit(solution)/shard_map/kv_gather/all_to_all | solution.py:25
  26.1 1.9 collective-permute-start
  28.0 0.8 copy.14.ids
  28.8 0.8 copy.15.shares
  29.5 0.1 pad_add_fusion.place
  29.6 0.3 collective-permute-done.far
  29.9 0.0 copy-done
  29.9 0.0 copy-start.1
  29.9 1.2 copy-done.1
  31.1 0.0 copy-start.2
  31.1 1.2 copy-done.2
  32.3 0.0 copy-start.3
  32.3 1.2 copy-done.3
  33.6 0.0 copy-start.4
  33.6 0.8 copy-done.4
  34.3 2.9 %attention.1 = (bf16[4,128,1024]{2,1,0:T(8,128)(2,1)}, bf16[16,48]{1,0:T(8,128)(2,1)S(1)}, f32[16,48]{1,0:T(8,128)S(1)}, bf16[1024,1024]{1,0:T(8,128)(2,1)}, bf16[512,1024]{1,0:T(8,128)(2,1)S(1)}) custom-call(s32[2]{0:T(128)S(1)} %pad_add_fusion.place, bf16[128,128]{1,0:T(8,128)(2,1)S(1)} %copy-done.4, bf16[1024,256]{1,0:T(8,128)(2,1)S(1)} %bitcast.19, ...), custom_call_target="tpu_custom_call" | custom-call | flops 268435456 | bytes 9474824 | tf_op jit(solution)/shard_map/attention/pallas_call | solution.py:42
  37.2 0.0 copy-start.6
  37.2 13.5 %all-to-all-start.1 = ((bf16[32,16,1024]{2,1,0:T(8,128)(2,1)}), bf16[32,16,1024]{2,1,0:T(8,128)(2,1)S(1)}, u32[]{:S(2)}, u32[]{:S(2)}) async-start(bf16[32,16,1024]{2,1,0:T(8,128)(2,1)} %bitcast.6), calls=%async_computation.1 | async-start | bytes 2097152 | tf_op jit(solution)/shard_map/projection/all_to_all | solution.py:25
  50.8 1.9 collective-permute-start.1
  52.7 25.8 %all-to-all-done.1 = bf16[32,16,1024]{2,1,0:T(8,128)(2,1)S(1)} async-done(((bf16[32,16,1024]{2,1,0:T(8,128)(2,1)}), bf16[32,16,1024]{2,1,0:T(8,128)(2,1)S(1)}, u32[]{:S(2)}, u32[]{:S(2)}) %all-to-all-start.1) | async-done | bytes 1048608 | tf_op jit(solution)/shard_map/projection/all_to_all | solution.py:25
  78.5 0.2 convert_reduce_fusion
  78.7 0.0 copy-done.6
  78.7 0.2 convolution_convert_fusion
  78.9 0.0 copy-start.5
  79.0 17.7 %all_to_all.31 = bf16[16,6,1024]{2,1,0:T(8,128)(2,1)S(1)} all-to-all(bf16[16,6,1024]{2,1,0:T(8,128)(2,1)S(1)} %bitcast.25), channel_id=1, replica_groups=mesh['x'=4,'yh'=2,'core'=2,'exp'=8,'hid'=4] {'yh','exp'}, dimensions={0} | all-to-all | bytes 393216 | tf_op jit(solution)/shard_map/dispatch/all_to_all | solution.py:25
  96.7 0.1 broadcast_in_dim.23
  96.8 1.0 broadcast_in_dim.24
  97.7 4.9 %all-to-all-start.3 = ((bf16[4,96,1024]{2,1,0:T(8,128)(2,1)}), bf16[4,96,1024]{2,1,0:T(8,128)(2,1)S(1)}, u32[]{:S(2)}, u32[]{:S(2)}) async-start(bf16[4,96,1024]{2,1,0:T(8,128)(2,1)} %broadcast_in_dim.24), calls=%async_computation.3 | async-start | bytes 1572864 | tf_op jit(solution)/shard_map/dispatch/all_to_all | solution.py:25
  102.7 1.9 collective-permute-start.5
  104.6 0.0 collective-permute-done.1.far
  104.6 7.1 %all-to-all-done.3 = bf16[4,96,1024]{2,1,0:T(8,128)(2,1)S(1)} async-done(((bf16[4,96,1024]{2,1,0:T(8,128)(2,1)}), bf16[4,96,1024]{2,1,0:T(8,128)(2,1)S(1)}, u32[]{:S(2)}, u32[]{:S(2)}) %all-to-all-start.3) | async-done | bytes 786464 | tf_op jit(solution)/shard_map/dispatch/all_to_all | solution.py:25
  111.7 0.0 copy-done.5
  111.7 4.8 %gate_up.1 = (bf16[400,512]{1,0:T(8,128)(2,1)S(1)}, bf16[400,512]{1,0:T(8,128)(2,1)S(1)}, bf16[400,512]{1,0:T(8,128)(2,1)S(1)}, bf16[400,512]{1,0:T(8,128)(2,1)S(1)}) custom-call(s32[1]{0:T(128)} %bitcast.7.place, bf16[384,1024]{1,0:T(8,128)(2,1)S(1)} %bitcast.23, f32[1,1024]{1,0:T(1,128)S(1)} %bitcast.24, bf16[1024,1024]{1,0:T(8,128)(2,1)} %get-tuple-element.17.near, ...), custom_call_target="tpu_custom_call" | custom-call | flops 1610612736 | bytes 6623236 | tf_op jit(solution)/shard_map/gate_up/pallas_call | solution.py:42
  116.4 4.2 %collective-permute-start.2 = (bf16[400,512]{1,0:T(8,128)(2,1)S(1)}, bf16[400,512]{1,0:T(8,128)(2,1)S(1)}, u32[]{:S(2)}, u32[]{:S(2)}) collective-permute-start(bf16[400,512]{1,0:T(8,128)(2,1)S(1)} %get-tuple-element.19), channel_id=1, source_target_pairs={{0,3},{1,2},{2,1},{3,0},{4,7},{5,6},{6,5},{7,4},{8,11},{9,10},{10,... | collective-permute-start | bytes 1228808 | tf_op jit(solution)/shard_map/gate_up/ppermute | solution.py:254
  120.7 2.7 %collective-permute-start.3 = (bf16[400,512]{1,0:T(8,128)(2,1)S(1)}, bf16[400,512]{1,0:T(8,128)(2,1)S(1)}, u32[]{:S(2)}, u32[]{:S(2)}) collective-permute-start(bf16[400,512]{1,0:T(8,128)(2,1)S(1)} %get-tuple-element.20), channel_id=1, source_target_pairs={{0,2},{1,3},{2,0},{3,1},{4,6},{5,7},{6,4},{7,5},{8,10},{9,11},{10,... | collective-permute-start | bytes 1228808 | tf_op jit(solution)/shard_map/gate_up/ppermute | solution.py:254
  123.4 3.1 %collective-permute-start.4 = (bf16[400,512]{1,0:T(8,128)(2,1)S(1)}, bf16[400,512]{1,0:T(8,128)(2,1)S(1)}, u32[]{:S(2)}, u32[]{:S(2)}) collective-permute-start(bf16[400,512]{1,0:T(8,128)(2,1)S(1)} %get-tuple-element.21), channel_id=1, source_target_pairs={{0,1},{1,0},{2,3},{3,2},{4,5},{5,4},{6,7},{7,6},{8,9},{9,8},{10,11... | collective-permute-start | bytes 1228808 | tf_op jit(solution)/shard_map/gate_up/ppermute | solution.py:254
  126.6 6.1 %collective-permute-done.2.refs_1_ = bf16[400,512]{1,0:T(8,128)(2,1)S(1)} collective-permute-done((bf16[400,512]{1,0:T(8,128)(2,1)S(1)}, bf16[400,512]{1,0:T(8,128)(2,1)S(1)}, u32[]{:S(2)}, u32[]{:S(2)}) %collective-permute-start.2) | collective-permute-done | bytes 409632 | tf_op jit(solution)/shard_map/gate_up/ppermute | solution.py:254
  132.7 19.3 %collective-permute-done.3.refs_2_ = bf16[400,512]{1,0:T(8,128)(2,1)S(1)} collective-permute-done((bf16[400,512]{1,0:T(8,128)(2,1)S(1)}, bf16[400,512]{1,0:T(8,128)(2,1)S(1)}, u32[]{:S(2)}, u32[]{:S(2)}) %collective-permute-start.3) | collective-permute-done | bytes 409632 | tf_op jit(solution)/shard_map/gate_up/ppermute | solution.py:254
  152.0 0.0 collective-permute-done.4.refs_3_
  152.0 0.3 active.1
  152.3 17.7 %all-gather = bf16[3072,128]{1,0:T(8,128)(2,1)S(1)} all-gather(bf16[768,128]{1,0:T(8,128)(2,1)S(1)} %active.1), channel_id=2, replica_groups=mesh['x'=4,'yh'=2,'core'=2,'exp'=8,'hid'=4] {'hid'}, dimensions={0}, use_global_device_ids=true | all-gather | bytes 983040 | tf_op jit(solution)/shard_map/active/all_gather | solution.py:257
  170.0 0.0 collective-permute-done.5.far
  170.0 1.0 down.1
  171.0 12.6 %all_to_all.32 = bf16[4,96,1024]{2,1,0:T(8,128)(2,1)S(1)} all-to-all(bf16[4,96,1024]{2,1,0:T(8,128)(2,1)S(1)} %bitcast.16), channel_id=1, replica_groups=mesh['x'=4,'yh'=2,'core'=2,'exp'=8,'hid'=4] {'x'}, dimensions={0} | all-to-all | bytes 1572864 | tf_op jit(solution)/shard_map/down/all_to_all | solution.py:25
  183.5 0.1 reduce_sum.31
  183.7 0.1 reshape.39
  183.8 20.6 %all_to_all.33 = bf16[16,6,1024]{2,1,0:T(8,128)(2,1)S(1)} all-to-all(bf16[16,6,1024]{2,1,0:T(8,128)(2,1)S(1)} %reshape.39), channel_id=1, replica_groups=mesh['x'=4,'yh'=2,'core'=2,'exp'=8,'hid'=4] {'yh','exp'}, dimensions={0} | all-to-all | bytes 393216 | tf_op jit(solution)/shard_map/down/all_to_all | solution.py:25
  204.3 0.1 reshape.40
  204.4 0.8 fusion
  (4 shorter events, 0.1 us)
Async XLA Ops:
  0.0 29.9 %copy-start = (bf16[128,4096]{1,0:T(8,128)(2,1)S(1)}, bf16[128,4096]{1,0:T(8,128)(2,1)}, u32[]{:S(2)}) copy-start(bf16[128,4096]{1,0:T(8,128)(2,1)} %weight.1) | copy-start | bytes 3145732
  26.1 3.8 %collective-permute-start = (bf16[1024,256]{1,0:T(8,128)(2,1)S(1)}, bf16[1024,256]{1,0:T(8,128)(2,1)S(1)}, u32[]{:S(2)}, u32[]{:S(2)}) collective-permute-start(bf16[1024,256]{1,0:T(8,128)(2,1)S(1)} %bitcast.18), channel_id=1, source_target_pairs={{0,32},{32,0},{1,33},{33,1},{2,34},{34,2},{3,35},{35,3},{4,36},{36... | collective-permute-start | bytes 1572872 | tf_op jit(solution)/shard_map/kv_gather/ppermute | solution.py:33
  29.9 1.2 copy-start.1
  31.1 1.2 copy-start.2
  32.3 1.2 copy-start.3
  33.6 0.8 copy-start.4
  37.2 41.4 %copy-start.6 = (bf16[16,1024]{1,0:T(8,128)(2,1)S(1)}, bf16[16,1024]{1,0:T(8,128)(2,1)}, u32[]{:S(2)}) copy-start(bf16[16,1024]{1,0:T(8,128)(2,1)} %param.14) | copy-start | bytes 98308
  37.2 41.3 %all-to-all-start.1 = ((bf16[32,16,1024]{2,1,0:T(8,128)(2,1)}), bf16[32,16,1024]{2,1,0:T(8,128)(2,1)S(1)}, u32[]{:S(2)}, u32[]{:S(2)}) async-start(bf16[32,16,1024]{2,1,0:T(8,128)(2,1)} %bitcast.6), calls=%async_computation.1 | async-start | bytes 2097152 | tf_op jit(solution)/shard_map/projection/all_to_all | solution.py:25
  50.8 53.8 %collective-permute-start.1 = (bf16[1024,1024]{1,0:T(8,128)(2,1)}, bf16[1024,1024]{1,0:T(8,128)(2,1)}, u32[]{:S(2)}, u32[]{:S(2)}) collective-permute-start(bf16[1024,1024]{1,0:T(8,128)(2,1)} %get-tuple-element.17.near), channel_id=1, source_target_pairs={{0,32},{32,0},{1,33},{33,1},{2,34},{34,2},{3,35},{35,3},{4,36},{36... | collective-permute-start | bytes 6291464 | tf_op jit(solution)/shard_map/attention/ppermute | solution.py:33
  78.9 32.8 %copy-start.5 = (f32[1024]{0:T(1024)S(1)}, f32[1024]{0:T(1024)}, u32[]{:S(2)}) copy-start(f32[1024]{0:T(1024)} %param.16) | copy-start | bytes 12292
  97.7 13.9 %all-to-all-start.3 = ((bf16[4,96,1024]{2,1,0:T(8,128)(2,1)}), bf16[4,96,1024]{2,1,0:T(8,128)(2,1)S(1)}, u32[]{:S(2)}, u32[]{:S(2)}) async-start(bf16[4,96,1024]{2,1,0:T(8,128)(2,1)} %broadcast_in_dim.24), calls=%async_computation.3 | async-start | bytes 1572864 | tf_op jit(solution)/shard_map/dispatch/all_to_all | solution.py:25
  102.7 67.3 %collective-permute-start.5 = (bf16[512,1024]{1,0:T(8,128)(2,1)S(1)}, bf16[512,1024]{1,0:T(8,128)(2,1)S(1)}, u32[]{:S(2)}, u32[]{:S(2)}) collective-permute-start(bf16[512,1024]{1,0:T(8,128)(2,1)S(1)} %get-tuple-element.22.near), channel_id=1, source_target_pairs={{0,32},{32,0},{1,33},{33,1},{2,34},{34,2},{3,35},{35,3},{4,36},{36... | collective-permute-start | bytes 3145736 | tf_op jit(solution)/shard_map/attention/ppermute | solution.py:33
  116.4 16.2 %collective-permute-start.2 = (bf16[400,512]{1,0:T(8,128)(2,1)S(1)}, bf16[400,512]{1,0:T(8,128)(2,1)S(1)}, u32[]{:S(2)}, u32[]{:S(2)}) collective-permute-start(bf16[400,512]{1,0:T(8,128)(2,1)S(1)} %get-tuple-element.19), channel_id=1, source_target_pairs={{0,3},{1,2},{2,1},{3,0},{4,7},{5,6},{6,5},{7,4},{8,11},{9,10},{10,... | collective-permute-start | bytes 1228808 | tf_op jit(solution)/shard_map/gate_up/ppermute | solution.py:254
  120.7 31.3 %collective-permute-start.3 = (bf16[400,512]{1,0:T(8,128)(2,1)S(1)}, bf16[400,512]{1,0:T(8,128)(2,1)S(1)}, u32[]{:S(2)}, u32[]{:S(2)}) collective-permute-start(bf16[400,512]{1,0:T(8,128)(2,1)S(1)} %get-tuple-element.20), channel_id=1, source_target_pairs={{0,2},{1,3},{2,0},{3,1},{4,6},{5,7},{6,4},{7,5},{8,10},{9,11},{10,... | collective-permute-start | bytes 1228808 | tf_op jit(solution)/shard_map/gate_up/ppermute | solution.py:254
  123.4 28.5 %collective-permute-start.4 = (bf16[400,512]{1,0:T(8,128)(2,1)S(1)}, bf16[400,512]{1,0:T(8,128)(2,1)S(1)}, u32[]{:S(2)}, u32[]{:S(2)}) collective-permute-start(bf16[400,512]{1,0:T(8,128)(2,1)S(1)} %get-tuple-element.21), channel_id=1, source_target_pairs={{0,1},{1,0},{2,3},{3,2},{4,5},{5,4},{6,7},{7,6},{8,9},{9,8},{10,11... | collective-permute-start | bytes 1228808 | tf_op jit(solution)/shard_map/gate_up/ppermute | solution.py:254

commit v6 on v5

--- a/solution.py
+++ b/solution.py
@@ -33,19 +33,19 @@
     return lax.ppermute(value, "core", [(0, 1), (1, 0)])
 
 
-def whole(kernel, out_shapes, flops, smem=0, held=(0, 0), scratch=()):
+def whole(kernel, out_shapes, flops, smem=0, held=(0, 0), space=pl.ANY, scratch=(), vmem=24):
     def call(*operands):
-        spaces = [pltpu.SMEM] * smem + [pltpu.VMEM] * (len(operands) - smem - held[0]) + [pl.ANY] * held[0]
-        out_spaces = [pltpu.VMEM] * (len(out_shapes) - held[1]) + [pl.ANY] * held[1]
+        spaces = [pltpu.SMEM] * smem + [pltpu.VMEM] * (len(operands) - smem - held[0]) + [space] * held[0]
+        out_spaces = [pltpu.VMEM] * (len(out_shapes) - held[1]) + [space] * held[1]
         moved = sum(math.prod(a.shape) * a.dtype.itemsize for a in operands)
         moved += sum(math.prod(a.shape) * a.dtype.itemsize for a in out_shapes)
         return pl.pallas_call(
             kernel,
             out_shape=out_shapes,
-            in_specs=[pl.BlockSpec(memory_space=space) for space in spaces],
-            out_specs=[pl.BlockSpec(memory_space=space) for space in out_spaces],
+            in_specs=[pl.BlockSpec(memory_space=each) for each in spaces],
+            out_specs=[pl.BlockSpec(memory_space=each) for each in out_spaces],
             scratch_shapes=scratch,
-            compiler_params=pltpu.CompilerParams(vmem_limit_bytes=24 * 1024 * 1024),
+            compiler_params=pltpu.CompilerParams(vmem_limit_bytes=vmem * 1024 * 1024),
             cost_estimate=pl.CostEstimate(flops=flops, bytes_accessed=moved, transcendentals=0),
         )(*operands)
 
@@ -56,17 +56,7 @@
     return lax.dot_general(left, right, (((1,), (1,)), ((), ())), preferred_element_type=F32)
 
 
-def attention_kernel(
-    place, query, near, far, weight, ids, shares, gate, up, down, out, selector, mixer, gate_up, down_out, sems
-):
-    columns = gate.shape[1]
-    copies = [
-        pltpu.make_async_copy(gate, gate_up.at[:, pl.ds(0, columns)], sems.at[0]),
-        pltpu.make_async_copy(up, gate_up.at[:, pl.ds(columns, columns)], sems.at[1]),
-        pltpu.make_async_copy(down, down_out, sems.at[2]),
-    ]
-    for copy in copies:
-        copy.start()
+def attention_kernel(place, query, near, far, weight, ids, shares, out, selector, mixer):
     ctx, core = place[0], place[1]
     rows, keys = query.shape[0], near.shape[0]
     spot = ctx * rows + lax.broadcasted_iota(jnp.int32, (rows, keys), 0)
@@ -89,39 +79,62 @@
         columns = weight[:, part * width : (part + 1) * width]
         out[part] = jnp.dot(attended, columns, preferred_element_type=F32).astype(BF16)
 
-    tokens, slots = mixer.shape
-    lane = lax.broadcasted_iota(jnp.int32, (tokens, 128), 1)
-    chosen = [ids[:, k : k + 1] for k in range(TOP)]
-    named = [(lane == chosen[k]).astype(F32) for k in range(TOP)]
-    earlier = lax.broadcasted_iota(jnp.int32, (tokens, tokens), 0) > lax.broadcasted_iota(
+    slots, tokens = mixer.shape
+    expert = lax.broadcasted_iota(jnp.int32, (EXPERTS, tokens), 0)
+    named = [(expert == ids[k : k + 1, :]).astype(F32) for k in range(TOP)]
+    later = lax.broadcasted_iota(jnp.int32, (tokens, tokens), 0) < lax.broadcasted_iota(
         jnp.int32, (tokens, tokens), 1
     )
-    before = jnp.dot(earlier.astype(BF16), (named[0] + named[1]).astype(BF16), preferred_element_type=F32)
-    slot_lane = lax.broadcasted_iota(jnp.int32, (tokens, slots), 1)
+    before = jnp.dot((named[0] + named[1]).astype(BF16), later.astype(BF16), preferred_element_type=F32)
+    line = lax.broadcasted_iota(jnp.int32, (slots, tokens), 0)
     mixed, picked = 0.0, 0.0
     for k in range(TOP):
-        slot = jnp.sum(before * named[k], axis=1, keepdims=True).astype(jnp.int32)
-        hit = (slot_lane == chosen[k] * CAP + slot).astype(F32)
+        slot = jnp.sum(before * named[k], axis=0, keepdims=True).astype(jnp.int32)
+        hit = (line == ids[k : k + 1, :] * CAP + slot).astype(F32)
         picked = picked + hit
-        mixed = mixed + hit * shares[:, k : k + 1]
+        mixed = mixed + hit * shares[k : k + 1, :]
     selector[...] = picked.astype(BF16)
     mixer[...] = mixed
+
+
+def stack_kernel(gate, up, down, after, out, sems):
+    depth, columns = gate.shape
+    copies = [
+        pltpu.make_async_copy(gate, out.at[pl.ds(0, depth), pl.ds(0, columns)], sems.at[0]),
+        pltpu.make_async_copy(up, out.at[pl.ds(0, depth), pl.ds(columns, columns)], sems.at[1]),
+        pltpu.make_async_copy(down, out.at[pl.ds(depth, columns), :], sems.at[2]),
+    ]
+    for copy in copies:
+        copy.start()
     for copy in copies:
         copy.wait()
 
 
-def gate_up_kernel(place, rows, gain, near, far, *outs):
+def select_kernel(arrived, residual, selector, weights, stream, outgoing):
+    mixed = sum(arrived[index].astype(F32) for index in range(arrived.shape[0]))
+    total = residual[...].astype(F32) + mixed
+    stream[...] = total
+    rows = jnp.dot(selector[...], total.astype(BF16), preferred_element_type=F32)
+    halves, experts, slots, _ = outgoing.shape
+    for expert in range(experts):
+        part = rows[expert * slots : (expert + 1) * slots, :].astype(BF16)
+        for half in range(halves):
+            outgoing[half, expert] = part
+
+
+def gate_up_kernel(place, rows, gain, gate_near, up_near, weights, *outs):
     hid = place[0]
     count, depth = rows.shape
     piece = outs[0].shape[1] // 4
+    columns = gate_near.shape[1]
+    gate_far, up_far = weights.at[:depth, :columns], weights.at[:depth, columns:]
     widened = rows[...].astype(F32)
     scaled = (widened * gain[...]).astype(BF16)
     for k, out in enumerate(outs):
         start = pl.multiple_of((hid ^ k) * piece, piece)
-        other = pl.multiple_of((hid ^ k) * piece + len(outs) * piece, piece)
-        for index, weight in enumerate((near, far)):
-            columns = jnp.concatenate([weight[:, pl.ds(start, piece)], weight[:, pl.ds(other, piece)]], axis=1)
-            product = jnp.dot(scaled, columns, preferred_element_type=F32)
+        for index, (gate, up) in enumerate(((gate_near, up_near), (gate_far, up_far))):
+            weight = jnp.concatenate([gate[:, pl.ds(start, piece)], up[:, pl.ds(start, piece)]], axis=1)
+            product = jnp.dot(scaled, weight, preferred_element_type=F32)
             out[:count, 2 * index * piece : 2 * (index + 1) * piece] = product.astype(BF16)
     square = widened * widened
     high = square.astype(BF16)
@@ -153,8 +166,9 @@
             out[index * count + first : index * count + first + piece, :] = active
 
 
-def down_kernel(active, near, far, out):
+def down_kernel(active, near, weights, out):
     count = out.shape[0]
+    far = weights.at[weights.shape[0] - near.shape[0] :, :]
     total = 0.0
     for index, weight in enumerate((near, far)):
         rows = slice(index * count, (index + 1) * count)
@@ -193,44 +207,36 @@
         far = other_core(near)
     with jax.named_scope("attention"):
         place = jnp.stack([lax.axis_index(CTX), lax.axis_index("core")]).astype(jnp.int32)
-        partials, selector, mixer, gate_up_near, down_near = whole(
+        partials, selector, mixer = whole(
             attention_kernel,
             [
                 shape((hid_count, tok_rows, width_part), BF16),
-                shape((row_count, EXPERTS * CAP), BF16),
-                shape((row_count, EXPERTS * CAP), F32),
-                shape((width_part, 2 * ff_part), BF16),
-                shape((ff_part, width_part), BF16),
+                shape((EXPERTS * CAP, row_count), BF16),
+                shape((EXPERTS * CAP, row_count), F32),
             ],
             flops=2 * tok_rows * HEAD * (4 * plane * tok_rows + D),
             smem=1,
-            held=(3, 2),
+        )(place, queries, near, far, out_weight, expert_ids.T, expert_weights.T)
+    with jax.named_scope("weight_exchange"):
+        (weights,) = whole(
+            stack_kernel,
+            [shape((width_part + ff_part, width_part), BF16)],
+            flops=0,
+            held=(4, 1),
             scratch=[pltpu.SemaphoreType.DMA((3,))],
-        )(
-            place,
-            queries,
-            near,
-            far,
-            out_weight,
-            expert_ids,
-            expert_weights,
-            gate_weight[0],
-            up_weight[0],
-            down_weight[0],
-        )
-        gate_up_far, down_far = other_core(gate_up_near), other_core(down_near)
+            vmem=58,
+        )(gate_weight[0], up_weight[0], down_weight[0], selector)
+        weights = other_core(weights)
     with jax.named_scope("projection"):
-        partials = partials.reshape(hid_count * exp_count, row_count, width_part)
-        mixed = jnp.sum(swap(partials, ("hid", "exp")).astype(F32), axis=0)
-        stream = residual.astype(F32) + mixed
-        stream_bf = stream.astype(BF16)
+        arrived = swap(partials.reshape(hid_count * exp_count, row_count, width_part), ("hid", "exp"))
+        stream, outgoing = whole(
+            select_kernel,
+            [shape((row_count, width_part), F32), shape((halves, exp_count, CAP, width_part), BF16)],
+            flops=2 * arrived.size,
+            held=(1, 0),
+        )(arrived, residual, selector, weights)
 
     with jax.named_scope("dispatch"):
-        outgoing = lax.dot_general(
-            selector, stream_bf, (((0,), (0,)), ((), ())), preferred_element_type=F32
-        ).astype(BF16)
-        outgoing = outgoing.reshape(1, exp_count, CAP, width_part)
-        outgoing = jnp.broadcast_to(outgoing, (halves, exp_count, CAP, width_part))
         arrived = swap(outgoing.reshape(halves * exp_count, CAP, width_part), ("yh", "exp"))
         arrived = spread(arrived.reshape(halves * exp_count * CAP, width_part), "x")
         count = lines * halves * exp_count * CAP
@@ -246,8 +252,9 @@
             lax.axis_index("hid").astype(jnp.int32).reshape(1),
             rows,
             norm_gain.reshape(1, width_part),
-            gate_up_near,
-            gate_up_far,
+            gate_weight[0],
+            up_weight[0],
+            weights,
         )
         arrivals = [parts[0]]
         for k in reversed(range(1, hid_count)):
@@ -258,14 +265,14 @@
     with jax.named_scope("down"):
         (back,) = whole(
             down_kernel, [shape((count, width_part), BF16)], flops=4 * count * ff_part * width_part
-        )(active, down_near, down_far)
+        )(active, down_weight[0], weights)
         back = swap(back.reshape(lines, count // lines, width_part), "x")
         back = jnp.sum(back.astype(F32), axis=0).astype(BF16)
         back = swap(back.reshape(halves * exp_count, CAP, width_part), ("yh", "exp"))
         back = back.reshape(halves, EXPERTS * CAP, width_part).astype(F32)
         back = jnp.sum(back, axis=0)
     with jax.named_scope("combine"):
-        combined = jnp.dot(mixer, back, precision=lax.Precision.HIGHEST)
+        combined = lax.dot_general(mixer, back, (((0,), (0,)), ((), ())), precision=lax.Precision.HIGHEST)
         return (stream + combined).astype(BF16)
 
 

time: 206 us -> 304 us (1.48)
  Pallas kernels: 8.97 us -> 103 us
  blocking collectives: 93.7 us -> 133 us
  waiting for transfers between devices: 58.6 us -> 36.2 us
  starting transfers between devices: 34.3 us -> 19.7 us
    pallas_call x4 -> x6, Pallas kernels: 8.97 us -> 103 us  [call(): pl.pallas_call(kernel, out_shape=out_shapes, in_specs=[pl.BlockSpec(memor...]
    all_to_all x4 -> x5, blocking collectives: 76 us -> 116 us  [swap(): return lax.all_to_all(value, axes, split_axis=0, concat_axis=0, tiled=True)]
    all_to_all x2 -> x1, waiting for transfers between devices: 32.9 us -> 9.25 us  [swap(): return lax.all_to_all(value, axes, split_axis=0, concat_axis=0, tiled=True)]
    all_to_all x2 -> x1, starting transfers between devices: 18.4 us -> 5.64 us  [swap(): return lax.all_to_all(value, axes, split_axis=0, concat_axis=0, tiled=True)]
    unnamed x16 -> x22, local copies, waits for them, and re-layouts: 5.96 us -> 6.4 us
  transfers between devices with their start and end apart: 8 -> 6, of which waited for: 5 -> 4; matrix products, arithmetic and copies ran while one was open for 1% -> 0% of each run, Pallas kernels for 2% -> 0%
where the time goes in v6:
time: 304 us
  blocking collectives  133 us (44%)
  Pallas kernels  103 us (34%)
  waiting for transfers between devices  36.2 us (12%)
  starting transfers between devices  19.7 us (6%)
  local copies, waits for them, and re-layouts  9.24 us (3%)
    all_to_all x5, blocking collectives, swap(): return lax.all_to_all(value, axes, split_axis=0, concat_axis=0, tiled=True)  116 us
    pallas_call x6, Pallas kernels, call(): pl.pallas_call(kernel, out_shape=out_shapes, in_specs=[pl.BlockSpec(memor...  103 us
    ppermute x3, waiting for transfers between devices, shards(): lax.ppermute(parts[k], 'hid', [(h, h ^ k) for h in range(hid_count)])  25.2 us
    all_gather x1, blocking collectives, shards(): active = lax.all_gather(active, 'hid', axis=0, tiled=False)  17.5 us
    ppermute x3, starting transfers between devices, shards(): lax.ppermute(parts[k], 'hid', [(h, h ^ k) for h in range(hid_count)])  10.1 us
    all_to_all x1, waiting for transfers between devices, swap(): return lax.all_to_all(value, axes, split_axis=0, concat_axis=0, tiled=True)  9.25 us
    unnamed x22, local copies, waits for them, and re-layouts  6.4 us
  transfers between devices with their start and end apart: 6, of which 4 were waited for; matrix products, arithmetic and copies ran while one was open for 0% of the time, Pallas kernels for 0%

profile of v6, /device:TPU:2, one launch (start us, length us, event | category | flops | bytes accessed | tf_op | source)
XLA Modules:
  0.0 303.6 jit_solution(10243304957524863904)
XLA Ops:
  0.0 0.8 pad_maximum_fusion
  0.8 25.2 %all_to_all.30 = bf16[8,128,256]{2,1,0:T(8,128)(2,1)S(1)} all-to-all(bf16[8,128,256]{2,1,0:T(8,128)(2,1)S(1)} %broadcast_in_dim.6), channel_id=1, replica_groups=mesh['x'=4,'yh'=2,'core'=2,'exp'=8,'hid'=4] {'x','yh'}, dimensions={0} | all-to-all | bytes 1048576 | tf_op jit(solution)/shard_map/kv_gather/all_to_all | solution.py:25
  26.0 1.9 collective-permute-start
  27.9 0.1 pad_add_fusion.place
  28.0 1.8 collective-permute-done.far
  29.8 0.0 copy-start.3
  29.8 1.2 copy-done.3
  31.0 0.0 copy-start.6
  31.0 0.8 copy-done.6
  31.8 0.0 copy-start.9
  31.8 0.7 copy-done.9
  32.4 0.0 copy-start.10
  32.4 0.7 copy-done.10
  33.1 1.7 attention.1
  34.8 0.0 copy-start.4
  34.8 0.6 copy-done.4
  35.4 0.0 copy-start.5
  35.4 0.0 copy-start.7
  35.4 96.4 %weight_exchange.1 = bf16[1536,1024]{1,0:T(8,128)(2,1)} custom-call(bf16[1024,512]{1,0:T(8,128)(2,1)} %bitcast.17, bf16[1024,512]{1,0:T(8,128)(2,1)} %bitcast.19, bf16[512,1024]{1,0:T(8,128)(2,1)} %bitcast.21, bf16[48,16]{1,0:T(8,128)(2,1)} %copy-done.4), custom_call_target="tpu_custom_call" | custom-call | bytes 6292992 | tf_op jit(solution)/shard_map/weight_exchange/pallas_call | solution.py:42
  131.8 2.0 collective-permute-start.1
  133.9 41.7 %all_to_all.31.arrived = bf16[32,16,1024]{2,1,0:T(8,128)(2,1)S(1)} all-to-all(bf16[32,16,1024]{2,1,0:T(8,128)(2,1)S(1)} %bitcast.27), channel_id=1, replica_groups=mesh['x'=4,'yh'=2,'core'=2,'exp'=8,'hid'=4] {'hid','exp'}, dimensions={0} | all-to-all | bytes 2097152 | tf_op jit(solution)/shard_map/projection/all_to_all | solution.py:25
  175.6 0.0 copy-start.8
  175.6 0.0 collective-permute-done.1.weights
  175.6 0.0 copy-done.5
  175.6 0.0 copy-done.7
  175.7 0.3 projection.1
  176.0 17.2 %all_to_all.32 = bf16[16,6,1024]{2,1,0:T(8,128)(2,1)S(1)} all-to-all(bf16[16,6,1024]{2,1,0:T(8,128)(2,1)S(1)} %bitcast.28), channel_id=1, replica_groups=mesh['x'=4,'yh'=2,'core'=2,'exp'=8,'hid'=4] {'yh','exp'}, dimensions={0} | all-to-all | bytes 393216 | tf_op jit(solution)/shard_map/dispatch/all_to_all | solution.py:25
  193.1 0.8 broadcast_in_dim.14
  193.9 1.9 broadcast_in_dim.15
  195.8 5.6 %all-to-all-start.3 = ((bf16[4,96,1024]{2,1,0:T(8,128)(2,1)}), bf16[4,96,1024]{2,1,0:T(8,128)(2,1)}, u32[]{:S(2)}, u32[]{:S(2)}) async-start(bf16[4,96,1024]{2,1,0:T(8,128)(2,1)} %broadcast_in_dim.15), calls=%async_computation.3 | async-start | bytes 1572864 | tf_op jit(solution)/shard_map/dispatch/all_to_all | solution.py:25
  201.4 9.3 %all-to-all-done.3 = bf16[4,96,1024]{2,1,0:T(8,128)(2,1)} async-done(((bf16[4,96,1024]{2,1,0:T(8,128)(2,1)}), bf16[4,96,1024]{2,1,0:T(8,128)(2,1)}, u32[]{:S(2)}, u32[]{:S(2)}) %all-to-all-start.3) | async-done | bytes 786464 | tf_op jit(solution)/shard_map/dispatch/all_to_all | solution.py:25
  210.7 0.0 copy-done.8
  210.7 0.0 copy-start
  210.7 1.2 copy-done
  211.9 0.0 copy-start.1
  211.9 1.2 copy-done.1
  213.1 0.0 copy-start.2
  213.2 3.5 %gate_up.1 = (bf16[400,512]{1,0:T(8,128)(2,1)S(1)}, bf16[400,512]{1,0:T(8,128)(2,1)S(1)}, bf16[400,512]{1,0:T(8,128)(2,1)S(1)}, bf16[400,512]{1,0:T(8,128)(2,1)S(1)}) custom-call(s32[1]{0:T(128)} %bitcast.9.place, bf16[384,1024]{1,0:T(8,128)(2,1)} %bitcast.11.rows, f32[1,1024]{1,0:T(1,128)S(1)} %bitcast.29, bf16[1024,512]{1,0:T(8,128)(2,1)S(1)} %bitcast.18, ...), custom_call_target="tpu_custom_call" | custom-call | flops 1610612736 | bytes 7671812 | tf_op jit(solution)/shard_map/gate_up/pallas_call | solution.py:42
  216.6 4.2 %collective-permute-start.2 = (bf16[400,512]{1,0:T(8,128)(2,1)S(1)}, bf16[400,512]{1,0:T(8,128)(2,1)S(1)}, u32[]{:S(2)}, u32[]{:S(2)}) collective-permute-start(bf16[400,512]{1,0:T(8,128)(2,1)S(1)} %get-tuple-element.20), channel_id=1, source_target_pairs={{0,3},{1,2},{2,1},{3,0},{4,7},{5,6},{6,5},{7,4},{8,11},{9,10},{10,... | collective-permute-start | bytes 1228808 | tf_op jit(solution)/shard_map/gate_up/ppermute | solution.py:261
  220.8 2.7 collective-permute-start.3
  223.6 3.2 %collective-permute-start.4 = (bf16[400,512]{1,0:T(8,128)(2,1)S(1)}, bf16[400,512]{1,0:T(8,128)(2,1)S(1)}, u32[]{:S(2)}, u32[]{:S(2)}) collective-permute-start(bf16[400,512]{1,0:T(8,128)(2,1)S(1)} %get-tuple-element.22), channel_id=1, source_target_pairs={{0,1},{1,0},{2,3},{3,2},{4,5},{5,4},{6,7},{7,6},{8,9},{9,8},{10,11... | collective-permute-start | bytes 1228808 | tf_op jit(solution)/shard_map/gate_up/ppermute | solution.py:261
  226.8 6.0 %collective-permute-done.2.refs_1_ = bf16[400,512]{1,0:T(8,128)(2,1)S(1)} collective-permute-done((bf16[400,512]{1,0:T(8,128)(2,1)S(1)}, bf16[400,512]{1,0:T(8,128)(2,1)S(1)}, u32[]{:S(2)}, u32[]{:S(2)}) %collective-permute-start.2) | collective-permute-done | bytes 409632 | tf_op jit(solution)/shard_map/gate_up/ppermute | solution.py:261
  232.8 19.2 %collective-permute-done.3.refs_2_ = bf16[400,512]{1,0:T(8,128)(2,1)S(1)} collective-permute-done((bf16[400,512]{1,0:T(8,128)(2,1)S(1)}, bf16[400,512]{1,0:T(8,128)(2,1)S(1)}, u32[]{:S(2)}, u32[]{:S(2)}) %collective-permute-start.3) | collective-permute-done | bytes 409632 | tf_op jit(solution)/shard_map/gate_up/ppermute | solution.py:261
  252.0 0.0 collective-permute-done.4.refs_3_
  252.0 0.3 active.1
  252.3 17.5 %all-gather = bf16[3072,128]{1,0:T(8,128)(2,1)S(1)} all-gather(bf16[768,128]{1,0:T(8,128)(2,1)S(1)} %active.1), channel_id=2, replica_groups=mesh['x'=4,'yh'=2,'core'=2,'exp'=8,'hid'=4] {'hid'}, dimensions={0}, use_global_device_ids=true | all-gather | bytes 983040 | tf_op jit(solution)/shard_map/active/all_gather | solution.py:264
  269.8 0.0 copy-done.2
  269.8 1.0 down.1
  270.8 11.8 %all_to_all.33 = bf16[4,96,1024]{2,1,0:T(8,128)(2,1)S(1)} all-to-all(bf16[4,96,1024]{2,1,0:T(8,128)(2,1)S(1)} %bitcast.23), channel_id=1, replica_groups=mesh['x'=4,'yh'=2,'core'=2,'exp'=8,'hid'=4] {'x'}, dimensions={0} | all-to-all | bytes 1572864 | tf_op jit(solution)/shard_map/down/all_to_all | solution.py:25
  282.6 0.1 reduce_sum.21
  282.7 0.1 reshape.37
  282.8 19.8 %all_to_all.34 = bf16[16,6,1024]{2,1,0:T(8,128)(2,1)S(1)} all-to-all(bf16[16,6,1024]{2,1,0:T(8,128)(2,1)S(1)} %reshape.37), channel_id=1, replica_groups=mesh['x'=4,'yh'=2,'core'=2,'exp'=8,'hid'=4] {'yh','exp'}, dimensions={0} | all-to-all | bytes 393216 | tf_op jit(solution)/shard_map/down/all_to_all | solution.py:25
  302.6 0.1 reshape.38
  302.7 0.3 fusion
  303.0 0.6 add_convert_fusion
  (2 shorter events, 0.1 us)
Async XLA Ops:
  26.0 3.8 %collective-permute-start = (bf16[1024,256]{1,0:T(8,128)(2,1)S(1)}, bf16[1024,256]{1,0:T(8,128)(2,1)S(1)}, u32[]{:S(2)}, u32[]{:S(2)}) collective-permute-start(bf16[1024,256]{1,0:T(8,128)(2,1)S(1)} %bitcast.25), channel_id=1, source_target_pairs={{0,32},{32,0},{1,33},{33,1},{2,34},{34,2},{3,35},{35,3},{4,36},{36... | collective-permute-start | bytes 1572872 | tf_op jit(solution)/shard_map/kv_gather/ppermute | solution.py:33
  29.8 1.2 copy-start.3
  31.0 0.8 copy-start.6
  31.8 0.7 copy-start.9
  32.4 0.7 copy-start.10
  34.8 0.6 copy-start.4
  35.4 140.2 %copy-start.5 = (bf16[48,16]{1,0:T(8,128)(2,1)S(1)}, bf16[48,16]{1,0:T(8,128)(2,1)}, u32[]{:S(2)}) copy-start(bf16[48,16]{1,0:T(8,128)(2,1)} %copy-done.4) | copy-start | bytes 4612
  35.4 140.2 %copy-start.7 = (bf16[16,1024]{1,0:T(8,128)(2,1)S(1)}, bf16[16,1024]{1,0:T(8,128)(2,1)}, u32[]{:S(2)}) copy-start(bf16[16,1024]{1,0:T(8,128)(2,1)} %residual.1) | copy-start | bytes 98308
  131.8 43.8 %collective-permute-start.1 = (bf16[1536,1024]{1,0:T(8,128)(2,1)}, bf16[1536,1024]{1,0:T(8,128)(2,1)S(1)}, u32[]{:S(2)}, u32[]{:S(2)}) collective-permute-start(bf16[1536,1024]{1,0:T(8,128)(2,1)} %weight_exchange.1), channel_id=1, source_target_pairs={{0,32},{32,0},{1,33},{33,1},{2,34},{34,2},{3,35},{35,3},{4,36},{36... | collective-permute-start | bytes 9437192 | tf_op jit(solution)/shard_map/weight_exchange/ppermute | solution.py:33
  175.6 35.1 %copy-start.8 = (f32[1024]{0:T(1024)S(1)}, f32[1024]{0:T(1024)}, u32[]{:S(2)}) copy-start(f32[1024]{0:T(1024)} %param.16) | copy-start | bytes 12292
  195.8 14.9 %all-to-all-start.3 = ((bf16[4,96,1024]{2,1,0:T(8,128)(2,1)}), bf16[4,96,1024]{2,1,0:T(8,128)(2,1)}, u32[]{:S(2)}, u32[]{:S(2)}) async-start(bf16[4,96,1024]{2,1,0:T(8,128)(2,1)} %broadcast_in_dim.15), calls=%async_computation.3 | async-start | bytes 1572864 | tf_op jit(solution)/shard_map/dispatch/all_to_all | solution.py:25
  210.7 1.2 copy-start
  211.9 1.2 copy-start.1
  213.1 56.6 %copy-start.2 = (bf16[1,512,1024]{2,1,0:T(8,128)(2,1)S(1)}, bf16[1,512,1024]{2,1,0:T(8,128)(2,1)}, u32[]{:S(2)}) copy-start(bf16[1,512,1024]{2,1,0:T(8,128)(2,1)} %param.19) | copy-start | bytes 3145732
  216.6 16.2 %collective-permute-start.2 = (bf16[400,512]{1,0:T(8,128)(2,1)S(1)}, bf16[400,512]{1,0:T(8,128)(2,1)S(1)}, u32[]{:S(2)}, u32[]{:S(2)}) collective-permute-start(bf16[400,512]{1,0:T(8,128)(2,1)S(1)} %get-tuple-element.20), channel_id=1, source_target_pairs={{0,3},{1,2},{2,1},{3,0},{4,7},{5,6},{6,5},{7,4},{8,11},{9,10},{10,... | collective-permute-start | bytes 1228808 | tf_op jit(solution)/shard_map/gate_up/ppermute | solution.py:261
  220.8 31.1 %collective-permute-start.3 = (bf16[400,512]{1,0:T(8,128)(2,1)S(1)}, bf16[400,512]{1,0:T(8,128)(2,1)S(1)}, u32[]{:S(2)}, u32[]{:S(2)}) collective-permute-start(bf16[400,512]{1,0:T(8,128)(2,1)S(1)} %get-tuple-element.21), channel_id=1, source_target_pairs={{0,2},{1,3},{2,0},{3,1},{4,6},{5,7},{6,4},{7,5},{8,10},{9,11},{10,... | collective-permute-start | bytes 1228808 | tf_op jit(solution)/shard_map/gate_up/ppermute | solution.py:261
  223.6 28.4 %collective-permute-start.4 = (bf16[400,512]{1,0:T(8,128)(2,1)S(1)}, bf16[400,512]{1,0:T(8,128)(2,1)S(1)}, u32[]{:S(2)}, u32[]{:S(2)}) collective-permute-start(bf16[400,512]{1,0:T(8,128)(2,1)S(1)} %get-tuple-element.22), channel_id=1, source_target_pairs={{0,1},{1,0},{2,3},{3,2},{4,5},{5,4},{6,7},{7,6},{8,9},{9,8},{10,11... | collective-permute-start | bytes 1228808 | tf_op jit(solution)/shard_map/gate_up/ppermute | solution.py:261

commit v7 on v6

--- a/solution.py
+++ b/solution.py
@@ -33,19 +33,17 @@
     return lax.ppermute(value, "core", [(0, 1), (1, 0)])
 
 
-def whole(kernel, out_shapes, flops, smem=0, held=(0, 0), space=pl.ANY, scratch=(), vmem=24):
+def whole(kernel, out_shapes, flops, smem=0, held=0):
     def call(*operands):
-        spaces = [pltpu.SMEM] * smem + [pltpu.VMEM] * (len(operands) - smem - held[0]) + [space] * held[0]
-        out_spaces = [pltpu.VMEM] * (len(out_shapes) - held[1]) + [space] * held[1]
+        spaces = [pltpu.SMEM] * smem + [pltpu.VMEM] * (len(operands) - smem - held) + [pl.ANY] * held
         moved = sum(math.prod(a.shape) * a.dtype.itemsize for a in operands)
         moved += sum(math.prod(a.shape) * a.dtype.itemsize for a in out_shapes)
         return pl.pallas_call(
             kernel,
             out_shape=out_shapes,
-            in_specs=[pl.BlockSpec(memory_space=each) for each in spaces],
-            out_specs=[pl.BlockSpec(memory_space=each) for each in out_spaces],
-            scratch_shapes=scratch,
-            compiler_params=pltpu.CompilerParams(vmem_limit_bytes=vmem * 1024 * 1024),
+            in_specs=[pl.BlockSpec(memory_space=space) for space in spaces],
+            out_specs=[pl.BlockSpec(memory_space=pltpu.VMEM)] * len(out_shapes),
+            compiler_params=pltpu.CompilerParams(vmem_limit_bytes=24 * 1024 * 1024),
             cost_estimate=pl.CostEstimate(flops=flops, bytes_accessed=moved, transcendentals=0),
         )(*operands)
 
@@ -56,7 +54,7 @@
     return lax.dot_general(left, right, (((1,), (1,)), ((), ())), preferred_element_type=F32)
 
 
-def attention_kernel(place, query, near, far, weight, ids, shares, out, selector, mixer):
+def attention_kernel(place, query, near, far, weight, routes, out, selector, mixer, zero):
     ctx, core = place[0], place[1]
     rows, keys = query.shape[0], near.shape[0]
     spot = ctx * rows + lax.broadcasted_iota(jnp.int32, (rows, keys), 0)
@@ -79,6 +77,7 @@
         columns = weight[:, part * width : (part + 1) * width]
         out[part] = jnp.dot(attended, columns, preferred_element_type=F32).astype(BF16)
 
+    ids, shares = routes[:TOP, :].astype(jnp.int32), routes[TOP:, :]
     slots, tokens = mixer.shape
     expert = lax.broadcasted_iota(jnp.int32, (EXPERTS, tokens), 0)
     named = [(expert == ids[k : k + 1, :]).astype(F32) for k in range(TOP)]
@@ -95,19 +94,7 @@
         mixed = mixed + hit * shares[k : k + 1, :]
     selector[...] = picked.astype(BF16)
     mixer[...] = mixed
-
-
-def stack_kernel(gate, up, down, after, out, sems):
-    depth, columns = gate.shape
-    copies = [
-        pltpu.make_async_copy(gate, out.at[pl.ds(0, depth), pl.ds(0, columns)], sems.at[0]),
-        pltpu.make_async_copy(up, out.at[pl.ds(0, depth), pl.ds(columns, columns)], sems.at[1]),
-        pltpu.make_async_copy(down, out.at[pl.ds(depth, columns), :], sems.at[2]),
-    ]
-    for copy in copies:
-        copy.start()
-    for copy in copies:
-        copy.wait()
+    zero[...] = jnp.zeros_like(zero)
 
 
 def select_kernel(arrived, residual, selector, weights, stream, outgoing):
@@ -206,34 +193,31 @@
         near = near.reshape(plane * tok_rows, 2 * HEAD)
         far = other_core(near)
     with jax.named_scope("attention"):
+        routes = jnp.concatenate([expert_ids.T.astype(F32), expert_weights.T], axis=0)
         place = jnp.stack([lax.axis_index(CTX), lax.axis_index("core")]).astype(jnp.int32)
-        partials, selector, mixer = whole(
+        partials, selector, mixer, zero = whole(
             attention_kernel,
             [
                 shape((hid_count, tok_rows, width_part), BF16),
                 shape((EXPERTS * CAP, row_count), BF16),
                 shape((EXPERTS * CAP, row_count), F32),
+                shape((16, 128), BF16),
             ],
             flops=2 * tok_rows * HEAD * (4 * plane * tok_rows + D),
             smem=1,
-        )(place, queries, near, far, out_weight, expert_ids.T, expert_weights.T)
+        )(place, queries, near, far, out_weight, routes)
     with jax.named_scope("weight_exchange"):
-        (weights,) = whole(
-            stack_kernel,
-            [shape((width_part + ff_part, width_part), BF16)],
-            flops=0,
-            held=(4, 1),
-            scratch=[pltpu.SemaphoreType.DMA((3,))],
-            vmem=58,
-        )(gate_weight[0], up_weight[0], down_weight[0], selector)
-        weights = other_core(weights)
+        weights = jnp.concatenate(
+            [jnp.concatenate([gate_weight[0], up_weight[0]], axis=1), down_weight[0]], axis=0
+        )
+        weights = other_core(weights + zero[0, 0])
     with jax.named_scope("projection"):
         arrived = swap(partials.reshape(hid_count * exp_count, row_count, width_part), ("hid", "exp"))
         stream, outgoing = whole(
             select_kernel,
             [shape((row_count, width_part), F32), shape((halves, exp_count, CAP, width_part), BF16)],
             flops=2 * arrived.size,
-            held=(1, 0),
+            held=1,
         )(arrived, residual, selector, weights)
 
     with jax.named_scope("dispatch"):

time: 304 us -> 213 us (0.70)
  Pallas kernels: 103 us -> 7.41 us
  other arithmetic: 1.65 us -> 7.89 us
    pallas_call x6 -> x5, Pallas kernels: 103 us -> 7.41 us  [call(): pl.pallas_call(kernel, out_shape=out_shapes, in_specs=[pl.BlockSpec(memor...]
    add x0 -> x1, other arithmetic: none -> 4.73 us  [shards(): weights = other_core(weights + zero[0, 0])]
    unnamed x22 -> x20, local copies, waits for them, and re-layouts: 6.4 us -> 4.45 us
  transfers between devices with their start and end apart: 6 -> 6, of which waited for: 4 -> 4; matrix products, arithmetic and copies ran while one was open for 0% -> 1% of each run, Pallas kernels for 0% -> 0%
where the time goes in v7:
time: 213 us; the launch traced here: 212 us
  blocking collectives  134 us (63%)
  waiting for transfers between devices  35.2 us (17%)
  starting transfers between devices  19.7 us (9%)
  other arithmetic  7.89 us (4%)
  local copies, waits for them, and re-layouts  7.81 us (4%)
  Pallas kernels  7.41 us (3%)
    all_to_all x5, blocking collectives, swap(): return lax.all_to_all(value, axes, split_axis=0, concat_axis=0, tiled=True)  116 us
    ppermute x3, waiting for transfers between devices, shards(): lax.ppermute(parts[k], 'hid', [(h, h ^ k) for h in range(hid_count)])  25.2 us
    all_gather x1, blocking collectives, shards(): active = lax.all_gather(active, 'hid', axis=0, tiled=False)  17.5 us
    ppermute x3, starting transfers between devices, shards(): lax.ppermute(parts[k], 'hid', [(h, h ^ k) for h in range(hid_count)])  10.1 us
    all_to_all x1, waiting for transfers between devices, swap(): return lax.all_to_all(value, axes, split_axis=0, concat_axis=0, tiled=True)  9.26 us
    pallas_call x5, Pallas kernels, call(): pl.pallas_call(kernel, out_shape=out_shapes, in_specs=[pl.BlockSpec(memor...  7.41 us
    all_to_all x1, starting transfers between devices, swap(): return lax.all_to_all(value, axes, split_axis=0, concat_axis=0, tiled=True)  5.64 us
    add x1, other arithmetic, shards(): weights = other_core(weights + zero[0, 0])  4.73 us
  transfers between devices with their start and end apart: 6, of which 4 were waited for; matrix products, arithmetic and copies ran while one was open for 1% of the time, Pallas kernels for 0%

profile of v7, /device:TPU:2, one launch (start us, length us, event | category | flops | bytes accessed | tf_op | source)
XLA Modules:
  0.0 212.3 jit_solution(7885016126950339554)
XLA Ops:
  0.0 0.0 copy-start.4
  0.0 0.0 copy-start
  0.0 0.0 copy-start.2
  0.0 0.9 pad_maximum_fusion
  1.0 25.3 %all_to_all.30 = bf16[8,128,256]{2,1,0:T(8,128)(2,1)} all-to-all(bf16[8,128,256]{2,1,0:T(8,128)(2,1)S(1)} %broadcast_in_dim.6), channel_id=1, replica_groups=mesh['x'=4,'yh'=2,'core'=2,'exp'=8,'hid'=4] {'x','yh'}, dimensions={0} | all-to-all | bytes 1048576 | tf_op jit(solution)/shard_map/kv_gather/all_to_all | solution.py:25
  26.3 1.9 collective-permute-start
  28.2 0.1 pad_add_fusion.place
  28.3 0.7 convert_bitcast_fusion
  28.9 0.7 pad_maximum_fusion.1.routes
  29.6 0.8 collective-permute-done.far
  30.4 0.0 copy-start.6
  30.4 1.2 copy-done.6
  31.6 0.0 copy-start.7
  31.6 0.8 copy-done.7
  32.4 2.3 %attention.1 = (bf16[4,128,1024]{2,1,0:T(8,128)(2,1)S(1)}, bf16[48,16]{1,0:T(8,128)(2,1)S(1)}, f32[48,16]{1,0:T(8,128)S(1)}, bf16[16,128]{1,0:T(8,128)(2,1)S(1)}) custom-call(s32[2]{0:T(128)S(1)} %pad_add_fusion.place, bf16[128,128]{1,0:T(8,128)(2,1)S(1)} %copy-done.7, bf16[1024,256]{1,0:T(8,128)(2,1)} %bitcast.2.near, ...), custom_call_target="tpu_custom_call" | custom-call | flops 268435456 | bytes 3187464 | tf_op jit(solution)/shard_map/attention/pallas_call | solution.py:41
  34.7 0.5 slice.3
  35.2 0.0 copy-done.4
  35.2 0.0 copy-done
  35.2 0.0 copy-done.2
  35.2 0.0 copy-start.8
  35.2 4.7 %maximum_add_fusion = bf16[1536,1024]{1,0:T(8,128)(2,1)S(1)} fusion(bf16[512,1024]{1,0:T(8,128)(2,1)S(1)} %bitcast.23, bf16[1024,512]{1,0:T(8,128)(2,1)S(1)} %bitcast.19, bf16[1024,512]{1,0:T(8,128)(2,1)S(1)} %bitcast.21, bf16[]{:T(256)} %bitcast.9), kind=kLoop, calls=%fused_computation | loop fusion | flops 12582912 | bytes 6291458 | tf_op jit(solution)/shard_map/weight_exchange/add | solution.py:213
  40.0 2.0 collective-permute-start.1
  42.0 41.7 %all_to_all.31.arrived = bf16[32,16,1024]{2,1,0:T(8,128)(2,1)S(1)} all-to-all(bf16[32,16,1024]{2,1,0:T(8,128)(2,1)S(1)} %bitcast.27), channel_id=1, replica_groups=mesh['x'=4,'yh'=2,'core'=2,'exp'=8,'hid'=4] {'hid','exp'}, dimensions={0} | all-to-all | bytes 2097152 | tf_op jit(solution)/shard_map/projection/all_to_all | solution.py:25
  83.8 0.0 collective-permute-done.1.weights
  83.8 0.0 copy-done.8
  83.8 0.0 copy-start.9
  83.8 0.3 projection.1
  84.1 17.2 %all_to_all.32 = bf16[16,6,1024]{2,1,0:T(8,128)(2,1)S(1)} all-to-all(bf16[16,6,1024]{2,1,0:T(8,128)(2,1)S(1)} %bitcast.28), channel_id=1, replica_groups=mesh['x'=4,'yh'=2,'core'=2,'exp'=8,'hid'=4] {'yh','exp'}, dimensions={0} | all-to-all | bytes 393216 | tf_op jit(solution)/shard_map/dispatch/all_to_all | solution.py:25
  101.2 0.7 broadcast_in_dim.14
  102.0 1.9 broadcast_in_dim.15
  103.9 5.6 %all-to-all-start.3 = ((bf16[4,96,1024]{2,1,0:T(8,128)(2,1)}), bf16[4,96,1024]{2,1,0:T(8,128)(2,1)}, u32[]{:S(2)}, u32[]{:S(2)}) async-start(bf16[4,96,1024]{2,1,0:T(8,128)(2,1)} %broadcast_in_dim.15), calls=%async_computation.3 | async-start | bytes 1572864 | tf_op jit(solution)/shard_map/dispatch/all_to_all | solution.py:25
  109.6 9.3 %all-to-all-done.3 = bf16[4,96,1024]{2,1,0:T(8,128)(2,1)} async-done(((bf16[4,96,1024]{2,1,0:T(8,128)(2,1)}), bf16[4,96,1024]{2,1,0:T(8,128)(2,1)}, u32[]{:S(2)}, u32[]{:S(2)}) %all-to-all-start.3) | async-done | bytes 786464 | tf_op jit(solution)/shard_map/dispatch/all_to_all | solution.py:25
  118.8 0.0 copy-done.9
  118.8 0.0 copy-start.1
  118.8 1.2 copy-done.1
  120.1 0.0 copy-start.3
  120.1 1.2 copy-done.3
  121.3 0.0 copy-start.5
  121.3 3.5 %gate_up.1 = (bf16[400,512]{1,0:T(8,128)(2,1)S(1)}, bf16[400,512]{1,0:T(8,128)(2,1)S(1)}, bf16[400,512]{1,0:T(8,128)(2,1)S(1)}, bf16[400,512]{1,0:T(8,128)(2,1)S(1)}) custom-call(s32[1]{0:T(128)} %bitcast.10.place, bf16[384,1024]{1,0:T(8,128)(2,1)} %bitcast.12.rows, f32[1,1024]{1,0:T(1,128)S(1)} %bitcast.29, bf16[1024,512]{1,0:T(8,128)(2,1)S(1)} %bitcast.22, ...), custom_call_target="tpu_custom_call" | custom-call | flops 1610612736 | bytes 7671812 | tf_op jit(solution)/shard_map/gate_up/pallas_call | solution.py:41
  124.8 4.2 %collective-permute-start.2 = (bf16[400,512]{1,0:T(8,128)(2,1)S(1)}, bf16[400,512]{1,0:T(8,128)(2,1)S(1)}, u32[]{:S(2)}, u32[]{:S(2)}) collective-permute-start(bf16[400,512]{1,0:T(8,128)(2,1)S(1)} %get-tuple-element.22), channel_id=1, source_target_pairs={{0,3},{1,2},{2,1},{3,0},{4,7},{5,6},{6,5},{7,4},{8,11},{9,10},{10,... | collective-permute-start | bytes 1228808 | tf_op jit(solution)/shard_map/gate_up/ppermute | solution.py:245
  129.0 2.7 %collective-permute-start.3 = (bf16[400,512]{1,0:T(8,128)(2,1)S(1)}, bf16[400,512]{1,0:T(8,128)(2,1)S(1)}, u32[]{:S(2)}, u32[]{:S(2)}) collective-permute-start(bf16[400,512]{1,0:T(8,128)(2,1)S(1)} %get-tuple-element.23), channel_id=1, source_target_pairs={{0,2},{1,3},{2,0},{3,1},{4,6},{5,7},{6,4},{7,5},{8,10},{9,11},{10,... | collective-permute-start | bytes 1228808 | tf_op jit(solution)/shard_map/gate_up/ppermute | solution.py:245
  131.7 3.2 %collective-permute-start.4 = (bf16[400,512]{1,0:T(8,128)(2,1)S(1)}, bf16[400,512]{1,0:T(8,128)(2,1)S(1)}, u32[]{:S(2)}, u32[]{:S(2)}) collective-permute-start(bf16[400,512]{1,0:T(8,128)(2,1)S(1)} %get-tuple-element.24), channel_id=1, source_target_pairs={{0,1},{1,0},{2,3},{3,2},{4,5},{5,4},{6,7},{7,6},{8,9},{9,8},{10,11... | collective-permute-start | bytes 1228808 | tf_op jit(solution)/shard_map/gate_up/ppermute | solution.py:245
  134.9 6.0 %collective-permute-done.2.refs_1_ = bf16[400,512]{1,0:T(8,128)(2,1)S(1)} collective-permute-done((bf16[400,512]{1,0:T(8,128)(2,1)S(1)}, bf16[400,512]{1,0:T(8,128)(2,1)S(1)}, u32[]{:S(2)}, u32[]{:S(2)}) %collective-permute-start.2) | collective-permute-done | bytes 409632 | tf_op jit(solution)/shard_map/gate_up/ppermute | solution.py:245
  140.9 19.2 %collective-permute-done.3.refs_2_ = bf16[400,512]{1,0:T(8,128)(2,1)S(1)} collective-permute-done((bf16[400,512]{1,0:T(8,128)(2,1)S(1)}, bf16[400,512]{1,0:T(8,128)(2,1)S(1)}, u32[]{:S(2)}, u32[]{:S(2)}) %collective-permute-start.3) | collective-permute-done | bytes 409632 | tf_op jit(solution)/shard_map/gate_up/ppermute | solution.py:245
  160.1 0.0 collective-permute-done.4.refs_3_
  160.1 0.3 active.1
  160.4 17.5 %all-gather = bf16[3072,128]{1,0:T(8,128)(2,1)S(1)} all-gather(bf16[768,128]{1,0:T(8,128)(2,1)S(1)} %active.1), channel_id=2, replica_groups=mesh['x'=4,'yh'=2,'core'=2,'exp'=8,'hid'=4] {'hid'}, dimensions={0}, use_global_device_ids=true | all-gather | bytes 983040 | tf_op jit(solution)/shard_map/active/all_gather | solution.py:248
  177.9 0.0 copy-done.5
  177.9 1.0 down.1
  178.9 11.8 %all_to_all.33 = bf16[4,96,1024]{2,1,0:T(8,128)(2,1)S(1)} all-to-all(bf16[4,96,1024]{2,1,0:T(8,128)(2,1)S(1)} %bitcast.25), channel_id=1, replica_groups=mesh['x'=4,'yh'=2,'core'=2,'exp'=8,'hid'=4] {'x'}, dimensions={0} | all-to-all | bytes 1572864 | tf_op jit(solution)/shard_map/down/all_to_all | solution.py:25
  190.7 0.1 reduce_sum.21
  190.9 0.1 reshape.37
  190.9 20.4 %all_to_all.34 = bf16[16,6,1024]{2,1,0:T(8,128)(2,1)S(1)} all-to-all(bf16[16,6,1024]{2,1,0:T(8,128)(2,1)S(1)} %reshape.37), channel_id=1, replica_groups=mesh['x'=4,'yh'=2,'core'=2,'exp'=8,'hid'=4] {'yh','exp'}, dimensions={0} | all-to-all | bytes 393216 | tf_op jit(solution)/shard_map/down/all_to_all | solution.py:25
  211.3 0.1 reshape.38
  211.4 0.3 fusion
  211.7 0.6 add_convert_fusion
  (2 shorter events, 0.1 us)
Async XLA Ops:
  0.0 35.2 %copy-start.4 = (bf16[1,512,1024]{2,1,0:T(8,128)(2,1)S(1)}, bf16[1,512,1024]{2,1,0:T(8,128)(2,1)}, u32[]{:S(2)}) copy-start(bf16[1,512,1024]{2,1,0:T(8,128)(2,1)} %param.19) | copy-start | bytes 3145732
  0.0 35.2 %copy-start = (bf16[1,1024,512]{2,1,0:T(8,128)(2,1)S(1)}, bf16[1,1024,512]{2,1,0:T(8,128)(2,1)}, u32[]{:S(2)}) copy-start(bf16[1,1024,512]{2,1,0:T(8,128)(2,1)} %param.18) | copy-start | bytes 3145732
  0.0 35.2 %copy-start.2 = (bf16[1,1024,512]{2,1,0:T(8,128)(2,1)S(1)}, bf16[1,1024,512]{2,1,0:T(8,128)(2,1)}, u32[]{:S(2)}) copy-start(bf16[1,1024,512]{2,1,0:T(8,128)(2,1)} %param.17) | copy-start | bytes 3145732
  26.3 4.1 %collective-permute-start = (bf16[1024,256]{1,0:T(8,128)(2,1)}, bf16[1024,256]{1,0:T(8,128)(2,1)}, u32[]{:S(2)}, u32[]{:S(2)}) collective-permute-start(bf16[1024,256]{1,0:T(8,128)(2,1)} %bitcast.2.near), channel_id=1, source_target_pairs={{0,32},{32,0},{1,33},{33,1},{2,34},{34,2},{3,35},{35,3},{4,36},{36... | collective-permute-start | bytes 1572872 | tf_op jit(solution)/shard_map/kv_gather/ppermute | solution.py:33
  30.4 1.2 copy-start.6
  31.6 0.8 copy-start.7
  35.2 48.5 %copy-start.8 = (bf16[16,1024]{1,0:T(8,128)(2,1)S(1)}, bf16[16,1024]{1,0:T(8,128)(2,1)}, u32[]{:S(2)}) copy-start(bf16[16,1024]{1,0:T(8,128)(2,1)} %residual.1) | copy-start | bytes 98308
  40.0 43.8 %collective-permute-start.1 = (bf16[1536,1024]{1,0:T(8,128)(2,1)S(1)}, bf16[1536,1024]{1,0:T(8,128)(2,1)S(1)}, u32[]{:S(2)}, u32[]{:S(2)}) collective-permute-start(bf16[1536,1024]{1,0:T(8,128)(2,1)S(1)} %maximum_add_fusion), channel_id=1, source_target_pairs={{0,32},{32,0},{1,33},{33,1},{2,34},{34,2},{3,35},{35,3},{4,36},{36... | collective-permute-start | bytes 9437192 | tf_op jit(solution)/shard_map/weight_exchange/ppermute | solution.py:33
  83.8 35.0 %copy-start.9 = (f32[1024]{0:T(1024)S(1)}, f32[1024]{0:T(1024)}, u32[]{:S(2)}) copy-start(f32[1024]{0:T(1024)} %param.16) | copy-start | bytes 12292
  103.9 14.9 %all-to-all-start.3 = ((bf16[4,96,1024]{2,1,0:T(8,128)(2,1)}), bf16[4,96,1024]{2,1,0:T(8,128)(2,1)}, u32[]{:S(2)}, u32[]{:S(2)}) async-start(bf16[4,96,1024]{2,1,0:T(8,128)(2,1)} %broadcast_in_dim.15), calls=%async_computation.3 | async-start | bytes 1572864 | tf_op jit(solution)/shard_map/dispatch/all_to_all | solution.py:25
  118.8 1.2 copy-start.1
  120.1 1.2 copy-start.3
  121.3 56.6 %copy-start.5 = (bf16[1,512,1024]{2,1,0:T(8,128)(2,1)S(1)}, bf16[1,512,1024]{2,1,0:T(8,128)(2,1)}, u32[]{:S(2)}) copy-start(bf16[1,512,1024]{2,1,0:T(8,128)(2,1)} %param.19) | copy-start | bytes 3145732
  124.8 16.2 %collective-permute-start.2 = (bf16[400,512]{1,0:T(8,128)(2,1)S(1)}, bf16[400,512]{1,0:T(8,128)(2,1)S(1)}, u32[]{:S(2)}, u32[]{:S(2)}) collective-permute-start(bf16[400,512]{1,0:T(8,128)(2,1)S(1)} %get-tuple-element.22), channel_id=1, source_target_pairs={{0,3},{1,2},{2,1},{3,0},{4,7},{5,6},{6,5},{7,4},{8,11},{9,10},{10,... | collective-permute-start | bytes 1228808 | tf_op jit(solution)/shard_map/gate_up/ppermute | solution.py:245
  129.0 31.1 %collective-permute-start.3 = (bf16[400,512]{1,0:T(8,128)(2,1)S(1)}, bf16[400,512]{1,0:T(8,128)(2,1)S(1)}, u32[]{:S(2)}, u32[]{:S(2)}) collective-permute-start(bf16[400,512]{1,0:T(8,128)(2,1)S(1)} %get-tuple-element.23), channel_id=1, source_target_pairs={{0,2},{1,3},{2,0},{3,1},{4,6},{5,7},{6,4},{7,5},{8,10},{9,11},{10,... | collective-permute-start | bytes 1228808 | tf_op jit(solution)/shard_map/gate_up/ppermute | solution.py:245
  131.7 28.4 %collective-permute-start.4 = (bf16[400,512]{1,0:T(8,128)(2,1)S(1)}, bf16[400,512]{1,0:T(8,128)(2,1)S(1)}, u32[]{:S(2)}, u32[]{:S(2)}) collective-permute-start(bf16[400,512]{1,0:T(8,128)(2,1)S(1)} %get-tuple-element.24), channel_id=1, source_target_pairs={{0,1},{1,0},{2,3},{3,2},{4,5},{5,4},{6,7},{7,6},{8,9},{9,8},{10,11... | collective-permute-start | bytes 1228808 | tf_op jit(solution)/shard_map/gate_up/ppermute | solution.py:245

commit v8 on v7

--- a/solution.py
+++ b/solution.py
@@ -33,9 +33,9 @@
     return lax.ppermute(value, "core", [(0, 1), (1, 0)])
 
 
-def whole(kernel, out_shapes, flops, smem=0, held=0):
+def whole(kernel, out_shapes, flops, smem=0, scratch=()):
     def call(*operands):
-        spaces = [pltpu.SMEM] * smem + [pltpu.VMEM] * (len(operands) - smem - held) + [pl.ANY] * held
+        spaces = [pltpu.SMEM] * smem + [pltpu.VMEM] * (len(operands) - smem)
         moved = sum(math.prod(a.shape) * a.dtype.itemsize for a in operands)
         moved += sum(math.prod(a.shape) * a.dtype.itemsize for a in out_shapes)
         return pl.pallas_call(
@@ -43,6 +43,7 @@
             out_shape=out_shapes,
             in_specs=[pl.BlockSpec(memory_space=space) for space in spaces],
             out_specs=[pl.BlockSpec(memory_space=pltpu.VMEM)] * len(out_shapes),
+            scratch_shapes=scratch,
             compiler_params=pltpu.CompilerParams(vmem_limit_bytes=24 * 1024 * 1024),
             cost_estimate=pl.CostEstimate(flops=flops, bytes_accessed=moved, transcendentals=0),
         )(*operands)
@@ -54,7 +55,8 @@
     return lax.dot_general(left, right, (((1,), (1,)), ((), ())), preferred_element_type=F32)
 
 
-def attention_kernel(place, query, near, far, weight, routes, out, selector, mixer, zero):
+def attention_kernel(place, query, near, far, weight, out, done):
+    done[...] = jnp.zeros_like(done)
     ctx, core = place[0], place[1]
     rows, keys = query.shape[0], near.shape[0]
     spot = ctx * rows + lax.broadcasted_iota(jnp.int32, (rows, keys), 0)
@@ -77,7 +79,15 @@
         columns = weight[:, part * width : (part + 1) * width]
         out[part] = jnp.dot(attended, columns, preferred_element_type=F32).astype(BF16)
 
-    ids, shares = routes[:TOP, :].astype(jnp.int32), routes[TOP:, :]
+
+def prepare_kernel(after, ids, shares, gate, up, selector, mixer, weights, sems):
+    columns = gate.shape[1]
+    copies = [
+        pltpu.make_async_copy(gate, weights.at[:, pl.ds(0, columns)], sems.at[0]),
+        pltpu.make_async_copy(up, weights.at[:, pl.ds(columns, columns)], sems.at[1]),
+    ]
+    for copy in copies:
+        copy.start()
     slots, tokens = mixer.shape
     expert = lax.broadcasted_iota(jnp.int32, (EXPERTS, tokens), 0)
     named = [(expert == ids[k : k + 1, :]).astype(F32) for k in range(TOP)]
@@ -94,10 +104,11 @@
         mixed = mixed + hit * shares[k : k + 1, :]
     selector[...] = picked.astype(BF16)
     mixer[...] = mixed
-    zero[...] = jnp.zeros_like(zero)
-
-
-def select_kernel(arrived, residual, selector, weights, stream, outgoing):
+    for copy in copies:
+        copy.wait()
+
+
+def select_kernel(arrived, residual, selector, stream, outgoing):
     mixed = sum(arrived[index].astype(F32) for index in range(arrived.shape[0]))
     total = residual[...].astype(F32) + mixed
     stream[...] = total
@@ -109,18 +120,20 @@
             outgoing[half, expert] = part
 
 
-def gate_up_kernel(place, rows, gain, gate_near, up_near, weights, *outs):
-    hid = place[0]
+def gate_up_kernel(place, rows, gain, near, far, down, *refs):
+    outs, (down_out, sem) = refs[:-2], refs[-2:]
+    copy = pltpu.make_async_copy(down, down_out, sem)
+    copy.start()
+    hid = place[2]
     count, depth = rows.shape
     piece = outs[0].shape[1] // 4
-    columns = gate_near.shape[1]
-    gate_far, up_far = weights.at[:depth, :columns], weights.at[:depth, columns:]
     widened = rows[...].astype(F32)
     scaled = (widened * gain[...]).astype(BF16)
     for k, out in enumerate(outs):
         start = pl.multiple_of((hid ^ k) * piece, piece)
-        for index, (gate, up) in enumerate(((gate_near, up_near), (gate_far, up_far))):
-            weight = jnp.concatenate([gate[:, pl.ds(start, piece)], up[:, pl.ds(start, piece)]], axis=1)
+        other = pl.multiple_of((hid ^ k) * piece + len(outs) * piece, piece)
+        for index, source in enumerate((near, far)):
+            weight = jnp.concatenate([source[:depth, pl.ds(start, piece)], source[:depth, pl.ds(other, piece)]], axis=1)
             product = jnp.dot(scaled, weight, preferred_element_type=F32)
             out[:count, 2 * index * piece : 2 * (index + 1) * piece] = product.astype(BF16)
     square = widened * widened
@@ -134,6 +147,7 @@
     tail = jnp.concatenate([tail, jnp.zeros((TAIL, 4 * piece - count), BF16)], axis=1)
     for out in outs:
         out[count:, :] = tail
+    copy.wait()
 
 
 def active_kernel(*refs):
@@ -153,9 +167,8 @@
             out[index * count + first : index * count + first + piece, :] = active
 
 
-def down_kernel(active, near, weights, out):
+def down_kernel(active, near, far, out):
     count = out.shape[0]
-    far = weights.at[weights.shape[0] - near.shape[0] :, :]
     total = 0.0
     for index, weight in enumerate((near, far)):
         rows = slice(index * count, (index + 1) * count)
@@ -193,32 +206,33 @@
         near = near.reshape(plane * tok_rows, 2 * HEAD)
         far = other_core(near)
     with jax.named_scope("attention"):
-        routes = jnp.concatenate([expert_ids.T.astype(F32), expert_weights.T], axis=0)
-        place = jnp.stack([lax.axis_index(CTX), lax.axis_index("core")]).astype(jnp.int32)
-        partials, selector, mixer, zero = whole(
+        place = [lax.axis_index(CTX), lax.axis_index("core"), lax.axis_index("hid")]
+        place = jnp.stack(place).astype(jnp.int32)
+        partials, done = whole(
             attention_kernel,
+            [shape((hid_count, tok_rows, width_part), BF16), shape((8, 128), F32)],
+            flops=2 * tok_rows * HEAD * (4 * plane * tok_rows + D),
+            smem=1,
+        )(place, queries, near, far, out_weight)
+    with jax.named_scope("prepare"):
+        selector, mixer, near_weights = whole(
+            prepare_kernel,
             [
-                shape((hid_count, tok_rows, width_part), BF16),
                 shape((EXPERTS * CAP, row_count), BF16),
                 shape((EXPERTS * CAP, row_count), F32),
-                shape((16, 128), BF16),
+                shape((width_part, 2 * ff_part), BF16),
             ],
-            flops=2 * tok_rows * HEAD * (4 * plane * tok_rows + D),
-            smem=1,
-        )(place, queries, near, far, out_weight, routes)
-    with jax.named_scope("weight_exchange"):
-        weights = jnp.concatenate(
-            [jnp.concatenate([gate_weight[0], up_weight[0]], axis=1), down_weight[0]], axis=0
-        )
-        weights = other_core(weights + zero[0, 0])
+            flops=0,
+            scratch=[pltpu.SemaphoreType.DMA((2,))],
+        )(done, expert_ids.T, expert_weights.T, gate_weight[0], up_weight[0])
+        far_weights = other_core(near_weights)
     with jax.named_scope("projection"):
         arrived = swap(partials.reshape(hid_count * exp_count, row_count, width_part), ("hid", "exp"))
         stream, outgoing = whole(
             select_kernel,
             [shape((row_count, width_part), F32), shape((halves, exp_count, CAP, width_part), BF16)],
             flops=2 * arrived.size,
-            held=1,
-        )(arrived, residual, selector, weights)
+        )(arrived, residual, selector)
 
     with jax.named_scope("dispatch"):
         arrived = swap(outgoing.reshape(halves * exp_count, CAP, width_part), ("yh", "exp"))
@@ -227,29 +241,31 @@
         rows = arrived.reshape(count, width_part)
 
     with jax.named_scope("gate_up"):
-        parts = whole(
+        *parts, near_down = whole(
             gate_up_kernel,
-            [shape((count + TAIL, 4 * piece), BF16)] * hid_count,
+            [shape((count + TAIL, 4 * piece), BF16)] * hid_count + [shape((ff_part, width_part), BF16)],
             flops=8 * count * width_part * ff_part,
             smem=1,
+            scratch=[pltpu.SemaphoreType.DMA],
         )(
-            lax.axis_index("hid").astype(jnp.int32).reshape(1),
+            place,
             rows,
             norm_gain.reshape(1, width_part),
-            gate_weight[0],
-            up_weight[0],
-            weights,
+            near_weights,
+            far_weights,
+            down_weight[0],
         )
         arrivals = [parts[0]]
         for k in reversed(range(1, hid_count)):
             arrivals.append(lax.ppermute(parts[k], "hid", [(h, h ^ k) for h in range(hid_count)]))
+        far_down = other_core(near_down)
     with jax.named_scope("active"):
         (active,) = whole(active_kernel, [shape((2 * count, piece), BF16)], flops=count * piece * 40)(*arrivals)
         active = lax.all_gather(active, "hid", axis=0, tiled=False)
     with jax.named_scope("down"):
         (back,) = whole(
             down_kernel, [shape((count, width_part), BF16)], flops=4 * count * ff_part * width_part
-        )(active, down_weight[0], weights)
+        )(active, near_down, far_down)
         back = swap(back.reshape(lines, count // lines, width_part), "x")
         back = jnp.sum(back.astype(F32), axis=0).astype(BF16)
         back = swap(back.reshape(halves * exp_count, CAP, width_part), ("yh", "exp"))

time: 213 us -> 209 us (0.981)
  the two profiles are of different devices: /device:TPU:2 before, /device:TPU:16 now
where the time goes in v8:
time: 209 us; the launch traced here: 208 us
  blocking collectives  95.8 us (46%)
  waiting for transfers between devices  63.8 us (31%)
  starting transfers between devices  31.4 us (15%)
  Pallas kernels  8.91 us (4%)
  local copies, waits for them, and re-layouts  5.66 us (3%)
    all_to_all x4, blocking collectives, swap(): return lax.all_to_all(value, axes, split_axis=0, concat_axis=0, tiled=True)  76.5 us
    all_to_all x2, waiting for transfers between devices, swap(): return lax.all_to_all(value, axes, split_axis=0, concat_axis=0, tiled=True)  32.4 us
    ppermute x3, waiting for transfers between devices, shards(): lax.ppermute(parts[k], 'hid', [(h, h ^ k) for h in range(hid_count)])  29.6 us
    all_gather x1, blocking collectives, shards(): active = lax.all_gather(active, 'hid', axis=0, tiled=False)  19.3 us
    all_to_all x2, starting transfers between devices, swap(): return lax.all_to_all(value, axes, split_axis=0, concat_axis=0, tiled=True)  16.4 us
    ppermute x3, starting transfers between devices, shards(): lax.ppermute(parts[k], 'hid', [(h, h ^ k) for h in range(hid_count)])  9.21 us
    pallas_call x6, Pallas kernels, call(): pl.pallas_call(kernel, out_shape=out_shapes, in_specs=[pl.BlockSpec(memor...  8.91 us
    ppermute x3, starting transfers between devices, other_core(): return lax.ppermute(value, 'core', [(0, 1), (1, 0)])  5.75 us
  transfers between devices with their start and end apart: 8, of which 5 were waited for; matrix products, arithmetic and copies ran while one was open for 1% of the time, Pallas kernels for 1%

profile of v8, /device:TPU:16, one launch (start us, length us, event | category | flops | bytes accessed | tf_op | source)
XLA Modules:
  0.0 207.7 jit_solution(3807861638464379073)
XLA Ops:
  0.0 0.0 copy-start
  0.0 0.9 pad_maximum_fusion
  0.9 27.2 %all_to_all.30 = bf16[8,128,256]{2,1,0:T(8,128)(2,1)S(1)} all-to-all(bf16[8,128,256]{2,1,0:T(8,128)(2,1)S(1)} %broadcast_in_dim.6), channel_id=1, replica_groups=mesh['x'=4,'yh'=2,'core'=2,'exp'=8,'hid'=4] {'x','yh'}, dimensions={0} | all-to-all | bytes 1048576 | tf_op jit(solution)/shard_map/kv_gather/all_to_all | solution.py:25
  28.1 1.9 collective-permute-start
  30.0 0.1 pad_add_fusion.place
  30.1 1.8 collective-permute-done.far
  31.9 0.0 copy-done
  31.9 0.0 copy-start.4
  31.9 0.8 copy-done.4
  32.6 0.0 copy-start.7
  32.6 0.0 copy-start.8
  32.6 2.6 %attention.1 = (bf16[4,128,1024]{2,1,0:T(8,128)(2,1)}, f32[8,128]{1,0:T(8,128)S(1)}) custom-call(s32[3]{0:T(128)S(1)} %pad_add_fusion.place, bf16[128,128]{1,0:T(8,128)(2,1)S(1)} %copy-done.4, bf16[1024,256]{1,0:T(8,128)(2,1)S(1)} %bitcast.21, bf16[1024,256]{1,0:T(8,128)(2,1)S(1)} %collective-permute-done.far, bf16[128,4096]{1,0:T(8,128)(2,1)S(1)} %copy-done), custom_call_target="tpu_custom_call" | custom-call | flops 268435456 | bytes 3182604 | tf_op jit(solution)/shard_map/attention/pallas_call | solution.py:41
  35.3 0.0 copy-start.5
  35.3 13.0 %all-to-all-start.1 = ((bf16[32,16,1024]{2,1,0:T(8,128)(2,1)}), bf16[32,16,1024]{2,1,0:T(8,128)(2,1)S(1)}, u32[]{:S(2)}, u32[]{:S(2)}) async-start(bf16[32,16,1024]{2,1,0:T(8,128)(2,1)} %bitcast.4), calls=%async_computation.1 | async-start | bytes 2097152 | tf_op jit(solution)/shard_map/projection/all_to_all | solution.py:25
  48.2 0.0 copy-done.7
  48.2 0.0 copy-done.8
  48.2 0.0 copy-start.1
  48.2 1.2 copy-done.1
  49.5 0.0 copy-start.2
  49.5 1.2 copy-done.2
  50.7 0.4 prepare.1
  51.1 1.9 collective-permute-start.1
  53.1 22.9 %all-to-all-done.1.arrived = bf16[32,16,1024]{2,1,0:T(8,128)(2,1)S(1)} async-done(((bf16[32,16,1024]{2,1,0:T(8,128)(2,1)}), bf16[32,16,1024]{2,1,0:T(8,128)(2,1)S(1)}, u32[]{:S(2)}, u32[]{:S(2)}) %all-to-all-start.1) | async-done | bytes 1048608 | tf_op jit(solution)/shard_map/projection/all_to_all | solution.py:25
  76.0 0.0 copy-done.5
  76.0 0.0 copy-start.6
  76.0 0.3 projection.1
  76.3 17.6 %all_to_all.31 = bf16[16,6,1024]{2,1,0:T(8,128)(2,1)S(1)} all-to-all(bf16[16,6,1024]{2,1,0:T(8,128)(2,1)S(1)} %bitcast.25), channel_id=1, replica_groups=mesh['x'=4,'yh'=2,'core'=2,'exp'=8,'hid'=4] {'yh','exp'}, dimensions={0} | all-to-all | bytes 393216 | tf_op jit(solution)/shard_map/dispatch/all_to_all | solution.py:25
  93.9 0.1 broadcast_in_dim.14
  93.9 1.0 broadcast_in_dim.15
  94.9 3.5 %all-to-all-start.3 = ((bf16[4,96,1024]{2,1,0:T(8,128)(2,1)}), bf16[4,96,1024]{2,1,0:T(8,128)(2,1)S(1)}, u32[]{:S(2)}, u32[]{:S(2)}) async-start(bf16[4,96,1024]{2,1,0:T(8,128)(2,1)} %broadcast_in_dim.15), calls=%async_computation.3 | async-start | bytes 1572864 | tf_op jit(solution)/shard_map/dispatch/all_to_all | solution.py:25
  98.4 0.0 collective-permute-done.1.far
  98.4 9.4 %all-to-all-done.3 = bf16[4,96,1024]{2,1,0:T(8,128)(2,1)S(1)} async-done(((bf16[4,96,1024]{2,1,0:T(8,128)(2,1)}), bf16[4,96,1024]{2,1,0:T(8,128)(2,1)S(1)}, u32[]{:S(2)}, u32[]{:S(2)}) %all-to-all-start.3) | async-done | bytes 786464 | tf_op jit(solution)/shard_map/dispatch/all_to_all | solution.py:25
  107.9 0.0 copy-done.6
  107.9 0.0 copy-start.3
  107.9 1.2 copy-done.3
  109.1 4.3 %gate_up.1 = (bf16[400,512]{1,0:T(8,128)(2,1)S(1)}, bf16[400,512]{1,0:T(8,128)(2,1)S(1)}, bf16[400,512]{1,0:T(8,128)(2,1)S(1)}, bf16[400,512]{1,0:T(8,128)(2,1)S(1)}, bf16[512,1024]{1,0:T(8,128)(2,1)S(1)}) custom-call(s32[3]{0:T(128)S(1)} %pad_add_fusion.place, bf16[384,1024]{1,0:T(8,128)(2,1)S(1)} %bitcast.19, f32[1,1024]{1,0:T(1,128)S(1)} %bitcast.26, ...), custom_call_target="tpu_custom_call" | custom-call | flops 1610612736 | bytes 8720396 | tf_op jit(solution)/shard_map/gate_up/pallas_call | solution.py:41
  113.4 1.9 collective-permute-start.5
  115.3 3.1 %collective-permute-start.2 = (bf16[400,512]{1,0:T(8,128)(2,1)S(1)}, bf16[400,512]{1,0:T(8,128)(2,1)S(1)}, u32[]{:S(2)}, u32[]{:S(2)}) collective-permute-start(bf16[400,512]{1,0:T(8,128)(2,1)S(1)} %get-tuple-element.25), channel_id=1, source_target_pairs={{0,3},{1,2},{2,1},{3,0},{4,7},{5,6},{6,5},{7,4},{8,11},{9,10},{10,... | collective-permute-start | bytes 1228808 | tf_op jit(solution)/shard_map/gate_up/ppermute | solution.py:260
  118.4 4.0 %collective-permute-start.3 = (bf16[400,512]{1,0:T(8,128)(2,1)S(1)}, bf16[400,512]{1,0:T(8,128)(2,1)S(1)}, u32[]{:S(2)}, u32[]{:S(2)}) collective-permute-start(bf16[400,512]{1,0:T(8,128)(2,1)S(1)} %get-tuple-element.26), channel_id=1, source_target_pairs={{0,2},{1,3},{2,0},{3,1},{4,6},{5,7},{6,4},{7,5},{8,10},{9,11},{10,... | collective-permute-start | bytes 1228808 | tf_op jit(solution)/shard_map/gate_up/ppermute | solution.py:260
  122.5 2.1 %collective-permute-start.4 = (bf16[400,512]{1,0:T(8,128)(2,1)S(1)}, bf16[400,512]{1,0:T(8,128)(2,1)S(1)}, u32[]{:S(2)}, u32[]{:S(2)}) collective-permute-start(bf16[400,512]{1,0:T(8,128)(2,1)S(1)} %get-tuple-element.27), channel_id=1, source_target_pairs={{0,1},{1,0},{2,3},{3,2},{4,5},{5,4},{6,7},{7,6},{8,9},{9,8},{10,11... | collective-permute-start | bytes 1228808 | tf_op jit(solution)/shard_map/gate_up/ppermute | solution.py:260
  124.6 22.5 %collective-permute-done.2.refs_1_ = bf16[400,512]{1,0:T(8,128)(2,1)S(1)} collective-permute-done((bf16[400,512]{1,0:T(8,128)(2,1)S(1)}, bf16[400,512]{1,0:T(8,128)(2,1)S(1)}, u32[]{:S(2)}, u32[]{:S(2)}) %collective-permute-start.2) | collective-permute-done | bytes 409632 | tf_op jit(solution)/shard_map/gate_up/ppermute | solution.py:260
  147.0 7.1 %collective-permute-done.3.refs_2_ = bf16[400,512]{1,0:T(8,128)(2,1)S(1)} collective-permute-done((bf16[400,512]{1,0:T(8,128)(2,1)S(1)}, bf16[400,512]{1,0:T(8,128)(2,1)S(1)}, u32[]{:S(2)}, u32[]{:S(2)}) %collective-permute-start.3) | collective-permute-done | bytes 409632 | tf_op jit(solution)/shard_map/gate_up/ppermute | solution.py:260
  154.1 0.0 collective-permute-done.4.refs_3_
  154.1 0.3 active.1
  154.5 19.3 %all-gather = bf16[3072,128]{1,0:T(8,128)(2,1)S(1)} all-gather(bf16[768,128]{1,0:T(8,128)(2,1)S(1)} %active.1), channel_id=2, replica_groups=mesh['x'=4,'yh'=2,'core'=2,'exp'=8,'hid'=4] {'hid'}, dimensions={0}, use_global_device_ids=true | all-gather | bytes 983040 | tf_op jit(solution)/shard_map/active/all_gather | solution.py:264
  173.8 0.0 collective-permute-done.5.far
  173.8 1.0 down.1
  174.8 12.7 %all_to_all.32 = bf16[4,96,1024]{2,1,0:T(8,128)(2,1)S(1)} all-to-all(bf16[4,96,1024]{2,1,0:T(8,128)(2,1)S(1)} %bitcast.17), channel_id=1, replica_groups=mesh['x'=4,'yh'=2,'core'=2,'exp'=8,'hid'=4] {'x'}, dimensions={0} | all-to-all | bytes 1572864 | tf_op jit(solution)/shard_map/down/all_to_all | solution.py:25
  187.4 0.1 reduce_sum.21
  187.6 0.1 reshape.33
  187.6 19.1 %all_to_all.33 = bf16[16,6,1024]{2,1,0:T(8,128)(2,1)S(1)} all-to-all(bf16[16,6,1024]{2,1,0:T(8,128)(2,1)S(1)} %reshape.33), channel_id=1, replica_groups=mesh['x'=4,'yh'=2,'core'=2,'exp'=8,'hid'=4] {'yh','exp'}, dimensions={0} | all-to-all | bytes 393216 | tf_op jit(solution)/shard_map/down/all_to_all | solution.py:25
  206.7 0.1 reshape.34
  206.8 0.9 fusion
  (2 shorter events, 0.1 us)
Async XLA Ops:
  0.0 31.9 %copy-start = (bf16[128,4096]{1,0:T(8,128)(2,1)S(1)}, bf16[128,4096]{1,0:T(8,128)(2,1)}, u32[]{:S(2)}) copy-start(bf16[128,4096]{1,0:T(8,128)(2,1)} %weight.1) | copy-start | bytes 3145732
  28.1 3.8 %collective-permute-start = (bf16[1024,256]{1,0:T(8,128)(2,1)S(1)}, bf16[1024,256]{1,0:T(8,128)(2,1)S(1)}, u32[]{:S(2)}, u32[]{:S(2)}) collective-permute-start(bf16[1024,256]{1,0:T(8,128)(2,1)S(1)} %bitcast.20), channel_id=1, source_target_pairs={{0,32},{32,0},{1,33},{33,1},{2,34},{34,2},{3,35},{35,3},{4,36},{36... | collective-permute-start | bytes 1572872 | tf_op jit(solution)/shard_map/kv_gather/ppermute | solution.py:33
  31.9 0.8 copy-start.4
  32.6 15.6 %copy-start.7 = (s32[16,2]{0,1:T(2,128)S(1)}, s32[16,2]{0,1:T(2,128)}, u32[]{:S(2)}) copy-start(s32[16,2]{0,1:T(2,128)} %param.20) | copy-start | bytes 388
  32.6 15.6 %copy-start.8 = (f32[16,2]{0,1:T(2,128)S(1)}, f32[16,2]{0,1:T(2,128)}, u32[]{:S(2)}) copy-start(f32[16,2]{0,1:T(2,128)} %param.21) | copy-start | bytes 388
  35.3 40.7 %copy-start.5 = (bf16[16,1024]{1,0:T(8,128)(2,1)S(1)}, bf16[16,1024]{1,0:T(8,128)(2,1)}, u32[]{:S(2)}) copy-start(bf16[16,1024]{1,0:T(8,128)(2,1)} %residual.1) | copy-start | bytes 98308
  35.3 40.7 %all-to-all-start.1 = ((bf16[32,16,1024]{2,1,0:T(8,128)(2,1)}), bf16[32,16,1024]{2,1,0:T(8,128)(2,1)S(1)}, u32[]{:S(2)}, u32[]{:S(2)}) async-start(bf16[32,16,1024]{2,1,0:T(8,128)(2,1)} %bitcast.4), calls=%async_computation.1 | async-start | bytes 2097152 | tf_op jit(solution)/shard_map/projection/all_to_all | solution.py:25
  48.2 1.2 copy-start.1
  49.5 1.2 copy-start.2
  51.1 47.3 %collective-permute-start.1 = (bf16[1024,1024]{1,0:T(8,128)(2,1)S(1)}, bf16[1024,1024]{1,0:T(8,128)(2,1)}, u32[]{:S(2)}, u32[]{:S(2)}) collective-permute-start(bf16[1024,1024]{1,0:T(8,128)(2,1)S(1)} %get-tuple-element.23.near), channel_id=1, source_target_pairs={{0,32},{32,0},{1,33},{33,1},{2,34},{34,2},{3,35},{35,3},{4,36},{36... | collective-permute-start | bytes 6291464 | tf_op jit(solution)/shard_map/prepare/ppermute | solution.py:33
  76.0 31.9 %copy-start.6 = (f32[1024]{0:T(1024)S(1)}, f32[1024]{0:T(1024)}, u32[]{:S(2)}) copy-start(f32[1024]{0:T(1024)} %param.16) | copy-start | bytes 12292
  94.9 13.0 %all-to-all-start.3 = ((bf16[4,96,1024]{2,1,0:T(8,128)(2,1)}), bf16[4,96,1024]{2,1,0:T(8,128)(2,1)S(1)}, u32[]{:S(2)}, u32[]{:S(2)}) async-start(bf16[4,96,1024]{2,1,0:T(8,128)(2,1)} %broadcast_in_dim.15), calls=%async_computation.3 | async-start | bytes 1572864 | tf_op jit(solution)/shard_map/dispatch/all_to_all | solution.py:25
  107.9 1.2 copy-start.3
  113.4 60.4 %collective-permute-start.5 = (bf16[512,1024]{1,0:T(8,128)(2,1)S(1)}, bf16[512,1024]{1,0:T(8,128)(2,1)S(1)}, u32[]{:S(2)}, u32[]{:S(2)}) collective-permute-start(bf16[512,1024]{1,0:T(8,128)(2,1)S(1)} %get-tuple-element.28.near), channel_id=1, source_target_pairs={{0,32},{32,0},{1,33},{33,1},{2,34},{34,2},{3,35},{35,3},{4,36},{36... | collective-permute-start | bytes 3145736 | tf_op jit(solution)/shard_map/gate_up/ppermute | solution.py:33
  115.3 31.7 %collective-permute-start.2 = (bf16[400,512]{1,0:T(8,128)(2,1)S(1)}, bf16[400,512]{1,0:T(8,128)(2,1)S(1)}, u32[]{:S(2)}, u32[]{:S(2)}) collective-permute-start(bf16[400,512]{1,0:T(8,128)(2,1)S(1)} %get-tuple-element.25), channel_id=1, source_target_pairs={{0,3},{1,2},{2,1},{3,0},{4,7},{5,6},{6,5},{7,4},{8,11},{9,10},{10,... | collective-permute-start | bytes 1228808 | tf_op jit(solution)/shard_map/gate_up/ppermute | solution.py:260
  118.4 35.7 %collective-permute-start.3 = (bf16[400,512]{1,0:T(8,128)(2,1)S(1)}, bf16[400,512]{1,0:T(8,128)(2,1)S(1)}, u32[]{:S(2)}, u32[]{:S(2)}) collective-permute-start(bf16[400,512]{1,0:T(8,128)(2,1)S(1)} %get-tuple-element.26), channel_id=1, source_target_pairs={{0,2},{1,3},{2,0},{3,1},{4,6},{5,7},{6,4},{7,5},{8,10},{9,11},{10,... | collective-permute-start | bytes 1228808 | tf_op jit(solution)/shard_map/gate_up/ppermute | solution.py:260
  122.5 31.7 %collective-permute-start.4 = (bf16[400,512]{1,0:T(8,128)(2,1)S(1)}, bf16[400,512]{1,0:T(8,128)(2,1)S(1)}, u32[]{:S(2)}, u32[]{:S(2)}) collective-permute-start(bf16[400,512]{1,0:T(8,128)(2,1)S(1)} %get-tuple-element.27), channel_id=1, source_target_pairs={{0,1},{1,0},{2,3},{3,2},{4,5},{5,4},{6,7},{7,6},{8,9},{9,8},{10,11... | collective-permute-start | bytes 1228808 | tf_op jit(solution)/shard_map/gate_up/ppermute | solution.py:260

commit v9 on v8

--- a/solution.py
+++ b/solution.py
@@ -33,9 +33,9 @@
     return lax.ppermute(value, "core", [(0, 1), (1, 0)])
 
 
-def whole(kernel, out_shapes, flops, smem=0, scratch=()):
+def whole(kernel, out_shapes, flops, smem=0, held=0, scratch=()):
     def call(*operands):
-        spaces = [pltpu.SMEM] * smem + [pltpu.VMEM] * (len(operands) - smem)
+        spaces = [pltpu.SMEM] * smem + [pltpu.VMEM] * (len(operands) - smem - held) + [pl.ANY] * held
         moved = sum(math.prod(a.shape) * a.dtype.itemsize for a in operands)
         moved += sum(math.prod(a.shape) * a.dtype.itemsize for a in out_shapes)
         return pl.pallas_call(
@@ -80,11 +80,12 @@
         out[part] = jnp.dot(attended, columns, preferred_element_type=F32).astype(BF16)
 
 
-def prepare_kernel(after, ids, shares, gate, up, selector, mixer, weights, sems):
+def prepare_kernel(after, ids, shares, gate, up, down, selector, mixer, weights, down_out, sems):
     columns = gate.shape[1]
     copies = [
         pltpu.make_async_copy(gate, weights.at[:, pl.ds(0, columns)], sems.at[0]),
         pltpu.make_async_copy(up, weights.at[:, pl.ds(columns, columns)], sems.at[1]),
+        pltpu.make_async_copy(down, down_out, sems.at[2]),
     ]
     for copy in copies:
         copy.start()
@@ -120,10 +121,7 @@
             outgoing[half, expert] = part
 
 
-def gate_up_kernel(place, rows, gain, near, far, down, *refs):
-    outs, (down_out, sem) = refs[:-2], refs[-2:]
-    copy = pltpu.make_async_copy(down, down_out, sem)
-    copy.start()
+def gate_up_kernel(place, rows, gain, near, far, down, *outs):
     hid = place[2]
     count, depth = rows.shape
     piece = outs[0].shape[1] // 4
@@ -147,7 +145,6 @@
     tail = jnp.concatenate([tail, jnp.zeros((TAIL, 4 * piece - count), BF16)], axis=1)
     for out in outs:
         out[count:, :] = tail
-    copy.wait()
 
 
 def active_kernel(*refs):
@@ -215,17 +212,18 @@
             smem=1,
         )(place, queries, near, far, out_weight)
     with jax.named_scope("prepare"):
-        selector, mixer, near_weights = whole(
+        selector, mixer, near_weights, near_down = whole(
             prepare_kernel,
             [
                 shape((EXPERTS * CAP, row_count), BF16),
                 shape((EXPERTS * CAP, row_count), F32),
                 shape((width_part, 2 * ff_part), BF16),
+                shape((ff_part, width_part), BF16),
             ],
             flops=0,
-            scratch=[pltpu.SemaphoreType.DMA((2,))],
-        )(done, expert_ids.T, expert_weights.T, gate_weight[0], up_weight[0])
-        far_weights = other_core(near_weights)
+            scratch=[pltpu.SemaphoreType.DMA((3,))],
+        )(done, expert_ids.T, expert_weights.T, gate_weight[0], up_weight[0], down_weight[0])
+        far_weights, far_down = other_core(near_weights), other_core(near_down)
     with jax.named_scope("projection"):
         arrived = swap(partials.reshape(hid_count * exp_count, row_count, width_part), ("hid", "exp"))
         stream, outgoing = whole(
@@ -241,24 +239,23 @@
         rows = arrived.reshape(count, width_part)
 
     with jax.named_scope("gate_up"):
-        *parts, near_down = whole(
+        parts = whole(
             gate_up_kernel,
-            [shape((count + TAIL, 4 * piece), BF16)] * hid_count + [shape((ff_part, width_part), BF16)],
+            [shape((count + TAIL, 4 * piece), BF16)] * hid_count,
             flops=8 * count * width_part * ff_part,
             smem=1,
-            scratch=[pltpu.SemaphoreType.DMA],
+            held=1,
         )(
             place,
             rows,
             norm_gain.reshape(1, width_part),
             near_weights,
             far_weights,
-            down_weight[0],
+            far_down,
         )
         arrivals = [parts[0]]
         for k in reversed(range(1, hid_count)):
             arrivals.append(lax.ppermute(parts[k], "hid", [(h, h ^ k) for h in range(hid_count)]))
-        far_down = other_core(near_down)
     with jax.named_scope("active"):
         (active,) = whole(active_kernel, [shape((2 * count, piece), BF16)], flops=count * piece * 40)(*arrivals)
         active = lax.all_gather(active, "hid", axis=0, tiled=False)

time: 209 us -> 202 us (0.967)
  the two profiles are of different devices: /device:TPU:16 before, /device:TPU:2 now
where the time goes in v9:
time: 202 us; the launch traced here: 201 us
  blocking collectives  94.1 us (47%)
  waiting for transfers between devices  53.7 us (27%)
  starting transfers between devices  34.9 us (17%)
  Pallas kernels  10.8 us (5%)
  local copies, waits for them, and re-layouts  5.66 us (3%)
    all_to_all x4, blocking collectives, swap(): return lax.all_to_all(value, axes, split_axis=0, concat_axis=0, tiled=True)  76.6 us
    all_to_all x2, waiting for transfers between devices, swap(): return lax.all_to_all(value, axes, split_axis=0, concat_axis=0, tiled=True)  26.7 us
    ppermute x3, waiting for transfers between devices, shards(): lax.ppermute(parts[k], 'hid', [(h, h ^ k) for h in range(hid_count)])  25.1 us
    all_to_all x2, starting transfers between devices, swap(): return lax.all_to_all(value, axes, split_axis=0, concat_axis=0, tiled=True)  18.5 us
    all_gather x1, blocking collectives, shards(): active = lax.all_gather(active, 'hid', axis=0, tiled=False)  17.5 us
    pallas_call x6, Pallas kernels, call(): pl.pallas_call(kernel, out_shape=out_shapes, in_specs=[pl.BlockSpec(memor...  10.8 us
    ppermute x3, starting transfers between devices, shards(): lax.ppermute(parts[k], 'hid', [(h, h ^ k) for h in range(hid_count)])  10.1 us
    ppermute x3, starting transfers between devices, other_core(): return lax.ppermute(value, 'core', [(0, 1), (1, 0)])  6.24 us
  transfers between devices with their start and end apart: 8, of which 5 were waited for; matrix products, arithmetic and copies ran while one was open for 1% of the time, Pallas kernels for 1%

profile of v9, /device:TPU:2, one launch (start us, length us, event | category | flops | bytes accessed | tf_op | source)
XLA Modules:
  0.0 201.4 jit_solution(15941255568407633655)
XLA Ops:
  0.0 0.0 copy-start
  0.0 0.9 pad_maximum_fusion
  0.9 25.2 %all_to_all.30 = bf16[8,128,256]{2,1,0:T(8,128)(2,1)S(1)} all-to-all(bf16[8,128,256]{2,1,0:T(8,128)(2,1)S(1)} %broadcast_in_dim.6), channel_id=1, replica_groups=mesh['x'=4,'yh'=2,'core'=2,'exp'=8,'hid'=4] {'x','yh'}, dimensions={0} | all-to-all | bytes 1048576 | tf_op jit(solution)/shard_map/kv_gather/all_to_all | solution.py:25
  26.1 1.9 collective-permute-start
  28.0 0.1 pad_add_fusion.place
  28.1 1.8 collective-permute-done.far
  29.9 0.0 copy-done
  29.9 0.0 copy-start.4
  29.9 0.8 copy-done.4
  30.6 0.0 copy-start.7
  30.6 0.0 copy-start.8
  30.6 2.6 %attention.1 = (bf16[4,128,1024]{2,1,0:T(8,128)(2,1)}, f32[8,128]{1,0:T(8,128)S(1)}) custom-call(s32[3]{0:T(128)S(1)} %pad_add_fusion.place, bf16[128,128]{1,0:T(8,128)(2,1)S(1)} %copy-done.4, bf16[1024,256]{1,0:T(8,128)(2,1)S(1)} %bitcast.21, bf16[1024,256]{1,0:T(8,128)(2,1)S(1)} %collective-permute-done.far, bf16[128,4096]{1,0:T(8,128)(2,1)S(1)} %copy-done), custom_call_target="tpu_custom_call" | custom-call | flops 268435456 | bytes 3182604 | tf_op jit(solution)/shard_map/attention/pallas_call | solution.py:41
  33.3 0.0 copy-start.5
  33.3 13.6 %all-to-all-start.1 = ((bf16[32,16,1024]{2,1,0:T(8,128)(2,1)}), bf16[32,16,1024]{2,1,0:T(8,128)(2,1)S(1)}, u32[]{:S(2)}, u32[]{:S(2)}) async-start(bf16[32,16,1024]{2,1,0:T(8,128)(2,1)} %bitcast.4), calls=%async_computation.1 | async-start | bytes 2097152 | tf_op jit(solution)/shard_map/projection/all_to_all | solution.py:25
  46.9 0.0 copy-done.7
  46.9 0.0 copy-done.8
  46.9 0.0 copy-start.1
  46.9 1.2 copy-done.1
  48.1 0.0 copy-start.2
  48.1 1.2 copy-done.2
  49.4 0.0 copy-start.3
  49.4 1.2 copy-done.3
  50.6 1.8 prepare.1
  52.4 1.9 collective-permute-start.1
  54.4 2.4 %collective-permute-start.2 = (bf16[512,1024]{1,0:T(8,128)(2,1)S(1)}, bf16[512,1024]{1,0:T(8,128)(2,1)S(1)}, u32[]{:S(2)}, u32[]{:S(2)}) collective-permute-start(bf16[512,1024]{1,0:T(8,128)(2,1)S(1)} %get-tuple-element.24.near), channel_id=1, source_target_pairs={{0,32},{32,0},{1,33},{33,1},{2,34},{34,2},{3,35},{35,3},{4,36},{36... | collective-permute-start | bytes 3145736 | tf_op jit(solution)/shard_map/prepare/ppermute | solution.py:33
  56.8 17.8 %all-to-all-done.1.arrived = bf16[32,16,1024]{2,1,0:T(8,128)(2,1)S(1)} async-done(((bf16[32,16,1024]{2,1,0:T(8,128)(2,1)}), bf16[32,16,1024]{2,1,0:T(8,128)(2,1)S(1)}, u32[]{:S(2)}, u32[]{:S(2)}) %all-to-all-start.1) | async-done | bytes 1048608 | tf_op jit(solution)/shard_map/projection/all_to_all | solution.py:25
  74.6 0.0 copy-done.5
  74.6 0.0 copy-start.6
  74.6 0.3 projection.1
  74.9 17.9 %all_to_all.31 = bf16[16,6,1024]{2,1,0:T(8,128)(2,1)S(1)} all-to-all(bf16[16,6,1024]{2,1,0:T(8,128)(2,1)S(1)} %bitcast.25), channel_id=1, replica_groups=mesh['x'=4,'yh'=2,'core'=2,'exp'=8,'hid'=4] {'yh','exp'}, dimensions={0} | all-to-all | bytes 393216 | tf_op jit(solution)/shard_map/dispatch/all_to_all | solution.py:25
  92.8 0.1 broadcast_in_dim.14
  92.8 1.0 broadcast_in_dim.15
  93.8 4.9 %all-to-all-start.3 = ((bf16[4,96,1024]{2,1,0:T(8,128)(2,1)}), bf16[4,96,1024]{2,1,0:T(8,128)(2,1)S(1)}, u32[]{:S(2)}, u32[]{:S(2)}) async-start(bf16[4,96,1024]{2,1,0:T(8,128)(2,1)} %broadcast_in_dim.15), calls=%async_computation.3 | async-start | bytes 1572864 | tf_op jit(solution)/shard_map/dispatch/all_to_all | solution.py:25
  98.8 0.0 collective-permute-done.2.down.far
  98.8 0.0 collective-permute-done.1.far
  98.8 9.0 %all-to-all-done.3 = bf16[4,96,1024]{2,1,0:T(8,128)(2,1)S(1)} async-done(((bf16[4,96,1024]{2,1,0:T(8,128)(2,1)}), bf16[4,96,1024]{2,1,0:T(8,128)(2,1)S(1)}, u32[]{:S(2)}, u32[]{:S(2)}) %all-to-all-start.3) | async-done | bytes 786464 | tf_op jit(solution)/shard_map/dispatch/all_to_all | solution.py:25
  107.7 0.0 copy-done.6
  107.7 4.8 %gate_up.1 = (bf16[400,512]{1,0:T(8,128)(2,1)S(1)}, bf16[400,512]{1,0:T(8,128)(2,1)S(1)}, bf16[400,512]{1,0:T(8,128)(2,1)S(1)}, bf16[400,512]{1,0:T(8,128)(2,1)S(1)}) custom-call(s32[3]{0:T(128)S(1)} %pad_add_fusion.place, bf16[384,1024]{1,0:T(8,128)(2,1)S(1)} %bitcast.19, f32[1,1024]{1,0:T(1,128)S(1)} %bitcast.26, ...), custom_call_target="tpu_custom_call" | custom-call | flops 1610612736 | bytes 7671820 | tf_op jit(solution)/shard_map/gate_up/pallas_call | solution.py:41
  112.5 4.2 %collective-permute-start.3 = (bf16[400,512]{1,0:T(8,128)(2,1)S(1)}, bf16[400,512]{1,0:T(8,128)(2,1)S(1)}, u32[]{:S(2)}, u32[]{:S(2)}) collective-permute-start(bf16[400,512]{1,0:T(8,128)(2,1)S(1)} %get-tuple-element.26), channel_id=1, source_target_pairs={{0,3},{1,2},{2,1},{3,0},{4,7},{5,6},{6,5},{7,4},{8,11},{9,10},{10,... | collective-permute-start | bytes 1228808 | tf_op jit(solution)/shard_map/gate_up/ppermute | solution.py:258
  116.7 2.7 %collective-permute-start.4 = (bf16[400,512]{1,0:T(8,128)(2,1)S(1)}, bf16[400,512]{1,0:T(8,128)(2,1)S(1)}, u32[]{:S(2)}, u32[]{:S(2)}) collective-permute-start(bf16[400,512]{1,0:T(8,128)(2,1)S(1)} %get-tuple-element.27), channel_id=1, source_target_pairs={{0,2},{1,3},{2,0},{3,1},{4,6},{5,7},{6,4},{7,5},{8,10},{9,11},{10,... | collective-permute-start | bytes 1228808 | tf_op jit(solution)/shard_map/gate_up/ppermute | solution.py:258
  119.4 3.3 %collective-permute-start.5 = (bf16[400,512]{1,0:T(8,128)(2,1)S(1)}, bf16[400,512]{1,0:T(8,128)(2,1)S(1)}, u32[]{:S(2)}, u32[]{:S(2)}) collective-permute-start(bf16[400,512]{1,0:T(8,128)(2,1)S(1)} %get-tuple-element.28), channel_id=1, source_target_pairs={{0,1},{1,0},{2,3},{3,2},{4,5},{5,4},{6,7},{7,6},{8,9},{9,8},{10,11... | collective-permute-start | bytes 1228808 | tf_op jit(solution)/shard_map/gate_up/ppermute | solution.py:258
  122.7 6.0 %collective-permute-done.3.refs_1_ = bf16[400,512]{1,0:T(8,128)(2,1)S(1)} collective-permute-done((bf16[400,512]{1,0:T(8,128)(2,1)S(1)}, bf16[400,512]{1,0:T(8,128)(2,1)S(1)}, u32[]{:S(2)}, u32[]{:S(2)}) %collective-permute-start.3) | collective-permute-done | bytes 409632 | tf_op jit(solution)/shard_map/gate_up/ppermute | solution.py:258
  128.7 19.1 %collective-permute-done.4.refs_2_ = bf16[400,512]{1,0:T(8,128)(2,1)S(1)} collective-permute-done((bf16[400,512]{1,0:T(8,128)(2,1)S(1)}, bf16[400,512]{1,0:T(8,128)(2,1)S(1)}, u32[]{:S(2)}, u32[]{:S(2)}) %collective-permute-start.4) | collective-permute-done | bytes 409632 | tf_op jit(solution)/shard_map/gate_up/ppermute | solution.py:258
  147.8 0.0 collective-permute-done.5.refs_3_
  147.8 0.3 active.1
  148.1 17.5 %all-gather = bf16[3072,128]{1,0:T(8,128)(2,1)S(1)} all-gather(bf16[768,128]{1,0:T(8,128)(2,1)S(1)} %active.1), channel_id=2, replica_groups=mesh['x'=4,'yh'=2,'core'=2,'exp'=8,'hid'=4] {'hid'}, dimensions={0}, use_global_device_ids=true | all-gather | bytes 983040 | tf_op jit(solution)/shard_map/active/all_gather | solution.py:261
  165.6 1.0 down.1
  166.6 11.8 %all_to_all.32 = bf16[4,96,1024]{2,1,0:T(8,128)(2,1)S(1)} all-to-all(bf16[4,96,1024]{2,1,0:T(8,128)(2,1)S(1)} %bitcast.17), channel_id=1, replica_groups=mesh['x'=4,'yh'=2,'core'=2,'exp'=8,'hid'=4] {'x'}, dimensions={0} | all-to-all | bytes 1572864 | tf_op jit(solution)/shard_map/down/all_to_all | solution.py:25
  178.4 0.1 reduce_sum.21
  178.6 0.1 reshape.33
  178.6 21.7 %all_to_all.33 = bf16[16,6,1024]{2,1,0:T(8,128)(2,1)S(1)} all-to-all(bf16[16,6,1024]{2,1,0:T(8,128)(2,1)S(1)} %reshape.33), channel_id=1, replica_groups=mesh['x'=4,'yh'=2,'core'=2,'exp'=8,'hid'=4] {'yh','exp'}, dimensions={0} | all-to-all | bytes 393216 | tf_op jit(solution)/shard_map/down/all_to_all | solution.py:25
  200.4 0.1 reshape.34
  200.5 0.9 fusion
  (2 shorter events, 0.1 us)
Async XLA Ops:
  0.0 29.9 %copy-start = (bf16[128,4096]{1,0:T(8,128)(2,1)S(1)}, bf16[128,4096]{1,0:T(8,128)(2,1)}, u32[]{:S(2)}) copy-start(bf16[128,4096]{1,0:T(8,128)(2,1)} %weight.1) | copy-start | bytes 3145732
  26.1 3.8 %collective-permute-start = (bf16[1024,256]{1,0:T(8,128)(2,1)S(1)}, bf16[1024,256]{1,0:T(8,128)(2,1)S(1)}, u32[]{:S(2)}, u32[]{:S(2)}) collective-permute-start(bf16[1024,256]{1,0:T(8,128)(2,1)S(1)} %bitcast.20), channel_id=1, source_target_pairs={{0,32},{32,0},{1,33},{33,1},{2,34},{34,2},{3,35},{35,3},{4,36},{36... | collective-permute-start | bytes 1572872 | tf_op jit(solution)/shard_map/kv_gather/ppermute | solution.py:33
  29.9 0.8 copy-start.4
  30.6 16.3 %copy-start.7 = (s32[16,2]{0,1:T(2,128)S(1)}, s32[16,2]{0,1:T(2,128)}, u32[]{:S(2)}) copy-start(s32[16,2]{0,1:T(2,128)} %param.20) | copy-start | bytes 388
  30.6 16.3 %copy-start.8 = (f32[16,2]{0,1:T(2,128)S(1)}, f32[16,2]{0,1:T(2,128)}, u32[]{:S(2)}) copy-start(f32[16,2]{0,1:T(2,128)} %param.21) | copy-start | bytes 388
  33.3 41.3 %copy-start.5 = (bf16[16,1024]{1,0:T(8,128)(2,1)S(1)}, bf16[16,1024]{1,0:T(8,128)(2,1)}, u32[]{:S(2)}) copy-start(bf16[16,1024]{1,0:T(8,128)(2,1)} %residual.1) | copy-start | bytes 98308
  33.3 41.3 %all-to-all-start.1 = ((bf16[32,16,1024]{2,1,0:T(8,128)(2,1)}), bf16[32,16,1024]{2,1,0:T(8,128)(2,1)S(1)}, u32[]{:S(2)}, u32[]{:S(2)}) async-start(bf16[32,16,1024]{2,1,0:T(8,128)(2,1)} %bitcast.4), calls=%async_computation.1 | async-start | bytes 2097152 | tf_op jit(solution)/shard_map/projection/all_to_all | solution.py:25
  46.9 1.2 copy-start.1
  48.1 1.2 copy-start.2
  49.4 1.2 copy-start.3
  52.4 46.3 %collective-permute-start.1 = (bf16[1024,1024]{1,0:T(8,128)(2,1)}, bf16[1024,1024]{1,0:T(8,128)(2,1)}, u32[]{:S(2)}, u32[]{:S(2)}) collective-permute-start(bf16[1024,1024]{1,0:T(8,128)(2,1)} %get-tuple-element.23.near), channel_id=1, source_target_pairs={{0,32},{32,0},{1,33},{33,1},{2,34},{34,2},{3,35},{35,3},{4,36},{36... | collective-permute-start | bytes 6291464 | tf_op jit(solution)/shard_map/prepare/ppermute | solution.py:33
  54.4 44.4 %collective-permute-start.2 = (bf16[512,1024]{1,0:T(8,128)(2,1)S(1)}, bf16[512,1024]{1,0:T(8,128)(2,1)S(1)}, u32[]{:S(2)}, u32[]{:S(2)}) collective-permute-start(bf16[512,1024]{1,0:T(8,128)(2,1)S(1)} %get-tuple-element.24.near), channel_id=1, source_target_pairs={{0,32},{32,0},{1,33},{33,1},{2,34},{34,2},{3,35},{35,3},{4,36},{36... | collective-permute-start | bytes 3145736 | tf_op jit(solution)/shard_map/prepare/ppermute | solution.py:33
  74.6 33.2 %copy-start.6 = (f32[1024]{0:T(1024)S(1)}, f32[1024]{0:T(1024)}, u32[]{:S(2)}) copy-start(f32[1024]{0:T(1024)} %param.16) | copy-start | bytes 12292
  93.8 13.9 %all-to-all-start.3 = ((bf16[4,96,1024]{2,1,0:T(8,128)(2,1)}), bf16[4,96,1024]{2,1,0:T(8,128)(2,1)S(1)}, u32[]{:S(2)}, u32[]{:S(2)}) async-start(bf16[4,96,1024]{2,1,0:T(8,128)(2,1)} %broadcast_in_dim.15), calls=%async_computation.3 | async-start | bytes 1572864 | tf_op jit(solution)/shard_map/dispatch/all_to_all | solution.py:25
  112.5 16.1 %collective-permute-start.3 = (bf16[400,512]{1,0:T(8,128)(2,1)S(1)}, bf16[400,512]{1,0:T(8,128)(2,1)S(1)}, u32[]{:S(2)}, u32[]{:S(2)}) collective-permute-start(bf16[400,512]{1,0:T(8,128)(2,1)S(1)} %get-tuple-element.26), channel_id=1, source_target_pairs={{0,3},{1,2},{2,1},{3,0},{4,7},{5,6},{6,5},{7,4},{8,11},{9,10},{10,... | collective-permute-start | bytes 1228808 | tf_op jit(solution)/shard_map/gate_up/ppermute | solution.py:258
  116.7 31.1 %collective-permute-start.4 = (bf16[400,512]{1,0:T(8,128)(2,1)S(1)}, bf16[400,512]{1,0:T(8,128)(2,1)S(1)}, u32[]{:S(2)}, u32[]{:S(2)}) collective-permute-start(bf16[400,512]{1,0:T(8,128)(2,1)S(1)} %get-tuple-element.27), channel_id=1, source_target_pairs={{0,2},{1,3},{2,0},{3,1},{4,6},{5,7},{6,4},{7,5},{8,10},{9,11},{10,... | collective-permute-start | bytes 1228808 | tf_op jit(solution)/shard_map/gate_up/ppermute | solution.py:258
  119.4 28.4 %collective-permute-start.5 = (bf16[400,512]{1,0:T(8,128)(2,1)S(1)}, bf16[400,512]{1,0:T(8,128)(2,1)S(1)}, u32[]{:S(2)}, u32[]{:S(2)}) collective-permute-start(bf16[400,512]{1,0:T(8,128)(2,1)S(1)} %get-tuple-element.28), channel_id=1, source_target_pairs={{0,1},{1,0},{2,3},{3,2},{4,5},{5,4},{6,7},{7,6},{8,9},{9,8},{10,11... | collective-permute-start | bytes 1228808 | tf_op jit(solution)/shard_map/gate_up/ppermute | solution.py:258

commit v10 on v9

--- a/solution.py
+++ b/solution.py
@@ -31,6 +31,10 @@
 
 def other_core(value):
     return lax.ppermute(value, "core", [(0, 1), (1, 0)])
+
+
+def to_peer(value, offset):
+    return lax.ppermute(value, "hid", [(h, h ^ offset) for h in range(lax.axis_size("hid"))])
 
 
 def whole(kernel, out_shapes, flops, smem=0, held=0, scratch=()):
@@ -81,12 +85,16 @@
 
 
 def prepare_kernel(after, ids, shares, gate, up, down, selector, mixer, weights, down_out, sems):
-    columns = gate.shape[1]
-    copies = [
-        pltpu.make_async_copy(gate, weights.at[:, pl.ds(0, columns)], sems.at[0]),
-        pltpu.make_async_copy(up, weights.at[:, pl.ds(columns, columns)], sems.at[1]),
-        pltpu.make_async_copy(down, down_out, sems.at[2]),
-    ]
+    peers = (sems.shape[0] - 1) // 2
+    piece = gate.shape[1] // peers
+    copies = [pltpu.make_async_copy(down, down_out, sems.at[2 * peers])]
+    for index in range(peers):
+        for which, source in enumerate((gate, up)):
+            place = 2 * index + which
+            taken = source.at[:, pl.ds(index * piece, piece)]
+            copies.append(
+                pltpu.make_async_copy(taken, weights.at[:, pl.ds(place * piece, piece)], sems.at[place])
+            )
     for copy in copies:
         copy.start()
     slots, tokens = mixer.shape
@@ -121,19 +129,25 @@
             outgoing[half, expert] = part
 
 
-def gate_up_kernel(place, rows, gain, near, far, down, *outs):
-    hid = place[2]
+def arrange_kernel(arrived, weights, down, out):
+    rows = jnp.concatenate([arrived[index].astype(F32) for index in range(arrived.shape[0])], axis=0).astype(BF16)
+    for index in range(out.shape[0]):
+        out[index] = rows
+
+
+def share_of(place, scaled, near, far, offset, out):
+    width = out.shape[1] // 2
+    start = pl.multiple_of((place[2] ^ offset) * width, width)
+    for index, source in enumerate((near, far)):
+        product = jnp.dot(scaled, source[:, pl.ds(start, width)], preferred_element_type=F32)
+        out[: scaled.shape[0], index * width : (index + 1) * width] = product.astype(BF16)
+
+
+def first_kernel(place, rows, gain, near, far, third, second, scaled_out, tail_out):
     count, depth = rows.shape
-    piece = outs[0].shape[1] // 4
     widened = rows[...].astype(F32)
     scaled = (widened * gain[...]).astype(BF16)
-    for k, out in enumerate(outs):
-        start = pl.multiple_of((hid ^ k) * piece, piece)
-        other = pl.multiple_of((hid ^ k) * piece + len(outs) * piece, piece)
-        for index, source in enumerate((near, far)):
-            weight = jnp.concatenate([source[:depth, pl.ds(start, piece)], source[:depth, pl.ds(other, piece)]], axis=1)
-            product = jnp.dot(scaled, weight, preferred_element_type=F32)
-            out[:count, 2 * index * piece : 2 * (index + 1) * piece] = product.astype(BF16)
+    scaled_out[...] = scaled
     square = widened * widened
     high = square.astype(BF16)
     low = (square - high.astype(F32)).astype(BF16)
@@ -142,9 +156,17 @@
     high = norm.astype(BF16).astype(F32)
     line = lax.broadcasted_iota(jnp.int32, norm.shape, 0)
     tail = jnp.where(line == 0, high, jnp.where(line == 1, norm - high, 0.0)).astype(BF16)
-    tail = jnp.concatenate([tail, jnp.zeros((TAIL, 4 * piece - count), BF16)], axis=1)
-    for out in outs:
-        out[count:, :] = tail
+    tail = jnp.concatenate([tail, jnp.zeros((TAIL, third.shape[1] - count), BF16)], axis=1)
+    for out in (third, second, tail_out):
+        out[out.shape[0] - TAIL :, :] = tail
+    share_of(place, scaled, near, far, 3, third)
+    share_of(place, scaled, near, far, 2, second)
+
+
+def last_kernel(place, scaled, tail, near, far, first, own):
+    for offset, out in ((1, first), (0, own)):
+        out[scaled.shape[0] :, :] = tail[...]
+        share_of(place, scaled[...], near, far, offset, out)
 
 
 def active_kernel(*refs):
@@ -221,7 +243,7 @@
                 shape((ff_part, width_part), BF16),
             ],
             flops=0,
-            scratch=[pltpu.SemaphoreType.DMA((3,))],
+            scratch=[pltpu.SemaphoreType.DMA((2 * hid_count + 1,))],
         )(done, expert_ids.T, expert_weights.T, gate_weight[0], up_weight[0], down_weight[0])
         far_weights, far_down = other_core(near_weights), other_core(near_down)
     with jax.named_scope("projection"):
@@ -234,28 +256,29 @@
 
     with jax.named_scope("dispatch"):
         arrived = swap(outgoing.reshape(halves * exp_count, CAP, width_part), ("yh", "exp"))
-        arrived = spread(arrived.reshape(halves * exp_count * CAP, width_part), "x")
+        (copies,) = whole(
+            arrange_kernel,
+            [shape((lines, halves * exp_count * CAP, width_part), BF16)],
+            flops=0,
+            held=2,
+        )(arrived, far_weights, far_down)
+        arrived = swap(copies, "x")
         count = lines * halves * exp_count * CAP
         rows = arrived.reshape(count, width_part)
 
     with jax.named_scope("gate_up"):
-        parts = whole(
-            gate_up_kernel,
-            [shape((count + TAIL, 4 * piece), BF16)] * hid_count,
-            flops=8 * count * width_part * ff_part,
+        part = shape((count + TAIL, 4 * piece), BF16)
+        third, second, scaled, tail = whole(
+            first_kernel,
+            [part, part, shape((count, width_part), BF16), shape((TAIL, 4 * piece), BF16)],
+            flops=4 * count * width_part * ff_part,
             smem=1,
-            held=1,
-        )(
-            place,
-            rows,
-            norm_gain.reshape(1, width_part),
-            near_weights,
-            far_weights,
-            far_down,
-        )
-        arrivals = [parts[0]]
-        for k in reversed(range(1, hid_count)):
-            arrivals.append(lax.ppermute(parts[k], "hid", [(h, h ^ k) for h in range(hid_count)]))
+        )(place, rows, norm_gain.reshape(1, width_part), near_weights, far_weights)
+        third, second = to_peer(third, 3), to_peer(second, 2)
+        first, own = whole(
+            last_kernel, [part, part], flops=4 * count * width_part * ff_part, smem=1
+        )(place, scaled, tail, near_weights, far_weights)
+        arrivals = [third, second, to_peer(first, 1), own]
     with jax.named_scope("active"):
         (active,) = whole(active_kernel, [shape((2 * count, piece), BF16)], flops=count * piece * 40)(*arrivals)
         active = lax.all_gather(active, "hid", axis=0, tiled=False)

time: 202 us -> 202 us (level)
  blocking collectives: 94.1 us -> 86.6 us
  waiting for transfers between devices: 53.7 us -> 57.8 us
  Pallas kernels: 10.8 us -> 14 us
    all_to_all x4, blocking collectives: 76.6 us -> 67.5 us  [swap(): return lax.all_to_all(value, axes, split_axis=0, concat_axis=0, tiled=True)]
    all_to_all x2, waiting for transfers between devices: 26.7 us -> 30.9 us  [swap(): return lax.all_to_all(value, axes, split_axis=0, concat_axis=0, tiled=True)]
    pallas_call x6 -> x8, Pallas kernels: 10.8 us -> 14 us  [call(): pl.pallas_call(kernel, out_shape=out_shapes, in_specs=[pl.BlockSpec(memor...]
    unnamed x18 -> x22, local copies, waits for them, and re-layouts: 4.45 us -> 4.9 us
  transfers between devices with their start and end apart: 8 -> 8, of which waited for: 5 -> 5; matrix products, arithmetic and copies ran while one was open for 1% -> 0% of each run, Pallas kernels for 1% -> 3%
where the time goes in v10:
time: 202 us; the launch traced here: 201 us
  blocking collectives  86.6 us (43%)
  waiting for transfers between devices  57.8 us (29%)
  starting transfers between devices  35.5 us (18%)
  Pallas kernels  14 us (7%)
  local copies, waits for them, and re-layouts  5.06 us (3%)
    all_to_all x4, blocking collectives, swap(): return lax.all_to_all(value, axes, split_axis=0, concat_axis=0, tiled=True)  67.5 us
    all_to_all x2, waiting for transfers between devices, swap(): return lax.all_to_all(value, axes, split_axis=0, concat_axis=0, tiled=True)  30.9 us
    ppermute x3, waiting for transfers between devices, to_peer(): lax.ppermute(value, 'hid', [(h, h ^ offset) for h in range(lax.axis_size(...  25.1 us
    all_gather x1, blocking collectives, shards(): active = lax.all_gather(active, 'hid', axis=0, tiled=False)  19.1 us
    all_to_all x2, starting transfers between devices, swap(): return lax.all_to_all(value, axes, split_axis=0, concat_axis=0, tiled=True)  19.1 us
    pallas_call x8, Pallas kernels, call(): pl.pallas_call(kernel, out_shape=out_shapes, in_specs=[pl.BlockSpec(memor...  14 us
    ppermute x3, starting transfers between devices, to_peer(): lax.ppermute(value, 'hid', [(h, h ^ offset) for h in range(lax.axis_size(...  10.1 us
    ppermute x3, starting transfers between devices, other_core(): return lax.ppermute(value, 'core', [(0, 1), (1, 0)])  6.23 us
  transfers between devices with their start and end apart: 8, of which 5 were waited for; matrix products, arithmetic and copies ran while one was open for 0% of the time, Pallas kernels for 3%

profile of v10, /device:TPU:2, one launch (start us, length us, event | category | flops | bytes accessed | tf_op | source)
XLA Modules:
  0.0 201.2 jit_solution(942481665830289458)
XLA Ops:
  0.0 0.0 copy-start
  0.0 0.9 pad_maximum_fusion
  0.9 25.2 %all_to_all.30 = bf16[8,128,256]{2,1,0:T(8,128)(2,1)S(1)} all-to-all(bf16[8,128,256]{2,1,0:T(8,128)(2,1)S(1)} %broadcast_in_dim.2), channel_id=1, replica_groups=mesh['x'=4,'yh'=2,'core'=2,'exp'=8,'hid'=4] {'x','yh'}, dimensions={0} | all-to-all | bytes 1048576 | tf_op jit(solution)/shard_map/kv_gather/all_to_all | solution.py:25
  26.1 1.9 collective-permute-start
  28.0 0.1 pad_add_fusion.place
  28.1 0.0 copy-start.1
  28.1 1.8 collective-permute-done.far
  29.9 0.0 copy-done
  29.9 0.0 copy-start.6
  29.9 0.8 copy-done.6
  30.6 0.0 copy-start.9
  30.6 0.0 copy-start.10
  30.6 1.6 attention.1
  32.3 0.0 copy-start.4
  32.3 1.0 copy-done.4
  33.3 0.0 copy-start.7
  33.3 13.8 %all-to-all-start.1 = ((bf16[32,16,1024]{2,1,0:T(8,128)(2,1)}), bf16[32,16,1024]{2,1,0:T(8,128)(2,1)}, u32[]{:S(2)}, u32[]{:S(2)}) async-start(bf16[32,16,1024]{2,1,0:T(8,128)(2,1)} %bitcast.25), calls=%async_computation.1 | async-start | bytes 2097152 | tf_op jit(solution)/shard_map/projection/all_to_all | solution.py:25
  47.0 0.0 copy-done.1
  47.0 0.0 copy-done.9
  47.0 0.0 copy-done.10
  47.1 0.0 copy-start.2
  47.1 1.2 copy-done.2
  48.3 0.0 copy-start.3
  48.3 1.2 copy-done.3
  49.5 2.6 %prepare.1 = (bf16[48,16]{1,0:T(8,128)(2,1)S(1)}, f32[48,16]{1,0:T(8,128)S(1)}, bf16[1024,1024]{1,0:T(8,128)(2,1)}, bf16[512,1024]{1,0:T(8,128)(2,1)}) custom-call(f32[8,128]{1,0:T(8,128)S(1)} %get-tuple-element.20.after, s32[2,16]{1,0:T(2,128)S(1)} %bitcast.28, f32[2,16]{1,0:T(2,128)S(1)} %bitcast.29, bf16[1024,512]{1,0:T(8,128)(2,1)S(1)} %bitcast.22, ...), custom_call_target="tpu_custom_call" | custom-call | bytes 6300416 | tf_op jit(solution)/shard_map/prepare/pallas_call | solution.py:45
  52.1 1.9 collective-permute-start.1
  54.0 2.4 %collective-permute-start.2 = (bf16[512,1024]{1,0:T(8,128)(2,1)}, bf16[512,1024]{1,0:T(8,128)(2,1)S(1)}, u32[]{:S(2)}, u32[]{:S(2)}) collective-permute-start(bf16[512,1024]{1,0:T(8,128)(2,1)} %get-tuple-element.26.near), channel_id=1, source_target_pairs={{0,32},{32,0},{1,33},{33,1},{2,34},{34,2},{3,35},{35,3},{4,36},{36... | collective-permute-start | bytes 3145736 | tf_op jit(solution)/shard_map/prepare/ppermute | solution.py:33
  56.4 18.2 %all-to-all-done.1.arrived = bf16[32,16,1024]{2,1,0:T(8,128)(2,1)} async-done(((bf16[32,16,1024]{2,1,0:T(8,128)(2,1)}), bf16[32,16,1024]{2,1,0:T(8,128)(2,1)}, u32[]{:S(2)}, u32[]{:S(2)}) %all-to-all-start.1) | async-done | bytes 1048608 | tf_op jit(solution)/shard_map/projection/all_to_all | solution.py:25
  74.7 0.0 copy-done.7
  74.7 1.5 projection.1
  76.2 0.0 copy-start.5
  76.2 0.7 copy-done.5
  76.9 5.4 %all-to-all-start.2 = ((bf16[16,6,1024]{2,1,0:T(8,128)(2,1)}), bf16[16,6,1024]{2,1,0:T(8,128)(2,1)S(1)}, u32[]{:S(2)}, u32[]{:S(2)}) async-start(bf16[16,6,1024]{2,1,0:T(8,128)(2,1)} %bitcast.26), calls=%async_computation.2 | async-start | bytes 524288 | tf_op jit(solution)/shard_map/dispatch/all_to_all | solution.py:25
  82.3 0.0 copy-start.8
  82.3 0.0 collective-permute-done.2.down.far
  82.3 0.0 collective-permute-done.1.weights.far
  82.3 12.7 %all-to-all-done.2.arrived = bf16[16,6,1024]{2,1,0:T(8,128)(2,1)S(1)} async-done(((bf16[16,6,1024]{2,1,0:T(8,128)(2,1)}), bf16[16,6,1024]{2,1,0:T(8,128)(2,1)S(1)}, u32[]{:S(2)}, u32[]{:S(2)}) %all-to-all-start.2) | async-done | bytes 196640 | tf_op jit(solution)/shard_map/dispatch/all_to_all | solution.py:25
  95.0 0.1 dispatch.1
  95.1 12.8 %all_to_all.31 = bf16[4,96,1024]{2,1,0:T(8,128)(2,1)S(1)} all-to-all(bf16[4,96,1024]{2,1,0:T(8,128)(2,1)S(1)} %dispatch.1), channel_id=1, replica_groups=mesh['x'=4,'yh'=2,'core'=2,'exp'=8,'hid'=4] {'x'}, dimensions={0} | all-to-all | bytes 1572864 | tf_op jit(solution)/shard_map/dispatch/all_to_all | solution.py:25
  107.9 0.0 copy-done.8
  107.9 3.0 %gate_up.2 = (bf16[400,512]{1,0:T(8,128)(2,1)S(1)}, bf16[400,512]{1,0:T(8,128)(2,1)S(1)}, bf16[384,1024]{1,0:T(8,128)(2,1)S(1)}, bf16[16,512]{1,0:T(8,128)(2,1)S(1)}) custom-call(s32[3]{0:T(128)S(1)} %pad_add_fusion.place, bf16[384,1024]{1,0:T(8,128)(2,1)S(1)} %bitcast.19, f32[1,1024]{1,0:T(1,128)S(1)} %bitcast.27, ...), custom_call_target="tpu_custom_call" | custom-call | flops 805306368 | bytes 6606860 | tf_op jit(solution)/shard_map/gate_up/pallas_call | solution.py:45
  111.0 4.1 %collective-permute-start.3 = (bf16[400,512]{1,0:T(8,128)(2,1)S(1)}, bf16[400,512]{1,0:T(8,128)(2,1)S(1)}, u32[]{:S(2)}, u32[]{:S(2)}) collective-permute-start(bf16[400,512]{1,0:T(8,128)(2,1)S(1)} %get-tuple-element.27), channel_id=1, source_target_pairs={{0,3},{1,2},{2,1},{3,0},{4,7},{5,6},{6,5},{7,4},{8,11},{9,10},{10,... | collective-permute-start | bytes 1228808 | tf_op jit(solution)/shard_map/gate_up/ppermute | solution.py:37
  115.1 3.2 %collective-permute-start.4 = (bf16[400,512]{1,0:T(8,128)(2,1)S(1)}, bf16[400,512]{1,0:T(8,128)(2,1)S(1)}, u32[]{:S(2)}, u32[]{:S(2)}) collective-permute-start(bf16[400,512]{1,0:T(8,128)(2,1)S(1)} %get-tuple-element.28), channel_id=1, source_target_pairs={{0,2},{1,3},{2,0},{3,1},{4,6},{5,7},{6,4},{7,5},{8,10},{9,11},{10,... | collective-permute-start | bytes 1228808 | tf_op jit(solution)/shard_map/gate_up/ppermute | solution.py:37
  118.3 2.6 %gate_up.3 = (bf16[400,512]{1,0:T(8,128)(2,1)S(1)}, bf16[400,512]{1,0:T(8,128)(2,1)S(1)}) custom-call(s32[3]{0:T(128)S(1)} %pad_add_fusion.place, bf16[384,1024]{1,0:T(8,128)(2,1)S(1)} %get-tuple-element.29.scaled, bf16[16,512]{1,0:T(8,128)(2,1)S(1)} %get-tuple-element.30.tail, bf16[1024,1024]{1,0:T(8,128)(2,1)} %get-tuple-element.25.near, ...), custom_call_target="tpu_custom_call" | custom-call | flops 805306368 | bytes 5816332 | tf_op jit(solution)/shard_map/gate_up/pallas_call | solution.py:45
  120.9 2.8 %collective-permute-start.5 = (bf16[400,512]{1,0:T(8,128)(2,1)S(1)}, bf16[400,512]{1,0:T(8,128)(2,1)S(1)}, u32[]{:S(2)}, u32[]{:S(2)}) collective-permute-start(bf16[400,512]{1,0:T(8,128)(2,1)S(1)} %get-tuple-element.31), channel_id=1, source_target_pairs={{0,1},{1,0},{2,3},{3,2},{4,5},{5,4},{6,7},{7,6},{8,9},{9,8},{10,11... | collective-permute-start | bytes 1228808 | tf_op jit(solution)/shard_map/gate_up/ppermute | solution.py:37
  123.7 3.0 %collective-permute-done.3.refs_0_ = bf16[400,512]{1,0:T(8,128)(2,1)S(1)} collective-permute-done((bf16[400,512]{1,0:T(8,128)(2,1)S(1)}, bf16[400,512]{1,0:T(8,128)(2,1)S(1)}, u32[]{:S(2)}, u32[]{:S(2)}) %collective-permute-start.3) | collective-permute-done | bytes 409632 | tf_op jit(solution)/shard_map/gate_up/ppermute | solution.py:37
  126.7 22.1 %collective-permute-done.4.refs_1_ = bf16[400,512]{1,0:T(8,128)(2,1)S(1)} collective-permute-done((bf16[400,512]{1,0:T(8,128)(2,1)S(1)}, bf16[400,512]{1,0:T(8,128)(2,1)S(1)}, u32[]{:S(2)}, u32[]{:S(2)}) %collective-permute-start.4) | collective-permute-done | bytes 409632 | tf_op jit(solution)/shard_map/gate_up/ppermute | solution.py:37
  148.8 0.0 collective-permute-done.5.refs_2_
  148.8 0.3 active.1
  149.2 19.1 %all-gather = bf16[3072,128]{1,0:T(8,128)(2,1)S(1)} all-gather(bf16[768,128]{1,0:T(8,128)(2,1)S(1)} %active.1), channel_id=2, replica_groups=mesh['x'=4,'yh'=2,'core'=2,'exp'=8,'hid'=4] {'hid'}, dimensions={0}, use_global_device_ids=true | all-gather | bytes 983040 | tf_op jit(solution)/shard_map/active/all_gather | solution.py:284
  168.3 2.2 %down.1 = bf16[384,1024]{1,0:T(8,128)(2,1)S(1)} custom-call(bf16[4,768,128]{2,1,0:T(8,128)(2,1)S(1)} %bitcast.18, bf16[512,1024]{1,0:T(8,128)(2,1)} %get-tuple-element.26.near, bf16[512,1024]{1,0:T(8,128)(2,1)S(1)} %collective-permute-done.2.down.far), custom_call_target="tpu_custom_call" | custom-call | flops 805306368 | bytes 3670016 | tf_op jit(solution)/shard_map/down/pallas_call | solution.py:45
  170.5 12.3 %all_to_all.32 = bf16[4,96,1024]{2,1,0:T(8,128)(2,1)S(1)} all-to-all(bf16[4,96,1024]{2,1,0:T(8,128)(2,1)S(1)} %bitcast.17), channel_id=1, replica_groups=mesh['x'=4,'yh'=2,'core'=2,'exp'=8,'hid'=4] {'x'}, dimensions={0} | all-to-all | bytes 1572864 | tf_op jit(solution)/shard_map/down/all_to_all | solution.py:25
  182.8 0.1 reduce_sum.21
  183.0 0.1 reshape.31
  183.1 17.1 %all_to_all.33 = bf16[16,6,1024]{2,1,0:T(8,128)(2,1)S(1)} all-to-all(bf16[16,6,1024]{2,1,0:T(8,128)(2,1)S(1)} %reshape.31), channel_id=1, replica_groups=mesh['x'=4,'yh'=2,'core'=2,'exp'=8,'hid'=4] {'yh','exp'}, dimensions={0} | all-to-all | bytes 393216 | tf_op jit(solution)/shard_map/down/all_to_all | solution.py:25
  200.2 0.1 reshape.32
  200.3 0.9 fusion
  (2 shorter events, 0.1 us)
Async XLA Ops:
  0.0 29.9 %copy-start = (bf16[128,4096]{1,0:T(8,128)(2,1)S(1)}, bf16[128,4096]{1,0:T(8,128)(2,1)}, u32[]{:S(2)}) copy-start(bf16[128,4096]{1,0:T(8,128)(2,1)} %weight.1) | copy-start | bytes 3145732
  26.1 3.8 %collective-permute-start = (bf16[1024,256]{1,0:T(8,128)(2,1)S(1)}, bf16[1024,256]{1,0:T(8,128)(2,1)S(1)}, u32[]{:S(2)}, u32[]{:S(2)}) collective-permute-start(bf16[1024,256]{1,0:T(8,128)(2,1)S(1)} %bitcast.20), channel_id=1, source_target_pairs={{0,32},{32,0},{1,33},{33,1},{2,34},{34,2},{3,35},{35,3},{4,36},{36... | collective-permute-start | bytes 1572872 | tf_op jit(solution)/shard_map/kv_gather/ppermute | solution.py:33
  28.1 18.9 %copy-start.1 = (bf16[1,1024,512]{2,1,0:T(8,128)(2,1)S(1)}, bf16[1,1024,512]{2,1,0:T(8,128)(2,1)}, u32[]{:S(2)}) copy-start(bf16[1,1024,512]{2,1,0:T(8,128)(2,1)} %param.17) | copy-start | bytes 3145732
  29.9 0.8 copy-start.6
  30.6 16.4 %copy-start.9 = (s32[16,2]{0,1:T(2,128)S(1)}, s32[16,2]{0,1:T(2,128)}, u32[]{:S(2)}) copy-start(s32[16,2]{0,1:T(2,128)} %param.20) | copy-start | bytes 388
  30.6 16.4 %copy-start.10 = (f32[16,2]{0,1:T(2,128)S(1)}, f32[16,2]{0,1:T(2,128)}, u32[]{:S(2)}) copy-start(f32[16,2]{0,1:T(2,128)} %param.21) | copy-start | bytes 388
  32.3 1.0 copy-start.4
  33.3 41.4 %copy-start.7 = (bf16[16,1024]{1,0:T(8,128)(2,1)S(1)}, bf16[16,1024]{1,0:T(8,128)(2,1)}, u32[]{:S(2)}) copy-start(bf16[16,1024]{1,0:T(8,128)(2,1)} %residual.1) | copy-start | bytes 98308
  33.3 41.4 %all-to-all-start.1 = ((bf16[32,16,1024]{2,1,0:T(8,128)(2,1)}), bf16[32,16,1024]{2,1,0:T(8,128)(2,1)}, u32[]{:S(2)}, u32[]{:S(2)}) async-start(bf16[32,16,1024]{2,1,0:T(8,128)(2,1)} %bitcast.25), calls=%async_computation.1 | async-start | bytes 2097152 | tf_op jit(solution)/shard_map/projection/all_to_all | solution.py:25
  47.1 1.2 copy-start.2
  48.3 1.2 copy-start.3
  52.1 30.2 %collective-permute-start.1 = (bf16[1024,1024]{1,0:T(8,128)(2,1)}, bf16[1024,1024]{1,0:T(8,128)(2,1)S(1)}, u32[]{:S(2)}, u32[]{:S(2)}) collective-permute-start(bf16[1024,1024]{1,0:T(8,128)(2,1)} %get-tuple-element.25.near), channel_id=1, source_target_pairs={{0,32},{32,0},{1,33},{33,1},{2,34},{34,2},{3,35},{35,3},{4,36},{36... | collective-permute-start | bytes 6291464 | tf_op jit(solution)/shard_map/prepare/ppermute | solution.py:33
  54.0 28.3 %collective-permute-start.2 = (bf16[512,1024]{1,0:T(8,128)(2,1)}, bf16[512,1024]{1,0:T(8,128)(2,1)S(1)}, u32[]{:S(2)}, u32[]{:S(2)}) collective-permute-start(bf16[512,1024]{1,0:T(8,128)(2,1)} %get-tuple-element.26.near), channel_id=1, source_target_pairs={{0,32},{32,0},{1,33},{33,1},{2,34},{34,2},{3,35},{35,3},{4,36},{36... | collective-permute-start | bytes 3145736 | tf_op jit(solution)/shard_map/prepare/ppermute | solution.py:33
  76.2 0.7 copy-start.5
  76.9 18.1 %all-to-all-start.2 = ((bf16[16,6,1024]{2,1,0:T(8,128)(2,1)}), bf16[16,6,1024]{2,1,0:T(8,128)(2,1)S(1)}, u32[]{:S(2)}, u32[]{:S(2)}) async-start(bf16[16,6,1024]{2,1,0:T(8,128)(2,1)} %bitcast.26), calls=%async_computation.2 | async-start | bytes 524288 | tf_op jit(solution)/shard_map/dispatch/all_to_all | solution.py:25
  82.3 25.6 %copy-start.8 = (f32[1024]{0:T(1024)S(1)}, f32[1024]{0:T(1024)}, u32[]{:S(2)}) copy-start(f32[1024]{0:T(1024)} %param.16) | copy-start | bytes 12292
  111.0 15.7 %collective-permute-start.3 = (bf16[400,512]{1,0:T(8,128)(2,1)S(1)}, bf16[400,512]{1,0:T(8,128)(2,1)S(1)}, u32[]{:S(2)}, u32[]{:S(2)}) collective-permute-start(bf16[400,512]{1,0:T(8,128)(2,1)S(1)} %get-tuple-element.27), channel_id=1, source_target_pairs={{0,3},{1,2},{2,1},{3,0},{4,7},{5,6},{6,5},{7,4},{8,11},{9,10},{10,... | collective-permute-start | bytes 1228808 | tf_op jit(solution)/shard_map/gate_up/ppermute | solution.py:37
  115.1 33.8 %collective-permute-start.4 = (bf16[400,512]{1,0:T(8,128)(2,1)S(1)}, bf16[400,512]{1,0:T(8,128)(2,1)S(1)}, u32[]{:S(2)}, u32[]{:S(2)}) collective-permute-start(bf16[400,512]{1,0:T(8,128)(2,1)S(1)} %get-tuple-element.28), channel_id=1, source_target_pairs={{0,2},{1,3},{2,0},{3,1},{4,6},{5,7},{6,4},{7,5},{8,10},{9,11},{10,... | collective-permute-start | bytes 1228808 | tf_op jit(solution)/shard_map/gate_up/ppermute | solution.py:37
  120.9 28.0 %collective-permute-start.5 = (bf16[400,512]{1,0:T(8,128)(2,1)S(1)}, bf16[400,512]{1,0:T(8,128)(2,1)S(1)}, u32[]{:S(2)}, u32[]{:S(2)}) collective-permute-start(bf16[400,512]{1,0:T(8,128)(2,1)S(1)} %get-tuple-element.31), channel_id=1, source_target_pairs={{0,1},{1,0},{2,3},{3,2},{4,5},{5,4},{6,7},{7,6},{8,9},{9,8},{10,11... | collective-permute-start | bytes 1228808 | tf_op jit(solution)/shard_map/gate_up/ppermute | solution.py:37

commit v11 on v10

--- a/solution.py
+++ b/solution.py
@@ -129,12 +129,6 @@
             outgoing[half, expert] = part
 
 
-def arrange_kernel(arrived, weights, down, out):
-    rows = jnp.concatenate([arrived[index].astype(F32) for index in range(arrived.shape[0])], axis=0).astype(BF16)
-    for index in range(out.shape[0]):
-        out[index] = rows
-
-
 def share_of(place, scaled, near, far, offset, out):
     width = out.shape[1] // 2
     start = pl.multiple_of((place[2] ^ offset) * width, width)
@@ -143,7 +137,13 @@
         out[: scaled.shape[0], index * width : (index + 1) * width] = product.astype(BF16)
 
 
-def first_kernel(place, rows, gain, near, far, third, second, scaled_out, tail_out):
+def tail_of(norm, lines):
+    high = norm.astype(BF16).astype(F32)
+    line = lax.broadcasted_iota(jnp.int32, (lines, norm.shape[1]), 0)
+    return jnp.where(line == 0, high, jnp.where(line == 1, norm - high, 0.0)).astype(BF16)
+
+
+def first_kernel(place, rows, gain, near, far, down, third, scaled_out, tail_out):
     count, depth = rows.shape
     widened = rows[...].astype(F32)
     scaled = (widened * gain[...]).astype(BF16)
@@ -152,21 +152,26 @@
     high = square.astype(BF16)
     low = (square - high.astype(F32)).astype(BF16)
     ones = jnp.ones((TAIL, depth), BF16)
-    norm = dot_nt(ones, high) + dot_nt(ones, low)
-    high = norm.astype(BF16).astype(F32)
-    line = lax.broadcasted_iota(jnp.int32, norm.shape, 0)
-    tail = jnp.where(line == 0, high, jnp.where(line == 1, norm - high, 0.0)).astype(BF16)
-    tail = jnp.concatenate([tail, jnp.zeros((TAIL, third.shape[1] - count), BF16)], axis=1)
-    for out in (third, second, tail_out):
-        out[out.shape[0] - TAIL :, :] = tail
+    norm = (dot_nt(ones, high) + dot_nt(ones, low))[:1, :]
+    norm = jnp.concatenate([norm, jnp.zeros((1, third.shape[1] - count), F32)], axis=1)
+    tail = tail_of(norm, TAIL)
+    third[count:, :] = tail
+    tail_out[...] = tail
     share_of(place, scaled, near, far, 3, third)
-    share_of(place, scaled, near, far, 2, second)
-
-
-def last_kernel(place, scaled, tail, near, far, first, own):
-    for offset, out in ((1, first), (0, own)):
+
+
+def others_kernel(place, scaled, tail, near, far, second, first, own):
+    for offset, out in ((2, second), (1, first), (0, own)):
         out[scaled.shape[0] :, :] = tail[...]
         share_of(place, scaled[...], near, far, offset, out)
+
+
+def pair_kernel(own, arrived, first, pair, first_out):
+    count = own.shape[0] - TAIL
+    pair[:count, :] = (own[:count, :].astype(F32) + arrived[:count, :].astype(F32)).astype(BF16)
+    tail = own[count:, :].astype(F32) + arrived[count:, :].astype(F32)
+    pair[count:, :] = tail_of(tail[0:1, :] + tail[1:2, :], TAIL)
+    first_out[...] = first[...]
 
 
 def active_kernel(*refs):
@@ -256,29 +261,25 @@
 
     with jax.named_scope("dispatch"):
         arrived = swap(outgoing.reshape(halves * exp_count, CAP, width_part), ("yh", "exp"))
-        (copies,) = whole(
-            arrange_kernel,
-            [shape((lines, halves * exp_count * CAP, width_part), BF16)],
-            flops=0,
-            held=2,
-        )(arrived, far_weights, far_down)
-        arrived = swap(copies, "x")
+        arrived = spread(arrived.reshape(halves * exp_count * CAP, width_part), "x")
         count = lines * halves * exp_count * CAP
         rows = arrived.reshape(count, width_part)
 
     with jax.named_scope("gate_up"):
         part = shape((count + TAIL, 4 * piece), BF16)
-        third, second, scaled, tail = whole(
+        third, scaled, tail = whole(
             first_kernel,
-            [part, part, shape((count, width_part), BF16), shape((TAIL, 4 * piece), BF16)],
-            flops=4 * count * width_part * ff_part,
+            [part, shape((count, width_part), BF16), shape((TAIL, 4 * piece), BF16)],
+            flops=2 * count * width_part * ff_part,
             smem=1,
-        )(place, rows, norm_gain.reshape(1, width_part), near_weights, far_weights)
-        third, second = to_peer(third, 3), to_peer(second, 2)
-        first, own = whole(
-            last_kernel, [part, part], flops=4 * count * width_part * ff_part, smem=1
+            held=1,
+        )(place, rows, norm_gain.reshape(1, width_part), near_weights, far_weights, far_down)
+        third = to_peer(third, 1)
+        second, first, own = whole(
+            others_kernel, [part] * 3, flops=6 * count * width_part * ff_part, smem=1
         )(place, scaled, tail, near_weights, far_weights)
-        arrivals = [third, second, to_peer(first, 1), own]
+        pair, first = whole(pair_kernel, [part] * 2, flops=count * piece * 8)(second, third, first)
+        arrivals = [to_peer(pair, 2), to_peer(first, 1), own]
     with jax.named_scope("active"):
         (active,) = whole(active_kernel, [shape((2 * count, piece), BF16)], flops=count * piece * 40)(*arrivals)
         active = lax.all_gather(active, "hid", axis=0, tiled=False)

time: 202 us -> 204 us (level)
  waiting for transfers between devices: 57.8 us -> 46.3 us
  blocking collectives: 86.6 us -> 97.5 us
    all_to_all x4, blocking collectives: 67.5 us -> 80.1 us  [swap(): return lax.all_to_all(value, axes, split_axis=0, concat_axis=0, tiled=True)]
    ppermute x3, waiting for transfers between devices: 25.1 us -> 16.6 us  [to_peer(): lax.ppermute(value, 'hid', [(h, h ^ offset) for h in range(lax.axis_size(...]
    all_to_all x2, waiting for transfers between devices: 30.9 us -> 28 us  [swap(): return lax.all_to_all(value, axes, split_axis=0, concat_axis=0, tiled=True)]
    broadcast_in_dim x1 -> x3, local copies, waits for them, and re-layouts: 0.03 us -> 2.69 us  [spread(): jnp.broadcast_to(value[None], (lax.axis_size(axes),) + value.shape)]
    unnamed x22 -> x20, local copies, waits for them, and re-layouts: 4.9 us -> 4.2 us
  transfers between devices with their start and end apart: 8 -> 8, of which waited for: 5 -> 6; matrix products, arithmetic and copies ran while one was open for 0% -> 1% of each run, Pallas kernels for 3% -> 3%
where the time goes in v11:
time: 204 us; the launch traced here: 203 us
  blocking collectives  97.5 us (48%)
  waiting for transfers between devices  46.3 us (23%)
  starting transfers between devices  36.2 us (18%)
  Pallas kernels  13.6 us (7%)
  local copies, waits for them, and re-layouts  7.02 us (3%)
    all_to_all x4, blocking collectives, swap(): return lax.all_to_all(value, axes, split_axis=0, concat_axis=0, tiled=True)  80.1 us
    all_to_all x2, waiting for transfers between devices, swap(): return lax.all_to_all(value, axes, split_axis=0, concat_axis=0, tiled=True)  28 us
    all_to_all x2, starting transfers between devices, swap(): return lax.all_to_all(value, axes, split_axis=0, concat_axis=0, tiled=True)  19.3 us
    all_gather x1, blocking collectives, shards(): active = lax.all_gather(active, 'hid', axis=0, tiled=False)  17.3 us
    ppermute x3, waiting for transfers between devices, to_peer(): lax.ppermute(value, 'hid', [(h, h ^ offset) for h in range(lax.axis_size(...  16.6 us
    pallas_call x8, Pallas kernels, call(): pl.pallas_call(kernel, out_shape=out_shapes, in_specs=[pl.BlockSpec(memor...  13.6 us
    ppermute x3, starting transfers between devices, to_peer(): lax.ppermute(value, 'hid', [(h, h ^ offset) for h in range(lax.axis_size(...  10.6 us
    ppermute x3, starting transfers between devices, other_core(): return lax.ppermute(value, 'core', [(0, 1), (1, 0)])  6.24 us
  transfers between devices with their start and end apart: 8, of which 6 were waited for; matrix products, arithmetic and copies ran while one was open for 1% of the time, Pallas kernels for 3%

profile of v11, /device:TPU:2, one launch (start us, length us, event | category | flops | bytes accessed | tf_op | source)
XLA Modules:
  0.0 202.8 jit_solution(16615140233739604234)
XLA Ops:
  0.0 0.0 copy-start
  0.0 0.9 pad_maximum_fusion
  0.9 25.2 %all_to_all.30 = bf16[8,128,256]{2,1,0:T(8,128)(2,1)S(1)} all-to-all(bf16[8,128,256]{2,1,0:T(8,128)(2,1)S(1)} %broadcast_in_dim.6), channel_id=1, replica_groups=mesh['x'=4,'yh'=2,'core'=2,'exp'=8,'hid'=4] {'x','yh'}, dimensions={0} | all-to-all | bytes 1048576 | tf_op jit(solution)/shard_map/kv_gather/all_to_all | solution.py:25
  26.1 1.9 collective-permute-start
  28.0 0.1 pad_add_fusion.place
  28.1 0.0 copy-start.1
  28.1 1.8 collective-permute-done.far
  29.9 0.0 copy-done
  29.9 0.0 copy-start.5
  29.9 0.8 copy-done.5
  30.6 0.0 copy-start.8
  30.6 0.0 copy-start.9
  30.6 1.6 attention.1
  32.3 0.0 copy-start.4
  32.3 1.0 copy-done.4
  33.3 0.0 copy-start.6
  33.3 13.7 %all-to-all-start.1 = ((bf16[32,16,1024]{2,1,0:T(8,128)(2,1)}), bf16[32,16,1024]{2,1,0:T(8,128)(2,1)}, u32[]{:S(2)}, u32[]{:S(2)}) async-start(bf16[32,16,1024]{2,1,0:T(8,128)(2,1)} %bitcast.24), calls=%async_computation.1 | async-start | bytes 2097152 | tf_op jit(solution)/shard_map/projection/all_to_all | solution.py:25
  47.0 0.0 copy-done.1
  47.0 0.0 copy-done.8
  47.0 0.0 copy-done.9
  47.0 0.0 copy-start.2
  47.1 1.2 copy-done.2
  48.3 0.0 copy-start.3
  48.3 1.2 copy-done.3
  49.5 1.9 prepare.1
  51.4 1.9 collective-permute-start.1
  53.4 2.4 %collective-permute-start.2 = (bf16[512,1024]{1,0:T(8,128)(2,1)}, bf16[512,1024]{1,0:T(8,128)(2,1)S(1)}, u32[]{:S(2)}, u32[]{:S(2)}) collective-permute-start(bf16[512,1024]{1,0:T(8,128)(2,1)} %get-tuple-element.28.near), channel_id=1, source_target_pairs={{0,32},{32,0},{1,33},{33,1},{2,34},{34,2},{3,35},{35,3},{4,36},{36... | collective-permute-start | bytes 3145736 | tf_op jit(solution)/shard_map/prepare/ppermute | solution.py:33
  55.8 18.9 %all-to-all-done.1.arrived = bf16[32,16,1024]{2,1,0:T(8,128)(2,1)} async-done(((bf16[32,16,1024]{2,1,0:T(8,128)(2,1)}), bf16[32,16,1024]{2,1,0:T(8,128)(2,1)}, u32[]{:S(2)}, u32[]{:S(2)}) %all-to-all-start.1) | async-done | bytes 1048608 | tf_op jit(solution)/shard_map/projection/all_to_all | solution.py:25
  74.7 0.0 copy-done.6
  74.7 0.0 copy-start.7
  74.7 1.5 projection.1
  76.2 17.9 %all_to_all.31 = bf16[16,6,1024]{2,1,0:T(8,128)(2,1)S(1)} all-to-all(bf16[16,6,1024]{2,1,0:T(8,128)(2,1)S(1)} %bitcast.25), channel_id=1, replica_groups=mesh['x'=4,'yh'=2,'core'=2,'exp'=8,'hid'=4] {'yh','exp'}, dimensions={0} | all-to-all | bytes 393216 | tf_op jit(solution)/shard_map/dispatch/all_to_all | solution.py:25
  94.1 0.7 broadcast_in_dim.14
  94.9 1.9 broadcast_in_dim.15
  96.8 5.6 %all-to-all-start.3 = ((bf16[4,96,1024]{2,1,0:T(8,128)(2,1)}), bf16[4,96,1024]{2,1,0:T(8,128)(2,1)}, u32[]{:S(2)}, u32[]{:S(2)}) async-start(bf16[4,96,1024]{2,1,0:T(8,128)(2,1)} %broadcast_in_dim.15), calls=%async_computation.3 | async-start | bytes 1572864 | tf_op jit(solution)/shard_map/dispatch/all_to_all | solution.py:25
  102.4 0.0 collective-permute-done.2.down.far
  102.4 0.0 collective-permute-done.1.far
  102.4 9.1 %all-to-all-done.3 = bf16[4,96,1024]{2,1,0:T(8,128)(2,1)} async-done(((bf16[4,96,1024]{2,1,0:T(8,128)(2,1)}), bf16[4,96,1024]{2,1,0:T(8,128)(2,1)}, u32[]{:S(2)}, u32[]{:S(2)}) %all-to-all-start.3) | async-done | bytes 786464 | tf_op jit(solution)/shard_map/dispatch/all_to_all | solution.py:25
  111.5 0.0 copy-done.7
  111.5 2.9 %gate_up.3 = (bf16[400,512]{1,0:T(8,128)(2,1)S(1)}, bf16[384,1024]{1,0:T(8,128)(2,1)S(1)}, bf16[16,512]{1,0:T(8,128)(2,1)S(1)}) custom-call(s32[3]{0:T(128)S(1)} %pad_add_fusion.place, bf16[384,1024]{1,0:T(8,128)(2,1)} %bitcast.11.rows, f32[1,1024]{1,0:T(1,128)S(1)} %bitcast.26, bf16[1024,1024]{1,0:T(8,128)(2,1)S(1)} %get-tuple-element.27.near, ...), custom_call_target="tpu_custom_call" | custom-call | flops 402653184 | bytes 7245836 | tf_op jit(solution)/shard_map/gate_up/pallas_call | solution.py:45
  114.4 3.5 %collective-permute-start.3 = (bf16[400,512]{1,0:T(8,128)(2,1)S(1)}, bf16[400,512]{1,0:T(8,128)(2,1)S(1)}, u32[]{:S(2)}, u32[]{:S(2)}) collective-permute-start(bf16[400,512]{1,0:T(8,128)(2,1)S(1)} %get-tuple-element.32), channel_id=1, source_target_pairs={{0,1},{1,0},{2,3},{3,2},{4,5},{5,4},{6,7},{7,6},{8,9},{9,8},{10,11... | collective-permute-start | bytes 1228808 | tf_op jit(solution)/shard_map/gate_up/ppermute | solution.py:37
  117.8 3.0 %gate_up.4 = (bf16[400,512]{1,0:T(8,128)(2,1)S(1)}, bf16[400,512]{1,0:T(8,128)(2,1)S(1)}, bf16[400,512]{1,0:T(8,128)(2,1)S(1)}) custom-call(s32[3]{0:T(128)S(1)} %pad_add_fusion.place, bf16[384,1024]{1,0:T(8,128)(2,1)S(1)} %get-tuple-element.29.scaled, bf16[16,512]{1,0:T(8,128)(2,1)S(1)} %get-tuple-element.30.tail, ...), custom_call_target="tpu_custom_call" | custom-call | flops 1207959552 | bytes 6225932 | tf_op jit(solution)/shard_map/gate_up/pallas_call | solution.py:45
  120.9 3.3 %collective-permute-done.3.arrived = bf16[400,512]{1,0:T(8,128)(2,1)S(1)} collective-permute-done((bf16[400,512]{1,0:T(8,128)(2,1)S(1)}, bf16[400,512]{1,0:T(8,128)(2,1)S(1)}, u32[]{:S(2)}, u32[]{:S(2)}) %collective-permute-start.3) | collective-permute-done | bytes 409632 | tf_op jit(solution)/shard_map/gate_up/ppermute | solution.py:37
  124.2 0.1 gate_up.5
  124.3 3.7 %collective-permute-start.4 = (bf16[400,512]{1,0:T(8,128)(2,1)S(1)}, bf16[400,512]{1,0:T(8,128)(2,1)S(1)}, u32[]{:S(2)}, u32[]{:S(2)}) collective-permute-start(bf16[400,512]{1,0:T(8,128)(2,1)S(1)} %get-tuple-element.34), channel_id=1, source_target_pairs={{0,2},{1,3},{2,0},{3,1},{4,6},{5,7},{6,4},{7,5},{8,10},{9,11},{10,... | collective-permute-start | bytes 1228808 | tf_op jit(solution)/shard_map/gate_up/ppermute | solution.py:37
  128.1 3.4 %collective-permute-start.5 = (bf16[400,512]{1,0:T(8,128)(2,1)S(1)}, bf16[400,512]{1,0:T(8,128)(2,1)S(1)}, u32[]{:S(2)}, u32[]{:S(2)}) collective-permute-start(bf16[400,512]{1,0:T(8,128)(2,1)S(1)} %get-tuple-element.35), channel_id=1, source_target_pairs={{0,1},{1,0},{2,3},{3,2},{4,5},{5,4},{6,7},{7,6},{8,9},{9,8},{10,11... | collective-permute-start | bytes 1228808 | tf_op jit(solution)/shard_map/gate_up/ppermute | solution.py:37
  131.5 11.3 %collective-permute-done.4.refs_0_ = bf16[400,512]{1,0:T(8,128)(2,1)S(1)} collective-permute-done((bf16[400,512]{1,0:T(8,128)(2,1)S(1)}, bf16[400,512]{1,0:T(8,128)(2,1)S(1)}, u32[]{:S(2)}, u32[]{:S(2)}) %collective-permute-start.4) | collective-permute-done | bytes 409632 | tf_op jit(solution)/shard_map/gate_up/ppermute | solution.py:37
  142.8 1.9 collective-permute-done.5.refs_1_
  144.7 0.3 active.1
  145.0 17.3 %all-gather = bf16[3072,128]{1,0:T(8,128)(2,1)S(1)} all-gather(bf16[768,128]{1,0:T(8,128)(2,1)S(1)} %active.1), channel_id=2, replica_groups=mesh['x'=4,'yh'=2,'core'=2,'exp'=8,'hid'=4] {'hid'}, dimensions={0}, use_global_device_ids=true | all-gather | bytes 983040 | tf_op jit(solution)/shard_map/active/all_gather | solution.py:285
  162.3 2.2 %down.1 = bf16[384,1024]{1,0:T(8,128)(2,1)S(1)} custom-call(bf16[4,768,128]{2,1,0:T(8,128)(2,1)S(1)} %bitcast.18, bf16[512,1024]{1,0:T(8,128)(2,1)} %get-tuple-element.28.near, bf16[512,1024]{1,0:T(8,128)(2,1)S(1)} %collective-permute-done.2.down.far), custom_call_target="tpu_custom_call" | custom-call | flops 805306368 | bytes 3670016 | tf_op jit(solution)/shard_map/down/pallas_call | solution.py:45
  164.5 11.9 %all_to_all.32 = bf16[4,96,1024]{2,1,0:T(8,128)(2,1)S(1)} all-to-all(bf16[4,96,1024]{2,1,0:T(8,128)(2,1)S(1)} %bitcast.17), channel_id=1, replica_groups=mesh['x'=4,'yh'=2,'core'=2,'exp'=8,'hid'=4] {'x'}, dimensions={0} | all-to-all | bytes 1572864 | tf_op jit(solution)/shard_map/down/all_to_all | solution.py:25
  176.4 0.1 reduce_sum.21
  176.6 0.1 reshape.33
  176.6 25.2 %all_to_all.33 = bf16[16,6,1024]{2,1,0:T(8,128)(2,1)S(1)} all-to-all(bf16[16,6,1024]{2,1,0:T(8,128)(2,1)S(1)} %reshape.33), channel_id=1, replica_groups=mesh['x'=4,'yh'=2,'core'=2,'exp'=8,'hid'=4] {'yh','exp'}, dimensions={0} | all-to-all | bytes 393216 | tf_op jit(solution)/shard_map/down/all_to_all | solution.py:25
  201.8 0.1 reshape.34
  201.9 0.9 fusion
  (2 shorter events, 0.1 us)
Async XLA Ops:
  0.0 29.9 %copy-start = (bf16[128,4096]{1,0:T(8,128)(2,1)S(1)}, bf16[128,4096]{1,0:T(8,128)(2,1)}, u32[]{:S(2)}) copy-start(bf16[128,4096]{1,0:T(8,128)(2,1)} %weight.1) | copy-start | bytes 3145732
  26.1 3.8 %collective-permute-start = (bf16[1024,256]{1,0:T(8,128)(2,1)S(1)}, bf16[1024,256]{1,0:T(8,128)(2,1)S(1)}, u32[]{:S(2)}, u32[]{:S(2)}) collective-permute-start(bf16[1024,256]{1,0:T(8,128)(2,1)S(1)} %bitcast.19), channel_id=1, source_target_pairs={{0,32},{32,0},{1,33},{33,1},{2,34},{34,2},{3,35},{35,3},{4,36},{36... | collective-permute-start | bytes 1572872 | tf_op jit(solution)/shard_map/kv_gather/ppermute | solution.py:33
  28.1 18.9 %copy-start.1 = (bf16[1,1024,512]{2,1,0:T(8,128)(2,1)S(1)}, bf16[1,1024,512]{2,1,0:T(8,128)(2,1)}, u32[]{:S(2)}) copy-start(bf16[1,1024,512]{2,1,0:T(8,128)(2,1)} %param.17) | copy-start | bytes 3145732
  29.9 0.8 copy-start.5
  30.6 16.4 %copy-start.8 = (s32[16,2]{0,1:T(2,128)S(1)}, s32[16,2]{0,1:T(2,128)}, u32[]{:S(2)}) copy-start(s32[16,2]{0,1:T(2,128)} %param.20) | copy-start | bytes 388
  30.6 16.4 %copy-start.9 = (f32[16,2]{0,1:T(2,128)S(1)}, f32[16,2]{0,1:T(2,128)}, u32[]{:S(2)}) copy-start(f32[16,2]{0,1:T(2,128)} %param.21) | copy-start | bytes 388
  32.3 1.0 copy-start.4
  33.3 41.4 %copy-start.6 = (bf16[16,1024]{1,0:T(8,128)(2,1)S(1)}, bf16[16,1024]{1,0:T(8,128)(2,1)}, u32[]{:S(2)}) copy-start(bf16[16,1024]{1,0:T(8,128)(2,1)} %residual.1) | copy-start | bytes 98308
  33.3 41.4 %all-to-all-start.1 = ((bf16[32,16,1024]{2,1,0:T(8,128)(2,1)}), bf16[32,16,1024]{2,1,0:T(8,128)(2,1)}, u32[]{:S(2)}, u32[]{:S(2)}) async-start(bf16[32,16,1024]{2,1,0:T(8,128)(2,1)} %bitcast.24), calls=%async_computation.1 | async-start | bytes 2097152 | tf_op jit(solution)/shard_map/projection/all_to_all | solution.py:25
  47.0 1.2 copy-start.2
  48.3 1.2 copy-start.3
  51.4 51.0 %collective-permute-start.1 = (bf16[1024,1024]{1,0:T(8,128)(2,1)S(1)}, bf16[1024,1024]{1,0:T(8,128)(2,1)}, u32[]{:S(2)}, u32[]{:S(2)}) collective-permute-start(bf16[1024,1024]{1,0:T(8,128)(2,1)S(1)} %get-tuple-element.27.near), channel_id=1, source_target_pairs={{0,32},{32,0},{1,33},{33,1},{2,34},{34,2},{3,35},{35,3},{4,36},{36... | collective-permute-start | bytes 6291464 | tf_op jit(solution)/shard_map/prepare/ppermute | solution.py:33
  53.4 49.0 %collective-permute-start.2 = (bf16[512,1024]{1,0:T(8,128)(2,1)}, bf16[512,1024]{1,0:T(8,128)(2,1)S(1)}, u32[]{:S(2)}, u32[]{:S(2)}) collective-permute-start(bf16[512,1024]{1,0:T(8,128)(2,1)} %get-tuple-element.28.near), channel_id=1, source_target_pairs={{0,32},{32,0},{1,33},{33,1},{2,34},{34,2},{3,35},{35,3},{4,36},{36... | collective-permute-start | bytes 3145736 | tf_op jit(solution)/shard_map/prepare/ppermute | solution.py:33
  74.7 36.8 %copy-start.7 = (f32[1024]{0:T(1024)S(1)}, f32[1024]{0:T(1024)}, u32[]{:S(2)}) copy-start(f32[1024]{0:T(1024)} %param.16) | copy-start | bytes 12292
  96.8 14.7 %all-to-all-start.3 = ((bf16[4,96,1024]{2,1,0:T(8,128)(2,1)}), bf16[4,96,1024]{2,1,0:T(8,128)(2,1)}, u32[]{:S(2)}, u32[]{:S(2)}) async-start(bf16[4,96,1024]{2,1,0:T(8,128)(2,1)} %broadcast_in_dim.15), calls=%async_computation.3 | async-start | bytes 1572864 | tf_op jit(solution)/shard_map/dispatch/all_to_all | solution.py:25
  114.4 9.8 %collective-permute-start.3 = (bf16[400,512]{1,0:T(8,128)(2,1)S(1)}, bf16[400,512]{1,0:T(8,128)(2,1)S(1)}, u32[]{:S(2)}, u32[]{:S(2)}) collective-permute-start(bf16[400,512]{1,0:T(8,128)(2,1)S(1)} %get-tuple-element.32), channel_id=1, source_target_pairs={{0,1},{1,0},{2,3},{3,2},{4,5},{5,4},{6,7},{7,6},{8,9},{9,8},{10,11... | collective-permute-start | bytes 1228808 | tf_op jit(solution)/shard_map/gate_up/ppermute | solution.py:37
  124.3 18.4 %collective-permute-start.4 = (bf16[400,512]{1,0:T(8,128)(2,1)S(1)}, bf16[400,512]{1,0:T(8,128)(2,1)S(1)}, u32[]{:S(2)}, u32[]{:S(2)}) collective-permute-start(bf16[400,512]{1,0:T(8,128)(2,1)S(1)} %get-tuple-element.34), channel_id=1, source_target_pairs={{0,2},{1,3},{2,0},{3,1},{4,6},{5,7},{6,4},{7,5},{8,10},{9,11},{10,... | collective-permute-start | bytes 1228808 | tf_op jit(solution)/shard_map/gate_up/ppermute | solution.py:37
  128.1 16.6 %collective-permute-start.5 = (bf16[400,512]{1,0:T(8,128)(2,1)S(1)}, bf16[400,512]{1,0:T(8,128)(2,1)S(1)}, u32[]{:S(2)}, u32[]{:S(2)}) collective-permute-start(bf16[400,512]{1,0:T(8,128)(2,1)S(1)} %get-tuple-element.35), channel_id=1, source_target_pairs={{0,1},{1,0},{2,3},{3,2},{4,5},{5,4},{6,7},{7,6},{8,9},{9,8},{10,11... | collective-permute-start | bytes 1228808 | tf_op jit(solution)/shard_map/gate_up/ppermute | solution.py:37

commit v12 on v11

--- a/solution.py
+++ b/solution.py
@@ -143,8 +143,16 @@
     return jnp.where(line == 0, high, jnp.where(line == 1, norm - high, 0.0)).astype(BF16)
 
 
-def first_kernel(place, rows, gain, near, far, down, third, scaled_out, tail_out):
+def first_kernel(place, rows, gain, near, far, third, scaled_out, tail_out, taken, sems):
     count, depth = rows.shape
+    width = third.shape[1] // 2
+    start = pl.multiple_of((place[2] ^ 3) * width, width)
+    copies = [
+        pltpu.make_async_copy(source.at[:, pl.ds(start, width)], taken.at[index], sems.at[index])
+        for index, source in enumerate((near, far))
+    ]
+    for copy in copies:
+        copy.start()
     widened = rows[...].astype(F32)
     scaled = (widened * gain[...]).astype(BF16)
     scaled_out[...] = scaled
@@ -157,7 +165,10 @@
     tail = tail_of(norm, TAIL)
     third[count:, :] = tail
     tail_out[...] = tail
-    share_of(place, scaled, near, far, 3, third)
+    for index, copy in enumerate(copies):
+        copy.wait()
+        product = jnp.dot(scaled, taken[index], preferred_element_type=F32)
+        third[:count, index * width : (index + 1) * width] = product.astype(BF16)
 
 
 def others_kernel(place, scaled, tail, near, far, second, first, own):
@@ -272,8 +283,9 @@
             [part, shape((count, width_part), BF16), shape((TAIL, 4 * piece), BF16)],
             flops=2 * count * width_part * ff_part,
             smem=1,
-            held=1,
-        )(place, rows, norm_gain.reshape(1, width_part), near_weights, far_weights, far_down)
+            held=2,
+            scratch=[pltpu.VMEM((2, width_part, 2 * piece), BF16), pltpu.SemaphoreType.DMA((2,))],
+        )(place, rows, norm_gain.reshape(1, width_part), near_weights, far_weights)
         third = to_peer(third, 1)
         second, first, own = whole(
             others_kernel, [part] * 3, flops=6 * count * width_part * ff_part, smem=1

time: 204 us -> 198 us (0.971)
  Pallas kernels: 13.6 us -> 9.65 us
  blocking collectives: 97.5 us -> 93.8 us
  waiting for transfers between devices: 46.3 us -> 49 us
    pallas_call x8, Pallas kernels: 13.6 us -> 9.65 us  [call(): pl.pallas_call(kernel, out_shape=out_shapes, in_specs=[pl.BlockSpec(memor...]
    all_to_all x4, blocking collectives: 80.1 us -> 76.3 us  [swap(): return lax.all_to_all(value, axes, split_axis=0, concat_axis=0, tiled=True)]
    unnamed x20 -> x24, local copies, waits for them, and re-layouts: 4.2 us -> 6.39 us
  transfers between devices with their start and end apart: 8 -> 8, of which waited for: 6 -> 6; matrix products, arithmetic and copies ran while one was open for 1% -> 1% of each run, Pallas kernels for 3% -> 2%
where the time goes in v12:
time: 198 us; the launch traced here: 197 us
  blocking collectives  93.8 us (47%)
  waiting for transfers between devices  49 us (25%)
  starting transfers between devices  34.9 us (18%)
  Pallas kernels  9.65 us (5%)
  local copies, waits for them, and re-layouts  7.62 us (4%)
    all_to_all x4, blocking collectives, swap(): return lax.all_to_all(value, axes, split_axis=0, concat_axis=0, tiled=True)  76.3 us
    all_to_all x2, waiting for transfers between devices, swap(): return lax.all_to_all(value, axes, split_axis=0, concat_axis=0, tiled=True)  29.1 us
    all_to_all x2, starting transfers between devices, swap(): return lax.all_to_all(value, axes, split_axis=0, concat_axis=0, tiled=True)  18.6 us
    ppermute x3, waiting for transfers between devices, to_peer(): lax.ppermute(value, 'hid', [(h, h ^ offset) for h in range(lax.axis_size(...  18.1 us
    all_gather x1, blocking collectives, shards(): active = lax.all_gather(active, 'hid', axis=0, tiled=False)  17.6 us
    ppermute x3, starting transfers between devices, to_peer(): lax.ppermute(value, 'hid', [(h, h ^ offset) for h in range(lax.axis_size(...  10.7 us
    pallas_call x8, Pallas kernels, call(): pl.pallas_call(kernel, out_shape=out_shapes, in_specs=[pl.BlockSpec(memor...  9.65 us
    unnamed x24, local copies, waits for them, and re-layouts  6.39 us
  transfers between devices with their start and end apart: 8, of which 6 were waited for; matrix products, arithmetic and copies ran while one was open for 1% of the time, Pallas kernels for 2%

profile of v12, /device:TPU:2, one launch (start us, length us, event | category | flops | bytes accessed | tf_op | source)
XLA Modules:
  0.0 197.2 jit_solution(9730605474431676292)
XLA Ops:
  0.0 0.0 copy-start.2
  0.0 0.9 pad_maximum_fusion
  0.9 25.2 %all_to_all.30 = bf16[8,128,256]{2,1,0:T(8,128)(2,1)S(1)} all-to-all(bf16[8,128,256]{2,1,0:T(8,128)(2,1)S(1)} %broadcast_in_dim.6), channel_id=1, replica_groups=mesh['x'=4,'yh'=2,'core'=2,'exp'=8,'hid'=4] {'x','yh'}, dimensions={0} | all-to-all | bytes 1048576 | tf_op jit(solution)/shard_map/kv_gather/all_to_all | solution.py:25
  26.1 1.9 collective-permute-start
  28.0 0.1 pad_add_fusion.place
  28.1 1.8 collective-permute-done.far
  29.9 0.0 copy-done.2
  29.9 0.0 copy-start.7
  29.9 0.8 copy-done.7
  30.6 0.0 copy-start.10
  30.6 0.0 copy-start.11
  30.6 1.6 attention.1
  32.3 0.0 copy-start.6
  32.3 1.0 copy-done.6
  33.3 0.0 copy-start.8
  33.3 13.6 %all-to-all-start.1 = ((bf16[32,16,1024]{2,1,0:T(8,128)(2,1)}), bf16[32,16,1024]{2,1,0:T(8,128)(2,1)S(1)}, u32[]{:S(2)}, u32[]{:S(2)}) async-start(bf16[32,16,1024]{2,1,0:T(8,128)(2,1)} %bitcast.25), calls=%async_computation.1 | async-start | bytes 2097152 | tf_op jit(solution)/shard_map/projection/all_to_all | solution.py:25
  46.9 0.0 copy-done.10
  46.9 0.0 copy-done.11
  46.9 0.0 copy-start.3
  46.9 1.2 copy-done.3
  48.2 0.0 copy-start.4
  48.2 1.2 copy-done.4
  49.4 0.0 copy-start.5
  49.4 1.2 copy-done.5
  50.6 0.9 prepare.1
  51.5 0.0 copy-start
  51.6 1.0 copy-done
  52.5 1.9 collective-permute-start.1
  54.4 20.1 %all-to-all-done.1.arrived = bf16[32,16,1024]{2,1,0:T(8,128)(2,1)S(1)} async-done(((bf16[32,16,1024]{2,1,0:T(8,128)(2,1)}), bf16[32,16,1024]{2,1,0:T(8,128)(2,1)S(1)}, u32[]{:S(2)}, u32[]{:S(2)}) %all-to-all-start.1) | async-done | bytes 1048608 | tf_op jit(solution)/shard_map/projection/all_to_all | solution.py:25
  74.6 0.0 copy-done.8
  74.6 0.0 copy-start.9
  74.6 0.3 projection.1
  74.9 17.9 %all_to_all.31 = bf16[16,6,1024]{2,1,0:T(8,128)(2,1)S(1)} all-to-all(bf16[16,6,1024]{2,1,0:T(8,128)(2,1)S(1)} %bitcast.26), channel_id=1, replica_groups=mesh['x'=4,'yh'=2,'core'=2,'exp'=8,'hid'=4] {'yh','exp'}, dimensions={0} | all-to-all | bytes 393216 | tf_op jit(solution)/shard_map/dispatch/all_to_all | solution.py:25
  92.8 0.1 broadcast_in_dim.14
  92.9 1.0 broadcast_in_dim.15
  93.9 4.9 %all-to-all-start.3 = ((bf16[4,96,1024]{2,1,0:T(8,128)(2,1)}), bf16[4,96,1024]{2,1,0:T(8,128)(2,1)S(1)}, u32[]{:S(2)}, u32[]{:S(2)}) async-start(bf16[4,96,1024]{2,1,0:T(8,128)(2,1)} %broadcast_in_dim.15), calls=%async_computation.3 | async-start | bytes 1572864 | tf_op jit(solution)/shard_map/dispatch/all_to_all | solution.py:25
  98.8 0.0 collective-permute-done.1.far
  98.8 9.0 %all-to-all-done.3 = bf16[4,96,1024]{2,1,0:T(8,128)(2,1)S(1)} async-done(((bf16[4,96,1024]{2,1,0:T(8,128)(2,1)}), bf16[4,96,1024]{2,1,0:T(8,128)(2,1)S(1)}, u32[]{:S(2)}, u32[]{:S(2)}) %all-to-all-start.3) | async-done | bytes 786464 | tf_op jit(solution)/shard_map/dispatch/all_to_all | solution.py:25
  107.7 0.0 copy-done.9
  107.7 0.0 copy-start.1
  107.7 2.4 %gate_up.3 = (bf16[400,512]{1,0:T(8,128)(2,1)S(1)}, bf16[384,1024]{1,0:T(8,128)(2,1)S(1)}, bf16[16,512]{1,0:T(8,128)(2,1)S(1)}) custom-call(s32[3]{0:T(128)S(1)} %pad_add_fusion.place, bf16[384,1024]{1,0:T(8,128)(2,1)S(1)} %bitcast.19, f32[1,1024]{1,0:T(1,128)S(1)} %bitcast.27, bf16[1024,1024]{1,0:T(8,128)(2,1)S(1)} %get-tuple-element.27.near, ...), custom_call_target="tpu_custom_call" | custom-call | flops 402653184 | bytes 6197260 | tf_op jit(solution)/shard_map/gate_up/pallas_call | solution.py:45
  110.1 3.5 %collective-permute-start.2 = (bf16[400,512]{1,0:T(8,128)(2,1)S(1)}, bf16[400,512]{1,0:T(8,128)(2,1)S(1)}, u32[]{:S(2)}, u32[]{:S(2)}) collective-permute-start(bf16[400,512]{1,0:T(8,128)(2,1)S(1)} %get-tuple-element.31), channel_id=1, source_target_pairs={{0,1},{1,0},{2,3},{3,2},{4,5},{5,4},{6,7},{7,6},{8,9},{9,8},{10,11... | collective-permute-start | bytes 1228808 | tf_op jit(solution)/shard_map/gate_up/ppermute | solution.py:37
  113.6 0.0 copy-done.1
  113.6 1.9 collective-permute-start.5
  115.6 3.0 %gate_up.4 = (bf16[400,512]{1,0:T(8,128)(2,1)S(1)}, bf16[400,512]{1,0:T(8,128)(2,1)S(1)}, bf16[400,512]{1,0:T(8,128)(2,1)S(1)}) custom-call(s32[3]{0:T(128)S(1)} %pad_add_fusion.place, bf16[384,1024]{1,0:T(8,128)(2,1)S(1)} %get-tuple-element.28.scaled, bf16[16,512]{1,0:T(8,128)(2,1)S(1)} %get-tuple-element.29.tail, ...), custom_call_target="tpu_custom_call" | custom-call | flops 1207959552 | bytes 6225932 | tf_op jit(solution)/shard_map/gate_up/pallas_call | solution.py:45
  118.6 1.4 collective-permute-done.2.arrived
  120.0 0.1 gate_up.5
  120.1 3.7 %collective-permute-start.3 = (bf16[400,512]{1,0:T(8,128)(2,1)S(1)}, bf16[400,512]{1,0:T(8,128)(2,1)S(1)}, u32[]{:S(2)}, u32[]{:S(2)}) collective-permute-start(bf16[400,512]{1,0:T(8,128)(2,1)S(1)} %get-tuple-element.33), channel_id=1, source_target_pairs={{0,2},{1,3},{2,0},{3,1},{4,6},{5,7},{6,4},{7,5},{8,10},{9,11},{10,... | collective-permute-start | bytes 1228808 | tf_op jit(solution)/shard_map/gate_up/ppermute | solution.py:37
  123.9 3.4 %collective-permute-start.4 = (bf16[400,512]{1,0:T(8,128)(2,1)S(1)}, bf16[400,512]{1,0:T(8,128)(2,1)S(1)}, u32[]{:S(2)}, u32[]{:S(2)}) collective-permute-start(bf16[400,512]{1,0:T(8,128)(2,1)S(1)} %get-tuple-element.34), channel_id=1, source_target_pairs={{0,1},{1,0},{2,3},{3,2},{4,5},{5,4},{6,7},{7,6},{8,9},{9,8},{10,11... | collective-permute-start | bytes 1228808 | tf_op jit(solution)/shard_map/gate_up/ppermute | solution.py:37
  127.3 14.9 %collective-permute-done.3.refs_0_ = bf16[400,512]{1,0:T(8,128)(2,1)S(1)} collective-permute-done((bf16[400,512]{1,0:T(8,128)(2,1)S(1)}, bf16[400,512]{1,0:T(8,128)(2,1)S(1)}, u32[]{:S(2)}, u32[]{:S(2)}) %collective-permute-start.3) | collective-permute-done | bytes 409632 | tf_op jit(solution)/shard_map/gate_up/ppermute | solution.py:37
  142.2 1.9 collective-permute-done.4.refs_1_
  144.0 0.3 active.1
  144.3 17.6 %all-gather = bf16[3072,128]{1,0:T(8,128)(2,1)S(1)} all-gather(bf16[768,128]{1,0:T(8,128)(2,1)S(1)} %active.1), channel_id=2, replica_groups=mesh['x'=4,'yh'=2,'core'=2,'exp'=8,'hid'=4] {'hid'}, dimensions={0}, use_global_device_ids=true | all-gather | bytes 983040 | tf_op jit(solution)/shard_map/active/all_gather | solution.py:297
  161.9 0.0 collective-permute-done.5.far
  161.9 1.0 down.1
  162.9 11.9 %all_to_all.32 = bf16[4,96,1024]{2,1,0:T(8,128)(2,1)S(1)} all-to-all(bf16[4,96,1024]{2,1,0:T(8,128)(2,1)S(1)} %bitcast.17), channel_id=1, replica_groups=mesh['x'=4,'yh'=2,'core'=2,'exp'=8,'hid'=4] {'x'}, dimensions={0} | all-to-all | bytes 1572864 | tf_op jit(solution)/shard_map/down/all_to_all | solution.py:25
  174.8 0.1 reduce_sum.21
  174.9 0.1 reshape.33
  175.0 21.3 %all_to_all.33 = bf16[16,6,1024]{2,1,0:T(8,128)(2,1)S(1)} all-to-all(bf16[16,6,1024]{2,1,0:T(8,128)(2,1)S(1)} %reshape.33), channel_id=1, replica_groups=mesh['x'=4,'yh'=2,'core'=2,'exp'=8,'hid'=4] {'yh','exp'}, dimensions={0} | all-to-all | bytes 393216 | tf_op jit(solution)/shard_map/down/all_to_all | solution.py:25
  196.3 0.1 reshape.34
  196.3 0.9 fusion
  (2 shorter events, 0.1 us)
Async XLA Ops:
  0.0 29.9 %copy-start.2 = (bf16[128,4096]{1,0:T(8,128)(2,1)S(1)}, bf16[128,4096]{1,0:T(8,128)(2,1)}, u32[]{:S(2)}) copy-start(bf16[128,4096]{1,0:T(8,128)(2,1)} %weight.1) | copy-start | bytes 3145732
  26.1 3.8 %collective-permute-start = (bf16[1024,256]{1,0:T(8,128)(2,1)S(1)}, bf16[1024,256]{1,0:T(8,128)(2,1)S(1)}, u32[]{:S(2)}, u32[]{:S(2)}) collective-permute-start(bf16[1024,256]{1,0:T(8,128)(2,1)S(1)} %bitcast.20), channel_id=1, source_target_pairs={{0,32},{32,0},{1,33},{33,1},{2,34},{34,2},{3,35},{35,3},{4,36},{36... | collective-permute-start | bytes 1572872 | tf_op jit(solution)/shard_map/kv_gather/ppermute | solution.py:33
  29.9 0.8 copy-start.7
  30.6 16.3 %copy-start.10 = (s32[16,2]{0,1:T(2,128)S(1)}, s32[16,2]{0,1:T(2,128)}, u32[]{:S(2)}) copy-start(s32[16,2]{0,1:T(2,128)} %param.20) | copy-start | bytes 388
  30.6 16.3 %copy-start.11 = (f32[16,2]{0,1:T(2,128)S(1)}, f32[16,2]{0,1:T(2,128)}, u32[]{:S(2)}) copy-start(f32[16,2]{0,1:T(2,128)} %param.21) | copy-start | bytes 388
  32.3 1.0 copy-start.6
  33.3 41.3 %copy-start.8 = (bf16[16,1024]{1,0:T(8,128)(2,1)S(1)}, bf16[16,1024]{1,0:T(8,128)(2,1)}, u32[]{:S(2)}) copy-start(bf16[16,1024]{1,0:T(8,128)(2,1)} %residual.1) | copy-start | bytes 98308
  33.3 41.3 %all-to-all-start.1 = ((bf16[32,16,1024]{2,1,0:T(8,128)(2,1)}), bf16[32,16,1024]{2,1,0:T(8,128)(2,1)S(1)}, u32[]{:S(2)}, u32[]{:S(2)}) async-start(bf16[32,16,1024]{2,1,0:T(8,128)(2,1)} %bitcast.25), calls=%async_computation.1 | async-start | bytes 2097152 | tf_op jit(solution)/shard_map/projection/all_to_all | solution.py:25
  46.9 1.2 copy-start.3
  48.2 1.2 copy-start.4
  49.4 1.2 copy-start.5
  51.5 1.0 copy-start
  52.5 46.3 %collective-permute-start.1 = (bf16[1024,1024]{1,0:T(8,128)(2,1)S(1)}, bf16[1024,1024]{1,0:T(8,128)(2,1)}, u32[]{:S(2)}, u32[]{:S(2)}) collective-permute-start(bf16[1024,1024]{1,0:T(8,128)(2,1)S(1)} %get-tuple-element.27.near), channel_id=1, source_target_pairs={{0,32},{32,0},{1,33},{33,1},{2,34},{34,2},{3,35},{35,3},{4,36},{36... | collective-permute-start | bytes 6291464 | tf_op jit(solution)/shard_map/prepare/ppermute | solution.py:33
  74.6 33.2 %copy-start.9 = (f32[1024]{0:T(1024)S(1)}, f32[1024]{0:T(1024)}, u32[]{:S(2)}) copy-start(f32[1024]{0:T(1024)} %param.16) | copy-start | bytes 12292
  93.9 13.9 %all-to-all-start.3 = ((bf16[4,96,1024]{2,1,0:T(8,128)(2,1)}), bf16[4,96,1024]{2,1,0:T(8,128)(2,1)S(1)}, u32[]{:S(2)}, u32[]{:S(2)}) async-start(bf16[4,96,1024]{2,1,0:T(8,128)(2,1)} %broadcast_in_dim.15), calls=%async_computation.3 | async-start | bytes 1572864 | tf_op jit(solution)/shard_map/dispatch/all_to_all | solution.py:25
  107.7 5.9 %copy-start.1 = (bf16[512,1024]{1,0:T(8,128)(2,1)S(1)}, bf16[512,1024]{1,0:T(8,128)(2,1)}, u32[]{:S(2)}) copy-start(bf16[512,1024]{1,0:T(8,128)(2,1)} %copy-done) | copy-start | bytes 3145732
  110.1 9.8 %collective-permute-start.2 = (bf16[400,512]{1,0:T(8,128)(2,1)S(1)}, bf16[400,512]{1,0:T(8,128)(2,1)S(1)}, u32[]{:S(2)}, u32[]{:S(2)}) collective-permute-start(bf16[400,512]{1,0:T(8,128)(2,1)S(1)} %get-tuple-element.31), channel_id=1, source_target_pairs={{0,1},{1,0},{2,3},{3,2},{4,5},{5,4},{6,7},{7,6},{8,9},{9,8},{10,11... | collective-permute-start | bytes 1228808 | tf_op jit(solution)/shard_map/gate_up/ppermute | solution.py:37
  113.6 48.2 %collective-permute-start.5 = (bf16[512,1024]{1,0:T(8,128)(2,1)S(1)}, bf16[512,1024]{1,0:T(8,128)(2,1)S(1)}, u32[]{:S(2)}, u32[]{:S(2)}) collective-permute-start(bf16[512,1024]{1,0:T(8,128)(2,1)S(1)} %copy-done.1), channel_id=1, source_target_pairs={{0,32},{32,0},{1,33},{33,1},{2,34},{34,2},{3,35},{35,3},{4,36},{36... | collective-permute-start | bytes 3145736 | tf_op jit(solution)/shard_map/prepare/ppermute | solution.py:33
  120.1 22.1 %collective-permute-start.3 = (bf16[400,512]{1,0:T(8,128)(2,1)S(1)}, bf16[400,512]{1,0:T(8,128)(2,1)S(1)}, u32[]{:S(2)}, u32[]{:S(2)}) collective-permute-start(bf16[400,512]{1,0:T(8,128)(2,1)S(1)} %get-tuple-element.33), channel_id=1, source_target_pairs={{0,2},{1,3},{2,0},{3,1},{4,6},{5,7},{6,4},{7,5},{8,10},{9,11},{10,... | collective-permute-start | bytes 1228808 | tf_op jit(solution)/shard_map/gate_up/ppermute | solution.py:37
  123.9 20.2 %collective-permute-start.4 = (bf16[400,512]{1,0:T(8,128)(2,1)S(1)}, bf16[400,512]{1,0:T(8,128)(2,1)S(1)}, u32[]{:S(2)}, u32[]{:S(2)}) collective-permute-start(bf16[400,512]{1,0:T(8,128)(2,1)S(1)} %get-tuple-element.34), channel_id=1, source_target_pairs={{0,1},{1,0},{2,3},{3,2},{4,5},{5,4},{6,7},{7,6},{8,9},{9,8},{10,11... | collective-permute-start | bytes 1228808 | tf_op jit(solution)/shard_map/gate_up/ppermute | solution.py:37

commit v13 on v12

--- a/solution.py
+++ b/solution.py
@@ -84,10 +84,10 @@
         out[part] = jnp.dot(attended, columns, preferred_element_type=F32).astype(BF16)
 
 
-def prepare_kernel(after, ids, shares, gate, up, down, selector, mixer, weights, down_out, sems):
-    peers = (sems.shape[0] - 1) // 2
+def prepare_kernel(after, ids, shares, gate, up, selector, mixer, weights, sems):
+    peers = sems.shape[0] // 2
     piece = gate.shape[1] // peers
-    copies = [pltpu.make_async_copy(down, down_out, sems.at[2 * peers])]
+    copies = []
     for index in range(peers):
         for which, source in enumerate((gate, up)):
             place = 2 * index + which
@@ -129,6 +129,12 @@
             outgoing[half, expert] = part
 
 
+def arrange_kernel(arrived, weights, out):
+    rows = jnp.concatenate([arrived[index].astype(F32) for index in range(arrived.shape[0])], axis=0).astype(BF16)
+    for index in range(out.shape[0]):
+        out[index] = rows
+
+
 def share_of(place, scaled, near, far, offset, out):
     width = out.shape[1] // 2
     start = pl.multiple_of((place[2] ^ offset) * width, width)
@@ -250,17 +256,17 @@
             smem=1,
         )(place, queries, near, far, out_weight)
     with jax.named_scope("prepare"):
-        selector, mixer, near_weights, near_down = whole(
+        selector, mixer, near_weights = whole(
             prepare_kernel,
             [
                 shape((EXPERTS * CAP, row_count), BF16),
                 shape((EXPERTS * CAP, row_count), F32),
                 shape((width_part, 2 * ff_part), BF16),
-                shape((ff_part, width_part), BF16),
             ],
             flops=0,
-            scratch=[pltpu.SemaphoreType.DMA((2 * hid_count + 1,))],
-        )(done, expert_ids.T, expert_weights.T, gate_weight[0], up_weight[0], down_weight[0])
+            scratch=[pltpu.SemaphoreType.DMA((2 * hid_count,))],
+        )(done, expert_ids.T, expert_weights.T, gate_weight[0], up_weight[0])
+        near_down = down_weight[0]
         far_weights, far_down = other_core(near_weights), other_core(near_down)
     with jax.named_scope("projection"):
         arrived = swap(partials.reshape(hid_count * exp_count, row_count, width_part), ("hid", "exp"))
@@ -272,7 +278,13 @@
 
     with jax.named_scope("dispatch"):
         arrived = swap(outgoing.reshape(halves * exp_count, CAP, width_part), ("yh", "exp"))
-        arrived = spread(arrived.reshape(halves * exp_count * CAP, width_part), "x")
+        (copies,) = whole(
+            arrange_kernel,
+            [shape((lines, halves * exp_count * CAP, width_part), BF16)],
+            flops=0,
+            held=1,
+        )(arrived, far_weights)
+        arrived = swap(copies, "x")
         count = lines * halves * exp_count * CAP
         rows = arrived.reshape(count, width_part)
 

time: 198 us -> 197 us (level)
  blocking collectives: 93.8 us -> 88.3 us
  waiting for transfers between devices: 49 us -> 52.9 us
  local copies, waits for them, and re-layouts: 7.62 us -> 4.36 us
  Pallas kernels: 9.65 us -> 11.8 us
    all_to_all x4, blocking collectives: 76.3 us -> 70.5 us  [swap(): return lax.all_to_all(value, axes, split_axis=0, concat_axis=0, tiled=True)]
    all_to_all x2, waiting for transfers between devices: 29.1 us -> 33.8 us  [swap(): return lax.all_to_all(value, axes, split_axis=0, concat_axis=0, tiled=True)]
    pallas_call x8 -> x9, Pallas kernels: 9.65 us -> 11.8 us  [call(): pl.pallas_call(kernel, out_shape=out_shapes, in_specs=[pl.BlockSpec(memor...]
    unnamed x24 -> x20, local copies, waits for them, and re-layouts: 6.39 us -> 4.2 us
  transfers between devices with their start and end apart: 8 -> 8, of which waited for: 6 -> 6; matrix products, arithmetic and copies ran while one was open for 1% -> 0% of each run, Pallas kernels for 2% -> 3%
where the time goes in v13:
time: 197 us; the launch traced here: 196 us
  blocking collectives  88.3 us (45%)
  waiting for transfers between devices  52.9 us (27%)
  starting transfers between devices  36.4 us (18%)
  Pallas kernels  11.8 us (6%)
  local copies, waits for them, and re-layouts  4.36 us (2%)
    all_to_all x4, blocking collectives, swap(): return lax.all_to_all(value, axes, split_axis=0, concat_axis=0, tiled=True)  70.5 us
    all_to_all x2, waiting for transfers between devices, swap(): return lax.all_to_all(value, axes, split_axis=0, concat_axis=0, tiled=True)  33.8 us
    all_to_all x2, starting transfers between devices, swap(): return lax.all_to_all(value, axes, split_axis=0, concat_axis=0, tiled=True)  19 us
    all_gather x1, blocking collectives, shards(): active = lax.all_gather(active, 'hid', axis=0, tiled=False)  17.9 us
    ppermute x3, waiting for transfers between devices, to_peer(): lax.ppermute(value, 'hid', [(h, h ^ offset) for h in range(lax.axis_size(...  17.4 us
    pallas_call x9, Pallas kernels, call(): pl.pallas_call(kernel, out_shape=out_shapes, in_specs=[pl.BlockSpec(memor...  11.8 us
    ppermute x3, starting transfers between devices, to_peer(): lax.ppermute(value, 'hid', [(h, h ^ offset) for h in range(lax.axis_size(...  11.7 us
    ppermute x3, starting transfers between devices, other_core(): return lax.ppermute(value, 'core', [(0, 1), (1, 0)])  5.75 us
  transfers between devices with their start and end apart: 8, of which 6 were waited for; matrix products, arithmetic and copies ran while one was open for 0% of the time, Pallas kernels for 3%

profile of v13, /device:TPU:2, one launch (start us, length us, event | category | flops | bytes accessed | tf_op | source)
XLA Modules:
  0.0 196.1 jit_solution(5705254568053429614)
XLA Ops:
  0.0 0.0 copy-start.1
  0.0 0.9 pad_maximum_fusion
  0.9 25.2 %all_to_all.30 = bf16[8,128,256]{2,1,0:T(8,128)(2,1)S(1)} all-to-all(bf16[8,128,256]{2,1,0:T(8,128)(2,1)S(1)} %broadcast_in_dim.2), channel_id=1, replica_groups=mesh['x'=4,'yh'=2,'core'=2,'exp'=8,'hid'=4] {'x','yh'}, dimensions={0} | all-to-all | bytes 1048576 | tf_op jit(solution)/shard_map/kv_gather/all_to_all | solution.py:25
  26.1 1.9 collective-permute-start
  28.0 0.1 pad_add_fusion.place
  28.1 1.8 collective-permute-done.far
  29.9 0.0 copy-done.1
  29.9 0.0 copy-start.5
  29.9 0.8 copy-done.5
  30.6 0.0 copy-start.8
  30.6 0.0 copy-start.9
  30.6 1.6 attention.1
  32.3 0.0 copy-start.4
  32.3 1.0 copy-done.4
  33.3 0.0 copy-start.6
  33.3 13.6 %all-to-all-start.1 = ((bf16[32,16,1024]{2,1,0:T(8,128)(2,1)}), bf16[32,16,1024]{2,1,0:T(8,128)(2,1)S(1)}, u32[]{:S(2)}, u32[]{:S(2)}) async-start(bf16[32,16,1024]{2,1,0:T(8,128)(2,1)} %bitcast.26), calls=%async_computation.1 | async-start | bytes 2097152 | tf_op jit(solution)/shard_map/projection/all_to_all | solution.py:25
  46.9 0.0 copy-done.8
  46.9 0.0 copy-done.9
  46.9 0.0 copy-start.2
  46.9 1.2 copy-done.2
  48.1 0.0 copy-start.3
  48.1 1.2 copy-done.3
  49.4 2.2 %prepare.1 = (bf16[48,16]{1,0:T(8,128)(2,1)S(1)}, f32[48,16]{1,0:T(8,128)S(1)}, bf16[1024,1024]{1,0:T(8,128)(2,1)}) custom-call(f32[8,128]{1,0:T(8,128)S(1)} %get-tuple-element.21.after, s32[2,16]{1,0:T(2,128)S(1)} %bitcast.28, f32[2,16]{1,0:T(2,128)S(1)} %bitcast.29, bf16[1024,512]{1,0:T(8,128)(2,1)S(1)} %bitcast.24, bf16[1024,512]{1,0:T(8,128)(2,1)S(1)} %bitcast.25), custom_call_target="tpu_custom_call" | custom-call | bytes 4203264 | tf_op jit(solution)/shard_map/prepare/pallas_call | solution.py:45
  51.6 1.9 collective-permute-start.1
  53.5 21.0 %all-to-all-done.1.arrived = bf16[32,16,1024]{2,1,0:T(8,128)(2,1)S(1)} async-done(((bf16[32,16,1024]{2,1,0:T(8,128)(2,1)}), bf16[32,16,1024]{2,1,0:T(8,128)(2,1)S(1)}, u32[]{:S(2)}, u32[]{:S(2)}) %all-to-all-start.1) | async-done | bytes 1048608 | tf_op jit(solution)/shard_map/projection/all_to_all | solution.py:25
  74.5 0.0 copy-done.6
  74.5 1.0 projection.1
  75.5 5.4 %all-to-all-start.2 = ((bf16[16,6,1024]{2,1,0:T(8,128)(2,1)}), bf16[16,6,1024]{2,1,0:T(8,128)(2,1)S(1)}, u32[]{:S(2)}, u32[]{:S(2)}) async-start(bf16[16,6,1024]{2,1,0:T(8,128)(2,1)} %bitcast.9), calls=%async_computation.2 | async-start | bytes 524288 | tf_op jit(solution)/shard_map/dispatch/all_to_all | solution.py:25
  80.9 0.0 copy-start.7
  80.9 0.0 collective-permute-done.1.weights.far
  81.0 12.7 %all-to-all-done.2.arrived = bf16[16,6,1024]{2,1,0:T(8,128)(2,1)S(1)} async-done(((bf16[16,6,1024]{2,1,0:T(8,128)(2,1)}), bf16[16,6,1024]{2,1,0:T(8,128)(2,1)S(1)}, u32[]{:S(2)}, u32[]{:S(2)}) %all-to-all-start.2) | async-done | bytes 196640 | tf_op jit(solution)/shard_map/dispatch/all_to_all | solution.py:25
  93.7 0.1 dispatch.1
  93.7 12.8 %all_to_all.31 = bf16[4,96,1024]{2,1,0:T(8,128)(2,1)S(1)} all-to-all(bf16[4,96,1024]{2,1,0:T(8,128)(2,1)S(1)} %dispatch.1), channel_id=1, replica_groups=mesh['x'=4,'yh'=2,'core'=2,'exp'=8,'hid'=4] {'x'}, dimensions={0} | all-to-all | bytes 1572864 | tf_op jit(solution)/shard_map/dispatch/all_to_all | solution.py:25
  106.6 0.0 copy-done.7
  106.6 0.0 copy-start
  106.6 2.6 %gate_up.3 = (bf16[400,512]{1,0:T(8,128)(2,1)S(1)}, bf16[384,1024]{1,0:T(8,128)(2,1)S(1)}, bf16[16,512]{1,0:T(8,128)(2,1)S(1)}) custom-call(s32[3]{0:T(128)S(1)} %pad_add_fusion.place, bf16[384,1024]{1,0:T(8,128)(2,1)S(1)} %bitcast.19, f32[1,1024]{1,0:T(1,128)S(1)} %bitcast.27, bf16[1024,1024]{1,0:T(8,128)(2,1)} %get-tuple-element.26.near, ...), custom_call_target="tpu_custom_call" | custom-call | flops 402653184 | bytes 6197260 | tf_op jit(solution)/shard_map/gate_up/pallas_call | solution.py:45
  109.2 3.5 %collective-permute-start.2 = (bf16[400,512]{1,0:T(8,128)(2,1)S(1)}, bf16[400,512]{1,0:T(8,128)(2,1)S(1)}, u32[]{:S(2)}, u32[]{:S(2)}) collective-permute-start(bf16[400,512]{1,0:T(8,128)(2,1)S(1)} %get-tuple-element.30), channel_id=1, source_target_pairs={{0,1},{1,0},{2,3},{3,2},{4,5},{5,4},{6,7},{7,6},{8,9},{9,8},{10,11... | collective-permute-start | bytes 1228808 | tf_op jit(solution)/shard_map/gate_up/ppermute | solution.py:37
  112.7 0.0 copy-done
  112.7 1.9 collective-permute-start.5
  114.6 3.0 %gate_up.4 = (bf16[400,512]{1,0:T(8,128)(2,1)S(1)}, bf16[400,512]{1,0:T(8,128)(2,1)S(1)}, bf16[400,512]{1,0:T(8,128)(2,1)S(1)}) custom-call(s32[3]{0:T(128)S(1)} %pad_add_fusion.place, bf16[384,1024]{1,0:T(8,128)(2,1)S(1)} %get-tuple-element.27.scaled, bf16[16,512]{1,0:T(8,128)(2,1)S(1)} %get-tuple-element.28.tail, ...), custom_call_target="tpu_custom_call" | custom-call | flops 1207959552 | bytes 6225932 | tf_op jit(solution)/shard_map/gate_up/pallas_call | solution.py:45
  117.6 1.4 collective-permute-done.2.arrived
  119.0 0.1 gate_up.5
  119.1 6.0 %collective-permute-start.3 = (bf16[400,512]{1,0:T(8,128)(2,1)S(1)}, bf16[400,512]{1,0:T(8,128)(2,1)S(1)}, u32[]{:S(2)}, u32[]{:S(2)}) collective-permute-start(bf16[400,512]{1,0:T(8,128)(2,1)S(1)} %get-tuple-element.32), channel_id=1, source_target_pairs={{0,2},{1,3},{2,0},{3,1},{4,6},{5,7},{6,4},{7,5},{8,10},{9,11},{10,... | collective-permute-start | bytes 1228808 | tf_op jit(solution)/shard_map/gate_up/ppermute | solution.py:37
  125.1 2.2 %collective-permute-start.4 = (bf16[400,512]{1,0:T(8,128)(2,1)S(1)}, bf16[400,512]{1,0:T(8,128)(2,1)S(1)}, u32[]{:S(2)}, u32[]{:S(2)}) collective-permute-start(bf16[400,512]{1,0:T(8,128)(2,1)S(1)} %get-tuple-element.33), channel_id=1, source_target_pairs={{0,1},{1,0},{2,3},{3,2},{4,5},{5,4},{6,7},{7,6},{8,9},{9,8},{10,11... | collective-permute-start | bytes 1228808 | tf_op jit(solution)/shard_map/gate_up/ppermute | solution.py:37
  127.3 14.0 %collective-permute-done.3.refs_0_ = bf16[400,512]{1,0:T(8,128)(2,1)S(1)} collective-permute-done((bf16[400,512]{1,0:T(8,128)(2,1)S(1)}, bf16[400,512]{1,0:T(8,128)(2,1)S(1)}, u32[]{:S(2)}, u32[]{:S(2)}) %collective-permute-start.3) | collective-permute-done | bytes 409632 | tf_op jit(solution)/shard_map/gate_up/ppermute | solution.py:37
  141.3 2.0 %collective-permute-done.4.refs_1_ = bf16[400,512]{1,0:T(8,128)(2,1)S(1)} collective-permute-done((bf16[400,512]{1,0:T(8,128)(2,1)S(1)}, bf16[400,512]{1,0:T(8,128)(2,1)S(1)}, u32[]{:S(2)}, u32[]{:S(2)}) %collective-permute-start.4) | collective-permute-done | bytes 409632 | tf_op jit(solution)/shard_map/gate_up/ppermute | solution.py:37
  143.3 0.3 active.1
  143.6 17.9 %all-gather = bf16[3072,128]{1,0:T(8,128)(2,1)S(1)} all-gather(bf16[768,128]{1,0:T(8,128)(2,1)S(1)} %active.1), channel_id=2, replica_groups=mesh['x'=4,'yh'=2,'core'=2,'exp'=8,'hid'=4] {'hid'}, dimensions={0}, use_global_device_ids=true | all-gather | bytes 983040 | tf_op jit(solution)/shard_map/active/all_gather | solution.py:309
  161.4 0.0 collective-permute-done.5.far
  161.4 1.0 down.1
  162.4 11.9 %all_to_all.32 = bf16[4,96,1024]{2,1,0:T(8,128)(2,1)S(1)} all-to-all(bf16[4,96,1024]{2,1,0:T(8,128)(2,1)S(1)} %bitcast.17), channel_id=1, replica_groups=mesh['x'=4,'yh'=2,'core'=2,'exp'=8,'hid'=4] {'x'}, dimensions={0} | all-to-all | bytes 1572864 | tf_op jit(solution)/shard_map/down/all_to_all | solution.py:25
  174.3 0.1 reduce_sum.21
  174.5 0.1 reshape.31
  174.6 20.5 %all_to_all.33 = bf16[16,6,1024]{2,1,0:T(8,128)(2,1)S(1)} all-to-all(bf16[16,6,1024]{2,1,0:T(8,128)(2,1)S(1)} %reshape.31), channel_id=1, replica_groups=mesh['x'=4,'yh'=2,'core'=2,'exp'=8,'hid'=4] {'yh','exp'}, dimensions={0} | all-to-all | bytes 393216 | tf_op jit(solution)/shard_map/down/all_to_all | solution.py:25
  195.1 0.1 reshape.32
  195.2 0.9 fusion
  (2 shorter events, 0.1 us)
Async XLA Ops:
  0.0 29.9 %copy-start.1 = (bf16[128,4096]{1,0:T(8,128)(2,1)S(1)}, bf16[128,4096]{1,0:T(8,128)(2,1)}, u32[]{:S(2)}) copy-start(bf16[128,4096]{1,0:T(8,128)(2,1)} %weight.1) | copy-start | bytes 3145732
  26.1 3.8 %collective-permute-start = (bf16[1024,256]{1,0:T(8,128)(2,1)S(1)}, bf16[1024,256]{1,0:T(8,128)(2,1)S(1)}, u32[]{:S(2)}, u32[]{:S(2)}) collective-permute-start(bf16[1024,256]{1,0:T(8,128)(2,1)S(1)} %bitcast.20), channel_id=1, source_target_pairs={{0,32},{32,0},{1,33},{33,1},{2,34},{34,2},{3,35},{35,3},{4,36},{36... | collective-permute-start | bytes 1572872 | tf_op jit(solution)/shard_map/kv_gather/ppermute | solution.py:33
  29.9 0.8 copy-start.5
  30.6 16.3 %copy-start.8 = (s32[16,2]{0,1:T(2,128)S(1)}, s32[16,2]{0,1:T(2,128)}, u32[]{:S(2)}) copy-start(s32[16,2]{0,1:T(2,128)} %param.20) | copy-start | bytes 388
  30.6 16.3 %copy-start.9 = (f32[16,2]{0,1:T(2,128)S(1)}, f32[16,2]{0,1:T(2,128)}, u32[]{:S(2)}) copy-start(f32[16,2]{0,1:T(2,128)} %param.21) | copy-start | bytes 388
  32.3 1.0 copy-start.4
  33.3 41.3 %copy-start.6 = (bf16[16,1024]{1,0:T(8,128)(2,1)S(1)}, bf16[16,1024]{1,0:T(8,128)(2,1)}, u32[]{:S(2)}) copy-start(bf16[16,1024]{1,0:T(8,128)(2,1)} %residual.1) | copy-start | bytes 98308
  33.3 41.3 %all-to-all-start.1 = ((bf16[32,16,1024]{2,1,0:T(8,128)(2,1)}), bf16[32,16,1024]{2,1,0:T(8,128)(2,1)S(1)}, u32[]{:S(2)}, u32[]{:S(2)}) async-start(bf16[32,16,1024]{2,1,0:T(8,128)(2,1)} %bitcast.26), calls=%async_computation.1 | async-start | bytes 2097152 | tf_op jit(solution)/shard_map/projection/all_to_all | solution.py:25
  46.9 1.2 copy-start.2
  48.1 1.2 copy-start.3
  51.6 29.4 %collective-permute-start.1 = (bf16[1024,1024]{1,0:T(8,128)(2,1)}, bf16[1024,1024]{1,0:T(8,128)(2,1)S(1)}, u32[]{:S(2)}, u32[]{:S(2)}) collective-permute-start(bf16[1024,1024]{1,0:T(8,128)(2,1)} %get-tuple-element.26.near), channel_id=1, source_target_pairs={{0,32},{32,0},{1,33},{33,1},{2,34},{34,2},{3,35},{35,3},{4,36},{36... | collective-permute-start | bytes 6291464 | tf_op jit(solution)/shard_map/prepare/ppermute | solution.py:33
  75.5 18.1 %all-to-all-start.2 = ((bf16[16,6,1024]{2,1,0:T(8,128)(2,1)}), bf16[16,6,1024]{2,1,0:T(8,128)(2,1)S(1)}, u32[]{:S(2)}, u32[]{:S(2)}) async-start(bf16[16,6,1024]{2,1,0:T(8,128)(2,1)} %bitcast.9), calls=%async_computation.2 | async-start | bytes 524288 | tf_op jit(solution)/shard_map/dispatch/all_to_all | solution.py:25
  80.9 25.6 %copy-start.7 = (f32[1024]{0:T(1024)S(1)}, f32[1024]{0:T(1024)}, u32[]{:S(2)}) copy-start(f32[1024]{0:T(1024)} %param.16) | copy-start | bytes 12292
  106.6 6.1 %copy-start = (bf16[1,512,1024]{2,1,0:T(8,128)(2,1)S(1)}, bf16[1,512,1024]{2,1,0:T(8,128)(2,1)}, u32[]{:S(2)}) copy-start(bf16[1,512,1024]{2,1,0:T(8,128)(2,1)} %param.19) | copy-start | bytes 3145732
  109.2 9.8 %collective-permute-start.2 = (bf16[400,512]{1,0:T(8,128)(2,1)S(1)}, bf16[400,512]{1,0:T(8,128)(2,1)S(1)}, u32[]{:S(2)}, u32[]{:S(2)}) collective-permute-start(bf16[400,512]{1,0:T(8,128)(2,1)S(1)} %get-tuple-element.30), channel_id=1, source_target_pairs={{0,1},{1,0},{2,3},{3,2},{4,5},{5,4},{6,7},{7,6},{8,9},{9,8},{10,11... | collective-permute-start | bytes 1228808 | tf_op jit(solution)/shard_map/gate_up/ppermute | solution.py:37
  112.7 48.8 %collective-permute-start.5 = (bf16[512,1024]{1,0:T(8,128)(2,1)S(1)}, bf16[512,1024]{1,0:T(8,128)(2,1)S(1)}, u32[]{:S(2)}, u32[]{:S(2)}) collective-permute-start(bf16[512,1024]{1,0:T(8,128)(2,1)S(1)} %bitcast.22), channel_id=1, source_target_pairs={{0,32},{32,0},{1,33},{33,1},{2,34},{34,2},{3,35},{35,3},{4,36},{36... | collective-permute-start | bytes 3145736 | tf_op jit(solution)/shard_map/prepare/ppermute | solution.py:33
  119.1 22.2 %collective-permute-start.3 = (bf16[400,512]{1,0:T(8,128)(2,1)S(1)}, bf16[400,512]{1,0:T(8,128)(2,1)S(1)}, u32[]{:S(2)}, u32[]{:S(2)}) collective-permute-start(bf16[400,512]{1,0:T(8,128)(2,1)S(1)} %get-tuple-element.32), channel_id=1, source_target_pairs={{0,2},{1,3},{2,0},{3,1},{4,6},{5,7},{6,4},{7,5},{8,10},{9,11},{10,... | collective-permute-start | bytes 1228808 | tf_op jit(solution)/shard_map/gate_up/ppermute | solution.py:37
  125.1 18.2 %collective-permute-start.4 = (bf16[400,512]{1,0:T(8,128)(2,1)S(1)}, bf16[400,512]{1,0:T(8,128)(2,1)S(1)}, u32[]{:S(2)}, u32[]{:S(2)}) collective-permute-start(bf16[400,512]{1,0:T(8,128)(2,1)S(1)} %get-tuple-element.33), channel_id=1, source_target_pairs={{0,1},{1,0},{2,3},{3,2},{4,5},{5,4},{6,7},{7,6},{8,9},{9,8},{10,11... | collective-permute-start | bytes 1228808 | tf_op jit(solution)/shard_map/gate_up/ppermute | solution.py:37

commit v14 on v13

--- a/solution.py
+++ b/solution.py
@@ -59,17 +59,18 @@
     return lax.dot_general(left, right, (((1,), (1,)), ((), ())), preferred_element_type=F32)
 
 
-def attention_kernel(place, query, near, far, weight, out, done):
+def attention_kernel(place, packed, near, far, weight, out, done):
     done[...] = jnp.zeros_like(done)
     ctx, core = place[0], place[1]
-    rows, keys = query.shape[0], near.shape[0]
+    rows, keys = packed.shape[0], near.shape[0]
+    query = packed[:, 2 * HEAD :]
     spot = ctx * rows + lax.broadcasted_iota(jnp.int32, (rows, keys), 0)
     column = lax.broadcasted_iota(jnp.int32, (rows, keys), 1)
     base = (column // rows) * (2 * rows) + column % rows
     scores = []
     for half, source in enumerate((near, far)):
         key_spot = base + (core ^ half) * rows
-        product = dot_nt(query[...], source[:, :HEAD]) * (1.0 / math.sqrt(HEAD))
+        product = dot_nt(query, source[:, :HEAD]) * (1.0 / math.sqrt(HEAD))
         scores.append(jnp.where(spot >= key_spot, product, -1e30))
     top = jnp.maximum(*(jnp.max(score, axis=1, keepdims=True) for score in scores))
     denom, total = 0.0, 0.0
@@ -218,6 +219,19 @@
     out[...] = total.astype(BF16)
 
 
+def combine_kernel(back, mixer, stream, out):
+    experts = back.shape[0] // 2
+    rows = [back[e].astype(F32) + back[experts + e].astype(F32) for e in range(experts)]
+    combined = lax.dot_general(
+        mixer[...],
+        jnp.concatenate(rows, axis=0),
+        (((0,), (0,)), ((), ())),
+        precision=lax.Precision.HIGHEST,
+        preferred_element_type=F32,
+    )
+    out[...] = (stream[...] + combined).astype(BF16)
+
+
 def shards(
     queries,
     key_heads,
@@ -243,7 +257,8 @@
     shape = jax.ShapeDtypeStruct
 
     with jax.named_scope("kv_gather"):
-        near = spread(jnp.concatenate([key_heads, value_heads], axis=1), PLANE)
+        packed = lax.optimization_barrier(jnp.concatenate([key_heads, value_heads, queries], axis=1))
+        near = spread(packed[:, : 2 * HEAD], PLANE)
         near = near.reshape(plane * tok_rows, 2 * HEAD)
         far = other_core(near)
     with jax.named_scope("attention"):
@@ -254,7 +269,7 @@
             [shape((hid_count, tok_rows, width_part), BF16), shape((8, 128), F32)],
             flops=2 * tok_rows * HEAD * (4 * plane * tok_rows + D),
             smem=1,
-        )(place, queries, near, far, out_weight)
+        )(place, packed, near, far, out_weight)
     with jax.named_scope("prepare"):
         selector, mixer, near_weights = whole(
             prepare_kernel,
@@ -314,11 +329,11 @@
         back = swap(back.reshape(lines, count // lines, width_part), "x")
         back = jnp.sum(back.astype(F32), axis=0).astype(BF16)
         back = swap(back.reshape(halves * exp_count, CAP, width_part), ("yh", "exp"))
-        back = back.reshape(halves, EXPERTS * CAP, width_part).astype(F32)
-        back = jnp.sum(back, axis=0)
     with jax.named_scope("combine"):
-        combined = lax.dot_general(mixer, back, (((0,), (0,)), ((), ())), precision=lax.Precision.HIGHEST)
-        return (stream + combined).astype(BF16)
+        (out,) = whole(combine_kernel, [shape((row_count, width_part), BF16)], flops=2 * back.size)(
+            back, mixer, stream
+        )
+    return out
 
 
 def solution(mesh):

time: 197 us -> 196 us (level)
    pallas_call x9 -> x10, Pallas kernels: 11.8 us -> 12.8 us  [call(): pl.pallas_call(kernel, out_shape=out_shapes, in_specs=[pl.BlockSpec(memor...]
    unnamed x20 -> x18, local copies, waits for them, and re-layouts: 4.2 us -> 3.45 us
where the time goes in v14:
time: 196 us; the launch traced here: 195 us
  blocking collectives  88.3 us (45%)
  waiting for transfers between devices  52.9 us (27%)
  starting transfers between devices  36.4 us (19%)
  Pallas kernels  12.8 us (7%)
  local copies, waits for them, and re-layouts  3.56 us (2%)
    all_to_all x4, blocking collectives, swap(): return lax.all_to_all(value, axes, split_axis=0, concat_axis=0, tiled=True)  70.5 us
    all_to_all x2, waiting for transfers between devices, swap(): return lax.all_to_all(value, axes, split_axis=0, concat_axis=0, tiled=True)  33.8 us
    all_to_all x2, starting transfers between devices, swap(): return lax.all_to_all(value, axes, split_axis=0, concat_axis=0, tiled=True)  19 us
    all_gather x1, blocking collectives, shards(): active = lax.all_gather(active, 'hid', axis=0, tiled=False)  17.8 us
    ppermute x3, waiting for transfers between devices, to_peer(): lax.ppermute(value, 'hid', [(h, h ^ offset) for h in range(lax.axis_size(...  17.4 us
    pallas_call x10, Pallas kernels, call(): pl.pallas_call(kernel, out_shape=out_shapes, in_specs=[pl.BlockSpec(memor...  12.8 us
    ppermute x3, starting transfers between devices, to_peer(): lax.ppermute(value, 'hid', [(h, h ^ offset) for h in range(lax.axis_size(...  11.6 us
    ppermute x3, starting transfers between devices, other_core(): return lax.ppermute(value, 'core', [(0, 1), (1, 0)])  5.75 us
  transfers between devices with their start and end apart: 8, of which 6 were waited for; matrix products, arithmetic and copies ran while one was open for 0% of the time, Pallas kernels for 3%

profile of v14, /device:TPU:2, one launch (start us, length us, event | category | flops | bytes accessed | tf_op | source)
XLA Modules:
  0.0 195.3 jit_solution(5923904006921608555)
XLA Ops:
  0.0 0.0 copy-start.1
  0.0 0.9 pad_maximum_fusion.packed
  1.0 25.2 %all_to_all.30 = bf16[8,128,256]{2,1,0:T(8,128)(2,1)S(1)} all-to-all(bf16[8,128,256]{2,1,0:T(8,128)(2,1)S(1)} %broadcast_in_dim.2), channel_id=1, replica_groups=mesh['x'=4,'yh'=2,'core'=2,'exp'=8,'hid'=4] {'x','yh'}, dimensions={0} | all-to-all | bytes 1048576 | tf_op jit(solution)/shard_map/kv_gather/all_to_all | solution.py:25
  26.1 1.9 collective-permute-start
  28.0 0.1 pad_add_fusion.place
  28.1 0.0 copy-start.7
  28.1 0.0 copy-start.8
  28.1 1.8 collective-permute-done.far
  29.9 0.0 copy-done.1
  29.9 1.6 attention.1
  31.6 0.0 copy-start.4
  31.6 1.0 copy-done.4
  32.5 0.0 copy-start.5
  32.5 13.6 %all-to-all-start.1 = ((bf16[32,16,1024]{2,1,0:T(8,128)(2,1)}), bf16[32,16,1024]{2,1,0:T(8,128)(2,1)S(1)}, u32[]{:S(2)}, u32[]{:S(2)}) async-start(bf16[32,16,1024]{2,1,0:T(8,128)(2,1)} %bitcast.24), calls=%async_computation.1 | async-start | bytes 2097152 | tf_op jit(solution)/shard_map/projection/all_to_all | solution.py:25
  46.2 0.0 copy-done.7
  46.2 0.0 copy-done.8
  46.2 0.0 copy-start.2
  46.2 1.2 copy-done.2
  47.4 0.0 copy-start.3
  47.4 1.2 copy-done.3
  48.7 2.2 %prepare.1 = (bf16[48,16]{1,0:T(8,128)(2,1)S(1)}, f32[48,16]{1,0:T(8,128)S(1)}, bf16[1024,1024]{1,0:T(8,128)(2,1)}) custom-call(f32[8,128]{1,0:T(8,128)S(1)} %get-tuple-element.21.after, s32[2,16]{1,0:T(2,128)S(1)} %bitcast.26, f32[2,16]{1,0:T(2,128)S(1)} %bitcast.27, bf16[1024,512]{1,0:T(8,128)(2,1)S(1)} %bitcast.22, bf16[1024,512]{1,0:T(8,128)(2,1)S(1)} %bitcast.23), custom_call_target="tpu_custom_call" | custom-call | bytes 4203264 | tf_op jit(solution)/shard_map/prepare/pallas_call | solution.py:45
  50.9 1.9 collective-permute-start.1
  52.8 21.1 %all-to-all-done.1.arrived = bf16[32,16,1024]{2,1,0:T(8,128)(2,1)S(1)} async-done(((bf16[32,16,1024]{2,1,0:T(8,128)(2,1)}), bf16[32,16,1024]{2,1,0:T(8,128)(2,1)S(1)}, u32[]{:S(2)}, u32[]{:S(2)}) %all-to-all-start.1) | async-done | bytes 1048608 | tf_op jit(solution)/shard_map/projection/all_to_all | solution.py:25
  73.8 0.0 copy-done.5
  73.8 1.0 projection.1
  74.9 5.4 %all-to-all-start.2 = ((bf16[16,6,1024]{2,1,0:T(8,128)(2,1)}), bf16[16,6,1024]{2,1,0:T(8,128)(2,1)S(1)}, u32[]{:S(2)}, u32[]{:S(2)}) async-start(bf16[16,6,1024]{2,1,0:T(8,128)(2,1)} %bitcast.9), calls=%async_computation.2 | async-start | bytes 524288 | tf_op jit(solution)/shard_map/dispatch/all_to_all | solution.py:25
  80.3 0.0 copy-start.6
  80.3 0.0 collective-permute-done.1.weights.far
  80.3 12.7 %all-to-all-done.2.arrived = bf16[16,6,1024]{2,1,0:T(8,128)(2,1)S(1)} async-done(((bf16[16,6,1024]{2,1,0:T(8,128)(2,1)}), bf16[16,6,1024]{2,1,0:T(8,128)(2,1)S(1)}, u32[]{:S(2)}, u32[]{:S(2)}) %all-to-all-start.2) | async-done | bytes 196640 | tf_op jit(solution)/shard_map/dispatch/all_to_all | solution.py:25
  93.0 0.1 dispatch.1
  93.0 12.8 %all_to_all.31 = bf16[4,96,1024]{2,1,0:T(8,128)(2,1)S(1)} all-to-all(bf16[4,96,1024]{2,1,0:T(8,128)(2,1)S(1)} %dispatch.1), channel_id=1, replica_groups=mesh['x'=4,'yh'=2,'core'=2,'exp'=8,'hid'=4] {'x'}, dimensions={0} | all-to-all | bytes 1572864 | tf_op jit(solution)/shard_map/dispatch/all_to_all | solution.py:25
  105.9 0.0 copy-done.6
  105.9 0.0 copy-start
  105.9 2.6 %gate_up.3 = (bf16[400,512]{1,0:T(8,128)(2,1)S(1)}, bf16[384,1024]{1,0:T(8,128)(2,1)S(1)}, bf16[16,512]{1,0:T(8,128)(2,1)S(1)}) custom-call(s32[3]{0:T(128)S(1)} %pad_add_fusion.place, bf16[384,1024]{1,0:T(8,128)(2,1)S(1)} %bitcast.17, f32[1,1024]{1,0:T(1,128)S(1)} %bitcast.25, bf16[1024,1024]{1,0:T(8,128)(2,1)} %get-tuple-element.24.near, ...), custom_call_target="tpu_custom_call" | custom-call | flops 402653184 | bytes 6197260 | tf_op jit(solution)/shard_map/gate_up/pallas_call | solution.py:45
  108.5 3.5 %collective-permute-start.2 = (bf16[400,512]{1,0:T(8,128)(2,1)S(1)}, bf16[400,512]{1,0:T(8,128)(2,1)S(1)}, u32[]{:S(2)}, u32[]{:S(2)}) collective-permute-start(bf16[400,512]{1,0:T(8,128)(2,1)S(1)} %get-tuple-element.28), channel_id=1, source_target_pairs={{0,1},{1,0},{2,3},{3,2},{4,5},{5,4},{6,7},{7,6},{8,9},{9,8},{10,11... | collective-permute-start | bytes 1228808 | tf_op jit(solution)/shard_map/gate_up/ppermute | solution.py:37
  112.0 0.0 copy-done
  112.0 1.9 collective-permute-start.5
  113.9 3.0 %gate_up.4 = (bf16[400,512]{1,0:T(8,128)(2,1)S(1)}, bf16[400,512]{1,0:T(8,128)(2,1)S(1)}, bf16[400,512]{1,0:T(8,128)(2,1)S(1)}) custom-call(s32[3]{0:T(128)S(1)} %pad_add_fusion.place, bf16[384,1024]{1,0:T(8,128)(2,1)S(1)} %get-tuple-element.25.scaled, bf16[16,512]{1,0:T(8,128)(2,1)S(1)} %get-tuple-element.26.tail, ...), custom_call_target="tpu_custom_call" | custom-call | flops 1207959552 | bytes 6225932 | tf_op jit(solution)/shard_map/gate_up/pallas_call | solution.py:45
  116.9 1.4 collective-permute-done.2.arrived
  118.3 0.1 gate_up.5
  118.4 6.0 %collective-permute-start.3 = (bf16[400,512]{1,0:T(8,128)(2,1)S(1)}, bf16[400,512]{1,0:T(8,128)(2,1)S(1)}, u32[]{:S(2)}, u32[]{:S(2)}) collective-permute-start(bf16[400,512]{1,0:T(8,128)(2,1)S(1)} %get-tuple-element.30), channel_id=1, source_target_pairs={{0,2},{1,3},{2,0},{3,1},{4,6},{5,7},{6,4},{7,5},{8,10},{9,11},{10,... | collective-permute-start | bytes 1228808 | tf_op jit(solution)/shard_map/gate_up/ppermute | solution.py:37
  124.4 2.2 %collective-permute-start.4 = (bf16[400,512]{1,0:T(8,128)(2,1)S(1)}, bf16[400,512]{1,0:T(8,128)(2,1)S(1)}, u32[]{:S(2)}, u32[]{:S(2)}) collective-permute-start(bf16[400,512]{1,0:T(8,128)(2,1)S(1)} %get-tuple-element.31), channel_id=1, source_target_pairs={{0,1},{1,0},{2,3},{3,2},{4,5},{5,4},{6,7},{7,6},{8,9},{9,8},{10,11... | collective-permute-start | bytes 1228808 | tf_op jit(solution)/shard_map/gate_up/ppermute | solution.py:37
  126.6 14.0 %collective-permute-done.3.refs_0_ = bf16[400,512]{1,0:T(8,128)(2,1)S(1)} collective-permute-done((bf16[400,512]{1,0:T(8,128)(2,1)S(1)}, bf16[400,512]{1,0:T(8,128)(2,1)S(1)}, u32[]{:S(2)}, u32[]{:S(2)}) %collective-permute-start.3) | collective-permute-done | bytes 409632 | tf_op jit(solution)/shard_map/gate_up/ppermute | solution.py:37
  140.6 2.0 %collective-permute-done.4.refs_1_ = bf16[400,512]{1,0:T(8,128)(2,1)S(1)} collective-permute-done((bf16[400,512]{1,0:T(8,128)(2,1)S(1)}, bf16[400,512]{1,0:T(8,128)(2,1)S(1)}, u32[]{:S(2)}, u32[]{:S(2)}) %collective-permute-start.4) | collective-permute-done | bytes 409632 | tf_op jit(solution)/shard_map/gate_up/ppermute | solution.py:37
  142.6 0.3 active.1
  142.9 17.8 %all-gather = bf16[3072,128]{1,0:T(8,128)(2,1)S(1)} all-gather(bf16[768,128]{1,0:T(8,128)(2,1)S(1)} %active.1), channel_id=2, replica_groups=mesh['x'=4,'yh'=2,'core'=2,'exp'=8,'hid'=4] {'hid'}, dimensions={0}, use_global_device_ids=true | all-gather | bytes 983040 | tf_op jit(solution)/shard_map/active/all_gather | solution.py:324
  160.7 0.0 collective-permute-done.5.far
  160.7 1.0 down.1
  161.7 11.9 %all_to_all.32 = bf16[4,96,1024]{2,1,0:T(8,128)(2,1)S(1)} all-to-all(bf16[4,96,1024]{2,1,0:T(8,128)(2,1)S(1)} %bitcast.15), channel_id=1, replica_groups=mesh['x'=4,'yh'=2,'core'=2,'exp'=8,'hid'=4] {'x'}, dimensions={0} | all-to-all | bytes 1572864 | tf_op jit(solution)/shard_map/down/all_to_all | solution.py:25
  173.6 0.1 reduce_sum.12
  173.7 0.1 reshape.28
  173.8 20.6 %all_to_all.33.back = bf16[16,6,1024]{2,1,0:T(8,128)(2,1)S(1)} all-to-all(bf16[16,6,1024]{2,1,0:T(8,128)(2,1)S(1)} %reshape.28), channel_id=1, replica_groups=mesh['x'=4,'yh'=2,'core'=2,'exp'=8,'hid'=4] {'yh','exp'}, dimensions={0} | all-to-all | bytes 393216 | tf_op jit(solution)/shard_map/down/all_to_all | solution.py:25
  194.4 0.9 combine.1
  (2 shorter events, 0.0 us)
Async XLA Ops:
  0.0 29.9 %copy-start.1 = (bf16[128,4096]{1,0:T(8,128)(2,1)S(1)}, bf16[128,4096]{1,0:T(8,128)(2,1)}, u32[]{:S(2)}) copy-start(bf16[128,4096]{1,0:T(8,128)(2,1)} %weight.1) | copy-start | bytes 3145732
  26.1 3.8 %collective-permute-start = (bf16[1024,256]{1,0:T(8,128)(2,1)S(1)}, bf16[1024,256]{1,0:T(8,128)(2,1)S(1)}, u32[]{:S(2)}, u32[]{:S(2)}) collective-permute-start(bf16[1024,256]{1,0:T(8,128)(2,1)S(1)} %bitcast.18), channel_id=1, source_target_pairs={{0,32},{32,0},{1,33},{33,1},{2,34},{34,2},{3,35},{35,3},{4,36},{36... | collective-permute-start | bytes 1572872 | tf_op jit(solution)/shard_map/kv_gather/ppermute | solution.py:33
  28.1 18.1 %copy-start.7 = (s32[16,2]{0,1:T(2,128)S(1)}, s32[16,2]{0,1:T(2,128)}, u32[]{:S(2)}) copy-start(s32[16,2]{0,1:T(2,128)} %param.20) | copy-start | bytes 388
  28.1 18.1 %copy-start.8 = (f32[16,2]{0,1:T(2,128)S(1)}, f32[16,2]{0,1:T(2,128)}, u32[]{:S(2)}) copy-start(f32[16,2]{0,1:T(2,128)} %param.21) | copy-start | bytes 388
  31.6 1.0 copy-start.4
  32.5 41.3 %copy-start.5 = (bf16[16,1024]{1,0:T(8,128)(2,1)S(1)}, bf16[16,1024]{1,0:T(8,128)(2,1)}, u32[]{:S(2)}) copy-start(bf16[16,1024]{1,0:T(8,128)(2,1)} %residual.1) | copy-start | bytes 98308
  32.5 41.3 %all-to-all-start.1 = ((bf16[32,16,1024]{2,1,0:T(8,128)(2,1)}), bf16[32,16,1024]{2,1,0:T(8,128)(2,1)S(1)}, u32[]{:S(2)}, u32[]{:S(2)}) async-start(bf16[32,16,1024]{2,1,0:T(8,128)(2,1)} %bitcast.24), calls=%async_computation.1 | async-start | bytes 2097152 | tf_op jit(solution)/shard_map/projection/all_to_all | solution.py:25
  46.2 1.2 copy-start.2
  47.4 1.2 copy-start.3
  50.9 29.4 %collective-permute-start.1 = (bf16[1024,1024]{1,0:T(8,128)(2,1)}, bf16[1024,1024]{1,0:T(8,128)(2,1)S(1)}, u32[]{:S(2)}, u32[]{:S(2)}) collective-permute-start(bf16[1024,1024]{1,0:T(8,128)(2,1)} %get-tuple-element.24.near), channel_id=1, source_target_pairs={{0,32},{32,0},{1,33},{33,1},{2,34},{34,2},{3,35},{35,3},{4,36},{36... | collective-permute-start | bytes 6291464 | tf_op jit(solution)/shard_map/prepare/ppermute | solution.py:33
  74.9 18.1 %all-to-all-start.2 = ((bf16[16,6,1024]{2,1,0:T(8,128)(2,1)}), bf16[16,6,1024]{2,1,0:T(8,128)(2,1)S(1)}, u32[]{:S(2)}, u32[]{:S(2)}) async-start(bf16[16,6,1024]{2,1,0:T(8,128)(2,1)} %bitcast.9), calls=%async_computation.2 | async-start | bytes 524288 | tf_op jit(solution)/shard_map/dispatch/all_to_all | solution.py:25
  80.3 25.6 %copy-start.6 = (f32[1024]{0:T(1024)S(1)}, f32[1024]{0:T(1024)}, u32[]{:S(2)}) copy-start(f32[1024]{0:T(1024)} %param.16) | copy-start | bytes 12292
  105.9 6.1 %copy-start = (bf16[1,512,1024]{2,1,0:T(8,128)(2,1)S(1)}, bf16[1,512,1024]{2,1,0:T(8,128)(2,1)}, u32[]{:S(2)}) copy-start(bf16[1,512,1024]{2,1,0:T(8,128)(2,1)} %param.19) | copy-start | bytes 3145732
  108.5 9.8 %collective-permute-start.2 = (bf16[400,512]{1,0:T(8,128)(2,1)S(1)}, bf16[400,512]{1,0:T(8,128)(2,1)S(1)}, u32[]{:S(2)}, u32[]{:S(2)}) collective-permute-start(bf16[400,512]{1,0:T(8,128)(2,1)S(1)} %get-tuple-element.28), channel_id=1, source_target_pairs={{0,1},{1,0},{2,3},{3,2},{4,5},{5,4},{6,7},{7,6},{8,9},{9,8},{10,11... | collective-permute-start | bytes 1228808 | tf_op jit(solution)/shard_map/gate_up/ppermute | solution.py:37
  112.0 48.7 %collective-permute-start.5 = (bf16[512,1024]{1,0:T(8,128)(2,1)S(1)}, bf16[512,1024]{1,0:T(8,128)(2,1)S(1)}, u32[]{:S(2)}, u32[]{:S(2)}) collective-permute-start(bf16[512,1024]{1,0:T(8,128)(2,1)S(1)} %bitcast.20), channel_id=1, source_target_pairs={{0,32},{32,0},{1,33},{33,1},{2,34},{34,2},{3,35},{35,3},{4,36},{36... | collective-permute-start | bytes 3145736 | tf_op jit(solution)/shard_map/prepare/ppermute | solution.py:33
  118.4 22.2 %collective-permute-start.3 = (bf16[400,512]{1,0:T(8,128)(2,1)S(1)}, bf16[400,512]{1,0:T(8,128)(2,1)S(1)}, u32[]{:S(2)}, u32[]{:S(2)}) collective-permute-start(bf16[400,512]{1,0:T(8,128)(2,1)S(1)} %get-tuple-element.30), channel_id=1, source_target_pairs={{0,2},{1,3},{2,0},{3,1},{4,6},{5,7},{6,4},{7,5},{8,10},{9,11},{10,... | collective-permute-start | bytes 1228808 | tf_op jit(solution)/shard_map/gate_up/ppermute | solution.py:37
  124.4 18.2 %collective-permute-start.4 = (bf16[400,512]{1,0:T(8,128)(2,1)S(1)}, bf16[400,512]{1,0:T(8,128)(2,1)S(1)}, u32[]{:S(2)}, u32[]{:S(2)}) collective-permute-start(bf16[400,512]{1,0:T(8,128)(2,1)S(1)} %get-tuple-element.31), channel_id=1, source_target_pairs={{0,1},{1,0},{2,3},{3,2},{4,5},{5,4},{6,7},{7,6},{8,9},{9,8},{10,11... | collective-permute-start | bytes 1228808 | tf_op jit(solution)/shard_map/gate_up/ppermute | solution.py:37

commit v15 on v14

--- a/solution.py
+++ b/solution.py
@@ -1,3 +1,4 @@
+import functools
 import math
 
 import jax
@@ -16,7 +17,7 @@
 EXPERTS = 8
 CAP = 6
 CTX = ("x", "yh", "core")
-PLANE = ("x", "yh")
+PLANE = ("yh", "x")
 F32, BF16 = jnp.float32, jnp.bfloat16
 TAIL = 16
 
@@ -59,14 +60,15 @@
     return lax.dot_general(left, right, (((1,), (1,)), ((), ())), preferred_element_type=F32)
 
 
-def attention_kernel(place, packed, near, far, weight, out, done):
+def attention_kernel(lines, place, packed, near, far, weight, out, done):
     done[...] = jnp.zeros_like(done)
     ctx, core = place[0], place[1]
     rows, keys = packed.shape[0], near.shape[0]
     query = packed[:, 2 * HEAD :]
     spot = ctx * rows + lax.broadcasted_iota(jnp.int32, (rows, keys), 0)
     column = lax.broadcasted_iota(jnp.int32, (rows, keys), 1)
-    base = (column // rows) * (2 * rows) + column % rows
+    block = column // rows
+    base = ((block % lines) * (keys // rows // lines) + block // lines) * (2 * rows) + column % rows
     scores = []
     for half, source in enumerate((near, far)):
         key_spot = base + (core ^ half) * rows
@@ -79,10 +81,12 @@
         denom = denom + jnp.sum(weights, axis=1, keepdims=True)
         total = total + jnp.dot(weights.astype(BF16), source[:, HEAD:], preferred_element_type=F32)
     attended = (total / denom).astype(BF16)
-    parts, _, width = out.shape
+    blocks, parts, tokens, width = out.shape
     for part in range(parts):
         columns = weight[:, part * width : (part + 1) * width]
-        out[part] = jnp.dot(attended, columns, preferred_element_type=F32).astype(BF16)
+        product = jnp.dot(attended, columns, preferred_element_type=F32).astype(BF16)
+        for index in range(blocks):
+            out[index, part] = product[index * tokens : (index + 1) * tokens, :]
 
 
 def prepare_kernel(after, ids, shares, gate, up, selector, mixer, weights, sems):
@@ -123,11 +127,11 @@
     total = residual[...].astype(F32) + mixed
     stream[...] = total
     rows = jnp.dot(selector[...], total.astype(BF16), preferred_element_type=F32)
-    halves, experts, slots, _ = outgoing.shape
+    experts, halves, slots, _ = outgoing.shape
     for expert in range(experts):
         part = rows[expert * slots : (expert + 1) * slots, :].astype(BF16)
         for half in range(halves):
-            outgoing[half, expert] = part
+            outgoing[expert, half] = part
 
 
 def arrange_kernel(arrived, weights, out):
@@ -220,8 +224,7 @@
 
 
 def combine_kernel(back, mixer, stream, out):
-    experts = back.shape[0] // 2
-    rows = [back[e].astype(F32) + back[experts + e].astype(F32) for e in range(experts)]
+    rows = [back[2 * e].astype(F32) + back[2 * e + 1].astype(F32) for e in range(back.shape[0] // 2)]
     combined = lax.dot_general(
         mixer[...],
         jnp.concatenate(rows, axis=0),
@@ -265,8 +268,8 @@
         place = [lax.axis_index(CTX), lax.axis_index("core"), lax.axis_index("hid")]
         place = jnp.stack(place).astype(jnp.int32)
         partials, done = whole(
-            attention_kernel,
-            [shape((hid_count, tok_rows, width_part), BF16), shape((8, 128), F32)],
+            functools.partial(attention_kernel, lines),
+            [shape((exp_count, hid_count, row_count, width_part), BF16), shape((8, 128), F32)],
             flops=2 * tok_rows * HEAD * (4 * plane * tok_rows + D),
             smem=1,
         )(place, packed, near, far, out_weight)
@@ -284,15 +287,15 @@
         near_down = down_weight[0]
         far_weights, far_down = other_core(near_weights), other_core(near_down)
     with jax.named_scope("projection"):
-        arrived = swap(partials.reshape(hid_count * exp_count, row_count, width_part), ("hid", "exp"))
+        arrived = swap(partials.reshape(exp_count * hid_count, row_count, width_part), ("exp", "hid"))
         stream, outgoing = whole(
             select_kernel,
-            [shape((row_count, width_part), F32), shape((halves, exp_count, CAP, width_part), BF16)],
+            [shape((row_count, width_part), F32), shape((exp_count, halves, CAP, width_part), BF16)],
             flops=2 * arrived.size,
         )(arrived, residual, selector)
 
     with jax.named_scope("dispatch"):
-        arrived = swap(outgoing.reshape(halves * exp_count, CAP, width_part), ("yh", "exp"))
+        arrived = swap(outgoing.reshape(exp_count * halves, CAP, width_part), ("exp", "yh"))
         (copies,) = whole(
             arrange_kernel,
             [shape((lines, halves * exp_count * CAP, width_part), BF16)],
@@ -328,7 +331,7 @@
         )(active, near_down, far_down)
         back = swap(back.reshape(lines, count // lines, width_part), "x")
         back = jnp.sum(back.astype(F32), axis=0).astype(BF16)
-        back = swap(back.reshape(halves * exp_count, CAP, width_part), ("yh", "exp"))
+        back = swap(back.reshape(exp_count * halves, CAP, width_part), ("exp", "yh"))
     with jax.named_scope("combine"):
         (out,) = whole(combine_kernel, [shape((row_count, width_part), BF16)], flops=2 * back.size)(
             back, mixer, stream

time: 196 us -> 197 us (level)
  no operation moved by 1% of the time
where the time goes in v15:
time: 197 us; the launch traced here: 196 us
  blocking collectives  87.2 us (44%)
  waiting for transfers between devices  54.2 us (28%)
  starting transfers between devices  37.4 us (19%)
  Pallas kernels  12.8 us (6%)
  local copies, waits for them, and re-layouts  3.56 us (2%)
    all_to_all x4, blocking collectives, swap(): return lax.all_to_all(value, axes, split_axis=0, concat_axis=0, tiled=True)  69.5 us
    all_to_all x2, waiting for transfers between devices, swap(): return lax.all_to_all(value, axes, split_axis=0, concat_axis=0, tiled=True)  34.7 us
    all_to_all x2, starting transfers between devices, swap(): return lax.all_to_all(value, axes, split_axis=0, concat_axis=0, tiled=True)  19.3 us
    all_gather x1, blocking collectives, shards(): active = lax.all_gather(active, 'hid', axis=0, tiled=False)  17.7 us
    ppermute x3, waiting for transfers between devices, to_peer(): lax.ppermute(value, 'hid', [(h, h ^ offset) for h in range(lax.axis_size(...  17.6 us
    pallas_call x10, Pallas kernels, call(): pl.pallas_call(kernel, out_shape=out_shapes, in_specs=[pl.BlockSpec(memor...  12.8 us
    ppermute x3, starting transfers between devices, to_peer(): lax.ppermute(value, 'hid', [(h, h ^ offset) for h in range(lax.axis_size(...  12.4 us
    ppermute x3, starting transfers between devices, other_core(): return lax.ppermute(value, 'core', [(0, 1), (1, 0)])  5.75 us
  transfers between devices with their start and end apart: 8, of which 6 were waited for; matrix products, arithmetic and copies ran while one was open for 0% of the time, Pallas kernels for 3%

profile of v15, /device:TPU:2, one launch (start us, length us, event | category | flops | bytes accessed | tf_op | source)
XLA Modules:
  0.0 196.4 jit_solution(12803875516178514240)
XLA Ops:
  0.0 0.0 copy-start.1
  0.0 0.9 pad_maximum_fusion.packed
  1.0 23.9 %all_to_all.30 = bf16[8,128,256]{2,1,0:T(8,128)(2,1)S(1)} all-to-all(bf16[8,128,256]{2,1,0:T(8,128)(2,1)S(1)} %broadcast_in_dim.2), channel_id=1, replica_groups=mesh['x'=4,'yh'=2,'core'=2,'exp'=8,'hid'=4] {'yh','x'}, dimensions={0} | all-to-all | bytes 1048576 | tf_op jit(solution)/shard_map/kv_gather/all_to_all | solution.py:26
  24.9 1.9 collective-permute-start
  26.8 0.1 pad_add_fusion.place
  26.9 0.0 copy-start.7
  26.9 0.0 copy-start.8
  26.9 1.8 collective-permute-done.far
  28.7 0.0 copy-done.1
  28.7 1.6 attention.1
  30.3 0.0 copy-start.4
  30.3 1.0 copy-done.4
  31.3 0.0 copy-start.5
  31.3 14.8 %all-to-all-start.1 = ((bf16[32,16,1024]{2,1,0:T(8,128)(2,1)}), bf16[32,16,1024]{2,1,0:T(8,128)(2,1)S(1)}, u32[]{:S(2)}, u32[]{:S(2)}) async-start(bf16[32,16,1024]{2,1,0:T(8,128)(2,1)} %bitcast.24), calls=%async_computation.1 | async-start | bytes 2097152 | tf_op jit(solution)/shard_map/projection/all_to_all | solution.py:26
  46.1 0.0 copy-done.7
  46.1 0.0 copy-done.8
  46.1 0.0 copy-start.2
  46.1 1.2 copy-done.2
  47.3 0.0 copy-start.3
  47.3 1.2 copy-done.3
  48.6 2.2 %prepare.1 = (bf16[48,16]{1,0:T(8,128)(2,1)S(1)}, f32[48,16]{1,0:T(8,128)S(1)}, bf16[1024,1024]{1,0:T(8,128)(2,1)}) custom-call(f32[8,128]{1,0:T(8,128)S(1)} %get-tuple-element.21.after, s32[2,16]{1,0:T(2,128)S(1)} %bitcast.26, f32[2,16]{1,0:T(2,128)S(1)} %bitcast.27, bf16[1024,512]{1,0:T(8,128)(2,1)S(1)} %bitcast.22, bf16[1024,512]{1,0:T(8,128)(2,1)S(1)} %bitcast.23), custom_call_target="tpu_custom_call" | custom-call | bytes 4203264 | tf_op jit(solution)/shard_map/prepare/pallas_call | solution.py:46
  50.7 1.9 collective-permute-start.1
  52.7 21.0 %all-to-all-done.1.arrived = bf16[32,16,1024]{2,1,0:T(8,128)(2,1)S(1)} async-done(((bf16[32,16,1024]{2,1,0:T(8,128)(2,1)}), bf16[32,16,1024]{2,1,0:T(8,128)(2,1)S(1)}, u32[]{:S(2)}, u32[]{:S(2)}) %all-to-all-start.1) | async-done | bytes 1048608 | tf_op jit(solution)/shard_map/projection/all_to_all | solution.py:26
  73.7 0.0 copy-done.5
  73.7 1.0 projection.1
  74.7 4.5 %all-to-all-start.2 = ((bf16[16,6,1024]{2,1,0:T(8,128)(2,1)}), bf16[16,6,1024]{2,1,0:T(8,128)(2,1)S(1)}, u32[]{:S(2)}, u32[]{:S(2)}) async-start(bf16[16,6,1024]{2,1,0:T(8,128)(2,1)} %bitcast.9), calls=%async_computation.2 | async-start | bytes 524288 | tf_op jit(solution)/shard_map/dispatch/all_to_all | solution.py:26
  79.3 0.0 copy-start.6
  79.3 0.0 collective-permute-done.1.weights.far
  79.3 13.7 %all-to-all-done.2.arrived = bf16[16,6,1024]{2,1,0:T(8,128)(2,1)S(1)} async-done(((bf16[16,6,1024]{2,1,0:T(8,128)(2,1)}), bf16[16,6,1024]{2,1,0:T(8,128)(2,1)S(1)}, u32[]{:S(2)}, u32[]{:S(2)}) %all-to-all-start.2) | async-done | bytes 196640 | tf_op jit(solution)/shard_map/dispatch/all_to_all | solution.py:26
  93.0 0.1 dispatch.1
  93.0 12.7 %all_to_all.31 = bf16[4,96,1024]{2,1,0:T(8,128)(2,1)S(1)} all-to-all(bf16[4,96,1024]{2,1,0:T(8,128)(2,1)S(1)} %dispatch.1), channel_id=1, replica_groups=mesh['x'=4,'yh'=2,'core'=2,'exp'=8,'hid'=4] {'x'}, dimensions={0} | all-to-all | bytes 1572864 | tf_op jit(solution)/shard_map/dispatch/all_to_all | solution.py:26
  105.8 0.0 copy-done.6
  105.8 0.0 copy-start
  105.8 2.6 %gate_up.3 = (bf16[400,512]{1,0:T(8,128)(2,1)S(1)}, bf16[384,1024]{1,0:T(8,128)(2,1)S(1)}, bf16[16,512]{1,0:T(8,128)(2,1)S(1)}) custom-call(s32[3]{0:T(128)S(1)} %pad_add_fusion.place, bf16[384,1024]{1,0:T(8,128)(2,1)S(1)} %bitcast.17, f32[1,1024]{1,0:T(1,128)S(1)} %bitcast.25, bf16[1024,1024]{1,0:T(8,128)(2,1)} %get-tuple-element.24.near, ...), custom_call_target="tpu_custom_call" | custom-call | flops 402653184 | bytes 6197260 | tf_op jit(solution)/shard_map/gate_up/pallas_call | solution.py:46
  108.4 4.7 %collective-permute-start.2 = (bf16[400,512]{1,0:T(8,128)(2,1)S(1)}, bf16[400,512]{1,0:T(8,128)(2,1)S(1)}, u32[]{:S(2)}, u32[]{:S(2)}) collective-permute-start(bf16[400,512]{1,0:T(8,128)(2,1)S(1)} %get-tuple-element.28), channel_id=1, source_target_pairs={{0,1},{1,0},{2,3},{3,2},{4,5},{5,4},{6,7},{7,6},{8,9},{9,8},{10,11... | collective-permute-start | bytes 1228808 | tf_op jit(solution)/shard_map/gate_up/ppermute | solution.py:38
  113.1 0.0 copy-done
  113.1 1.9 collective-permute-start.5
  115.0 3.0 %gate_up.4 = (bf16[400,512]{1,0:T(8,128)(2,1)S(1)}, bf16[400,512]{1,0:T(8,128)(2,1)S(1)}, bf16[400,512]{1,0:T(8,128)(2,1)S(1)}) custom-call(s32[3]{0:T(128)S(1)} %pad_add_fusion.place, bf16[384,1024]{1,0:T(8,128)(2,1)S(1)} %get-tuple-element.25.scaled, bf16[16,512]{1,0:T(8,128)(2,1)S(1)} %get-tuple-element.26.tail, ...), custom_call_target="tpu_custom_call" | custom-call | flops 1207959552 | bytes 6225932 | tf_op jit(solution)/shard_map/gate_up/pallas_call | solution.py:46
  118.0 0.9 collective-permute-done.2.arrived
  119.0 0.1 gate_up.5
  119.1 4.9 %collective-permute-start.3 = (bf16[400,512]{1,0:T(8,128)(2,1)S(1)}, bf16[400,512]{1,0:T(8,128)(2,1)S(1)}, u32[]{:S(2)}, u32[]{:S(2)}) collective-permute-start(bf16[400,512]{1,0:T(8,128)(2,1)S(1)} %get-tuple-element.30), channel_id=1, source_target_pairs={{0,2},{1,3},{2,0},{3,1},{4,6},{5,7},{6,4},{7,5},{8,10},{9,11},{10,... | collective-permute-start | bytes 1228808 | tf_op jit(solution)/shard_map/gate_up/ppermute | solution.py:38
  124.0 2.8 %collective-permute-start.4 = (bf16[400,512]{1,0:T(8,128)(2,1)S(1)}, bf16[400,512]{1,0:T(8,128)(2,1)S(1)}, u32[]{:S(2)}, u32[]{:S(2)}) collective-permute-start(bf16[400,512]{1,0:T(8,128)(2,1)S(1)} %get-tuple-element.31), channel_id=1, source_target_pairs={{0,1},{1,0},{2,3},{3,2},{4,5},{5,4},{6,7},{7,6},{8,9},{9,8},{10,11... | collective-permute-start | bytes 1228808 | tf_op jit(solution)/shard_map/gate_up/ppermute | solution.py:38
  126.8 14.7 %collective-permute-done.3.refs_0_ = bf16[400,512]{1,0:T(8,128)(2,1)S(1)} collective-permute-done((bf16[400,512]{1,0:T(8,128)(2,1)S(1)}, bf16[400,512]{1,0:T(8,128)(2,1)S(1)}, u32[]{:S(2)}, u32[]{:S(2)}) %collective-permute-start.3) | collective-permute-done | bytes 409632 | tf_op jit(solution)/shard_map/gate_up/ppermute | solution.py:38
  141.5 2.0 %collective-permute-done.4.refs_1_ = bf16[400,512]{1,0:T(8,128)(2,1)S(1)} collective-permute-done((bf16[400,512]{1,0:T(8,128)(2,1)S(1)}, bf16[400,512]{1,0:T(8,128)(2,1)S(1)}, u32[]{:S(2)}, u32[]{:S(2)}) %collective-permute-start.4) | collective-permute-done | bytes 409632 | tf_op jit(solution)/shard_map/gate_up/ppermute | solution.py:38
  143.5 0.3 active.1
  143.8 17.7 %all-gather = bf16[3072,128]{1,0:T(8,128)(2,1)S(1)} all-gather(bf16[768,128]{1,0:T(8,128)(2,1)S(1)} %active.1), channel_id=2, replica_groups=mesh['x'=4,'yh'=2,'core'=2,'exp'=8,'hid'=4] {'hid'}, dimensions={0}, use_global_device_ids=true | all-gather | bytes 983040 | tf_op jit(solution)/shard_map/active/all_gather | solution.py:327
  161.5 0.0 collective-permute-done.5.far
  161.5 1.0 down.1
  162.5 11.9 %all_to_all.32 = bf16[4,96,1024]{2,1,0:T(8,128)(2,1)S(1)} all-to-all(bf16[4,96,1024]{2,1,0:T(8,128)(2,1)S(1)} %bitcast.15), channel_id=1, replica_groups=mesh['x'=4,'yh'=2,'core'=2,'exp'=8,'hid'=4] {'x'}, dimensions={0} | all-to-all | bytes 1572864 | tf_op jit(solution)/shard_map/down/all_to_all | solution.py:26
  174.4 0.1 reduce_sum.12
  174.5 0.1 reshape.28
  174.6 20.9 %all_to_all.33.back = bf16[16,6,1024]{2,1,0:T(8,128)(2,1)S(1)} all-to-all(bf16[16,6,1024]{2,1,0:T(8,128)(2,1)S(1)} %reshape.28), channel_id=1, replica_groups=mesh['x'=4,'yh'=2,'core'=2,'exp'=8,'hid'=4] {'exp','yh'}, dimensions={0} | all-to-all | bytes 393216 | tf_op jit(solution)/shard_map/down/all_to_all | solution.py:26
  195.5 0.9 combine.1
  (2 shorter events, 0.0 us)
Async XLA Ops:
  0.0 28.7 %copy-start.1 = (bf16[128,4096]{1,0:T(8,128)(2,1)S(1)}, bf16[128,4096]{1,0:T(8,128)(2,1)}, u32[]{:S(2)}) copy-start(bf16[128,4096]{1,0:T(8,128)(2,1)} %weight.1) | copy-start | bytes 3145732
  24.9 3.8 %collective-permute-start = (bf16[1024,256]{1,0:T(8,128)(2,1)S(1)}, bf16[1024,256]{1,0:T(8,128)(2,1)S(1)}, u32[]{:S(2)}, u32[]{:S(2)}) collective-permute-start(bf16[1024,256]{1,0:T(8,128)(2,1)S(1)} %bitcast.18), channel_id=1, source_target_pairs={{0,32},{32,0},{1,33},{33,1},{2,34},{34,2},{3,35},{35,3},{4,36},{36... | collective-permute-start | bytes 1572872 | tf_op jit(solution)/shard_map/kv_gather/ppermute | solution.py:34
  26.9 19.2 %copy-start.7 = (s32[16,2]{0,1:T(2,128)S(1)}, s32[16,2]{0,1:T(2,128)}, u32[]{:S(2)}) copy-start(s32[16,2]{0,1:T(2,128)} %param.20) | copy-start | bytes 388
  26.9 19.2 %copy-start.8 = (f32[16,2]{0,1:T(2,128)S(1)}, f32[16,2]{0,1:T(2,128)}, u32[]{:S(2)}) copy-start(f32[16,2]{0,1:T(2,128)} %param.21) | copy-start | bytes 388
  30.3 1.0 copy-start.4
  31.3 42.4 %copy-start.5 = (bf16[16,1024]{1,0:T(8,128)(2,1)S(1)}, bf16[16,1024]{1,0:T(8,128)(2,1)}, u32[]{:S(2)}) copy-start(bf16[16,1024]{1,0:T(8,128)(2,1)} %residual.1) | copy-start | bytes 98308
  31.3 42.4 %all-to-all-start.1 = ((bf16[32,16,1024]{2,1,0:T(8,128)(2,1)}), bf16[32,16,1024]{2,1,0:T(8,128)(2,1)S(1)}, u32[]{:S(2)}, u32[]{:S(2)}) async-start(bf16[32,16,1024]{2,1,0:T(8,128)(2,1)} %bitcast.24), calls=%async_computation.1 | async-start | bytes 2097152 | tf_op jit(solution)/shard_map/projection/all_to_all | solution.py:26
  46.1 1.2 copy-start.2
  47.3 1.2 copy-start.3
  50.7 28.5 %collective-permute-start.1 = (bf16[1024,1024]{1,0:T(8,128)(2,1)}, bf16[1024,1024]{1,0:T(8,128)(2,1)S(1)}, u32[]{:S(2)}, u32[]{:S(2)}) collective-permute-start(bf16[1024,1024]{1,0:T(8,128)(2,1)} %get-tuple-element.24.near), channel_id=1, source_target_pairs={{0,32},{32,0},{1,33},{33,1},{2,34},{34,2},{3,35},{35,3},{4,36},{36... | collective-permute-start | bytes 6291464 | tf_op jit(solution)/shard_map/prepare/ppermute | solution.py:34
  74.7 18.3 %all-to-all-start.2 = ((bf16[16,6,1024]{2,1,0:T(8,128)(2,1)}), bf16[16,6,1024]{2,1,0:T(8,128)(2,1)S(1)}, u32[]{:S(2)}, u32[]{:S(2)}) async-start(bf16[16,6,1024]{2,1,0:T(8,128)(2,1)} %bitcast.9), calls=%async_computation.2 | async-start | bytes 524288 | tf_op jit(solution)/shard_map/dispatch/all_to_all | solution.py:26
  79.3 26.5 %copy-start.6 = (f32[1024]{0:T(1024)S(1)}, f32[1024]{0:T(1024)}, u32[]{:S(2)}) copy-start(f32[1024]{0:T(1024)} %param.16) | copy-start | bytes 12292
  105.8 7.3 %copy-start = (bf16[1,512,1024]{2,1,0:T(8,128)(2,1)S(1)}, bf16[1,512,1024]{2,1,0:T(8,128)(2,1)}, u32[]{:S(2)}) copy-start(bf16[1,512,1024]{2,1,0:T(8,128)(2,1)} %param.19) | copy-start | bytes 3145732
  108.4 10.6 %collective-permute-start.2 = (bf16[400,512]{1,0:T(8,128)(2,1)S(1)}, bf16[400,512]{1,0:T(8,128)(2,1)S(1)}, u32[]{:S(2)}, u32[]{:S(2)}) collective-permute-start(bf16[400,512]{1,0:T(8,128)(2,1)S(1)} %get-tuple-element.28), channel_id=1, source_target_pairs={{0,1},{1,0},{2,3},{3,2},{4,5},{5,4},{6,7},{7,6},{8,9},{9,8},{10,11... | collective-permute-start | bytes 1228808 | tf_op jit(solution)/shard_map/gate_up/ppermute | solution.py:38
  113.1 48.4 %collective-permute-start.5 = (bf16[512,1024]{1,0:T(8,128)(2,1)S(1)}, bf16[512,1024]{1,0:T(8,128)(2,1)S(1)}, u32[]{:S(2)}, u32[]{:S(2)}) collective-permute-start(bf16[512,1024]{1,0:T(8,128)(2,1)S(1)} %bitcast.20), channel_id=1, source_target_pairs={{0,32},{32,0},{1,33},{33,1},{2,34},{34,2},{3,35},{35,3},{4,36},{36... | collective-permute-start | bytes 3145736 | tf_op jit(solution)/shard_map/prepare/ppermute | solution.py:34
  119.1 22.4 %collective-permute-start.3 = (bf16[400,512]{1,0:T(8,128)(2,1)S(1)}, bf16[400,512]{1,0:T(8,128)(2,1)S(1)}, u32[]{:S(2)}, u32[]{:S(2)}) collective-permute-start(bf16[400,512]{1,0:T(8,128)(2,1)S(1)} %get-tuple-element.30), channel_id=1, source_target_pairs={{0,2},{1,3},{2,0},{3,1},{4,6},{5,7},{6,4},{7,5},{8,10},{9,11},{10,... | collective-permute-start | bytes 1228808 | tf_op jit(solution)/shard_map/gate_up/ppermute | solution.py:38
  124.0 19.5 %collective-permute-start.4 = (bf16[400,512]{1,0:T(8,128)(2,1)S(1)}, bf16[400,512]{1,0:T(8,128)(2,1)S(1)}, u32[]{:S(2)}, u32[]{:S(2)}) collective-permute-start(bf16[400,512]{1,0:T(8,128)(2,1)S(1)} %get-tuple-element.31), channel_id=1, source_target_pairs={{0,1},{1,0},{2,3},{3,2},{4,5},{5,4},{6,7},{7,6},{8,9},{9,8},{10,11... | collective-permute-start | bytes 1228808 | tf_op jit(solution)/shard_map/gate_up/ppermute | solution.py:38

commit v16 on v14

--- a/solution.py
+++ b/solution.py
@@ -79,10 +79,12 @@
         denom = denom + jnp.sum(weights, axis=1, keepdims=True)
         total = total + jnp.dot(weights.astype(BF16), source[:, HEAD:], preferred_element_type=F32)
     attended = (total / denom).astype(BF16)
-    parts, _, width = out.shape
+    blocks, parts, tokens, width = out.shape
     for part in range(parts):
         columns = weight[:, part * width : (part + 1) * width]
-        out[part] = jnp.dot(attended, columns, preferred_element_type=F32).astype(BF16)
+        product = jnp.dot(attended, columns, preferred_element_type=F32).astype(BF16)
+        for index in range(blocks):
+            out[index, part] = product[index * tokens : (index + 1) * tokens, :]
 
 
 def prepare_kernel(after, ids, shares, gate, up, selector, mixer, weights, sems):
@@ -163,12 +165,12 @@
     widened = rows[...].astype(F32)
     scaled = (widened * gain[...]).astype(BF16)
     scaled_out[...] = scaled
-    square = widened * widened
-    high = square.astype(BF16)
-    low = (square - high.astype(F32)).astype(BF16)
-    ones = jnp.ones((TAIL, depth), BF16)
-    norm = (dot_nt(ones, high) + dot_nt(ones, low))[:1, :]
-    norm = jnp.concatenate([norm, jnp.zeros((1, third.shape[1] - count), F32)], axis=1)
+    same = lax.broadcasted_iota(jnp.int32, (128, 128), 0) == lax.broadcasted_iota(jnp.int32, (128, 128), 1)
+    norms = []
+    for first in range(0, count, 128):
+        block = rows[first : first + 128, :]
+        norms.append(jnp.sum(jnp.where(same, dot_nt(block, block), 0.0), axis=0, keepdims=True))
+    norm = jnp.concatenate(norms + [jnp.zeros((1, third.shape[1] - count), F32)], axis=1)
     tail = tail_of(norm, TAIL)
     third[count:, :] = tail
     tail_out[...] = tail
@@ -266,7 +268,7 @@
         place = jnp.stack(place).astype(jnp.int32)
         partials, done = whole(
             attention_kernel,
-            [shape((hid_count, tok_rows, width_part), BF16), shape((8, 128), F32)],
+            [shape((exp_count, hid_count, row_count, width_part), BF16), shape((8, 128), F32)],
             flops=2 * tok_rows * HEAD * (4 * plane * tok_rows + D),
             smem=1,
         )(place, packed, near, far, out_weight)
@@ -284,7 +286,7 @@
         near_down = down_weight[0]
         far_weights, far_down = other_core(near_weights), other_core(near_down)
     with jax.named_scope("projection"):
-        arrived = swap(partials.reshape(hid_count * exp_count, row_count, width_part), ("hid", "exp"))
+        arrived = swap(partials.reshape(exp_count * hid_count, row_count, width_part), ("exp", "hid"))
         stream, outgoing = whole(
             select_kernel,
             [shape((row_count, width_part), F32), shape((halves, exp_count, CAP, width_part), BF16)],

time: 196 us -> 196 us (level)
  no operation moved by 1% of the time
where the time goes in v16:
time: 196 us
  blocking collectives  88 us (45%)
  waiting for transfers between devices  52.5 us (27%)
  starting transfers between devices  37.5 us (19%)
  Pallas kernels  12.8 us (7%)
  local copies, waits for them, and re-layouts  3.56 us (2%)
    all_to_all x4, blocking collectives, swap(): return lax.all_to_all(value, axes, split_axis=0, concat_axis=0, tiled=True)  69.8 us
    all_to_all x2, waiting for transfers between devices, swap(): return lax.all_to_all(value, axes, split_axis=0, concat_axis=0, tiled=True)  33.7 us
    all_to_all x2, starting transfers between devices, swap(): return lax.all_to_all(value, axes, split_axis=0, concat_axis=0, tiled=True)  18.4 us
    all_gather x1, blocking collectives, shards(): active = lax.all_gather(active, 'hid', axis=0, tiled=False)  18.2 us
    ppermute x3, waiting for transfers between devices, to_peer(): lax.ppermute(value, 'hid', [(h, h ^ offset) for h in range(lax.axis_size(...  17 us
    ppermute x3, starting transfers between devices, to_peer(): lax.ppermute(value, 'hid', [(h, h ^ offset) for h in range(lax.axis_size(...  13.3 us
    pallas_call x10, Pallas kernels, call(): pl.pallas_call(kernel, out_shape=out_shapes, in_specs=[pl.BlockSpec(memor...  12.8 us
    ppermute x3, starting transfers between devices, other_core(): return lax.ppermute(value, 'core', [(0, 1), (1, 0)])  5.75 us
  transfers between devices with their start and end apart: 8, of which 6 were waited for; matrix products, arithmetic and copies ran while one was open for 0% of the time, Pallas kernels for 3%

profile of v16, /device:TPU:2, one launch (start us, length us, event | category | flops | bytes accessed | tf_op | source)
XLA Modules:
  0.0 195.7 jit_solution(16205938566806398418)
XLA Ops:
  0.0 0.0 copy-start.1
  0.0 0.9 pad_maximum_fusion.packed
  1.0 25.2 %all_to_all.30 = bf16[8,128,256]{2,1,0:T(8,128)(2,1)S(1)} all-to-all(bf16[8,128,256]{2,1,0:T(8,128)(2,1)S(1)} %broadcast_in_dim.2), channel_id=1, replica_groups=mesh['x'=4,'yh'=2,'core'=2,'exp'=8,'hid'=4] {'x','yh'}, dimensions={0} | all-to-all | bytes 1048576 | tf_op jit(solution)/shard_map/kv_gather/all_to_all | solution.py:25
  26.1 1.9 collective-permute-start
  28.0 0.1 pad_add_fusion.place
  28.1 0.0 copy-start.7
  28.1 0.0 copy-start.8
  28.1 1.8 collective-permute-done.far
  29.9 0.0 copy-done.1
  29.9 1.6 attention.1
  31.6 0.0 copy-start.4
  31.6 1.0 copy-done.4
  32.5 0.0 copy-start.5
  32.5 13.6 %all-to-all-start.1 = ((bf16[32,16,1024]{2,1,0:T(8,128)(2,1)}), bf16[32,16,1024]{2,1,0:T(8,128)(2,1)S(1)}, u32[]{:S(2)}, u32[]{:S(2)}) async-start(bf16[32,16,1024]{2,1,0:T(8,128)(2,1)} %bitcast.24), calls=%async_computation.1 | async-start | bytes 2097152 | tf_op jit(solution)/shard_map/projection/all_to_all | solution.py:25
  46.2 0.0 copy-done.7
  46.2 0.0 copy-done.8
  46.2 0.0 copy-start.2
  46.2 1.2 copy-done.2
  47.4 0.0 copy-start.3
  47.4 1.2 copy-done.3
  48.7 2.2 %prepare.1 = (bf16[48,16]{1,0:T(8,128)(2,1)S(1)}, f32[48,16]{1,0:T(8,128)S(1)}, bf16[1024,1024]{1,0:T(8,128)(2,1)}) custom-call(f32[8,128]{1,0:T(8,128)S(1)} %get-tuple-element.21.after, s32[2,16]{1,0:T(2,128)S(1)} %bitcast.26, f32[2,16]{1,0:T(2,128)S(1)} %bitcast.27, bf16[1024,512]{1,0:T(8,128)(2,1)S(1)} %bitcast.22, bf16[1024,512]{1,0:T(8,128)(2,1)S(1)} %bitcast.23), custom_call_target="tpu_custom_call" | custom-call | bytes 4203264 | tf_op jit(solution)/shard_map/prepare/pallas_call | solution.py:45
  50.9 1.9 collective-permute-start.1
  52.8 21.0 %all-to-all-done.1.arrived = bf16[32,16,1024]{2,1,0:T(8,128)(2,1)S(1)} async-done(((bf16[32,16,1024]{2,1,0:T(8,128)(2,1)}), bf16[32,16,1024]{2,1,0:T(8,128)(2,1)S(1)}, u32[]{:S(2)}, u32[]{:S(2)}) %all-to-all-start.1) | async-done | bytes 1048608 | tf_op jit(solution)/shard_map/projection/all_to_all | solution.py:25
  73.8 0.0 copy-done.5
  73.8 1.0 projection.1
  74.8 4.8 %all-to-all-start.2 = ((bf16[16,6,1024]{2,1,0:T(8,128)(2,1)}), bf16[16,6,1024]{2,1,0:T(8,128)(2,1)S(1)}, u32[]{:S(2)}, u32[]{:S(2)}) async-start(bf16[16,6,1024]{2,1,0:T(8,128)(2,1)} %bitcast.9), calls=%async_computation.2 | async-start | bytes 524288 | tf_op jit(solution)/shard_map/dispatch/all_to_all | solution.py:25
  79.6 0.0 copy-start.6
  79.6 0.0 collective-permute-done.1.weights.far
  79.6 12.6 %all-to-all-done.2.arrived = bf16[16,6,1024]{2,1,0:T(8,128)(2,1)S(1)} async-done(((bf16[16,6,1024]{2,1,0:T(8,128)(2,1)}), bf16[16,6,1024]{2,1,0:T(8,128)(2,1)S(1)}, u32[]{:S(2)}, u32[]{:S(2)}) %all-to-all-start.2) | async-done | bytes 196640 | tf_op jit(solution)/shard_map/dispatch/all_to_all | solution.py:25
  92.3 0.1 dispatch.1
  92.3 12.4 %all_to_all.31 = bf16[4,96,1024]{2,1,0:T(8,128)(2,1)S(1)} all-to-all(bf16[4,96,1024]{2,1,0:T(8,128)(2,1)S(1)} %dispatch.1), channel_id=1, replica_groups=mesh['x'=4,'yh'=2,'core'=2,'exp'=8,'hid'=4] {'x'}, dimensions={0} | all-to-all | bytes 1572864 | tf_op jit(solution)/shard_map/dispatch/all_to_all | solution.py:25
  104.7 0.0 copy-done.6
  104.7 0.0 copy-start
  104.7 2.7 %gate_up.3 = (bf16[400,512]{1,0:T(8,128)(2,1)S(1)}, bf16[384,1024]{1,0:T(8,128)(2,1)S(1)}, bf16[16,512]{1,0:T(8,128)(2,1)S(1)}) custom-call(s32[3]{0:T(128)S(1)} %pad_add_fusion.place, bf16[384,1024]{1,0:T(8,128)(2,1)S(1)} %bitcast.17, f32[1,1024]{1,0:T(1,128)S(1)} %bitcast.25, bf16[1024,1024]{1,0:T(8,128)(2,1)} %get-tuple-element.24.near, ...), custom_call_target="tpu_custom_call" | custom-call | flops 402653184 | bytes 6197260 | tf_op jit(solution)/shard_map/gate_up/pallas_call | solution.py:45
  107.4 4.8 %collective-permute-start.2 = (bf16[400,512]{1,0:T(8,128)(2,1)S(1)}, bf16[400,512]{1,0:T(8,128)(2,1)S(1)}, u32[]{:S(2)}, u32[]{:S(2)}) collective-permute-start(bf16[400,512]{1,0:T(8,128)(2,1)S(1)} %get-tuple-element.28), channel_id=1, source_target_pairs={{0,1},{1,0},{2,3},{3,2},{4,5},{5,4},{6,7},{7,6},{8,9},{9,8},{10,11... | collective-permute-start | bytes 1228808 | tf_op jit(solution)/shard_map/gate_up/ppermute | solution.py:37
  112.2 0.0 copy-done
  112.2 1.9 collective-permute-start.5
  114.1 3.0 %gate_up.4 = (bf16[400,512]{1,0:T(8,128)(2,1)S(1)}, bf16[400,512]{1,0:T(8,128)(2,1)S(1)}, bf16[400,512]{1,0:T(8,128)(2,1)S(1)}) custom-call(s32[3]{0:T(128)S(1)} %pad_add_fusion.place, bf16[384,1024]{1,0:T(8,128)(2,1)S(1)} %get-tuple-element.25.scaled, bf16[16,512]{1,0:T(8,128)(2,1)S(1)} %get-tuple-element.26.tail, ...), custom_call_target="tpu_custom_call" | custom-call | flops 1207959552 | bytes 6225932 | tf_op jit(solution)/shard_map/gate_up/pallas_call | solution.py:45
  117.2 0.9 collective-permute-done.2.arrived
  118.1 0.1 gate_up.5
  118.2 6.3 %collective-permute-start.3 = (bf16[400,512]{1,0:T(8,128)(2,1)S(1)}, bf16[400,512]{1,0:T(8,128)(2,1)S(1)}, u32[]{:S(2)}, u32[]{:S(2)}) collective-permute-start(bf16[400,512]{1,0:T(8,128)(2,1)S(1)} %get-tuple-element.30), channel_id=1, source_target_pairs={{0,2},{1,3},{2,0},{3,1},{4,6},{5,7},{6,4},{7,5},{8,10},{9,11},{10,... | collective-permute-start | bytes 1228808 | tf_op jit(solution)/shard_map/gate_up/ppermute | solution.py:37
  124.6 2.2 %collective-permute-start.4 = (bf16[400,512]{1,0:T(8,128)(2,1)S(1)}, bf16[400,512]{1,0:T(8,128)(2,1)S(1)}, u32[]{:S(2)}, u32[]{:S(2)}) collective-permute-start(bf16[400,512]{1,0:T(8,128)(2,1)S(1)} %get-tuple-element.31), channel_id=1, source_target_pairs={{0,1},{1,0},{2,3},{3,2},{4,5},{5,4},{6,7},{7,6},{8,9},{9,8},{10,11... | collective-permute-start | bytes 1228808 | tf_op jit(solution)/shard_map/gate_up/ppermute | solution.py:37
  126.8 14.1 %collective-permute-done.3.refs_0_ = bf16[400,512]{1,0:T(8,128)(2,1)S(1)} collective-permute-done((bf16[400,512]{1,0:T(8,128)(2,1)S(1)}, bf16[400,512]{1,0:T(8,128)(2,1)S(1)}, u32[]{:S(2)}, u32[]{:S(2)}) %collective-permute-start.3) | collective-permute-done | bytes 409632 | tf_op jit(solution)/shard_map/gate_up/ppermute | solution.py:37
  140.8 2.0 %collective-permute-done.4.refs_1_ = bf16[400,512]{1,0:T(8,128)(2,1)S(1)} collective-permute-done((bf16[400,512]{1,0:T(8,128)(2,1)S(1)}, bf16[400,512]{1,0:T(8,128)(2,1)S(1)}, u32[]{:S(2)}, u32[]{:S(2)}) %collective-permute-start.4) | collective-permute-done | bytes 409632 | tf_op jit(solution)/shard_map/gate_up/ppermute | solution.py:37
  142.8 0.3 active.1
  143.1 18.2 %all-gather = bf16[3072,128]{1,0:T(8,128)(2,1)S(1)} all-gather(bf16[768,128]{1,0:T(8,128)(2,1)S(1)} %active.1), channel_id=2, replica_groups=mesh['x'=4,'yh'=2,'core'=2,'exp'=8,'hid'=4] {'hid'}, dimensions={0}, use_global_device_ids=true | all-gather | bytes 983040 | tf_op jit(solution)/shard_map/active/all_gather | solution.py:326
  161.3 0.0 collective-permute-done.5.far
  161.3 1.0 down.1
  162.3 11.9 %all_to_all.32 = bf16[4,96,1024]{2,1,0:T(8,128)(2,1)S(1)} all-to-all(bf16[4,96,1024]{2,1,0:T(8,128)(2,1)S(1)} %bitcast.15), channel_id=1, replica_groups=mesh['x'=4,'yh'=2,'core'=2,'exp'=8,'hid'=4] {'x'}, dimensions={0} | all-to-all | bytes 1572864 | tf_op jit(solution)/shard_map/down/all_to_all | solution.py:25
  174.2 0.1 reduce_sum.12
  174.3 0.1 reshape.28
  174.4 20.4 %all_to_all.33.back = bf16[16,6,1024]{2,1,0:T(8,128)(2,1)S(1)} all-to-all(bf16[16,6,1024]{2,1,0:T(8,128)(2,1)S(1)} %reshape.28), channel_id=1, replica_groups=mesh['x'=4,'yh'=2,'core'=2,'exp'=8,'hid'=4] {'yh','exp'}, dimensions={0} | all-to-all | bytes 393216 | tf_op jit(solution)/shard_map/down/all_to_all | solution.py:25
  194.8 0.9 combine.1
  (2 shorter events, 0.0 us)
Async XLA Ops:
  0.0 29.9 %copy-start.1 = (bf16[128,4096]{1,0:T(8,128)(2,1)S(1)}, bf16[128,4096]{1,0:T(8,128)(2,1)}, u32[]{:S(2)}) copy-start(bf16[128,4096]{1,0:T(8,128)(2,1)} %weight.1) | copy-start | bytes 3145732
  26.1 3.8 %collective-permute-start = (bf16[1024,256]{1,0:T(8,128)(2,1)S(1)}, bf16[1024,256]{1,0:T(8,128)(2,1)S(1)}, u32[]{:S(2)}, u32[]{:S(2)}) collective-permute-start(bf16[1024,256]{1,0:T(8,128)(2,1)S(1)} %bitcast.18), channel_id=1, source_target_pairs={{0,32},{32,0},{1,33},{33,1},{2,34},{34,2},{3,35},{35,3},{4,36},{36... | collective-permute-start | bytes 1572872 | tf_op jit(solution)/shard_map/kv_gather/ppermute | solution.py:33
  28.1 18.1 %copy-start.7 = (s32[16,2]{0,1:T(2,128)S(1)}, s32[16,2]{0,1:T(2,128)}, u32[]{:S(2)}) copy-start(s32[16,2]{0,1:T(2,128)} %param.20) | copy-start | bytes 388
  28.1 18.1 %copy-start.8 = (f32[16,2]{0,1:T(2,128)S(1)}, f32[16,2]{0,1:T(2,128)}, u32[]{:S(2)}) copy-start(f32[16,2]{0,1:T(2,128)} %param.21) | copy-start | bytes 388
  31.6 1.0 copy-start.4
  32.5 41.3 %copy-start.5 = (bf16[16,1024]{1,0:T(8,128)(2,1)S(1)}, bf16[16,1024]{1,0:T(8,128)(2,1)}, u32[]{:S(2)}) copy-start(bf16[16,1024]{1,0:T(8,128)(2,1)} %residual.1) | copy-start | bytes 98308
  32.5 41.3 %all-to-all-start.1 = ((bf16[32,16,1024]{2,1,0:T(8,128)(2,1)}), bf16[32,16,1024]{2,1,0:T(8,128)(2,1)S(1)}, u32[]{:S(2)}, u32[]{:S(2)}) async-start(bf16[32,16,1024]{2,1,0:T(8,128)(2,1)} %bitcast.24), calls=%async_computation.1 | async-start | bytes 2097152 | tf_op jit(solution)/shard_map/projection/all_to_all | solution.py:25
  46.2 1.2 copy-start.2
  47.4 1.2 copy-start.3
  50.9 28.8 %collective-permute-start.1 = (bf16[1024,1024]{1,0:T(8,128)(2,1)}, bf16[1024,1024]{1,0:T(8,128)(2,1)S(1)}, u32[]{:S(2)}, u32[]{:S(2)}) collective-permute-start(bf16[1024,1024]{1,0:T(8,128)(2,1)} %get-tuple-element.24.near), channel_id=1, source_target_pairs={{0,32},{32,0},{1,33},{33,1},{2,34},{34,2},{3,35},{35,3},{4,36},{36... | collective-permute-start | bytes 6291464 | tf_op jit(solution)/shard_map/prepare/ppermute | solution.py:33
  74.8 17.5 %all-to-all-start.2 = ((bf16[16,6,1024]{2,1,0:T(8,128)(2,1)}), bf16[16,6,1024]{2,1,0:T(8,128)(2,1)S(1)}, u32[]{:S(2)}, u32[]{:S(2)}) async-start(bf16[16,6,1024]{2,1,0:T(8,128)(2,1)} %bitcast.9), calls=%async_computation.2 | async-start | bytes 524288 | tf_op jit(solution)/shard_map/dispatch/all_to_all | solution.py:25
  79.6 25.1 %copy-start.6 = (f32[1024]{0:T(1024)S(1)}, f32[1024]{0:T(1024)}, u32[]{:S(2)}) copy-start(f32[1024]{0:T(1024)} %param.16) | copy-start | bytes 12292
  104.7 7.4 %copy-start = (bf16[1,512,1024]{2,1,0:T(8,128)(2,1)S(1)}, bf16[1,512,1024]{2,1,0:T(8,128)(2,1)}, u32[]{:S(2)}) copy-start(bf16[1,512,1024]{2,1,0:T(8,128)(2,1)} %param.19) | copy-start | bytes 3145732
  107.4 10.7 %collective-permute-start.2 = (bf16[400,512]{1,0:T(8,128)(2,1)S(1)}, bf16[400,512]{1,0:T(8,128)(2,1)S(1)}, u32[]{:S(2)}, u32[]{:S(2)}) collective-permute-start(bf16[400,512]{1,0:T(8,128)(2,1)S(1)} %get-tuple-element.28), channel_id=1, source_target_pairs={{0,1},{1,0},{2,3},{3,2},{4,5},{5,4},{6,7},{7,6},{8,9},{9,8},{10,11... | collective-permute-start | bytes 1228808 | tf_op jit(solution)/shard_map/gate_up/ppermute | solution.py:37
  112.2 49.1 %collective-permute-start.5 = (bf16[512,1024]{1,0:T(8,128)(2,1)S(1)}, bf16[512,1024]{1,0:T(8,128)(2,1)S(1)}, u32[]{:S(2)}, u32[]{:S(2)}) collective-permute-start(bf16[512,1024]{1,0:T(8,128)(2,1)S(1)} %bitcast.20), channel_id=1, source_target_pairs={{0,32},{32,0},{1,33},{33,1},{2,34},{34,2},{3,35},{35,3},{4,36},{36... | collective-permute-start | bytes 3145736 | tf_op jit(solution)/shard_map/prepare/ppermute | solution.py:33
  118.2 22.6 %collective-permute-start.3 = (bf16[400,512]{1,0:T(8,128)(2,1)S(1)}, bf16[400,512]{1,0:T(8,128)(2,1)S(1)}, u32[]{:S(2)}, u32[]{:S(2)}) collective-permute-start(bf16[400,512]{1,0:T(8,128)(2,1)S(1)} %get-tuple-element.30), channel_id=1, source_target_pairs={{0,2},{1,3},{2,0},{3,1},{4,6},{5,7},{6,4},{7,5},{8,10},{9,11},{10,... | collective-permute-start | bytes 1228808 | tf_op jit(solution)/shard_map/gate_up/ppermute | solution.py:37
  124.6 18.3 %collective-permute-start.4 = (bf16[400,512]{1,0:T(8,128)(2,1)S(1)}, bf16[400,512]{1,0:T(8,128)(2,1)S(1)}, u32[]{:S(2)}, u32[]{:S(2)}) collective-permute-start(bf16[400,512]{1,0:T(8,128)(2,1)S(1)} %get-tuple-element.31), channel_id=1, source_target_pairs={{0,1},{1,0},{2,3},{3,2},{4,5},{5,4},{6,7},{7,6},{8,9},{9,8},{10,11... | collective-permute-start | bytes 1228808 | tf_op jit(solution)/shard_map/gate_up/ppermute | solution.py:37

commit v17 on v14

--- a/solution.py
+++ b/solution.py
@@ -130,7 +130,7 @@
             outgoing[half, expert] = part
 
 
-def arrange_kernel(arrived, weights, out):
+def arrange_kernel(arrived, weights, down, out):
     rows = jnp.concatenate([arrived[index].astype(F32) for index in range(arrived.shape[0])], axis=0).astype(BF16)
     for index in range(out.shape[0]):
         out[index] = rows
@@ -297,8 +297,8 @@
             arrange_kernel,
             [shape((lines, halves * exp_count * CAP, width_part), BF16)],
             flops=0,
-            held=1,
-        )(arrived, far_weights)
+            held=2,
+        )(arrived, far_weights, far_down)
         arrived = swap(copies, "x")
         count = lines * halves * exp_count * CAP
         rows = arrived.reshape(count, width_part)

time: 196 us -> 199 us (1.015)
  no operation moved by 1% of the time
where the time goes in v17:
time: 199 us; the launch traced here: 198 us
  blocking collectives  88.8 us (45%)
  waiting for transfers between devices  53.1 us (27%)
  starting transfers between devices  37 us (19%)
  Pallas kernels  14.5 us (7%)
  local copies, waits for them, and re-layouts  3.03 us (2%)
    all_to_all x4, blocking collectives, swap(): return lax.all_to_all(value, axes, split_axis=0, concat_axis=0, tiled=True)  71.8 us
    all_to_all x2, waiting for transfers between devices, swap(): return lax.all_to_all(value, axes, split_axis=0, concat_axis=0, tiled=True)  32.5 us
    all_to_all x2, starting transfers between devices, swap(): return lax.all_to_all(value, axes, split_axis=0, concat_axis=0, tiled=True)  19.2 us
    ppermute x3, waiting for transfers between devices, to_peer(): lax.ppermute(value, 'hid', [(h, h ^ offset) for h in range(lax.axis_size(...  18.8 us
    all_gather x1, blocking collectives, shards(): active = lax.all_gather(active, 'hid', axis=0, tiled=False)  17 us
    pallas_call x10, Pallas kernels, call(): pl.pallas_call(kernel, out_shape=out_shapes, in_specs=[pl.BlockSpec(memor...  14.5 us
    ppermute x3, starting transfers between devices, to_peer(): lax.ppermute(value, 'hid', [(h, h ^ offset) for h in range(lax.axis_size(...  11.6 us
    ppermute x3, starting transfers between devices, other_core(): return lax.ppermute(value, 'core', [(0, 1), (1, 0)])  6.24 us
  transfers between devices with their start and end apart: 8, of which 6 were waited for; matrix products, arithmetic and copies ran while one was open for 0% of the time, Pallas kernels for 3%

profile of v17, /device:TPU:2, one launch (start us, length us, event | category | flops | bytes accessed | tf_op | source)
XLA Modules:
  0.0 197.8 jit_solution(10280003661304300537)
XLA Ops:
  0.0 0.0 copy-start
  0.0 0.9 pad_maximum_fusion.packed
  1.0 25.2 %all_to_all.30 = bf16[8,128,256]{2,1,0:T(8,128)(2,1)S(1)} all-to-all(bf16[8,128,256]{2,1,0:T(8,128)(2,1)S(1)} %broadcast_in_dim.2), channel_id=1, replica_groups=mesh['x'=4,'yh'=2,'core'=2,'exp'=8,'hid'=4] {'x','yh'}, dimensions={0} | all-to-all | bytes 1048576 | tf_op jit(solution)/shard_map/kv_gather/all_to_all | solution.py:25
  26.1 1.9 collective-permute-start
  28.0 0.1 pad_add_fusion.place
  28.1 0.0 copy-start.1
  28.1 0.0 copy-start.7
  28.1 0.0 copy-start.8
  28.1 1.8 collective-permute-done.far
  29.9 0.0 copy-done
  29.9 1.6 attention.1
  31.6 0.0 copy-start.3
  31.6 1.0 copy-done.3
  32.5 0.0 copy-start.5
  32.5 13.8 %all-to-all-start.1 = ((bf16[32,16,1024]{2,1,0:T(8,128)(2,1)}), bf16[32,16,1024]{2,1,0:T(8,128)(2,1)}, u32[]{:S(2)}, u32[]{:S(2)}) async-start(bf16[32,16,1024]{2,1,0:T(8,128)(2,1)} %bitcast.22), calls=%async_computation.1 | async-start | bytes 2097152 | tf_op jit(solution)/shard_map/projection/all_to_all | solution.py:25
  46.3 0.0 copy-done.1
  46.3 0.0 copy-done.7
  46.3 0.0 copy-done.8
  46.3 0.0 copy-start.2
  46.4 1.2 copy-done.2
  47.6 2.2 %prepare.1 = (bf16[48,16]{1,0:T(8,128)(2,1)S(1)}, f32[48,16]{1,0:T(8,128)S(1)}, bf16[1024,1024]{1,0:T(8,128)(2,1)}) custom-call(f32[8,128]{1,0:T(8,128)S(1)} %get-tuple-element.21.after, s32[2,16]{1,0:T(2,128)S(1)} %bitcast.25, f32[2,16]{1,0:T(2,128)S(1)} %bitcast.26, bf16[1024,512]{1,0:T(8,128)(2,1)S(1)} %bitcast.20, bf16[1024,512]{1,0:T(8,128)(2,1)S(1)} %bitcast.21), custom_call_target="tpu_custom_call" | custom-call | bytes 4203264 | tf_op jit(solution)/shard_map/prepare/pallas_call | solution.py:45
  49.8 1.9 collective-permute-start.1
  51.7 2.4 %collective-permute-start.2 = (bf16[512,1024]{1,0:T(8,128)(2,1)}, bf16[512,1024]{1,0:T(8,128)(2,1)S(1)}, u32[]{:S(2)}, u32[]{:S(2)}) collective-permute-start(bf16[512,1024]{1,0:T(8,128)(2,1)} %bitcast.10.near), channel_id=1, source_target_pairs={{0,32},{32,0},{1,33},{33,1},{2,34},{34,2},{3,35},{35,3},{4,36},{36... | collective-permute-start | bytes 3145736 | tf_op jit(solution)/shard_map/prepare/ppermute | solution.py:33
  54.1 19.8 %all-to-all-done.1.arrived = bf16[32,16,1024]{2,1,0:T(8,128)(2,1)} async-done(((bf16[32,16,1024]{2,1,0:T(8,128)(2,1)}), bf16[32,16,1024]{2,1,0:T(8,128)(2,1)}, u32[]{:S(2)}, u32[]{:S(2)}) %all-to-all-start.1) | async-done | bytes 1048608 | tf_op jit(solution)/shard_map/projection/all_to_all | solution.py:25
  73.9 0.0 copy-done.5
  73.9 1.5 projection.1
  75.5 0.0 copy-start.4
  75.5 0.7 copy-done.4
  76.2 5.4 %all-to-all-start.2 = ((bf16[16,6,1024]{2,1,0:T(8,128)(2,1)}), bf16[16,6,1024]{2,1,0:T(8,128)(2,1)S(1)}, u32[]{:S(2)}, u32[]{:S(2)}) async-start(bf16[16,6,1024]{2,1,0:T(8,128)(2,1)} %bitcast.23), calls=%async_computation.2 | async-start | bytes 524288 | tf_op jit(solution)/shard_map/dispatch/all_to_all | solution.py:25
  81.6 0.0 copy-start.6
  81.6 0.0 collective-permute-done.2.down.far
  81.6 0.0 collective-permute-done.1.weights.far
  81.6 12.7 %all-to-all-done.2.arrived = bf16[16,6,1024]{2,1,0:T(8,128)(2,1)S(1)} async-done(((bf16[16,6,1024]{2,1,0:T(8,128)(2,1)}), bf16[16,6,1024]{2,1,0:T(8,128)(2,1)S(1)}, u32[]{:S(2)}, u32[]{:S(2)}) %all-to-all-start.2) | async-done | bytes 196640 | tf_op jit(solution)/shard_map/dispatch/all_to_all | solution.py:25
  94.3 0.1 dispatch.1
  94.4 12.8 %all_to_all.31 = bf16[4,96,1024]{2,1,0:T(8,128)(2,1)S(1)} all-to-all(bf16[4,96,1024]{2,1,0:T(8,128)(2,1)S(1)} %dispatch.1), channel_id=1, replica_groups=mesh['x'=4,'yh'=2,'core'=2,'exp'=8,'hid'=4] {'x'}, dimensions={0} | all-to-all | bytes 1572864 | tf_op jit(solution)/shard_map/dispatch/all_to_all | solution.py:25
  107.2 0.0 copy-done.6
  107.2 2.6 %gate_up.3 = (bf16[400,512]{1,0:T(8,128)(2,1)S(1)}, bf16[384,1024]{1,0:T(8,128)(2,1)S(1)}, bf16[16,512]{1,0:T(8,128)(2,1)S(1)}) custom-call(s32[3]{0:T(128)S(1)} %pad_add_fusion.place, bf16[384,1024]{1,0:T(8,128)(2,1)S(1)} %bitcast.17, f32[1,1024]{1,0:T(1,128)S(1)} %bitcast.24, bf16[1024,1024]{1,0:T(8,128)(2,1)} %get-tuple-element.24.near, ...), custom_call_target="tpu_custom_call" | custom-call | flops 402653184 | bytes 6197260 | tf_op jit(solution)/shard_map/gate_up/pallas_call | solution.py:45
  109.8 3.5 %collective-permute-start.3 = (bf16[400,512]{1,0:T(8,128)(2,1)S(1)}, bf16[400,512]{1,0:T(8,128)(2,1)S(1)}, u32[]{:S(2)}, u32[]{:S(2)}) collective-permute-start(bf16[400,512]{1,0:T(8,128)(2,1)S(1)} %get-tuple-element.28), channel_id=1, source_target_pairs={{0,1},{1,0},{2,3},{3,2},{4,5},{5,4},{6,7},{7,6},{8,9},{9,8},{10,11... | collective-permute-start | bytes 1228808 | tf_op jit(solution)/shard_map/gate_up/ppermute | solution.py:37
  113.3 3.0 %gate_up.4 = (bf16[400,512]{1,0:T(8,128)(2,1)S(1)}, bf16[400,512]{1,0:T(8,128)(2,1)S(1)}, bf16[400,512]{1,0:T(8,128)(2,1)S(1)}) custom-call(s32[3]{0:T(128)S(1)} %pad_add_fusion.place, bf16[384,1024]{1,0:T(8,128)(2,1)S(1)} %get-tuple-element.25.scaled, bf16[16,512]{1,0:T(8,128)(2,1)S(1)} %get-tuple-element.26.tail, ...), custom_call_target="tpu_custom_call" | custom-call | flops 1207959552 | bytes 6225932 | tf_op jit(solution)/shard_map/gate_up/pallas_call | solution.py:45
  116.3 3.3 %collective-permute-done.3.arrived = bf16[400,512]{1,0:T(8,128)(2,1)S(1)} collective-permute-done((bf16[400,512]{1,0:T(8,128)(2,1)S(1)}, bf16[400,512]{1,0:T(8,128)(2,1)S(1)}, u32[]{:S(2)}, u32[]{:S(2)}) %collective-permute-start.3) | collective-permute-done | bytes 409632 | tf_op jit(solution)/shard_map/gate_up/ppermute | solution.py:37
  119.7 0.1 gate_up.5
  119.8 6.2 %collective-permute-start.4 = (bf16[400,512]{1,0:T(8,128)(2,1)S(1)}, bf16[400,512]{1,0:T(8,128)(2,1)S(1)}, u32[]{:S(2)}, u32[]{:S(2)}) collective-permute-start(bf16[400,512]{1,0:T(8,128)(2,1)S(1)} %get-tuple-element.30), channel_id=1, source_target_pairs={{0,2},{1,3},{2,0},{3,1},{4,6},{5,7},{6,4},{7,5},{8,10},{9,11},{10,... | collective-permute-start | bytes 1228808 | tf_op jit(solution)/shard_map/gate_up/ppermute | solution.py:37
  126.0 2.0 %collective-permute-start.5 = (bf16[400,512]{1,0:T(8,128)(2,1)S(1)}, bf16[400,512]{1,0:T(8,128)(2,1)S(1)}, u32[]{:S(2)}, u32[]{:S(2)}) collective-permute-start(bf16[400,512]{1,0:T(8,128)(2,1)S(1)} %get-tuple-element.31), channel_id=1, source_target_pairs={{0,1},{1,0},{2,3},{3,2},{4,5},{5,4},{6,7},{7,6},{8,9},{9,8},{10,11... | collective-permute-start | bytes 1228808 | tf_op jit(solution)/shard_map/gate_up/ppermute | solution.py:37
  128.0 12.6 %collective-permute-done.4.refs_0_ = bf16[400,512]{1,0:T(8,128)(2,1)S(1)} collective-permute-done((bf16[400,512]{1,0:T(8,128)(2,1)S(1)}, bf16[400,512]{1,0:T(8,128)(2,1)S(1)}, u32[]{:S(2)}, u32[]{:S(2)}) %collective-permute-start.4) | collective-permute-done | bytes 409632 | tf_op jit(solution)/shard_map/gate_up/ppermute | solution.py:37
  140.5 2.9 %collective-permute-done.5.refs_1_ = bf16[400,512]{1,0:T(8,128)(2,1)S(1)} collective-permute-done((bf16[400,512]{1,0:T(8,128)(2,1)S(1)}, bf16[400,512]{1,0:T(8,128)(2,1)S(1)}, u32[]{:S(2)}, u32[]{:S(2)}) %collective-permute-start.5) | collective-permute-done | bytes 409632 | tf_op jit(solution)/shard_map/gate_up/ppermute | solution.py:37
  143.4 0.3 active.1
  143.7 17.0 %all-gather = bf16[3072,128]{1,0:T(8,128)(2,1)S(1)} all-gather(bf16[768,128]{1,0:T(8,128)(2,1)S(1)} %active.1), channel_id=2, replica_groups=mesh['x'=4,'yh'=2,'core'=2,'exp'=8,'hid'=4] {'hid'}, dimensions={0}, use_global_device_ids=true | all-gather | bytes 983040 | tf_op jit(solution)/shard_map/active/all_gather | solution.py:324
  160.7 2.2 %down.1 = bf16[384,1024]{1,0:T(8,128)(2,1)S(1)} custom-call(bf16[4,768,128]{2,1,0:T(8,128)(2,1)S(1)} %bitcast.16, bf16[512,1024]{1,0:T(8,128)(2,1)} %bitcast.10.near, bf16[512,1024]{1,0:T(8,128)(2,1)S(1)} %collective-permute-done.2.down.far), custom_call_target="tpu_custom_call" | custom-call | flops 805306368 | bytes 3670016 | tf_op jit(solution)/shard_map/down/pallas_call | solution.py:45
  162.9 11.9 %all_to_all.32 = bf16[4,96,1024]{2,1,0:T(8,128)(2,1)S(1)} all-to-all(bf16[4,96,1024]{2,1,0:T(8,128)(2,1)S(1)} %bitcast.15), channel_id=1, replica_groups=mesh['x'=4,'yh'=2,'core'=2,'exp'=8,'hid'=4] {'x'}, dimensions={0} | all-to-all | bytes 1572864 | tf_op jit(solution)/shard_map/down/all_to_all | solution.py:25
  174.8 0.1 reduce_sum.12
  174.9 0.1 reshape.28
  175.0 21.9 %all_to_all.33.back = bf16[16,6,1024]{2,1,0:T(8,128)(2,1)S(1)} all-to-all(bf16[16,6,1024]{2,1,0:T(8,128)(2,1)S(1)} %reshape.28), channel_id=1, replica_groups=mesh['x'=4,'yh'=2,'core'=2,'exp'=8,'hid'=4] {'yh','exp'}, dimensions={0} | all-to-all | bytes 393216 | tf_op jit(solution)/shard_map/down/all_to_all | solution.py:25
  196.9 0.9 combine.1
  (2 shorter events, 0.0 us)
Async XLA Ops:
  0.0 29.9 %copy-start = (bf16[128,4096]{1,0:T(8,128)(2,1)S(1)}, bf16[128,4096]{1,0:T(8,128)(2,1)}, u32[]{:S(2)}) copy-start(bf16[128,4096]{1,0:T(8,128)(2,1)} %weight.1) | copy-start | bytes 3145732
  26.1 3.8 %collective-permute-start = (bf16[1024,256]{1,0:T(8,128)(2,1)S(1)}, bf16[1024,256]{1,0:T(8,128)(2,1)S(1)}, u32[]{:S(2)}, u32[]{:S(2)}) collective-permute-start(bf16[1024,256]{1,0:T(8,128)(2,1)S(1)} %bitcast.18), channel_id=1, source_target_pairs={{0,32},{32,0},{1,33},{33,1},{2,34},{34,2},{3,35},{35,3},{4,36},{36... | collective-permute-start | bytes 1572872 | tf_op jit(solution)/shard_map/kv_gather/ppermute | solution.py:33
  28.1 18.2 %copy-start.1 = (bf16[1,1024,512]{2,1,0:T(8,128)(2,1)S(1)}, bf16[1,1024,512]{2,1,0:T(8,128)(2,1)}, u32[]{:S(2)}) copy-start(bf16[1,1024,512]{2,1,0:T(8,128)(2,1)} %param.17) | copy-start | bytes 3145732
  28.1 18.2 %copy-start.7 = (s32[16,2]{0,1:T(2,128)S(1)}, s32[16,2]{0,1:T(2,128)}, u32[]{:S(2)}) copy-start(s32[16,2]{0,1:T(2,128)} %param.20) | copy-start | bytes 388
  28.1 18.2 %copy-start.8 = (f32[16,2]{0,1:T(2,128)S(1)}, f32[16,2]{0,1:T(2,128)}, u32[]{:S(2)}) copy-start(f32[16,2]{0,1:T(2,128)} %param.21) | copy-start | bytes 388
  31.6 1.0 copy-start.3
  32.5 41.4 %copy-start.5 = (bf16[16,1024]{1,0:T(8,128)(2,1)S(1)}, bf16[16,1024]{1,0:T(8,128)(2,1)}, u32[]{:S(2)}) copy-start(bf16[16,1024]{1,0:T(8,128)(2,1)} %residual.1) | copy-start | bytes 98308
  32.5 41.4 %all-to-all-start.1 = ((bf16[32,16,1024]{2,1,0:T(8,128)(2,1)}), bf16[32,16,1024]{2,1,0:T(8,128)(2,1)}, u32[]{:S(2)}, u32[]{:S(2)}) async-start(bf16[32,16,1024]{2,1,0:T(8,128)(2,1)} %bitcast.22), calls=%async_computation.1 | async-start | bytes 2097152 | tf_op jit(solution)/shard_map/projection/all_to_all | solution.py:25
  46.3 1.2 copy-start.2
  49.8 31.9 %collective-permute-start.1 = (bf16[1024,1024]{1,0:T(8,128)(2,1)}, bf16[1024,1024]{1,0:T(8,128)(2,1)S(1)}, u32[]{:S(2)}, u32[]{:S(2)}) collective-permute-start(bf16[1024,1024]{1,0:T(8,128)(2,1)} %get-tuple-element.24.near), channel_id=1, source_target_pairs={{0,32},{32,0},{1,33},{33,1},{2,34},{34,2},{3,35},{35,3},{4,36},{36... | collective-permute-start | bytes 6291464 | tf_op jit(solution)/shard_map/prepare/ppermute | solution.py:33
  51.7 29.9 %collective-permute-start.2 = (bf16[512,1024]{1,0:T(8,128)(2,1)}, bf16[512,1024]{1,0:T(8,128)(2,1)S(1)}, u32[]{:S(2)}, u32[]{:S(2)}) collective-permute-start(bf16[512,1024]{1,0:T(8,128)(2,1)} %bitcast.10.near), channel_id=1, source_target_pairs={{0,32},{32,0},{1,33},{33,1},{2,34},{34,2},{3,35},{35,3},{4,36},{36... | collective-permute-start | bytes 3145736 | tf_op jit(solution)/shard_map/prepare/ppermute | solution.py:33
  75.5 0.7 copy-start.4
  76.2 18.1 %all-to-all-start.2 = ((bf16[16,6,1024]{2,1,0:T(8,128)(2,1)}), bf16[16,6,1024]{2,1,0:T(8,128)(2,1)S(1)}, u32[]{:S(2)}, u32[]{:S(2)}) async-start(bf16[16,6,1024]{2,1,0:T(8,128)(2,1)} %bitcast.23), calls=%async_computation.2 | async-start | bytes 524288 | tf_op jit(solution)/shard_map/dispatch/all_to_all | solution.py:25
  81.6 25.6 %copy-start.6 = (f32[1024]{0:T(1024)S(1)}, f32[1024]{0:T(1024)}, u32[]{:S(2)}) copy-start(f32[1024]{0:T(1024)} %param.16) | copy-start | bytes 12292
  109.8 9.8 %collective-permute-start.3 = (bf16[400,512]{1,0:T(8,128)(2,1)S(1)}, bf16[400,512]{1,0:T(8,128)(2,1)S(1)}, u32[]{:S(2)}, u32[]{:S(2)}) collective-permute-start(bf16[400,512]{1,0:T(8,128)(2,1)S(1)} %get-tuple-element.28), channel_id=1, source_target_pairs={{0,1},{1,0},{2,3},{3,2},{4,5},{5,4},{6,7},{7,6},{8,9},{9,8},{10,11... | collective-permute-start | bytes 1228808 | tf_op jit(solution)/shard_map/gate_up/ppermute | solution.py:37
  119.8 20.8 %collective-permute-start.4 = (bf16[400,512]{1,0:T(8,128)(2,1)S(1)}, bf16[400,512]{1,0:T(8,128)(2,1)S(1)}, u32[]{:S(2)}, u32[]{:S(2)}) collective-permute-start(bf16[400,512]{1,0:T(8,128)(2,1)S(1)} %get-tuple-element.30), channel_id=1, source_target_pairs={{0,2},{1,3},{2,0},{3,1},{4,6},{5,7},{6,4},{7,5},{8,10},{9,11},{10,... | collective-permute-start | bytes 1228808 | tf_op jit(solution)/shard_map/gate_up/ppermute | solution.py:37
  126.0 17.4 %collective-permute-start.5 = (bf16[400,512]{1,0:T(8,128)(2,1)S(1)}, bf16[400,512]{1,0:T(8,128)(2,1)S(1)}, u32[]{:S(2)}, u32[]{:S(2)}) collective-permute-start(bf16[400,512]{1,0:T(8,128)(2,1)S(1)} %get-tuple-element.31), channel_id=1, source_target_pairs={{0,1},{1,0},{2,3},{3,2},{4,5},{5,4},{6,7},{7,6},{8,9},{9,8},{10,11... | collective-permute-start | bytes 1228808 | tf_op jit(solution)/shard_map/gate_up/ppermute | solution.py:37

commit v18 on v14

--- a/solution.py
+++ b/solution.py
@@ -79,10 +79,12 @@
         denom = denom + jnp.sum(weights, axis=1, keepdims=True)
         total = total + jnp.dot(weights.astype(BF16), source[:, HEAD:], preferred_element_type=F32)
     attended = (total / denom).astype(BF16)
-    parts, _, width = out.shape
+    blocks, parts, tokens, width = out.shape
     for part in range(parts):
         columns = weight[:, part * width : (part + 1) * width]
-        out[part] = jnp.dot(attended, columns, preferred_element_type=F32).astype(BF16)
+        product = jnp.dot(attended, columns, preferred_element_type=F32).astype(BF16)
+        for index in range(blocks):
+            out[index, part] = product[index * tokens : (index + 1) * tokens, :]
 
 
 def prepare_kernel(after, ids, shares, gate, up, selector, mixer, weights, sems):
@@ -266,7 +268,7 @@
         place = jnp.stack(place).astype(jnp.int32)
         partials, done = whole(
             attention_kernel,
-            [shape((hid_count, tok_rows, width_part), BF16), shape((8, 128), F32)],
+            [shape((exp_count, hid_count, row_count, width_part), BF16), shape((8, 128), F32)],
             flops=2 * tok_rows * HEAD * (4 * plane * tok_rows + D),
             smem=1,
         )(place, packed, near, far, out_weight)
@@ -284,7 +286,7 @@
         near_down = down_weight[0]
         far_weights, far_down = other_core(near_weights), other_core(near_down)
     with jax.named_scope("projection"):
-        arrived = swap(partials.reshape(hid_count * exp_count, row_count, width_part), ("hid", "exp"))
+        arrived = swap(partials.reshape(exp_count * hid_count, row_count, width_part), ("exp", "hid"))
         stream, outgoing = whole(
             select_kernel,
             [shape((row_count, width_part), F32), shape((halves, exp_count, CAP, width_part), BF16)],

time: 196 us -> 196 us (level)
  no operation moved by 1% of the time
where the time goes in v18:
time: 196 us
  blocking collectives  88 us (45%)
  waiting for transfers between devices  52.5 us (27%)
  starting transfers between devices  37.5 us (19%)
  Pallas kernels  12.8 us (7%)
  local copies, waits for them, and re-layouts  3.56 us (2%)
    all_to_all x4, blocking collectives, swap(): return lax.all_to_all(value, axes, split_axis=0, concat_axis=0, tiled=True)  69.8 us
    all_to_all x2, waiting for transfers between devices, swap(): return lax.all_to_all(value, axes, split_axis=0, concat_axis=0, tiled=True)  33.7 us
    all_to_all x2, starting transfers between devices, swap(): return lax.all_to_all(value, axes, split_axis=0, concat_axis=0, tiled=True)  18.4 us
    all_gather x1, blocking collectives, shards(): active = lax.all_gather(active, 'hid', axis=0, tiled=False)  18.2 us
    ppermute x3, waiting for transfers between devices, to_peer(): lax.ppermute(value, 'hid', [(h, h ^ offset) for h in range(lax.axis_size(...  17 us
    ppermute x3, starting transfers between devices, to_peer(): lax.ppermute(value, 'hid', [(h, h ^ offset) for h in range(lax.axis_size(...  13.3 us
    pallas_call x10, Pallas kernels, call(): pl.pallas_call(kernel, out_shape=out_shapes, in_specs=[pl.BlockSpec(memor...  12.8 us
    ppermute x3, starting transfers between devices, other_core(): return lax.ppermute(value, 'core', [(0, 1), (1, 0)])  5.75 us
  transfers between devices with their start and end apart: 8, of which 6 were waited for; matrix products, arithmetic and copies ran while one was open for 0% of the time, Pallas kernels for 3%

profile of v18, /device:TPU:2, one launch (start us, length us, event | category | flops | bytes accessed | tf_op | source)
XLA Modules:
  0.0 195.6 jit_solution(8122562241156049445)
XLA Ops:
  0.0 0.0 copy-start.1
  0.0 0.9 pad_maximum_fusion.packed
  1.0 25.2 %all_to_all.30 = bf16[8,128,256]{2,1,0:T(8,128)(2,1)S(1)} all-to-all(bf16[8,128,256]{2,1,0:T(8,128)(2,1)S(1)} %broadcast_in_dim.2), channel_id=1, replica_groups=mesh['x'=4,'yh'=2,'core'=2,'exp'=8,'hid'=4] {'x','yh'}, dimensions={0} | all-to-all | bytes 1048576 | tf_op jit(solution)/shard_map/kv_gather/all_to_all | solution.py:25
  26.1 1.9 collective-permute-start
  28.0 0.1 pad_add_fusion.place
  28.1 0.0 copy-start.7
  28.1 0.0 copy-start.8
  28.1 1.8 collective-permute-done.far
  29.9 0.0 copy-done.1
  29.9 1.6 attention.1
  31.6 0.0 copy-start.4
  31.6 1.0 copy-done.4
  32.5 0.0 copy-start.5
  32.5 13.6 %all-to-all-start.1 = ((bf16[32,16,1024]{2,1,0:T(8,128)(2,1)}), bf16[32,16,1024]{2,1,0:T(8,128)(2,1)S(1)}, u32[]{:S(2)}, u32[]{:S(2)}) async-start(bf16[32,16,1024]{2,1,0:T(8,128)(2,1)} %bitcast.24), calls=%async_computation.1 | async-start | bytes 2097152 | tf_op jit(solution)/shard_map/projection/all_to_all | solution.py:25
  46.2 0.0 copy-done.7
  46.2 0.0 copy-done.8
  46.2 0.0 copy-start.2
  46.2 1.2 copy-done.2
  47.4 0.0 copy-start.3
  47.4 1.2 copy-done.3
  48.7 2.2 %prepare.1 = (bf16[48,16]{1,0:T(8,128)(2,1)S(1)}, f32[48,16]{1,0:T(8,128)S(1)}, bf16[1024,1024]{1,0:T(8,128)(2,1)}) custom-call(f32[8,128]{1,0:T(8,128)S(1)} %get-tuple-element.21.after, s32[2,16]{1,0:T(2,128)S(1)} %bitcast.26, f32[2,16]{1,0:T(2,128)S(1)} %bitcast.27, bf16[1024,512]{1,0:T(8,128)(2,1)S(1)} %bitcast.22, bf16[1024,512]{1,0:T(8,128)(2,1)S(1)} %bitcast.23), custom_call_target="tpu_custom_call" | custom-call | bytes 4203264 | tf_op jit(solution)/shard_map/prepare/pallas_call | solution.py:45
  50.9 1.9 collective-permute-start.1
  52.8 21.0 %all-to-all-done.1.arrived = bf16[32,16,1024]{2,1,0:T(8,128)(2,1)S(1)} async-done(((bf16[32,16,1024]{2,1,0:T(8,128)(2,1)}), bf16[32,16,1024]{2,1,0:T(8,128)(2,1)S(1)}, u32[]{:S(2)}, u32[]{:S(2)}) %all-to-all-start.1) | async-done | bytes 1048608 | tf_op jit(solution)/shard_map/projection/all_to_all | solution.py:25
  73.8 0.0 copy-done.5
  73.8 1.0 projection.1
  74.8 4.8 %all-to-all-start.2 = ((bf16[16,6,1024]{2,1,0:T(8,128)(2,1)}), bf16[16,6,1024]{2,1,0:T(8,128)(2,1)S(1)}, u32[]{:S(2)}, u32[]{:S(2)}) async-start(bf16[16,6,1024]{2,1,0:T(8,128)(2,1)} %bitcast.9), calls=%async_computation.2 | async-start | bytes 524288 | tf_op jit(solution)/shard_map/dispatch/all_to_all | solution.py:25
  79.6 0.0 copy-start.6
  79.6 0.0 collective-permute-done.1.weights.far
  79.6 12.6 %all-to-all-done.2.arrived = bf16[16,6,1024]{2,1,0:T(8,128)(2,1)S(1)} async-done(((bf16[16,6,1024]{2,1,0:T(8,128)(2,1)}), bf16[16,6,1024]{2,1,0:T(8,128)(2,1)S(1)}, u32[]{:S(2)}, u32[]{:S(2)}) %all-to-all-start.2) | async-done | bytes 196640 | tf_op jit(solution)/shard_map/dispatch/all_to_all | solution.py:25
  92.3 0.1 dispatch.1
  92.3 12.4 %all_to_all.31 = bf16[4,96,1024]{2,1,0:T(8,128)(2,1)S(1)} all-to-all(bf16[4,96,1024]{2,1,0:T(8,128)(2,1)S(1)} %dispatch.1), channel_id=1, replica_groups=mesh['x'=4,'yh'=2,'core'=2,'exp'=8,'hid'=4] {'x'}, dimensions={0} | all-to-all | bytes 1572864 | tf_op jit(solution)/shard_map/dispatch/all_to_all | solution.py:25
  104.7 0.0 copy-done.6
  104.7 0.0 copy-start
  104.7 2.6 %gate_up.3 = (bf16[400,512]{1,0:T(8,128)(2,1)S(1)}, bf16[384,1024]{1,0:T(8,128)(2,1)S(1)}, bf16[16,512]{1,0:T(8,128)(2,1)S(1)}) custom-call(s32[3]{0:T(128)S(1)} %pad_add_fusion.place, bf16[384,1024]{1,0:T(8,128)(2,1)S(1)} %bitcast.17, f32[1,1024]{1,0:T(1,128)S(1)} %bitcast.25, bf16[1024,1024]{1,0:T(8,128)(2,1)} %get-tuple-element.24.near, ...), custom_call_target="tpu_custom_call" | custom-call | flops 402653184 | bytes 6197260 | tf_op jit(solution)/shard_map/gate_up/pallas_call | solution.py:45
  107.3 4.8 %collective-permute-start.2 = (bf16[400,512]{1,0:T(8,128)(2,1)S(1)}, bf16[400,512]{1,0:T(8,128)(2,1)S(1)}, u32[]{:S(2)}, u32[]{:S(2)}) collective-permute-start(bf16[400,512]{1,0:T(8,128)(2,1)S(1)} %get-tuple-element.28), channel_id=1, source_target_pairs={{0,1},{1,0},{2,3},{3,2},{4,5},{5,4},{6,7},{7,6},{8,9},{9,8},{10,11... | collective-permute-start | bytes 1228808 | tf_op jit(solution)/shard_map/gate_up/ppermute | solution.py:37
  112.1 0.0 copy-done
  112.1 1.9 collective-permute-start.5
  114.1 3.0 %gate_up.4 = (bf16[400,512]{1,0:T(8,128)(2,1)S(1)}, bf16[400,512]{1,0:T(8,128)(2,1)S(1)}, bf16[400,512]{1,0:T(8,128)(2,1)S(1)}) custom-call(s32[3]{0:T(128)S(1)} %pad_add_fusion.place, bf16[384,1024]{1,0:T(8,128)(2,1)S(1)} %get-tuple-element.25.scaled, bf16[16,512]{1,0:T(8,128)(2,1)S(1)} %get-tuple-element.26.tail, ...), custom_call_target="tpu_custom_call" | custom-call | flops 1207959552 | bytes 6225932 | tf_op jit(solution)/shard_map/gate_up/pallas_call | solution.py:45
  117.1 0.9 collective-permute-done.2.arrived
  118.0 0.1 gate_up.5
  118.1 6.3 %collective-permute-start.3 = (bf16[400,512]{1,0:T(8,128)(2,1)S(1)}, bf16[400,512]{1,0:T(8,128)(2,1)S(1)}, u32[]{:S(2)}, u32[]{:S(2)}) collective-permute-start(bf16[400,512]{1,0:T(8,128)(2,1)S(1)} %get-tuple-element.30), channel_id=1, source_target_pairs={{0,2},{1,3},{2,0},{3,1},{4,6},{5,7},{6,4},{7,5},{8,10},{9,11},{10,... | collective-permute-start | bytes 1228808 | tf_op jit(solution)/shard_map/gate_up/ppermute | solution.py:37
  124.5 2.2 %collective-permute-start.4 = (bf16[400,512]{1,0:T(8,128)(2,1)S(1)}, bf16[400,512]{1,0:T(8,128)(2,1)S(1)}, u32[]{:S(2)}, u32[]{:S(2)}) collective-permute-start(bf16[400,512]{1,0:T(8,128)(2,1)S(1)} %get-tuple-element.31), channel_id=1, source_target_pairs={{0,1},{1,0},{2,3},{3,2},{4,5},{5,4},{6,7},{7,6},{8,9},{9,8},{10,11... | collective-permute-start | bytes 1228808 | tf_op jit(solution)/shard_map/gate_up/ppermute | solution.py:37
  126.7 14.1 %collective-permute-done.3.refs_0_ = bf16[400,512]{1,0:T(8,128)(2,1)S(1)} collective-permute-done((bf16[400,512]{1,0:T(8,128)(2,1)S(1)}, bf16[400,512]{1,0:T(8,128)(2,1)S(1)}, u32[]{:S(2)}, u32[]{:S(2)}) %collective-permute-start.3) | collective-permute-done | bytes 409632 | tf_op jit(solution)/shard_map/gate_up/ppermute | solution.py:37
  140.8 2.0 %collective-permute-done.4.refs_1_ = bf16[400,512]{1,0:T(8,128)(2,1)S(1)} collective-permute-done((bf16[400,512]{1,0:T(8,128)(2,1)S(1)}, bf16[400,512]{1,0:T(8,128)(2,1)S(1)}, u32[]{:S(2)}, u32[]{:S(2)}) %collective-permute-start.4) | collective-permute-done | bytes 409632 | tf_op jit(solution)/shard_map/gate_up/ppermute | solution.py:37
  142.8 0.3 active.1
  143.0 18.2 %all-gather = bf16[3072,128]{1,0:T(8,128)(2,1)S(1)} all-gather(bf16[768,128]{1,0:T(8,128)(2,1)S(1)} %active.1), channel_id=2, replica_groups=mesh['x'=4,'yh'=2,'core'=2,'exp'=8,'hid'=4] {'hid'}, dimensions={0}, use_global_device_ids=true | all-gather | bytes 983040 | tf_op jit(solution)/shard_map/active/all_gather | solution.py:326
  161.2 0.0 collective-permute-done.5.far
  161.2 1.0 down.1
  162.2 11.9 %all_to_all.32 = bf16[4,96,1024]{2,1,0:T(8,128)(2,1)S(1)} all-to-all(bf16[4,96,1024]{2,1,0:T(8,128)(2,1)S(1)} %bitcast.15), channel_id=1, replica_groups=mesh['x'=4,'yh'=2,'core'=2,'exp'=8,'hid'=4] {'x'}, dimensions={0} | all-to-all | bytes 1572864 | tf_op jit(solution)/shard_map/down/all_to_all | solution.py:25
  174.1 0.1 reduce_sum.12
  174.3 0.1 reshape.28
  174.3 20.4 %all_to_all.33.back = bf16[16,6,1024]{2,1,0:T(8,128)(2,1)S(1)} all-to-all(bf16[16,6,1024]{2,1,0:T(8,128)(2,1)S(1)} %reshape.28), channel_id=1, replica_groups=mesh['x'=4,'yh'=2,'core'=2,'exp'=8,'hid'=4] {'yh','exp'}, dimensions={0} | all-to-all | bytes 393216 | tf_op jit(solution)/shard_map/down/all_to_all | solution.py:25
  194.7 0.9 combine.1
  (2 shorter events, 0.0 us)
Async XLA Ops:
  0.0 29.9 %copy-start.1 = (bf16[128,4096]{1,0:T(8,128)(2,1)S(1)}, bf16[128,4096]{1,0:T(8,128)(2,1)}, u32[]{:S(2)}) copy-start(bf16[128,4096]{1,0:T(8,128)(2,1)} %weight.1) | copy-start | bytes 3145732
  26.1 3.8 %collective-permute-start = (bf16[1024,256]{1,0:T(8,128)(2,1)S(1)}, bf16[1024,256]{1,0:T(8,128)(2,1)S(1)}, u32[]{:S(2)}, u32[]{:S(2)}) collective-permute-start(bf16[1024,256]{1,0:T(8,128)(2,1)S(1)} %bitcast.18), channel_id=1, source_target_pairs={{0,32},{32,0},{1,33},{33,1},{2,34},{34,2},{3,35},{35,3},{4,36},{36... | collective-permute-start | bytes 1572872 | tf_op jit(solution)/shard_map/kv_gather/ppermute | solution.py:33
  28.1 18.1 %copy-start.7 = (s32[16,2]{0,1:T(2,128)S(1)}, s32[16,2]{0,1:T(2,128)}, u32[]{:S(2)}) copy-start(s32[16,2]{0,1:T(2,128)} %param.20) | copy-start | bytes 388
  28.1 18.1 %copy-start.8 = (f32[16,2]{0,1:T(2,128)S(1)}, f32[16,2]{0,1:T(2,128)}, u32[]{:S(2)}) copy-start(f32[16,2]{0,1:T(2,128)} %param.21) | copy-start | bytes 388
  31.6 1.0 copy-start.4
  32.5 41.3 %copy-start.5 = (bf16[16,1024]{1,0:T(8,128)(2,1)S(1)}, bf16[16,1024]{1,0:T(8,128)(2,1)}, u32[]{:S(2)}) copy-start(bf16[16,1024]{1,0:T(8,128)(2,1)} %residual.1) | copy-start | bytes 98308
  32.5 41.3 %all-to-all-start.1 = ((bf16[32,16,1024]{2,1,0:T(8,128)(2,1)}), bf16[32,16,1024]{2,1,0:T(8,128)(2,1)S(1)}, u32[]{:S(2)}, u32[]{:S(2)}) async-start(bf16[32,16,1024]{2,1,0:T(8,128)(2,1)} %bitcast.24), calls=%async_computation.1 | async-start | bytes 2097152 | tf_op jit(solution)/shard_map/projection/all_to_all | solution.py:25
  46.2 1.2 copy-start.2
  47.4 1.2 copy-start.3
  50.9 28.8 %collective-permute-start.1 = (bf16[1024,1024]{1,0:T(8,128)(2,1)}, bf16[1024,1024]{1,0:T(8,128)(2,1)S(1)}, u32[]{:S(2)}, u32[]{:S(2)}) collective-permute-start(bf16[1024,1024]{1,0:T(8,128)(2,1)} %get-tuple-element.24.near), channel_id=1, source_target_pairs={{0,32},{32,0},{1,33},{33,1},{2,34},{34,2},{3,35},{35,3},{4,36},{36... | collective-permute-start | bytes 6291464 | tf_op jit(solution)/shard_map/prepare/ppermute | solution.py:33
  74.8 17.5 %all-to-all-start.2 = ((bf16[16,6,1024]{2,1,0:T(8,128)(2,1)}), bf16[16,6,1024]{2,1,0:T(8,128)(2,1)S(1)}, u32[]{:S(2)}, u32[]{:S(2)}) async-start(bf16[16,6,1024]{2,1,0:T(8,128)(2,1)} %bitcast.9), calls=%async_computation.2 | async-start | bytes 524288 | tf_op jit(solution)/shard_map/dispatch/all_to_all | solution.py:25
  79.6 25.1 %copy-start.6 = (f32[1024]{0:T(1024)S(1)}, f32[1024]{0:T(1024)}, u32[]{:S(2)}) copy-start(f32[1024]{0:T(1024)} %param.16) | copy-start | bytes 12292
  104.7 7.4 %copy-start = (bf16[1,512,1024]{2,1,0:T(8,128)(2,1)S(1)}, bf16[1,512,1024]{2,1,0:T(8,128)(2,1)}, u32[]{:S(2)}) copy-start(bf16[1,512,1024]{2,1,0:T(8,128)(2,1)} %param.19) | copy-start | bytes 3145732
  107.3 10.7 %collective-permute-start.2 = (bf16[400,512]{1,0:T(8,128)(2,1)S(1)}, bf16[400,512]{1,0:T(8,128)(2,1)S(1)}, u32[]{:S(2)}, u32[]{:S(2)}) collective-permute-start(bf16[400,512]{1,0:T(8,128)(2,1)S(1)} %get-tuple-element.28), channel_id=1, source_target_pairs={{0,1},{1,0},{2,3},{3,2},{4,5},{5,4},{6,7},{7,6},{8,9},{9,8},{10,11... | collective-permute-start | bytes 1228808 | tf_op jit(solution)/shard_map/gate_up/ppermute | solution.py:37
  112.1 49.1 %collective-permute-start.5 = (bf16[512,1024]{1,0:T(8,128)(2,1)S(1)}, bf16[512,1024]{1,0:T(8,128)(2,1)S(1)}, u32[]{:S(2)}, u32[]{:S(2)}) collective-permute-start(bf16[512,1024]{1,0:T(8,128)(2,1)S(1)} %bitcast.20), channel_id=1, source_target_pairs={{0,32},{32,0},{1,33},{33,1},{2,34},{34,2},{3,35},{35,3},{4,36},{36... | collective-permute-start | bytes 3145736 | tf_op jit(solution)/shard_map/prepare/ppermute | solution.py:33
  118.1 22.6 %collective-permute-start.3 = (bf16[400,512]{1,0:T(8,128)(2,1)S(1)}, bf16[400,512]{1,0:T(8,128)(2,1)S(1)}, u32[]{:S(2)}, u32[]{:S(2)}) collective-permute-start(bf16[400,512]{1,0:T(8,128)(2,1)S(1)} %get-tuple-element.30), channel_id=1, source_target_pairs={{0,2},{1,3},{2,0},{3,1},{4,6},{5,7},{6,4},{7,5},{8,10},{9,11},{10,... | collective-permute-start | bytes 1228808 | tf_op jit(solution)/shard_map/gate_up/ppermute | solution.py:37
  124.5 18.3 %collective-permute-start.4 = (bf16[400,512]{1,0:T(8,128)(2,1)S(1)}, bf16[400,512]{1,0:T(8,128)(2,1)S(1)}, u32[]{:S(2)}, u32[]{:S(2)}) collective-permute-start(bf16[400,512]{1,0:T(8,128)(2,1)S(1)} %get-tuple-element.31), channel_id=1, source_target_pairs={{0,1},{1,0},{2,3},{3,2},{4,5},{5,4},{6,7},{7,6},{8,9},{9,8},{10,11... | collective-permute-start | bytes 1228808 | tf_op jit(solution)/shard_map/gate_up/ppermute | solution.py:37
